TPU v7x, 128 devices: a whole 4x4x4 slice. The times are simulated.
128 devices in a mesh: mp: 8 (over z, core), dp: 16 (over y, x).
Axes of the slice: x: 4, y: 4, z: 4, core: 2. Of those that a mesh axis runs over, the one named last changes fastest.
Arguments:
- token_ids: int32 [16, 1024], P('dp'), may hold values from 0 to 49151
- targets: int32 [16, 256], replicated, may hold values from 0 to 49151
- loss_rows: int32 [16, 256], P('dp'), may hold values from 0 to 1023, as said below
- selections: int32 [3, 16, 1024], replicated, may hold values from 0 to 1, as said below
- boundary: int32 [16], replicated, may hold values from 0 to 768, as said below
- pack_master: float32 [2463360], P(('mp', 'dp')), may hold values from -2 to 2
- pack_first: float32 [2463360], P(('mp', 'dp')), may hold values from -0.00021362305 to 0.00021362305
- pack_second: float32 [2463360], P(('mp', 'dp')), may hold values from 9.294645e-10 to 3.6827839e-09
- mlp_master: float32 [3, 2560, 960], P(None, ('mp', 'dp')), may hold values from -1 to 1
- mlp_first: float32 [3, 2560, 960], P(None, ('mp', 'dp')), may hold values from -0.00021362305 to 0.00021362305
- mlp_second: float32 [3, 2560, 960], P(None, ('mp', 'dp')), may hold values from 9.294645e-10 to 3.6827839e-09
- table_master: float32 [49152, 960], P(('mp', 'dp')), may hold values from -0.387298335 to 0.387298335
- table_first: float32 [49152, 960], P(('mp', 'dp')), may hold values from -0.00021362305 to 0.00021362305
- table_second: float32 [49152, 960], P(('mp', 'dp')), may hold values from 9.294645e-10 to 3.6827839e-09
Outputs:
- pack_new: float32 [2463360], P(('mp', 'dp'))
- pack_first_new: float32 [2463360], P(('mp', 'dp'))
- pack_second_new: float32 [2463360], P(('mp', 'dp'))
- mlp_new: float32 [3, 2560, 960], P(None, ('mp', 'dp'))
- mlp_first_new: float32 [3, 2560, 960], P(None, ('mp', 'dp'))
- mlp_second_new: float32 [3, 2560, 960], P(None, ('mp', 'dp'))
- table_new: float32 [49152, 960], P(('mp', 'dp'))
- table_first_new: float32 [49152, 960], P(('mp', 'dp'))
- table_second_new: float32 [49152, 960], P(('mp', 'dp'))
- loss_sum: float32 [], replicated
- grad_norm: float32 [], replicated
Inputs may be any that keep to these rules, and one draw needn't show every extreme that they name: `loss_rows`: sorted distinct rows of the group, 256 of them. `selections`: the selection of each recursion is contained in that of the recursion before. boundary[0] is 0; every other entry lies between 256 and 768.
All inputs are finite; a program needn't handle non-finite values.
Results may differ from a plain program's by a relative error of at most 0.018.
Values may be sent and summed in bfloat16 or wider, within the bound.
No kernel may reach another device: no remote copies, remote signals or barrier semaphores. Data moves between devices by JAX's collectives and lax.ppermute only.
A program may use at most 320 MiB of HBM per device.

v0:
```python
import jax
import jax.numpy as jnp
from jax import lax
from jax.sharding import PartitionSpec as P

D = 960
HEADS = 15
KV_HEADS = 5
HEAD_DIM = 64
RECUR = 3
STEP = 10
TOK_DEV = 128


EPS_NORM = 1e-05
ROPE_BASE = 10000.0
ROUTER_LOSS = 0.1
CLIP_NORM = 1.0
LEARN_RATE = 0.05
BETA_ONE = 0.9
BETA_TWO = 0.95
ADAM_EPS = 1e-08
DECAY = 0.1
MASKED = -1e30
HIGHEST = lax.Precision.HIGHEST
BFLOAT = jnp.bfloat16
FLOAT = jnp.float32


def from_behind(value, axis, steps):
    count = lax.axis_size(axis)
    leading, last = (max(0, -steps), min(count, count - steps))
    return lax.ppermute(value, axis, [(source, source + steps) for source in range(leading, last)])


def joined(part, axis, combine):
    gathered = jax.tree.map(lambda a: lax.all_gather(a, axis), part)

    def take(source):
        return jax.tree.map(lambda a: lax.dynamic_index_in_dim(a, source, 0, False), gathered)

    return lax.fori_loop(
        1, lax.axis_size(axis), lambda source, state: combine(state, take(source)), take(0)
    )


def rms_scale(values, weight):
    return values * lax.rsqrt(jnp.mean(values * values, axis=-1, keepdims=True) + EPS_NORM) * weight


def rms_back(values, weight, grad_out):
    inverse = lax.rsqrt(jnp.mean(values * values, axis=-1, keepdims=True) + EPS_NORM)
    weighted = grad_out * weight
    grad_values = inverse * weighted - values * (inverse * inverse * inverse) * jnp.mean(
        weighted * values, axis=-1, keepdims=True
    )
    return (grad_values, jnp.sum(grad_out * values * inverse, axis=0))


def rotate(values, positions):
    half = HEAD_DIM // 2
    freqs = ROPE_BASE ** (-jnp.arange(half, dtype=FLOAT) / half)
    angles = positions.astype(FLOAT)[:, None] * freqs[None, :]
    cosine = jnp.cos(angles)[:, None, :]
    sine = jnp.sin(angles)[:, None, :]
    first = values[..., :half]
    second = values[..., half:]
    return jnp.concatenate(
        [first * cosine - second * sine, second * cosine + first * sine], axis=-1
    )


def unpack(packed):
    query_cols = HEADS * HEAD_DIM
    kv_cols = KV_HEADS * HEAD_DIM
    shapes = [(D, query_cols), (D, kv_cols), (D, kv_cols), (query_cols, D), (3, D), (RECUR, D)]
    pieces = []
    offset = 0
    for piece_shape in shapes:
        length = piece_shape[0] * piece_shape[1]
        pieces.append(packed[offset : offset + length].reshape(piece_shape))
        offset = offset + length
    return pieces


def doc_ids(rows, boundary, group_rows):
    group = jnp.floor_divide(rows, group_rows)
    start = boundary[jnp.clip(group, 0, boundary.shape[0] - 1)]
    return group - (rows - group * group_rows < start).astype(jnp.int32)


def visible(query_rows, key_rows, key_sel, boundary, group_rows):
    same = (
        doc_ids(query_rows, boundary, group_rows)[:, None]
        == doc_ids(key_rows, boundary, group_rows)[None, :]
    )
    earlier = key_rows[None, :] <= query_rows[:, None]
    picked = (key_sel[None, :] > 0) | (key_rows[None, :] == query_rows[:, None])
    return same & earlier & picked & (key_rows[None, :] >= 0)


def contract_rows(left, right):
    return lax.dot_general(left, right, (((0,), (0,)), ((), ())), preferred_element_type=FLOAT)


def contract_cols(left, right):
    return lax.dot_general(left, right, (((1,), (1,)), ((), ())), preferred_element_type=FLOAT)


def join_stats(first_stats, second_stats):
    top = jnp.maximum(first_stats[0], second_stats[0])
    total = first_stats[1] * jnp.exp(first_stats[0] - top) + second_stats[1] * jnp.exp(
        second_stats[0] - top
    )
    return (top, total, first_stats[2] + second_stats[2])


def adam_update(master, first, second, grad, clip):
    grad = grad * clip
    first_new = BETA_ONE * first + (1.0 - BETA_ONE) * grad
    second_new = BETA_TWO * second + (1.0 - BETA_TWO) * grad * grad
    corr_one = 1.0 - BETA_ONE**STEP
    corr_two = 1.0 - BETA_TWO**STEP
    master_new = master - LEARN_RATE * (
        first_new / corr_one / (jnp.sqrt(second_new / corr_two) + ADAM_EPS) + DECAY * master
    )
    return (master_new, first_new, second_new)


def gather_rows(values):
    return lax.all_gather(values, "mp", axis=0, tiled=True)


def sum_rows(values):
    return lax.psum_scatter(values, "mp", scatter_dimension=0, tiled=True)


def shards(
    token_ids,
    targets,
    loss_rows,
    selections,
    boundary,
    pack_master,
    pack_first,
    pack_second,
    mlp_master,
    mlp_first,
    mlp_second,
    table_master,
    table_first,
    table_second,
):
    model_count = lax.axis_size("mp")
    model_index = lax.axis_index("mp")
    data_index = lax.axis_index("dp")
    group_rows = token_ids.shape[1]
    own_rows = group_rows // model_count
    groups_per = HEADS // KV_HEADS
    scale = HEAD_DIM ** (-0.5)
    pack_weights = lax.all_gather(pack_master.astype(BFLOAT), ("mp", "dp"), axis=0, tiled=True)
    mlp_weights, table = (
        lax.all_gather(mlp_master.astype(BFLOAT), "dp", axis=1, tiled=True),
        lax.all_gather(table_master.astype(BFLOAT), "dp", axis=0, tiled=True),
    )
    w_query, w_key, w_value, w_out, gains_low, router_low = unpack(pack_weights)
    gains = gains_low.astype(FLOAT)
    router = router_low.astype(FLOAT)
    gate_w = mlp_weights[0]
    up_w = mlp_weights[1]
    down_w = mlp_weights[2]
    vocab_local = table.shape[0]
    first_row = data_index * group_rows + model_index * own_rows
    query_rows = first_row + jnp.arange(own_rows, dtype=jnp.int32)
    key_rows = (data_index - 1) * group_rows + jnp.arange(2 * group_rows, dtype=jnp.int32)
    flat_sel = selections.reshape(RECUR, -1)
    own_sel = lax.dynamic_slice_in_dim(flat_sel, first_row, own_rows, axis=1)
    key_sel = jnp.take(flat_sel, jnp.clip(key_rows, 0), axis=1)
    masks = [
        visible(query_rows, key_rows, key_sel[step], boundary, group_rows) for step in range(RECUR)
    ]

    def attention_scores(queries, keys_cat, mask):
        grouped_q = queries.reshape(own_rows, KV_HEADS, groups_per, HEAD_DIM)
        scores = (
            jnp.einsum("tkgd,skd->kgts", grouped_q, keys_cat, preferred_element_type=FLOAT) * scale
        )
        return jnp.where(mask[None, None], scores, MASKED)

    def split_pair(key_pair):
        return (
            key_pair[:, 0].reshape(-1, KV_HEADS, HEAD_DIM),
            key_pair[:, 1].reshape(-1, KV_HEADS, HEAD_DIM),
        )

    group_ids = token_ids[0]
    local_ids = group_ids - model_index * vocab_local
    inside = ((local_ids >= 0) & (local_ids < vocab_local)).astype(FLOAT)
    clipped_ids = jnp.clip(local_ids, 0, vocab_local - 1)
    looked = jnp.take(table, clipped_ids, axis=0).astype(FLOAT) * inside[:, None]
    hidden = sum_rows(looked)
    saves = []
    penalty_total = jnp.zeros((), FLOAT)
    for step in range(RECUR):
        forward_normed = rms_scale(hidden, gains[0]).astype(BFLOAT)
        forward_queries = rotate(
            jnp.dot(forward_normed, w_query, preferred_element_type=FLOAT).reshape(
                own_rows, HEADS, HEAD_DIM
            ),
            query_rows,
        ).astype(BFLOAT)
        keys_own = rotate(
            jnp.dot(forward_normed, w_key, preferred_element_type=FLOAT).reshape(
                own_rows, KV_HEADS, HEAD_DIM
            ),
            query_rows,
        ).astype(BFLOAT)
        values_own = jnp.dot(forward_normed, w_value, preferred_element_type=FLOAT).astype(BFLOAT)
        pair = jnp.stack([keys_own.reshape(own_rows, -1), values_own], axis=1)
        group_pair = lax.all_gather(pair, "mp", axis=0, tiled=True)
        prev_pair = from_behind(group_pair, "dp", 1)
        forward_key_pair = jnp.concatenate([prev_pair, group_pair], axis=0)
        forward_keys_cat, forward_values_cat = split_pair(forward_key_pair)
        forward_scores = attention_scores(forward_queries, forward_keys_cat, masks[step])
        forward_top = jnp.max(forward_scores, axis=-1, keepdims=True)
        expo = jnp.exp(forward_scores - forward_top)
        total = jnp.sum(expo, axis=-1, keepdims=True)
        forward_probs = (expo / total).astype(BFLOAT)
        forward_log_total = forward_top + jnp.log(total)
        forward_attended = (
            jnp.einsum(
                "kgts,skd->tkgd", forward_probs, forward_values_cat, preferred_element_type=FLOAT
            )
            .astype(BFLOAT)
            .reshape(own_rows, HEADS * HEAD_DIM)
        )
        forward_mixed = hidden + jnp.dot(forward_attended, w_out, preferred_element_type=FLOAT)
        normed_two = rms_scale(forward_mixed, gains[1]).astype(BFLOAT)
        forward_mlp_input = gather_rows(normed_two)
        forward_gate_pre = contract_cols(forward_mlp_input, gate_w)
        forward_up_pre = contract_cols(forward_mlp_input, up_w)
        forward_inner = (jax.nn.silu(forward_gate_pre) * forward_up_pre).astype(BFLOAT)
        forward_branch = forward_mixed + sum_rows(
            jnp.dot(forward_inner, down_w, preferred_element_type=FLOAT)
        )
        forward_logit = jnp.dot(hidden, router[step], precision=HIGHEST)
        forward_chosen = own_sel[step].astype(FLOAT)
        forward_weight_sel = forward_chosen * jax.nn.sigmoid(forward_logit)
        new_hidden = hidden + forward_weight_sel[:, None] * (forward_branch - hidden)
        penalty = jnp.sum(jax.nn.softplus(forward_logit) - forward_chosen * forward_logit)
        forward_saved = (
            hidden,
            forward_normed,
            forward_queries,
            forward_key_pair,
            forward_log_total,
            forward_attended,
            forward_mixed,
            forward_mlp_input,
            forward_gate_pre,
            forward_up_pre,
            forward_inner,
            forward_branch,
            forward_logit,
        )
        hidden, saved, penalty = (new_hidden, forward_saved, penalty)
        saves.append(saved)
        penalty_total = penalty_total + penalty
    normed_final = rms_scale(hidden, gains[2]).astype(BFLOAT)
    final_rows = gather_rows(normed_final)
    picked = jnp.take(final_rows, loss_rows[0], axis=0)
    row_targets = lax.dynamic_index_in_dim(targets, data_index, 0, keepdims=False)
    shard_start = model_index * vocab_local
    logits = contract_cols(picked, table)
    local_targets = row_targets - shard_start
    onehot = (
        jnp.arange(table.shape[0], dtype=jnp.int32)[None, :] == local_targets[:, None]
    ).astype(FLOAT)
    local_top = jnp.max(logits, axis=-1)
    stats = (
        local_top,
        jnp.sum(jnp.exp(logits - local_top[:, None]), axis=-1),
        jnp.sum(logits * onehot, axis=-1),
    )
    top, exp_sum, target_sum = joined(stats, "mp", join_stats)
    log_norm = top + jnp.log(exp_sum)
    cross = log_norm - target_sum
    per_device = cross.shape[0] // model_count
    loss_part = (
        jnp.sum(lax.dynamic_slice_in_dim(cross, model_index * per_device, per_device))
        + ROUTER_LOSS * penalty_total
    )
    grad_logits = ((jnp.exp(logits - log_norm[:, None]) - onehot) * (1.0 / TOK_DEV)).astype(BFLOAT)
    head_grad = contract_rows(grad_logits, picked)
    grad_head_rows = jnp.dot(grad_logits, table, preferred_element_type=FLOAT)
    scattered = jnp.zeros((group_rows, D), FLOAT).at[loss_rows[0]].add(grad_head_rows)
    grad_hidden, grad_gain_final = rms_back(hidden, gains[2], sum_rows(scattered))
    totals = None
    router_rows = [None] * RECUR
    for step in reversed(range(RECUR)):
        grad_new = grad_hidden
        backward_saved = saves[step]
        (
            backward_hidden,
            normed,
            backward_queries,
            backward_key_pair,
            log_total,
            attended,
            mixed,
            mlp_input,
            gate_pre,
            up_pre,
            inner,
            branch,
            logit,
        ) = backward_saved
        chosen = own_sel[step].astype(FLOAT)
        sigma = jax.nn.sigmoid(logit)
        weight_sel = chosen * sigma
        grad_branch = weight_sel[:, None] * grad_new
        grad_weight = jnp.sum(grad_new * (branch - backward_hidden), axis=-1)
        grad_logit = grad_weight * chosen * sigma * (1.0 - sigma) + ROUTER_LOSS / TOK_DEV * (
            sigma - chosen
        )
        backward_grad_hidden = (
            grad_new - weight_sel[:, None] * grad_new + grad_logit[:, None] * router[step][None, :]
        )
        grad_router = jnp.dot(grad_logit, backward_hidden, precision=HIGHEST)
        grad_rows = gather_rows(grad_branch.astype(BFLOAT))
        grad_down = contract_rows(inner, grad_rows)
        grad_inner = contract_cols(grad_rows, down_w)
        sigma_gate = jax.nn.sigmoid(gate_pre)
        grad_gate = (
            grad_inner * up_pre * sigma_gate * (1.0 + gate_pre * (1.0 - sigma_gate))
        ).astype(BFLOAT)
        grad_up = (grad_inner * gate_pre * sigma_gate).astype(BFLOAT)
        grad_gate_w = contract_rows(grad_gate, mlp_input)
        grad_up_w = contract_rows(grad_up, mlp_input)
        grad_normed_two = sum_rows(
            jnp.dot(grad_gate, gate_w, preferred_element_type=FLOAT)
            + jnp.dot(grad_up, up_w, preferred_element_type=FLOAT)
        )
        grad_mixed_norm, grad_gain_two = rms_back(mixed, gains[1], grad_normed_two)
        grad_mixed = grad_branch + grad_mixed_norm
        backward_grad_hidden = backward_grad_hidden + grad_mixed
        grad_attn = grad_mixed.astype(BFLOAT)
        grad_w_out = contract_rows(attended, grad_attn)
        grad_attended = (
            contract_cols(grad_attn, w_out)
            .astype(BFLOAT)
            .reshape(own_rows, KV_HEADS, groups_per, HEAD_DIM)
        )
        backward_keys_cat, values_cat = split_pair(backward_key_pair)
        backward_scores = attention_scores(backward_queries, backward_keys_cat, masks[step])
        probs_full = jnp.exp(backward_scores - log_total)
        probs = probs_full.astype(BFLOAT)
        grad_probs = jnp.einsum(
            "tkgd,skd->kgts", grad_attended, values_cat, preferred_element_type=FLOAT
        )
        delta = jnp.sum(probs_full * grad_probs, axis=-1, keepdims=True)
        grad_scores = (probs_full * (grad_probs - delta)).astype(BFLOAT)
        backward_grouped_q = backward_queries.reshape(own_rows, KV_HEADS, groups_per, HEAD_DIM)
        grad_queries = (
            jnp.einsum(
                "kgts,skd->tkgd", grad_scores, backward_keys_cat, preferred_element_type=FLOAT
            )
            * scale
        )
        grad_keys = (
            jnp.einsum(
                "kgts,tkgd->skd", grad_scores, backward_grouped_q, preferred_element_type=FLOAT
            )
            * scale
        )
        grad_values = jnp.einsum(
            "kgts,tkgd->skd", probs, grad_attended, preferred_element_type=FLOAT
        )
        grad_pair = jnp.stack(
            [grad_keys.reshape(2 * group_rows, -1), grad_values.reshape(2 * group_rows, -1)], axis=1
        )
        own_part = lax.psum_scatter(
            grad_pair[group_rows:].astype(jnp.bfloat16), "mp", scatter_dimension=0, tiled=True
        ).astype(jnp.float32)
        prev_part = lax.psum_scatter(
            grad_pair[:group_rows].astype(jnp.bfloat16), "mp", scatter_dimension=0, tiled=True
        ).astype(jnp.float32)
        grad_own = own_part + from_behind(prev_part.astype(jnp.bfloat16), "dp", -1).astype(
            prev_part.dtype
        )
        grad_key_pre = (
            rotate(grad_own[:, 0].reshape(own_rows, KV_HEADS, HEAD_DIM), -query_rows)
            .reshape(own_rows, -1)
            .astype(BFLOAT)
        )
        grad_value_pre = grad_own[:, 1].astype(BFLOAT)
        grad_query_pre = (
            rotate(grad_queries.reshape(own_rows, HEADS, HEAD_DIM), -query_rows)
            .reshape(own_rows, -1)
            .astype(BFLOAT)
        )
        grad_normed = (
            contract_cols(grad_query_pre, w_query)
            + contract_cols(grad_key_pre, w_key)
            + contract_cols(grad_value_pre, w_value)
        )
        grad_hidden_norm, grad_gain_one = rms_back(backward_hidden, gains[0], grad_normed)
        backward_grad_hidden = backward_grad_hidden + grad_hidden_norm
        grads = (
            contract_rows(normed, grad_query_pre),
            contract_rows(normed, grad_key_pre),
            contract_rows(normed, grad_value_pre),
            grad_w_out,
            grad_gain_one,
            grad_gain_two,
            grad_gate_w,
            grad_up_w,
            grad_down,
        )
        grad_hidden, grads, grad_router = (backward_grad_hidden, grads, grad_router)
        router_rows[step] = grad_router
        totals = (
            grads
            if totals is None
            else tuple((a_term + b_term for a_term, b_term in zip(totals, grads)))
        )
    grad_embed = gather_rows(grad_hidden.astype(BFLOAT)).astype(FLOAT) * inside[:, None]
    grad_table = jax.ops.segment_sum(grad_embed, clipped_ids, num_segments=vocab_local)
    grad_table = grad_table + head_grad
    gain_grads = jnp.stack([totals[4], totals[5], grad_gain_final])
    flat = jnp.concatenate(
        [
            totals[0].reshape(-1),
            totals[1].reshape(-1),
            totals[2].reshape(-1),
            totals[3].reshape(-1),
            gain_grads.reshape(-1),
            jnp.stack(router_rows).reshape(-1),
        ]
    )
    pack_grad = lax.psum_scatter(flat, ("mp", "dp"), scatter_dimension=0, tiled=True)
    mlp_grad, table_grad = (
        lax.psum_scatter(
            jnp.stack([totals[6], totals[7], totals[8]]).astype(jnp.bfloat16),
            "dp",
            scatter_dimension=1,
            tiled=True,
        ).astype(jnp.float32),
        lax.psum_scatter(
            grad_table.astype(jnp.bfloat16), "dp", scatter_dimension=0, tiled=True
        ).astype(jnp.float32),
    )
    squares = (
        jnp.sum(pack_grad * pack_grad)
        + jnp.sum(mlp_grad * mlp_grad)
        + jnp.sum(table_grad * table_grad)
    )
    total_squares, loss_sum = lax.psum((squares, loss_part), ("mp", "dp"))
    grad_norm = jnp.sqrt(total_squares)
    clip = CLIP_NORM / jnp.maximum(grad_norm, CLIP_NORM)
    pack_new, pack_first_new, pack_second_new = adam_update(
        pack_master, pack_first, pack_second, pack_grad, clip
    )
    mlp_new, mlp_first_new, mlp_second_new = adam_update(
        mlp_master, mlp_first, mlp_second, mlp_grad, clip
    )
    table_new, table_first_new, table_second_new = adam_update(
        table_master, table_first, table_second, table_grad, clip
    )
    return (
        pack_new,
        pack_first_new,
        pack_second_new,
        mlp_new,
        mlp_first_new,
        mlp_second_new,
        table_new,
        table_first_new,
        table_second_new,
        loss_sum,
        grad_norm,
    )


def solution(mesh):
    placed = (
        P("dp", None),
        P(),
        P("dp", None),
        P(),
        P(),
        P(("mp", "dp")),
        P(("mp", "dp")),
        P(("mp", "dp")),
        P(None, ("mp", "dp"), None),
        P(None, ("mp", "dp"), None),
        P(None, ("mp", "dp"), None),
        P(("mp", "dp"), None),
        P(("mp", "dp"), None),
        P(("mp", "dp"), None),
    )
    return jax.shard_map(
        shards,
        mesh=mesh,
        in_specs=placed,
        out_specs=(
            P(("mp", "dp")),
            P(("mp", "dp")),
            P(("mp", "dp")),
            P(None, ("mp", "dp"), None),
            P(None, ("mp", "dp"), None),
            P(None, ("mp", "dp"), None),
            P(("mp", "dp"), None),
            P(("mp", "dp"), None),
            P(("mp", "dp"), None),
            P(),
            P(),
        ),
        check_vma=False,
    )
```

profile of v0, /device:TPU:1, one launch (start us, length us, event | category | flops | bytes accessed | tf_op | source)
XLA Modules:
  0.0 1899.8 jit_solution(13090572461210828289)
XLA Ops:
  16.0 10.1 negate_convert_fusion
  27.6 82.3 %all-gather.20.cloned.1.call-done = bf16[6144,960]{0,1:T(8,128)(2,1)} async-done(((bf16[384,960]{0,1:T(8,128)(2,1)}), bf16[6144,960]{0,1:T(8,128)(2,1)}) %all-gather.20.cloned.1.call-update) | async-done | bytes 11796496 | tf_op jit(solution)/shard_map/all_gather | solution.py:164
  109.9 16.5 copy.139
  126.4 11.2 gather_fusion
  144.2 79.5 %all-reduce.8.cloned.1.call-done = bf16[2463360]{0:T(1024)(128)(2,1)} async-done(((bf16[2463360]{0:T(1024)(128)(2,1)}), bf16[2463360]{0:T(1024)(128)(2,1)}) %all-reduce.8.cloned.1.call-update) | async-done | bytes 4926736
  244.0 8.9 gather_fusion.1
  283.8 12.3 collective-permute-done
  305.4 7.8 fusion.9
  334.0 20.6 %all-gather.24.cloned.1.call-done = bf16[1024,960]{0,1:T(8,128)(2,1)} async-done(((bf16[128,960]{0,1:T(8,128)(2,1)}), bf16[1024,960]{0,1:T(8,128)(2,1)}) %all-gather.24.cloned.1.call-update) | async-done | bytes 1966096 | tf_op jit(solution)/shard_map/all_gather | solution.py:131
  367.1 31.6 %reduce-scatter.31.cloned.1.call-done = f32[128,960]{0,1:T(8,128)} async-done(((f32[1024,960]{0,1:T(8,128)}), f32[128,960]{0,1:T(8,128)}) %reduce-scatter.31.cloned.1.call-update) | async-done | bytes 491536 | tf_op jit(solution)/shard_map/reduce_scatter | solution.py:135
  403.0 26.7 %all-gather.28.cloned.1.call-done = bf16[1024,2,320]{0,2,1:T(8,128)(2,1)} async-done(((bf16[128,2,320]{0,2,1:T(8,128)(2,1)}), bf16[1024,2,320]{0,2,1:T(8,128)(2,1)}) %all-gather.28.cloned.1.call-update) | async-done | bytes 1310736 | tf_op jit(solution)/shard_map/all_gather | solution.py:220
  429.7 11.4 collective-permute-start.1
  443.4 17.6 collective-permute-done.1
  469.0 7.6 fusion.10
  487.1 29.6 %all-gather.30.cloned.1.call-done = bf16[1024,960]{0,1:T(8,128)(2,1)} async-done(((bf16[128,960]{0,1:T(8,128)(2,1)}), bf16[1024,960]{0,1:T(8,128)(2,1)}) %all-gather.30.cloned.1.call-update) | async-done | bytes 1966096 | tf_op jit(solution)/shard_map/all_gather | solution.py:131
  527.1 33.6 %reduce-scatter.33.cloned.1.call-done = f32[128,960]{0,1:T(8,128)} async-done(((f32[1024,960]{0,1:T(8,128)}), f32[128,960]{0,1:T(8,128)}) %reduce-scatter.33.cloned.1.call-update) | async-done | bytes 491536 | tf_op jit(solution)/shard_map/reduce_scatter | solution.py:135
  564.7 26.7 %all-gather.32.cloned.1.call-done = bf16[1024,2,320]{0,2,1:T(8,128)(2,1)} async-done(((bf16[128,2,320]{0,2,1:T(8,128)(2,1)}), bf16[1024,2,320]{0,2,1:T(8,128)(2,1)}) %all-gather.32.cloned.1.call-update) | async-done | bytes 1310736 | tf_op jit(solution)/shard_map/all_gather | solution.py:220
  597.1 25.5 %collective-permute-done.2 = bf16[1024,2,320]{0,2,1:T(8,128)(2,1)S(1)} collective-permute-done((bf16[1024,2,320]{0,2,1:T(8,128)(2,1)}, bf16[1024,2,320]{0,2,1:T(8,128)(2,1)S(1)}, u32[]{:S(2)}, u32[]{:S(2)}) %collective-permute-start.2) | collective-permute-done | bytes 1310752 | tf_op jit(solution)/shard_map/ppermute | solution.py:33
  648.2 29.6 %all-gather.34.cloned.1.call-done = bf16[1024,960]{0,1:T(8,128)(2,1)} async-done(((bf16[128,960]{0,1:T(8,128)(2,1)}), bf16[1024,960]{0,1:T(8,128)(2,1)}) %all-gather.34.cloned.1.call-update) | async-done | bytes 1966096 | tf_op jit(solution)/shard_map/all_gather | solution.py:131
  688.2 33.6 %reduce-scatter.35.cloned.1.call-done = f32[128,960]{0,1:T(8,128)} async-done(((f32[1024,960]{0,1:T(8,128)}), f32[128,960]{0,1:T(8,128)}) %reduce-scatter.35.cloned.1.call-update) | async-done | bytes 491536 | tf_op jit(solution)/shard_map/reduce_scatter | solution.py:135
  726.0 28.0 %all-gather.36.cloned.1.call-done = bf16[1024,960]{0,1:T(8,128)(2,1)} async-done(((bf16[128,960]{0,1:T(8,128)(2,1)}), bf16[1024,960]{0,1:T(8,128)(2,1)}) %all-gather.36.cloned.1.call-update) | async-done | bytes 1966096 | tf_op jit(solution)/shard_map/all_gather | solution.py:131
  771.5 9.8 all-gather.5
  781.4 8.1 all-gather.4
  789.5 9.5 all-gather.3
  800.1 10.9 fusion.141
  822.1 33.2 %reduce-scatter.37.cloned.1.call-done = f32[128,960]{0,1:T(8,128)} async-done(((f32[1024,960]{0,1:T(8,128)}), f32[128,960]{0,1:T(8,128)}) %reduce-scatter.37.cloned.1.call-update) | async-done | bytes 491536 | tf_op jit(solution)/shard_map/reduce_scatter | solution.py:135
  859.9 29.0 %all-gather.38.cloned.1.call-done = bf16[1024,960]{0,1:T(8,128)(2,1)} async-done(((bf16[128,960]{0,1:T(8,128)(2,1)}), bf16[1024,960]{0,1:T(8,128)(2,1)}) %all-gather.38.cloned.1.call-update) | async-done | bytes 1966096 | tf_op jit(solution)/shard_map/all_gather | solution.py:131
  897.5 35.1 %reduce-scatter.39.cloned.1.call-done = f32[128,960]{0,1:T(8,128)} async-done(((f32[1024,960]{0,1:T(8,128)}), f32[128,960]{0,1:T(8,128)}) %reduce-scatter.39.cloned.1.call-update) | async-done | bytes 491536 | tf_op jit(solution)/shard_map/reduce_scatter | solution.py:135
  938.0 15.0 fusion.6
  980.0 22.1 %reduce-scatter.49.cloned.1.call-done = bf16[128,640]{1,0:T(8,128)(2,1)} async-done(((bf16[1024,640]{1,0:T(8,128)(2,1)}), bf16[128,640]{1,0:T(8,128)(2,1)}) %reduce-scatter.49.cloned.1.call-update) | async-done | bytes 163856
  1006.3 29.4 %reduce-scatter.47.cloned.1.call-done = bf16[128,640]{1,0:T(8,128)(2,1)} async-done(((bf16[1024,640]{1,0:T(8,128)(2,1)}), bf16[128,640]{1,0:T(8,128)(2,1)}) %reduce-scatter.47.cloned.1.call-update) | async-done | bytes 163856
  1043.5 29.2 %all-gather.40.cloned.1.call-done = bf16[1024,960]{0,1:T(8,128)(2,1)} async-done(((bf16[128,960]{0,1:T(8,128)(2,1)}), bf16[1024,960]{0,1:T(8,128)(2,1)}) %all-gather.40.cloned.1.call-update) | async-done | bytes 1966096 | tf_op jit(solution)/shard_map/all_gather | solution.py:131
  1082.0 34.5 %reduce-scatter.41.cloned.1.call-done = f32[128,960]{0,1:T(8,128)} async-done(((f32[1024,960]{0,1:T(8,128)}), f32[128,960]{0,1:T(8,128)}) %reduce-scatter.41.cloned.1.call-update) | async-done | bytes 491536 | tf_op jit(solution)/shard_map/reduce_scatter | solution.py:135
  1121.5 15.1 fusion.3
  1161.9 23.9 %reduce-scatter.53.cloned.1.call-done = bf16[128,640]{1,0:T(8,128)(2,1)} async-done(((bf16[1024,640]{1,0:T(8,128)(2,1)}), bf16[128,640]{1,0:T(8,128)(2,1)}) %reduce-scatter.53.cloned.1.call-update) | async-done | bytes 163856
  1188.9 31.2 %reduce-scatter.51.cloned.1.call-done = bf16[128,640]{1,0:T(8,128)(2,1)} async-done(((bf16[1024,640]{1,0:T(8,128)(2,1)}), bf16[128,640]{1,0:T(8,128)(2,1)}) %reduce-scatter.51.cloned.1.call-update) | async-done | bytes 163856
  1228.2 29.0 %all-gather.42.cloned.1.call-done = bf16[1024,960]{0,1:T(8,128)(2,1)} async-done(((bf16[128,960]{0,1:T(8,128)(2,1)}), bf16[1024,960]{0,1:T(8,128)(2,1)}) %all-gather.42.cloned.1.call-update) | async-done | bytes 1966096 | tf_op jit(solution)/shard_map/all_gather | solution.py:131
  1267.0 33.9 %reduce-scatter.43.cloned.1.call-done = f32[128,960]{0,1:T(8,128)} async-done(((f32[1024,960]{0,1:T(8,128)}), f32[128,960]{0,1:T(8,128)}) %reduce-scatter.43.cloned.1.call-update) | async-done | bytes 491536 | tf_op jit(solution)/shard_map/reduce_scatter | solution.py:135
  1305.6 15.1 fusion
  1359.9 9.5 reduce-scatter.57.cloned.1.call-done
  1371.9 31.7 %reduce-scatter.55.cloned.1.call-done = bf16[128,640]{1,0:T(8,128)(2,1)} async-done(((bf16[1024,640]{1,0:T(8,128)(2,1)}), bf16[128,640]{1,0:T(8,128)(2,1)}) %reduce-scatter.55.cloned.1.call-update) | async-done | bytes 163856
  1466.4 76.2 %concatenate.90 = f32[2463360]{0:T(1024)} concatenate(f32[921600]{0:T(1024)} %reshape.1222, f32[307200]{0:T(1024)} %reshape.1223, f32[307200]{0:T(1024)S(1)} %copy-done.78, f32[921600]{0:T(1024)} %reshape.1225, f32[2880]{0:T(1024)S(1)} %reshape.1226, f32[2880]{0:T(1024)S(1)} %reshape.1227), dimensions={0} | concatenate | bytes 19706880 | tf_op jit(solution)/shard_map/concatenate | solution.py:431
  1543.6 14.6 fusion.86
  1567.7 27.8 %scatter_fusion = f32[6144,960]{1,0:T(8,128)} fusion(f32[6144,960]{1,0:T(8,128)} %fusion.86, s32[1024]{0:T(1024)S(1)} %bitcast.596, f32[1024,960]{1,0:T(8,128)} %copy.166), kind=kCustom, calls=%fused_computation.4 | custom fusion | flops 983040 | bytes 11800576 | tf_op jit(solution)/shard_map/scatter-add | solution.py:428
  1595.4 13.5 convert_element_type.505
  1618.8 89.8 %all-reduce.10.cloned.1.call-done = f32[2463360]{0:T(1024)} async-done(((f32[2463360]{0:T(1024)}), f32[2463360]{0:T(1024)}) %all-reduce.10.cloned.1.call-update) | async-done | bytes 9853456
  1711.5 93.3 %reduce-scatter.45.cloned.1.call-done = bf16[384,960]{1,0:T(8,128)(2,1)} async-done(((bf16[6144,960]{1,0:T(8,128)(2,1)}), bf16[384,960]{1,0:T(8,128)(2,1)}) %reduce-scatter.45.cloned.1.call-update) | async-done | bytes 737296 | tf_op jit(solution)/shard_map/reduce_scatter | solution.py:449
  1810.6 64.8 %all-reduce.3 = (f32[]{:T(128)}, f32[]{:T(128)}) all-reduce(f32[]{:T(128)S(6)} %add.836, f32[]{:T(128)S(6)} %add.858), channel_id=1, replica_groups=mesh['mp'=8,'dp'=16] {'mp','dp'}, use_global_device_ids=true, to_apply=%region_60.61 | all-reduce | flops 2 | bytes 16 | tf_op jit(solution)/shard_map/psum | solution.py:458
  (896 shorter events, 488.0 us)
Async XLA Ops:
  8.0 101.8 %all-gather.20.cloned.1.call-start = ((), (), s32[]{:S(2)}) async-start(), calls=%async_computation.15 | async-start | bytes 12533760 | tf_op jit(solution)/shard_map/all_gather | solution.py:164
  10.4 213.3 %all-reduce.8.cloned.1.call-start = ((), (), s32[]{:S(2)}) async-start(), calls=%async_computation.37 | async-start | bytes 9854976
  14.7 214.0 %reduce-scatter.29.cloned.1.call-start = ((), (), s32[]{:S(2)}) async-start(), calls=%async_computation.16 | async-start | bytes 4423680 | tf_op jit(solution)/shard_map/reduce_scatter | solution.py:135
  26.2 113.9 %copy-start.171 = (f32[1,1024]{1,0:T(1,128)}, f32[1,1024]{1,0:T(1,128)S(1)}, u32[]{:S(2)}) copy-start(f32[1,1024]{1,0:T(1,128)S(1)} %and_convert_fusion) | copy-start | bytes 12292
  144.2 120.3 %all-gather.22.cloned.1.call-start = ((), (), s32[]{:S(2)}) async-start(), calls=%async_computation.17 | async-start | bytes 1474560 | tf_op jit(solution)/shard_map/all_gather | solution.py:220
  228.6 334.0 %copy-start.141 = (f32[960]{0:T(1024)}, f32[960]{0:T(1024)S(1)}, u32[]{:S(2)}) copy-start(f32[960]{0:T(1024)S(1)} %get-tuple-element.374) | copy-start | bytes 11524
  228.6 706.1 %copy-start.145 = (f32[960]{0:T(1024)}, f32[960]{0:T(1024)S(1)}, u32[]{:S(2)}) copy-start(f32[960]{0:T(1024)S(1)} %get-tuple-element.373) | copy-start | bytes 11524
  231.6 49.9 %copy-start.32 = (bf16[128,960]{0,1:T(8,128)(2,1)}, bf16[128,960]{0,1:T(8,128)(2,1)S(1)}, u32[]{:S(2)}) copy-start(bf16[128,960]{0,1:T(8,128)(2,1)S(1)} %multiply_convert_fusion.19) | copy-start | bytes 737284
  233.2 91.1 %all-gather.26.cloned.1.call-start = ((), (), s32[]{:S(2)}) async-start(), calls=%async_computation.19 | async-start | bytes 2785280 | tf_op jit(solution)/shard_map/all_gather | solution.py:163
  234.1 120.6 %all-gather.24.cloned.1.call-start = ((), (), s32[]{:S(2)}) async-start(), calls=%async_computation.18 | async-start | bytes 2211840 | tf_op jit(solution)/shard_map/all_gather | solution.py:131
  264.5 31.6 %collective-permute-start = (bf16[1024,2,320]{0,2,1:T(8,128)(2,1)}, bf16[1024,2,320]{0,2,1:T(8,128)(2,1)}, u32[]{:S(2)}, u32[]{:S(2)}) collective-permute-start(bf16[1024,2,320]{0,2,1:T(8,128)(2,1)} %all-gather.22.cloned.1.call-done), channel_id=1, source_target_pairs={{0,1},{1,2},{2,3},{3,4},{4,5},{5,6},{6,7},{7,8},{8,9},{9,10},{10,1... | collective-permute-start | bytes 3932168 | tf_op jit(solution)/shard_map/ppermute | solution.py:33
  324.2 74.4 %reduce-scatter.31.cloned.1.call-start = ((), (), s32[]{:S(2)}) async-start(), calls=%async_computation.20 | async-start | bytes 4423680 | tf_op jit(solution)/shard_map/reduce_scatter | solution.py:135
  363.5 66.2 %all-gather.28.cloned.1.call-start = ((), (), s32[]{:S(2)}) async-start(), calls=%async_computation.21 | async-start | bytes 1474560 | tf_op jit(solution)/shard_map/all_gather | solution.py:220
  364.7 160.9 %copy-start.204 = (f32[128]{0:T(128)}, f32[128]{0:T(128)S(1)}, u32[]{:S(2)}) copy-start(f32[128]{0:T(128)S(1)} %get-tuple-element.237) | copy-start | bytes 1540
  364.7 322.0 %copy-start.206 = (f32[128]{0:T(128)}, f32[128]{0:T(128)S(1)}, u32[]{:S(2)}) copy-start(f32[128]{0:T(128)S(1)} %get-tuple-element.236) | copy-start | bytes 1540
  401.4 41.9 %copy-start.34 = (bf16[128,960]{0,1:T(8,128)(2,1)}, bf16[128,960]{0,1:T(8,128)(2,1)S(1)}, u32[]{:S(2)}) copy-start(bf16[128,960]{0,1:T(8,128)(2,1)S(1)} %multiply_convert_fusion.17) | copy-start | bytes 737284
  402.9 113.7 %all-gather.30.cloned.1.call-start = ((), (), s32[]{:S(2)}) async-start(), calls=%async_computation.22 | async-start | bytes 2211840 | tf_op jit(solution)/shard_map/all_gather | solution.py:131
  429.7 31.3 %collective-permute-start.1 = (bf16[1024,2,320]{0,2,1:T(8,128)(2,1)}, bf16[1024,2,320]{0,2,1:T(8,128)(2,1)S(1)}, u32[]{:S(2)}, u32[]{:S(2)}) collective-permute-start(bf16[1024,2,320]{0,2,1:T(8,128)(2,1)} %all-gather.28.cloned.1.call-done), channel_id=1, source_target_pairs={{0,1},{1,2},{2,3},{3,4},{4,5},{5,6},{6,7},{7,8},{8,9},{9,10},{10,1... | collective-permute-start | bytes 3932168 | tf_op jit(solution)/shard_map/ppermute | solution.py:33
  487.0 73.6 %reduce-scatter.33.cloned.1.call-start = ((), (), s32[]{:S(2)}) async-start(), calls=%async_computation.23 | async-start | bytes 4423680 | tf_op jit(solution)/shard_map/reduce_scatter | solution.py:135
  525.5 65.8 %all-gather.32.cloned.1.call-start = ((), (), s32[]{:S(2)}) async-start(), calls=%async_computation.24 | async-start | bytes 1474560 | tf_op jit(solution)/shard_map/all_gather | solution.py:220
  564.6 113.1 %all-gather.34.cloned.1.call-start = ((), (), s32[]{:S(2)}) async-start(), calls=%async_computation.25 | async-start | bytes 2211840 | tf_op jit(solution)/shard_map/all_gather | solution.py:131
  591.3 31.3 %collective-permute-start.2 = (bf16[1024,2,320]{0,2,1:T(8,128)(2,1)}, bf16[1024,2,320]{0,2,1:T(8,128)(2,1)S(1)}, u32[]{:S(2)}, u32[]{:S(2)}) collective-permute-start(bf16[1024,2,320]{0,2,1:T(8,128)(2,1)} %all-gather.32.cloned.1.call-done), channel_id=1, source_target_pairs={{0,1},{1,2},{2,3},{3,4},{4,5},{5,6},{6,7},{7,8},{8,9},{9,10},{10,1... | collective-permute-start | bytes 3932168 | tf_op jit(solution)/shard_map/ppermute | solution.py:33
  648.1 73.6 %reduce-scatter.35.cloned.1.call-start = ((), (), s32[]{:S(2)}) async-start(), calls=%async_computation.26 | async-start | bytes 4423680 | tf_op jit(solution)/shard_map/reduce_scatter | solution.py:135
  686.6 39.4 %copy-start.222 = (s32[1,256]{1,0:T(1,128)S(1)}, s32[1,256]{1,0:T(1,128)}, u32[]{:S(2)}) copy-start(s32[1,256]{1,0:T(1,128)} %param.18) | copy-start | bytes 3076
  686.6 67.4 %all-gather.36.cloned.1.call-start = ((), (), s32[]{:S(2)}) async-start(), calls=%async_computation.27 | async-start | bytes 2211840 | tf_op jit(solution)/shard_map/all_gather | solution.py:131
  688.2 246.6 %copy-start.186 = (f32[128]{0:T(128)}, f32[128]{0:T(128)S(1)}, u32[]{:S(2)}) copy-start(f32[128]{0:T(128)S(1)} %get-tuple-element.298) | copy-start | bytes 1540
  724.8 130.4 %reduce-scatter.37.cloned.1.call-start = ((), (), s32[]{:S(2)}) async-start(), calls=%async_computation.28 | async-start | bytes 4423680 | tf_op jit(solution)/shard_map/reduce_scatter | solution.py:135
  726.0 74.2 %copy-start.184 = (s32[1,256]{1,0:T(1,128)}, s32[1,256]{1,0:T(1,128)S(1)}, u32[]{:S(2)}) copy-start(s32[1,256]{1,0:T(1,128)S(1)} %dynamic-slice_subtract_fusion) | copy-start | bytes 3076
  822.0 66.8 %all-gather.38.cloned.1.call-start = ((), (), s32[]{:S(2)}) async-start(), calls=%async_computation.29 | async-start | bytes 2211840 | tf_op jit(solution)/shard_map/all_gather | solution.py:131
  859.7 73.0 %reduce-scatter.39.cloned.1.call-start = ((), (), s32[]{:S(2)}) async-start(), calls=%async_computation.30 | async-start | bytes 4423680 | tf_op jit(solution)/shard_map/reduce_scatter | solution.py:135
  897.5 104.6 %reduce-scatter.49.cloned.1.call-start = ((), (), s32[]{:S(2)}) async-start(), calls=%async_computation.39 | async-start | bytes 1474560
  970.7 65.0 %reduce-scatter.47.cloned.1.call-start = ((), (), s32[]{:S(2)}) async-start(), calls=%async_computation.38 | async-start | bytes 1474560
  973.2 99.5 %all-gather.40.cloned.1.call-start = ((), (), s32[]{:S(2)}) async-start(), calls=%async_computation.31 | async-start | bytes 2211840 | tf_op jit(solution)/shard_map/all_gather | solution.py:131
  1003.8 33.6 %collective-permute-start.3 = (bf16[128,2,320]{0,2,1:T(8,128)(2,1)}, bf16[128,2,320]{0,2,1:T(8,128)(2,1)}, u32[]{:S(2)}, u32[]{:S(2)}) collective-permute-start(bf16[128,2,320]{0,2,1:T(8,128)(2,1)} %bitcast.191), channel_id=1, source_target_pairs={{1,0},{2,1},{3,2},{4,3},{5,4},{6,5},{7,6},{8,7},{9,8},{10,9},{11,1... | collective-permute-start | bytes 491528 | tf_op jit(solution)/shard_map/ppermute | solution.py:33
  1043.5 73.0 %reduce-scatter.41.cloned.1.call-start = ((), (), s32[]{:S(2)}) async-start(), calls=%async_computation.32 | async-start | bytes 4423680 | tf_op jit(solution)/shard_map/reduce_scatter | solution.py:135
  1081.3 104.4 %reduce-scatter.53.cloned.1.call-start = ((), (), s32[]{:S(2)}) async-start(), calls=%async_computation.41 | async-start | bytes 1474560
  1154.4 65.7 %reduce-scatter.51.cloned.1.call-start = ((), (), s32[]{:S(2)}) async-start(), calls=%async_computation.40 | async-start | bytes 1474560
  1156.9 100.2 %all-gather.42.cloned.1.call-start = ((), (), s32[]{:S(2)}) async-start(), calls=%async_computation.33 | async-start | bytes 2211840 | tf_op jit(solution)/shard_map/all_gather | solution.py:131
  1187.5 34.3 %collective-permute-start.4 = (bf16[128,2,320]{0,2,1:T(8,128)(2,1)}, bf16[128,2,320]{0,2,1:T(8,128)(2,1)}, u32[]{:S(2)}, u32[]{:S(2)}) collective-permute-start(bf16[128,2,320]{0,2,1:T(8,128)(2,1)} %bitcast.198), channel_id=1, source_target_pairs={{1,0},{2,1},{3,2},{4,3},{5,4},{6,5},{7,6},{8,7},{9,8},{10,9},{11,1... | collective-permute-start | bytes 491528 | tf_op jit(solution)/shard_map/ppermute | solution.py:33
  1227.9 73.0 %reduce-scatter.43.cloned.1.call-start = ((), (), s32[]{:S(2)}) async-start(), calls=%async_computation.34 | async-start | bytes 4423680 | tf_op jit(solution)/shard_map/reduce_scatter | solution.py:135
  1265.7 37.5 %copy-start.190 = (f32[128]{0:T(128)S(1)}, f32[128]{0:T(128)}, u32[]{:S(2)}) copy-start(f32[128]{0:T(128)} %copy-done.188) | copy-start | bytes 1540
  1265.8 103.7 %reduce-scatter.57.cloned.1.call-start = ((), (), s32[]{:S(2)}) async-start(), calls=%async_computation.43 | async-start | bytes 1474560
  1338.1 65.5 %reduce-scatter.55.cloned.1.call-start = ((), (), s32[]{:S(2)}) async-start(), calls=%async_computation.42 | async-start | bytes 1474560
  1345.5 212.7 %all-gather.44.cloned.1.call-start = ((), (), s32[]{:S(2)}) async-start(), calls=%async_computation.35 | async-start | bytes 2211840 | tf_op jit(solution)/shard_map/all_gather | solution.py:131
  1370.5 34.2 %collective-permute-start.5 = (bf16[128,2,320]{0,2,1:T(8,128)(2,1)S(1)}, bf16[128,2,320]{0,2,1:T(8,128)(2,1)S(1)}, u32[]{:S(2)}, u32[]{:S(2)}) collective-permute-start(bf16[128,2,320]{0,2,1:T(8,128)(2,1)S(1)} %bitcast.588), channel_id=1, source_target_pairs={{1,0},{2,1},{3,2},{4,3},{5,4},{6,5},{7,6},{8,7},{9,8},{10,9},{11,1... | collective-permute-start | bytes 491528 | tf_op jit(solution)/shard_map/ppermute | solution.py:33
  1409.8 207.4 %all-reduce.12.cloned.1.call-start = ((), (), s32[]{:S(2)}) async-start(), calls=%async_computation.45 | async-start | bytes 3932160
  1430.3 278.3 %all-reduce.10.cloned.1.call-start = ((), (), s32[]{:S(2)}) async-start(), calls=%async_computation.44 | async-start | bytes 19709952
  1542.6 262.2 %reduce-scatter.45.cloned.1.call-start = ((), (), s32[]{:S(2)}) async-start(), calls=%async_computation.36 | async-start | bytes 13369344 | tf_op jit(solution)/shard_map/reduce_scatter | solution.py:449
  (242 other events, 1808.1 us)
Sparse Core Ops, SparseCore 0:
  11.5 98.2 all-gather.19
  144.3 36.9 reduce-scatter.28
  233.3 23.1 all-gather.21
  259.3 63.6 all-gather.25
  325.2 29.3 all-gather.23
  363.6 34.9 reduce-scatter.30
  403.1 26.5 all-gather.27
  487.1 29.4 all-gather.29
  525.6 34.9 reduce-scatter.32
  564.7 26.5 all-gather.31
  648.2 29.4 all-gather.33
  686.7 34.9 reduce-scatter.34
  725.0 29.0 all-gather.35
  822.1 33.0 reduce-scatter.36
  859.8 29.0 all-gather.37
  897.6 34.9 reduce-scatter.38
  970.8 31.1 reduce-scatter.48
  1004.4 31.1 reduce-scatter.46
  1043.6 29.0 all-gather.39
  1081.4 34.9 reduce-scatter.40
  1154.5 31.1 reduce-scatter.52
  1188.9 31.1 reduce-scatter.50
  1228.1 29.0 all-gather.41
  1265.9 34.9 reduce-scatter.42
  1338.2 31.1 reduce-scatter.56
  1372.4 31.1 reduce-scatter.54
  1409.9 29.0 all-gather.43
  1442.7 88.2 all-reduce.11
  1542.7 165.8 all-reduce.9
  1712.3 92.4 reduce-scatter.44
Sparse Core Ops, SparseCore 1:
  15.9 207.7 all-reduce.7
where the time goes:
time: 1920 us; the launch traced here: 1900 us
  waiting for transfers between devices  1030 us (54%)
  matrix products  271 us (14%)
  local copies, waits for them, and re-layouts  258 us (13%)
  other arithmetic  193 us (10%)
  blocking collectives  92.3 us (5%)
  between operations  26.6 us (1%)
  starting transfers between devices  25.8 us (1%)
    unnamed x40, waiting for transfers between devices  318 us
    reduce_scatter x8, waiting for transfers between devices, sum_rows(): return lax.psum_scatter(values, 'mp', scatter_dimension=0, tiled=True)  235 us
    all_gather x8, waiting for transfers between devices, gather_rows(): return lax.all_gather(values, 'mp', axis=0, tiled=True)  195 us
    reduce_scatter x1, waiting for transfers between devices, shards(): lax.psum_scatter(grad_table.astype(jnp.bfloat16), 'dp', scatter_dimension...  93.3 us
    all_gather x1, waiting for transfers between devices, shards(): lax.all_gather(table_master.astype(BFLOAT), 'dp', axis=0, tiled=True)  82.3 us
    concatenate x1, local copies, waits for them, and re-layouts, shards(): jnp.concatenate([totals[0].reshape(-1), totals[1].reshape(-1), totals[2]....  76.2 us
    unnamed x535, local copies, waits for them, and re-layouts  70.7 us
    psum x1, blocking collectives, shards(): total_squares, loss_sum = lax.psum((squares, loss_part), ('mp', 'dp'))  64.8 us
  transfers between devices with their start and end apart: 37, of which 29 were waited for; matrix products, arithmetic and copies ran while one was open for 21% of the time, Pallas kernels for 0%

commit v1 on v0

v1 whole, which is shorter than its diff:
```python
import functools

import jax
import jax.numpy as jnp
from jax import lax
from jax.experimental import pallas as pl
from jax.experimental.pallas import tpu as pltpu
from jax.sharding import Mesh
from jax.sharding import PartitionSpec as P

D = 960
HEADS = 15
KV_HEADS = 5
HEAD_DIM = 64
FF = 2560
RECUR = 3
STEP = 10
TOK_DEV = 128
ROWS = 1024
MP = 8
DP = 16
VOCAB_MP = 6144
VOCAB_DEV = 384
UNITS = 20
PACK_DEV = 19245
PACK_ROWS = 2566
PACK_PAD = 2688
CAP = 24

EPS_NORM = 1e-05
ROPE_BASE = 10000.0
ROUTER_LOSS = 0.1
CLIP_NORM = 1.0
LEARN_RATE = 0.05
BETA_ONE = 0.9
BETA_TWO = 0.95
ADAM_EPS = 1e-08
DECAY = 0.1
MASKED = -1e30
HIGHEST = lax.Precision.HIGHEST
BFLOAT = jnp.bfloat16
FLOAT = jnp.float32
DP_AXES = ("y", "x")
ALL_AXES = ("z", "core", "y", "x")


def shift(value, axis, steps):
    return lax.ppermute(value, axis, [(i, (i + steps) % 4) for i in range(4)])


def swap(value):
    return lax.ppermute(value, "core", [(0, 1), (1, 0)])


def shift_group(value, steps):
    pairs = [(i, i + steps) for i in range(DP) if 0 <= i + steps < DP]
    return lax.ppermute(value, DP_AXES, pairs)


def gather_group(value):
    parts = jnp.stack([value] + [shift(value, "z", -k) for k in (1, 2, 3)])
    return jnp.stack([parts, swap(parts)])


def scatter_group(blocks, kind=BFLOAT):
    half = (blocks[0].astype(FLOAT) + swap(blocks[1].astype(BFLOAT)).astype(FLOAT)).astype(BFLOAT)
    total = half[0].astype(FLOAT)
    for k in (1, 2, 3):
        total = total + shift(half[k], "z", k).astype(FLOAT)
    return total.astype(kind)


def sum_all(value):
    value = value + swap(value)
    for axis in ("z", "y", "x"):
        value = value + shift(value, axis, 1) + shift(value, axis, 2) + shift(value, axis, 3)
    return value


def rms_scale(values, weight):
    return values * lax.rsqrt(jnp.mean(values * values, axis=-1, keepdims=True) + EPS_NORM) * weight


def rms_back(values, weight, grad_out):
    inverse = lax.rsqrt(jnp.mean(values * values, axis=-1, keepdims=True) + EPS_NORM)
    weighted = grad_out * weight
    grad_values = inverse * weighted - values * (inverse * inverse * inverse) * jnp.mean(
        weighted * values, axis=-1, keepdims=True
    )
    return (grad_values, jnp.sum(grad_out * values * inverse, axis=0))


def rotation(positions):
    half = HEAD_DIM // 2
    freqs = ROPE_BASE ** (-jnp.arange(half, dtype=FLOAT) / half)
    angles = positions.astype(FLOAT)[:, None] * freqs[None, :]
    return jnp.cos(angles)[:, None, :], jnp.sin(angles)[:, None, :]


def rotate(values, cosine, sine):
    half = HEAD_DIM // 2
    first = values[..., :half]
    second = values[..., half:]
    return jnp.concatenate(
        [first * cosine - second * sine, second * cosine + first * sine], axis=-1
    )


def mm(left, right):
    return jnp.dot(left, right, preferred_element_type=FLOAT)


def contract_rows(left, right):
    return lax.dot_general(left, right, (((0,), (0,)), ((), ())), preferred_element_type=FLOAT)


def contract_cols(left, right):
    return lax.dot_general(left, right, (((1,), (1,)), ((), ())), preferred_element_type=FLOAT)


def reorder(blocks, order):
    hit = order[:, None] == jnp.arange(MP)[None, :]
    return jnp.sum(jnp.where(hit[:, :, None], blocks[..., None, :, :], 0), axis=-2)


def tie(*values):
    return lax.optimization_barrier(values)


def group_gather(pair):
    own = [pair]
    for k in (1, 2, 3):
        own.append(lax.ppermute(pair, "z", [((i + k) % 4, i) for i in range(4) if (i + k) % 4 < i]))
    prev = []
    for k in range(4):
        pairs = []
        for i in range(3):
            for g in range(1, DP):
                pairs.append((((i + k) % 4) * DP + g - 1, i * DP + g))
        prev.append(lax.ppermute(pair, ("z",) + DP_AXES, pairs))
    own = jnp.concatenate(own, axis=0)
    prev = jnp.concatenate(prev, axis=0)
    return prev, own, swap(prev), swap(own)


def group_scatter(prev, own, prev_far, own_far):
    own = (own.astype(FLOAT) + swap(own_far).astype(FLOAT)).astype(BFLOAT).reshape(4, TOK_DEV, -1)
    prev = (prev.astype(FLOAT) + swap(prev_far).astype(FLOAT)).astype(BFLOAT).reshape(4, TOK_DEV, -1)
    total = own[0].astype(FLOAT)
    for k in (1, 2, 3):
        pairs = [(i, (i + k) % 4) for i in range(4) if (i + k) % 4 < i]
        total = total + lax.ppermute(own[k], "z", pairs).astype(FLOAT)
    for k in range(4):
        pairs = []
        for i in range(3):
            for g in range(1, DP):
                pairs.append((i * DP + g, ((i + k) % 4) * DP + g - 1))
        total = total + lax.ppermute(prev[k], ("z",) + DP_AXES, pairs).astype(FLOAT)
    return total


def nn(left, right):
    return jnp.dot(left, right, preferred_element_type=FLOAT)


def head_rows(ref, head):
    return jnp.concatenate(
        [ref[:, 64 * (3 * head + i) : 64 * (3 * head + i) + 64] for i in range(3)], axis=0
    )


def attend_kernel(query_ref, kv0, kv1, kv2, kv3, bias_ref, out_ref, log_ref):
    for head in range(KV_HEADS):
        queries = head_rows(query_ref, head)
        top = None
        for part, kv_ref in enumerate((kv0, kv1, kv2, kv3)):
            keys = kv_ref[:, 64 * head : 64 * head + 64]
            values = kv_ref[:, 320 + 64 * head : 320 + 64 * head + 64]
            bias = bias_ref[512 * part : 512 * part + 512, :]
            scores = contract_cols(keys, queries) + jnp.concatenate([bias, bias, bias], axis=1)
            part_top = jnp.max(scores, axis=0, keepdims=True)
            new_top = part_top if top is None else jnp.maximum(top, part_top)
            expo = jnp.exp(scores - new_top)
            part_total = jnp.sum(expo, axis=0, keepdims=True)
            part_out = contract_rows(values, expo.astype(BFLOAT))
            if top is None:
                total, out = part_total, part_out
            else:
                shrink = jnp.exp(top - new_top)
                total, out = total * shrink + part_total, out * shrink + part_out
            top = new_top
        out = (out / total).T.astype(BFLOAT)
        for i in range(3):
            place = 64 * (3 * head + i)
            out_ref[:, place : place + 64] = out[128 * i : 128 * i + 128]
        log_ref[head : head + 1, :] = top + jnp.log(total)


def attend(queries, pairs, bias):
    return pl.pallas_call(
        attend_kernel,
        out_shape=(
            jax.ShapeDtypeStruct((TOK_DEV, HEADS * HEAD_DIM), BFLOAT),
            jax.ShapeDtypeStruct((8, 3 * TOK_DEV), FLOAT),
        ),
        cost_estimate=pl.CostEstimate(
            flops=12_000_000_000, bytes_accessed=5_000_000, transcendentals=4_000_000
        ),
        compiler_params=pltpu.CompilerParams(vmem_limit_bytes=32 * 1024 * 1024),
    )(queries, *pairs, bias)


def attend_back_kernel(
    query_ref, kv0, kv1, kv2, kv3, bias_ref, log_ref, att_ref, grad_ref, dq_ref, d0, d1, d2, d3
):
    for head in range(KV_HEADS):
        queries = head_rows(query_ref, head)
        grads = head_rows(grad_ref, head)
        outs = head_rows(att_ref, head)
        delta = jnp.sum((grads.astype(FLOAT) * outs.astype(FLOAT)).T, axis=0, keepdims=True)
        log_total = log_ref[head : head + 1, :]
        back = None
        for part, (kv_ref, d_ref) in enumerate(((kv0, d0), (kv1, d1), (kv2, d2), (kv3, d3))):
            keys = kv_ref[:, 64 * head : 64 * head + 64]
            values = kv_ref[:, 320 + 64 * head : 320 + 64 * head + 64]
            bias = bias_ref[512 * part : 512 * part + 512, :]
            probs = jnp.exp(
                contract_cols(keys, queries) + jnp.concatenate([bias, bias, bias], axis=1) - log_total
            )
            grad_scores = (probs * (contract_cols(values, grads) - delta)).astype(BFLOAT)
            d_ref[:, 64 * head : 64 * head + 64] = nn(grad_scores, queries).astype(BFLOAT)
            d_ref[:, 320 + 64 * head : 320 + 64 * head + 64] = nn(
                probs.astype(BFLOAT), grads
            ).astype(BFLOAT)
            part_back = contract_rows(keys, grad_scores)
            back = part_back if back is None else back + part_back
        back = back.T * (HEAD_DIM**-0.5)
        for i in range(3):
            place = 64 * (3 * head + i)
            dq_ref[:, place : place + 64] = back[128 * i : 128 * i + 128]


def attend_back(queries, pairs, bias, log_total, attended, grads):
    side = jax.ShapeDtypeStruct((4 * TOK_DEV, 640), BFLOAT)
    return pl.pallas_call(
        attend_back_kernel,
        out_shape=(jax.ShapeDtypeStruct((TOK_DEV, HEADS * HEAD_DIM), FLOAT), side, side, side, side),
        cost_estimate=pl.CostEstimate(
            flops=20_000_000_000, bytes_accessed=9_000_000, transcendentals=4_000_000
        ),
        compiler_params=pltpu.CompilerParams(vmem_limit_bytes=32 * 1024 * 1024),
    )(queries, *pairs, bias, log_total, attended, grads)


HEAD_BLOCK = 512


def head_kernel(rows_ref, near_ref, final_ref, target_ref, table_ref, logit_ref, pick_ref, stat_ref):
    step = pl.program_id(0)

    @pl.when(step == 0)
    def first():
        hot = (rows_ref[...] == near_ref[...]).astype(FLOAT).astype(BFLOAT)
        pick_ref[...] = nn(hot, final_ref[...]).astype(BFLOAT)
        lane = lax.broadcasted_iota(jnp.int32, (256, 128), 1)
        stat_ref[...] = jnp.where(lane == 0, MASKED, 0.0)

    logits = contract_cols(pick_ref[...], table_ref[...])
    logit_ref[...] = logits
    place = step * HEAD_BLOCK + lax.broadcasted_iota(jnp.int32, (256, HEAD_BLOCK), 1)
    hit = jnp.sum(jnp.where(place == target_ref[...], logits, 0.0), axis=1, keepdims=True)
    old = stat_ref[:, 0:1]
    top = jnp.maximum(old, jnp.max(logits, axis=1, keepdims=True))
    total = stat_ref[:, 1:2] * jnp.exp(old - top) + jnp.sum(
        jnp.exp(logits - top), axis=1, keepdims=True
    )
    stat_ref[:, 1:2] = total
    stat_ref[:, 2:3] = stat_ref[:, 2:3] + hit
    stat_ref[:, 0:1] = top


def head(loss_rows, near_rows, final_rows, local_targets, table):
    def whole(shape):
        return pl.BlockSpec(shape, lambda i: (0, 0))

    return pl.pallas_call(
        head_kernel,
        grid=(VOCAB_MP // HEAD_BLOCK,),
        in_specs=[
            whole((256, 1)),
            whole((1, ROWS)),
            whole((ROWS, D)),
            whole((256, 1)),
            pl.BlockSpec((HEAD_BLOCK, D), lambda i: (i, 0)),
        ],
        out_specs=[
            pl.BlockSpec((256, HEAD_BLOCK), lambda i: (0, i)),
            whole((256, D)),
            whole((256, 128)),
        ],
        out_shape=(
            jax.ShapeDtypeStruct((256, VOCAB_MP), FLOAT),
            jax.ShapeDtypeStruct((256, D), BFLOAT),
            jax.ShapeDtypeStruct((256, 128), FLOAT),
        ),
        compiler_params=pltpu.CompilerParams(vmem_limit_bytes=32 * 1024 * 1024),
    )(loss_rows, near_rows, final_rows, local_targets, table)


def head_back_kernel(
    rows_ref, near_ref, target_ref, norm_ref, logit_ref, pick_ref, table_ref, grad_ref, out_ref, sum_ref
):
    step = pl.program_id(0)
    place = step * HEAD_BLOCK + lax.broadcasted_iota(jnp.int32, (256, HEAD_BLOCK), 1)
    probs = jnp.exp(logit_ref[...] - norm_ref[...])
    hit = jnp.where(place == target_ref[...], 1.0, 0.0)
    grads = ((probs - hit) * (1.0 / TOK_DEV)).astype(BFLOAT)
    grad_ref[...] = contract_rows(grads, pick_ref[...]).astype(BFLOAT)
    part = nn(grads, table_ref[...])

    @pl.when(step == 0)
    def first():
        sum_ref[...] = part

    @pl.when(step > 0)
    def later():
        sum_ref[...] += part

    @pl.when(step == pl.num_programs(0) - 1)
    def last():
        hot = (rows_ref[...] == near_ref[...]).astype(FLOAT).astype(BFLOAT)
        out_ref[...] = contract_rows(hot, sum_ref[...].astype(BFLOAT)).astype(BFLOAT)


def head_back(loss_rows, near_rows, local_targets, log_norm, logits, picked, table):
    def whole(shape):
        return pl.BlockSpec(shape, lambda i: (0, 0))

    return pl.pallas_call(
        head_back_kernel,
        grid=(VOCAB_MP // HEAD_BLOCK,),
        in_specs=[
            whole((256, 1)),
            whole((1, ROWS)),
            whole((256, 1)),
            whole((256, 1)),
            pl.BlockSpec((256, HEAD_BLOCK), lambda i: (0, i)),
            whole((256, D)),
            pl.BlockSpec((HEAD_BLOCK, D), lambda i: (i, 0)),
        ],
        out_specs=[pl.BlockSpec((HEAD_BLOCK, D), lambda i: (i, 0)), whole((ROWS, D))],
        out_shape=(
            jax.ShapeDtypeStruct((VOCAB_MP, D), BFLOAT),
            jax.ShapeDtypeStruct((ROWS, D), BFLOAT),
        ),
        scratch_shapes=[pltpu.VMEM((256, D), FLOAT)],
        compiler_params=pltpu.CompilerParams(vmem_limit_bytes=32 * 1024 * 1024),
    )(loss_rows, near_rows, local_targets, log_norm, logits, picked, table)


def mlp_grad_kernel(added, which_ref, *refs):
    lefts, rights, refs = refs[0:3], refs[3:6], refs[6:]
    for i in range(3):
        total = contract_rows(lefts[i][...], rights[i][...])
        if added:
            total = total + refs[0][i].astype(FLOAT)
        refs[-1][i] = total.astype(BFLOAT)


def mlp_grads(which, lefts, rights, received=None):
    added = received is not None
    block = 256
    rows = lefts[0].shape[0]
    steps = FF // 2 // block
    out_spec = pl.BlockSpec((3, block, D), lambda i, half: (0, i, 0))
    return pl.pallas_call(
        functools.partial(mlp_grad_kernel, added),
        grid_spec=pltpu.PrefetchScalarGridSpec(
            num_scalar_prefetch=1,
            grid=(steps,),
            in_specs=[pl.BlockSpec((rows, block), lambda i, half: (0, half[0] * steps + i))] * 3
            + [pl.BlockSpec((rows, D), lambda i, half: (0, 0))] * 3
            + [out_spec] * added,
            out_specs=out_spec,
        ),
        out_shape=jax.ShapeDtypeStruct((3, FF // 2, D), BFLOAT),
        compiler_params=pltpu.CompilerParams(vmem_limit_bytes=32 * 1024 * 1024),
    )(which.reshape(1), *lefts, *rights, *([received] if added else []))


def pack_grad_kernel(
    starts_ref, normed_ref, dq_ref, dk_ref, dv_ref, att_ref, grad_ref, rows_ref, mine_ref, other_ref, buf
):
    buf[0:960, :] = contract_rows(normed_ref[...], dq_ref[...]).astype(BFLOAT)
    buf[1600:2560, :] = contract_rows(att_ref[...], grad_ref[...]).astype(BFLOAT)
    buf[2560:2576, :] = rows_ref[...].astype(BFLOAT)
    buf[2576:2688, :] = jnp.zeros((112, D), BFLOAT)
    line = lax.broadcasted_iota(jnp.int32, (960, 320), 0)
    place = lax.broadcasted_iota(jnp.int32, (960, 320), 1)
    for first, ref in ((960, dk_ref), (1280, dv_ref)):
        full = contract_rows(normed_ref[...], ref[...]).astype(BFLOAT)
        for i in range(3):
            chosen = (line == 3 * place + i).astype(FLOAT).astype(BFLOAT)
            buf[first : first + 320, 320 * i : 320 * i + 320] = contract_rows(chosen, full).astype(
                BFLOAT
            )
    for i in range(4):
        mine_ref[i] = buf[pl.ds(pl.multiple_of(starts_ref[i], 16), 352), :]
        other_ref[i] = buf[pl.ds(pl.multiple_of(starts_ref[4 + i], 16), 352), :]


def pack_grads(starts, *parts):
    side = jax.ShapeDtypeStruct((4, 352, D), BFLOAT)
    return pl.pallas_call(
        pack_grad_kernel,
        in_specs=[pl.BlockSpec(memory_space=pltpu.SMEM)]
        + [pl.BlockSpec(memory_space=pltpu.VMEM)] * len(parts),
        out_shape=(side, side),
        scratch_shapes=[pltpu.VMEM((PACK_PAD, D), BFLOAT)],
        compiler_params=pltpu.CompilerParams(vmem_limit_bytes=40 * 1024 * 1024),
    )(starts, *parts)


def adam_update(master, first, second, grad, clip):
    grad = grad * clip
    first_new = BETA_ONE * first + (1.0 - BETA_ONE) * grad
    second_new = BETA_TWO * second + (1.0 - BETA_TWO) * grad * grad
    corr_one = 1.0 - BETA_ONE**STEP
    corr_two = 1.0 - BETA_TWO**STEP
    master_new = master - LEARN_RATE * (
        first_new / corr_one / (jnp.sqrt(second_new / corr_two) + ADAM_EPS) + DECAY * master
    )
    return (master_new, first_new, second_new)


def pack_row(device):
    return (1283 * device) // 64


def join_kernel(blocks_ref, out_ref):
    step = pl.program_id(0)
    first = jnp.minimum((step * (128 * 64)) // 1283, 118)
    first = (first // 2) * 2
    window = blocks_ref[pl.ds(pl.multiple_of(first * 24, 48), 240), :]
    row = step * 128 + lax.broadcasted_iota(jnp.int32, (128, 240), 0)
    place = lax.broadcasted_iota(jnp.int32, (128, 240), 1)
    device = (place * 2731) >> 16
    source = ((1283 * (first + device)) >> 6) + place - 24 * device
    chosen = (source == row).astype(FLOAT).astype(BFLOAT)
    out_ref[...] = jnp.dot(chosen, window, preferred_element_type=FLOAT).astype(BFLOAT)


def join_pack(blocks):
    return pl.pallas_call(
        join_kernel,
        grid=(PACK_PAD // 128,),
        in_specs=[pl.BlockSpec((128 * 24, D), lambda i: (0, 0))],
        out_specs=pl.BlockSpec((128, D), lambda i: (i, 0)),
        out_shape=jax.ShapeDtypeStruct((PACK_PAD, D), BFLOAT),
        compiler_params=pltpu.CompilerParams(vmem_limit_bytes=32 * 1024 * 1024),
    )(blocks)


def stage(value, axis, index):
    total = lax.dynamic_index_in_dim(value, index, 0, False).astype(FLOAT)
    for k in (1, 2, 3):
        sent = lax.dynamic_index_in_dim(value, (index + k) % 4, 0, False)
        total = total + shift(sent, axis, k).astype(FLOAT)
    return total


def stage_near(value, axis):
    total = value[0].astype(FLOAT)
    for k in (1, 2, 3):
        total = total + shift(value[k], axis, -k).astype(FLOAT)
    return total


def shards(
    token_ids,
    targets,
    loss_rows,
    selections,
    boundary,
    pack_master,
    pack_first,
    pack_second,
    mlp_master,
    mlp_first,
    mlp_second,
    table_master,
    table_first,
    table_second,
):
    z = lax.axis_index("z")
    core = lax.axis_index("core")
    y = lax.axis_index("y")
    x = lax.axis_index("x")
    model_index = z * 2 + core
    data_index = y * 4 + x
    device = model_index * DP + data_index
    groups_per = HEADS // KV_HEADS
    scale = HEAD_DIM ** (-0.5)
    own_table = table_master.astype(BFLOAT)

    near = jnp.stack([((z + k) % 4) * 2 + (core ^ j) for j in (0, 1) for k in range(4)])
    near_rows = (near[:, None] * TOK_DEV + jnp.arange(TOK_DEV, dtype=jnp.int32)[None, :]).reshape(-1)

    pack_offset = PACK_DEV * device - D * pack_row(device)
    pack_block = lax.dynamic_update_slice(
        jnp.zeros((24 * D,), BFLOAT), pack_master.astype(BFLOAT), (pack_offset,)
    ).reshape(24, D)
    pack_blocks = lax.all_gather(pack_block, ALL_AXES, axis=0, tiled=True)
    mlp_own = mlp_master.astype(BFLOAT)
    mlp_quad = jnp.concatenate([mlp_own] + [shift(mlp_own, "z", k) for k in (1, 2, 3)], axis=1)
    mlp_blocks = lax.all_gather(mlp_quad.reshape(3 * 80, D), ("core", "y", "x"), axis=0, tiled=True)
    table = lax.all_gather(own_table, DP_AXES, axis=0, tiled=True)

    group_ids = token_ids[0]
    near_ids = reorder(group_ids.reshape(MP, TOK_DEV), near).reshape(-1)
    local_ids = near_ids - model_index * VOCAB_MP
    inside = (local_ids >= 0) & (local_ids < VOCAB_MP)
    high = local_ids >> 7
    low = local_ids & 127
    high_hot = (high[:, None] == jnp.arange(48)[None, :]).astype(BFLOAT)
    low_hot = (low[:, None] == jnp.arange(128)[None, :]).astype(BFLOAT)
    present = (contract_rows(high_hot, low_hot) > 0).reshape(DP, VOCAB_DEV)
    before = (jnp.arange(VOCAB_DEV)[:, None] < jnp.arange(VOCAB_DEV)[None, :]).astype(BFLOAT)
    slots = mm(present.astype(BFLOAT), before)
    asked = present & (slots < CAP)
    over = jnp.max(jnp.where(present & (slots >= CAP), 1.0, 0.0))
    over = sum_all(jnp.full((1, 128), over, FLOAT))[0, 0] > 0
    slot_table = jnp.where(asked, slots, 255.0).reshape(48, 128).astype(BFLOAT)
    token_slot = jnp.sum(mm(high_hot, slot_table) * low_hot.astype(FLOAT), axis=-1)
    token_place = jnp.where(
        inside & (token_slot < CAP), (high // 3) * CAP + token_slot.astype(jnp.int32), -1
    )
    place_hot = (token_place[:, None] == jnp.arange(DP * CAP)[None, :]).astype(BFLOAT)
    match = asked[:, None, :] & (slots[:, None, :] == jnp.arange(CAP, dtype=FLOAT)[None, :, None])
    request = (
        jnp.sum(jnp.where(match, jnp.arange(1, VOCAB_DEV + 1, dtype=FLOAT)[None, None, :], 0.0), axis=-1)
        - 1.0
    )
    request = lax.all_to_all(request, DP_AXES, 0, 0, tiled=True)
    owner_hot = (
        request.reshape(-1)[:, None] == jnp.arange(VOCAB_DEV, dtype=FLOAT)[None, :]
    ).astype(BFLOAT)
    sent_rows = mm(owner_hot, own_table).astype(BFLOAT)
    asked_rows = lax.all_to_all(sent_rows, DP_AXES, 0, 0, tiled=True)

    def looked_sparse():
        return mm(place_hot, asked_rows).astype(BFLOAT)

    def looked_dense():
        full = lax.all_gather(own_table, DP_AXES, axis=0, tiled=True)
        rows = jnp.take(full, jnp.clip(local_ids, 0, VOCAB_MP - 1), axis=0)
        return jnp.where(inside[:, None], rows, jnp.zeros_like(rows))

    looked = lax.cond(over, looked_dense, looked_sparse)
    looked, pack_blocks = tie(looked, pack_blocks)
    hidden = scatter_group(looked.reshape(2, 4, TOK_DEV, D), FLOAT)

    pack_weights = join_pack(pack_blocks)
    w_query = pack_weights[:960]
    w_key = pack_weights[960:1280].reshape(D, KV_HEADS * HEAD_DIM)
    w_value = pack_weights[1280:1600].reshape(D, KV_HEADS * HEAD_DIM)
    w_out = pack_weights[1600:2560]
    gains = pack_weights[2560:2563].astype(FLOAT)
    router = pack_weights[2563:2566].astype(FLOAT)
    mlp_weights = (
        mlp_blocks.reshape(2, 4, 4, 3, 80, D).transpose(3, 0, 2, 1, 4, 5).reshape(3, FF, D)
    )
    gate_w = mlp_weights[0]
    up_w = mlp_weights[1]
    down_w = mlp_weights[2]

    first_row = data_index * ROWS + model_index * TOK_DEV
    query_rows = first_row + jnp.arange(TOK_DEV, dtype=jnp.int32)
    cosine, sine = rotation(query_rows)
    group_sel = selections.reshape(RECUR, DP, MP, TOK_DEV)
    prev_index = jnp.maximum(data_index - 1, 0)
    here_sel = lax.dynamic_index_in_dim(group_sel, data_index, 1, False)
    own_sel = lax.dynamic_index_in_dim(here_sel, model_index, 1, False)
    near_sel = reorder(here_sel, near).reshape(RECUR, ROWS)
    prev_sel = reorder(lax.dynamic_index_in_dim(group_sel, prev_index, 1, False), near)
    prev_sel = prev_sel.reshape(RECUR, ROWS)
    start = lax.dynamic_index_in_dim(boundary, data_index, 0, False)
    prev_start = lax.dynamic_index_in_dim(boundary, prev_index, 0, False)
    place = (model_index * TOK_DEV + jnp.arange(TOK_DEV, dtype=jnp.int32))[None, None, :]
    key_place = near_rows[None, :, None]
    own_seen = (
        (key_place <= place)
        & ((key_place < start) == (place < start))
        & ((near_sel[:, :, None] > 0) | (key_place == place))
    )
    prev_seen = (
        (data_index > 0) & (place < start) & (key_place >= prev_start) & (prev_sel[:, :, None] > 0)
    )
    biases = jnp.concatenate(
        [prev_seen[:, :512], own_seen[:, :512], prev_seen[:, 512:], own_seen[:, 512:]], axis=1
    )
    biases = jnp.where(biases, 0.0, MASKED)

    saves = []
    penalty_total = jnp.zeros((), FLOAT)
    for step in range(RECUR):
        normed = rms_scale(hidden, gains[0]).astype(BFLOAT)
        keys_own = rotate(mm(normed, w_key).reshape(TOK_DEV, KV_HEADS, HEAD_DIM), cosine, sine)
        values_own = mm(normed, w_value)
        pair = jnp.concatenate([keys_own.reshape(TOK_DEV, -1), values_own], axis=1).astype(BFLOAT)
        pairs = group_gather(pair)
        queries = (
            rotate(mm(normed, w_query).reshape(TOK_DEV, HEADS, HEAD_DIM), cosine, sine) * scale
        ).astype(BFLOAT)
        attended, log_total = attend(queries.reshape(TOK_DEV, -1), pairs, biases[step])
        mixed = hidden + mm(attended, w_out)
        mlp_input = rms_scale(mixed, gains[1]).astype(BFLOAT)
        gate_pre = contract_cols(mlp_input, gate_w)
        up_pre = contract_cols(mlp_input, up_w)
        inner = (jax.nn.silu(gate_pre) * up_pre).astype(BFLOAT)
        branch = mixed + mm(inner, down_w)
        logit = jnp.dot(hidden, router[step], precision=HIGHEST)
        chosen = own_sel[step].astype(FLOAT)
        weight_sel = chosen * jax.nn.sigmoid(logit)
        new_hidden = hidden + weight_sel[:, None] * (branch - hidden)
        penalty_total = penalty_total + jnp.sum(jax.nn.softplus(logit) - chosen * logit)
        saves.append(
            (
                hidden,
                normed,
                queries,
                pairs,
                log_total,
                attended,
                mixed,
                mlp_input,
                gate_pre,
                up_pre,
                inner,
                branch,
                logit,
            )
        )
        hidden = new_hidden

    normed_final = rms_scale(hidden, gains[2]).astype(BFLOAT)
    final_rows = gather_group(normed_final).reshape(ROWS, D)
    row_targets = lax.dynamic_index_in_dim(targets, data_index, 0, keepdims=False)
    head_args = (loss_rows[0][:, None], near_rows[None, :])
    local_targets = (row_targets - model_index * VOCAB_MP)[:, None]
    logits, picked, stats = head(*head_args, final_rows, local_targets, table)
    stats = stats[:, :3].T

    def join_stats(parts):
        top = parts[0][0]
        for part in parts[1:]:
            top = jnp.maximum(top, part[0])
        total = sum(part[1] * jnp.exp(part[0] - top) for part in parts)
        return jnp.stack([top, total, sum(part[2] for part in parts)])

    stats = join_stats([stats, swap(stats)])
    stats = join_stats([stats] + [shift(stats, "z", k) for k in (1, 2, 3)])
    log_norm = stats[0] + jnp.log(stats[1])
    cross = log_norm - stats[2]
    per_device = cross.shape[0] // MP
    loss_part = (
        jnp.sum(lax.dynamic_slice_in_dim(cross, model_index * per_device, per_device))
        + ROUTER_LOSS * penalty_total
    )
    head_grad, scattered = head_back(
        *head_args, local_targets, log_norm[:, None], logits, picked, table
    )
    grad_final = scatter_group(scattered.reshape(2, 4, TOK_DEV, D), FLOAT)
    grad_hidden, grad_gain_final = rms_back(hidden, gains[2], grad_final)
    head_grad = lax.psum_scatter(head_grad, DP_AXES, scatter_dimension=0, tiled=True)

    kept = []
    mlp_parts = []
    router_rows = [None] * RECUR
    gain_one = jnp.zeros((D,), FLOAT)
    gain_two = jnp.zeros((D,), FLOAT)
    for step in reversed(range(RECUR)):
        grad_new = grad_hidden
        (
            hidden_in,
            normed,
            queries,
            pairs,
            log_total,
            attended,
            mixed,
            mlp_input,
            gate_pre,
            up_pre,
            inner,
            branch,
            logit,
        ) = saves[step]
        chosen = own_sel[step].astype(FLOAT)
        sigma = jax.nn.sigmoid(logit)
        weight_sel = chosen * sigma
        grad_branch = weight_sel[:, None] * grad_new
        grad_weight = jnp.sum(grad_new * (branch - hidden_in), axis=-1)
        grad_logit = grad_weight * chosen * sigma * (1.0 - sigma) + ROUTER_LOSS / TOK_DEV * (
            sigma - chosen
        )
        grad_in = (
            grad_new - weight_sel[:, None] * grad_new + grad_logit[:, None] * router[step][None, :]
        )
        router_rows[step] = jnp.dot(grad_logit, hidden_in, precision=HIGHEST)
        grad_rows = grad_branch.astype(BFLOAT)
        grad_inner = contract_cols(grad_rows, down_w)
        sigma_gate = jax.nn.sigmoid(gate_pre)
        grad_gate = (
            grad_inner * up_pre * sigma_gate * (1.0 + gate_pre * (1.0 - sigma_gate))
        ).astype(BFLOAT)
        grad_up = (grad_inner * gate_pre * sigma_gate).astype(BFLOAT)
        mlp_parts.append((grad_gate, grad_up, inner, mlp_input, mlp_input, grad_rows))
        grad_normed_two = mm(grad_gate, gate_w) + mm(grad_up, up_w)
        grad_mixed_norm, part_two = rms_back(mixed, gains[1], grad_normed_two)
        gain_two = gain_two + part_two
        grad_mixed = grad_branch + grad_mixed_norm
        grad_in = grad_in + grad_mixed
        grad_attn = grad_mixed.astype(BFLOAT)
        grad_attended = (
            contract_cols(grad_attn, w_out).astype(BFLOAT)
        )
        if step == 0:
            mlp_kept = [jnp.concatenate(parts, axis=0) for parts in zip(*mlp_parts)]
            far = mlp_grads(1 - core, mlp_kept[:3], mlp_kept[3:])
            grad_attended, far, head_grad = tie(grad_attended, far, head_grad)
            far = swap(far)
        grad_queries, *grad_sides = attend_back(
            queries.reshape(TOK_DEV, -1), pairs, biases[step], log_total, attended, grad_attended
        )
        if step == 0:
            far, *grad_sides = tie(far, *grad_sides)
            mlp_half = mlp_grads(core, mlp_kept[:3], mlp_kept[3:], far)
        grad_own = group_scatter(*grad_sides)
        grad_query_pre = (
            rotate(grad_queries.reshape(TOK_DEV, HEADS, HEAD_DIM), cosine, -sine)
            .reshape(TOK_DEV, -1)
            .astype(BFLOAT)
        )
        grad_key_pre = (
            rotate(grad_own[:, :320].reshape(TOK_DEV, KV_HEADS, HEAD_DIM), cosine, -sine)
            .reshape(TOK_DEV, -1)
            .astype(BFLOAT)
        )
        grad_value_pre = grad_own[:, 320:].astype(BFLOAT)
        grad_normed = (
            contract_cols(grad_query_pre, w_query)
            + contract_cols(grad_key_pre, w_key)
            + contract_cols(grad_value_pre, w_value)
        )
        grad_hidden_norm, part_one = rms_back(hidden_in, gains[0], grad_normed)
        gain_one = gain_one + part_one
        grad_hidden = grad_in + grad_hidden_norm
        kept.append(
            (
                normed,
                grad_query_pre,
                grad_key_pre,
                grad_value_pre,
                attended,
                grad_attn,
            )
        )
    (
        normed_all,
        grad_query_all,
        grad_key_all,
        grad_value_all,
        attended_all,
        grad_attn_all,
    ) = [jnp.concatenate(parts, axis=0) for parts in zip(*kept)]

    mlp_half = mlp_half.reshape(3, 4, 4, 80, D)
    cols = mlp_half[..., :512].transpose(1, 2, 0, 3, 4)
    part = stage(stage(cols, "x", x).astype(BFLOAT), "y", y).astype(BFLOAT)
    left = stage_near(part.reshape(3, 4, UNITS, -1).transpose(1, 0, 2, 3), "z")
    cols = mlp_half[..., 512:].transpose(2, 1, 0, 3, 4)
    part = stage(stage(cols, "y", y).astype(BFLOAT), "x", x).astype(BFLOAT)
    right = stage_near(part.reshape(3, 4, UNITS, -1).transpose(1, 0, 2, 3), "z")
    mlp_grad = jnp.concatenate([left, right], axis=-1)

    def aligned_row(which):
        return (pack_row(which) // 16) * 16

    small = jnp.concatenate(
        [
            jnp.stack([gain_one, gain_two, grad_gain_final] + router_rows),
            jnp.zeros((10, D), FLOAT),
        ]
    )
    starts = jnp.stack(
        [aligned_row(DP * (2 * i + c)) for c in (core, 1 - core) for i in range(4)]
    ).astype(jnp.int32)
    mine, other = pack_grads(
        starts,
        normed_all,
        grad_query_all,
        grad_key_all,
        grad_value_all,
        attended_all,
        grad_attn_all,
        small,
    )
    half = (mine.astype(FLOAT) + swap(other).astype(FLOAT)).astype(BFLOAT)

    def y_windows(value):
        return jnp.stack([value[..., 80 * i : 80 * i + 112, :] for i in range(4)])

    def x_windows(value):
        return jnp.stack([value[..., i : i + 48, :] for i in (0, 16, 40, 56)])

    part = stage(y_windows(half[..., :512]), "y", y).astype(BFLOAT)
    part = stage(part, "z", z).astype(BFLOAT)
    left = stage(x_windows(part), "x", x)
    part = stage(half[..., 512:], "z", z).astype(BFLOAT)
    part = stage(y_windows(part), "y", y).astype(BFLOAT)
    right = stage(x_windows(part), "x", x)
    part = jnp.concatenate([left, right], axis=-1).reshape(-1)
    begin = aligned_row(DP * model_index) + 80 * y + (20 * x) // 8 * 8
    pack_grad = lax.dynamic_slice(part, (PACK_DEV * device - D * begin,), (PACK_DEV,))

    grad_embed = gather_group(grad_hidden.astype(BFLOAT)).reshape(ROWS, D)

    unique = contract_rows(place_hot, grad_embed).astype(BFLOAT)
    unique = lax.all_to_all(unique, DP_AXES, 0, 0, tiled=True)

    def embed_sparse():
        return contract_rows(owner_hot, unique)

    def embed_dense():
        kept_rows = grad_embed.astype(FLOAT) * inside.astype(FLOAT)[:, None]
        sums = jax.ops.segment_sum(
            kept_rows, jnp.clip(local_ids, 0, VOCAB_MP - 1), num_segments=VOCAB_MP
        )
        return lax.psum_scatter(
            sums.astype(BFLOAT), DP_AXES, scatter_dimension=0, tiled=True
        ).astype(FLOAT)

    table_grad = head_grad.astype(FLOAT) + lax.cond(over, embed_dense, embed_sparse)

    squares = (
        jnp.sum(pack_grad * pack_grad)
        + jnp.sum(mlp_grad * mlp_grad)
        + jnp.sum(table_grad * table_grad)
    )
    lane = lax.broadcasted_iota(jnp.int32, (1, 128), 1)
    sums = sum_all(jnp.where(lane == 0, squares, loss_part))
    total_squares = sums[0, 0]
    loss_sum = sums[0, 1]
    grad_norm = jnp.sqrt(total_squares)
    clip = CLIP_NORM / jnp.maximum(grad_norm, CLIP_NORM)
    pack_new, pack_first_new, pack_second_new = adam_update(
        pack_master, pack_first, pack_second, pack_grad, clip
    )
    mlp_new, mlp_first_new, mlp_second_new = adam_update(
        mlp_master, mlp_first, mlp_second, mlp_grad, clip
    )
    table_new, table_first_new, table_second_new = adam_update(
        table_master, table_first, table_second, table_grad, clip
    )
    return (
        pack_new,
        pack_first_new,
        pack_second_new,
        mlp_new,
        mlp_first_new,
        mlp_second_new,
        table_new,
        table_first_new,
        table_second_new,
        loss_sum,
        grad_norm,
    )


def solution(mesh):
    grid = Mesh(mesh.devices.reshape(4, 2, 4, 4), ALL_AXES)
    owners = (P(ALL_AXES), P(None, ALL_AXES, None), P(ALL_AXES, None))
    group = P(DP_AXES, None)
    masters = tuple(spec for spec in owners for _ in range(3))
    return jax.shard_map(
        shards,
        mesh=grid,
        in_specs=(group, P(), group, P(), P()) + masters,
        out_specs=masters + (P(), P()),
        check_vma=False,
    )
```

time: 1920 us -> 1040 us (0.54)
  waiting for transfers between devices: 1030 us -> 257 us
  starting transfers between devices: 25.8 us -> 228 us
  matrix products: 271 us -> 109 us
  Pallas kernels: 0 us -> 124 us
  blocking collectives: 92.3 us -> 0 us
  local copies, waits for them, and re-layouts: 258 us -> 170 us
  other arithmetic: 193 us -> 106 us
    reduce_scatter x9 -> x1, waiting for transfers between devices: 329 us -> 0.01 us  [shards(): lax.psum_scatter(head_grad, DP_AXES, scatter_dimension=0, tiled=True)]
    unnamed x40 -> x4, waiting for transfers between devices: 318 us -> 1.08 us
    all_gather x13 -> x3, waiting for transfers between devices: 331 us -> 59.9 us  [the longest x1 59.8 us: shards(): pack_blocks = lax.all_gather(pack_block, ALL_AXES, axis=0, tiled=True)]
    ppermute x6 -> x135, starting transfers between devices: 22 us -> 214 us  [the longest x72 91.6 us: shift(): return lax.ppermute(value, axis, [(i, (i + steps) % 4) for i in range(4)])]
    ppermute x6 -> x135, waiting for transfers between devices: 55.4 us -> 187 us  [the longest x72 153 us: shift(): return lax.ppermute(value, axis, [(i, (i + steps) % 4) for i in range(4)])]
    pallas_call x0 -> x12, Pallas kernels: none -> 124 us  [the longest x3 38.6 us: attend_back(): pl.pallas_call(attend_back_kernel, out_shape=(jax.ShapeDtypeStruct((TOK_D...]
    dot_general x46 -> x31, matrix products: 167 us -> 49.7 us  [the longest x25 39.7 us: mm(): return jnp.dot(left, right, preferred_element_type=FLOAT)]
    concatenate x4, local copies, waits for them, and re-layouts: 76.6 us -> 2.91 us  [the longest x3 2.02 us: group_gather(): prev = jnp.concatenate(prev, axis=0)]
  transfers between devices with their start and end apart: 37 -> 142, of which waited for: 29 -> 62; matrix products, arithmetic and copies ran while one was open for 21% -> 29% of each run, Pallas kernels for 0% -> 10%
where the time goes in v1:
time: 1040 us; the launch traced here: 1020 us
  waiting for transfers between devices  257 us (25%)
  starting transfers between devices  228 us (22%)
  local copies, waits for them, and re-layouts  170 us (16%)
  Pallas kernels  124 us (12%)
  matrix products  109 us (10%)
  other arithmetic  106 us (10%)
  between operations  26.9 us (3%)
    ppermute x72, waiting for transfers between devices, shift(): return lax.ppermute(value, axis, [(i, (i + steps) % 4) for i in range(4)])  153 us
    ppermute x72, starting transfers between devices, shift(): return lax.ppermute(value, axis, [(i, (i + steps) % 4) for i in range(4)])  91.6 us
    unnamed x562, local copies, waits for them, and re-layouts  71.4 us
    all_gather x1, waiting for transfers between devices, shards(): pack_blocks = lax.all_gather(pack_block, ALL_AXES, axis=0, tiled=True)  59.8 us
    dot_general x21, matrix products, contract_cols(): lax.dot_general(left, right, (((1,), (1,)), ((), ())), preferred_element_...  54.1 us
    dot_general x25, matrix products, mm(): return jnp.dot(left, right, preferred_element_type=FLOAT)  39.7 us
    pallas_call x3, Pallas kernels, attend_back(): pl.pallas_call(attend_back_kernel, out_shape=(jax.ShapeDtypeStruct((TOK_D...  38.6 us
    ppermute x12, starting transfers between devices, group_gather(): prev.append(lax.ppermute(pair, ('z',) + DP_AXES, pairs))  37.1 us
  transfers between devices with their start and end apart: 142, of which 62 were waited for; matrix products, arithmetic and copies ran while one was open for 29% of the time, Pallas kernels for 10%

profile of v1, /device:TPU:1, one launch (start us, length us, event | category | flops | bytes accessed | tf_op | source)
XLA Modules:
  0.0 1020.5 jit_solution(3464874332154826251)
XLA Ops:
  13.4 6.8 all-to-all-start
  56.0 7.7 conditional.2
  79.7 59.8 %all-gather.7.cloned.1.call-done.blocks_ref = bf16[3072,960]{1,0:T(8,128)(2,1)} async-done(((bf16[24,960]{1,0:T(8,128)(2,1)}), bf16[3072,960]{1,0:T(8,128)(2,1)}) %all-gather.7.cloned.1.call-update) | async-done | bytes 5898256 | tf_op jit(solution)/shard_map/all_gather | solution.py:513
  147.3 5.2 shard_map.221
  168.0 6.5 collective-permute-done.11
  184.8 4.8 collective-permute-start.16
  195.3 4.5 collective-permute-start.19
  215.4 11.0 %shard_map.222 = (bf16[128,960]{1,0:T(8,128)(2,1)S(1)}, f32[8,384]{1,0:T(8,128)S(1)}) custom-call(bf16[128,960]{1,0:T(8,128)(2,1)S(1)} %copy.535.query_ref, bf16[512,640]{1,0:T(8,128)(2,1)} %constant_dynamic-update-slice_fusion.kv0, bf16[512,640]{1,0:T(8,128)(2,1)} %pad_maximum_fusion.14.kv1, bf16[512,640]{1,0:T(8,128)(2,1)} %collective-permute-done.21.kv2, ...), custom_call_target="tpu_custom_call" | custom-call | flops 12000000000 | bytes 5000000 | tf_op jit(solution)/shard_map/pallas_call | solution.py:200
  230.0 7.3 fusion.159
  255.2 7.2 collective-permute-start.26
  276.9 5.8 collective-permute-start.31
  294.8 11.0 %shard_map.223 = (bf16[128,960]{1,0:T(8,128)(2,1)S(1)}, f32[8,384]{1,0:T(8,128)S(1)}) custom-call(bf16[128,960]{1,0:T(8,128)(2,1)S(1)} %copy.544.query_ref, bf16[512,640]{1,0:T(8,128)(2,1)} %constant_dynamic-update-slice_fusion.4.kv0, bf16[512,640]{1,0:T(8,128)(2,1)S(1)} %pad_maximum_fusion.15.kv1, bf16[512,640]{1,0:T(8,128)(2,1)} %collective-permute-done.33.kv2, ...), custom_call_target="tpu_custom_call" | custom-call | flops 12000000000 | bytes 5000000 | tf_op jit(solution)/shard_map/pallas_call | solution.py:200
  310.7 5.9 multiply_convert_fusion.7
  328.4 5.3 collective-permute-start.37
  342.9 7.3 collective-permute-start.40
  361.4 10.9 %shard_map.224 = (bf16[128,960]{1,0:T(8,128)(2,1)S(1)}, f32[8,384]{1,0:T(8,128)S(1)}) custom-call(bf16[128,960]{1,0:T(8,128)(2,1)S(1)} %copy.563.query_ref, bf16[512,640]{1,0:T(8,128)(2,1)} %constant_dynamic-update-slice_fusion.8.kv0, bf16[512,640]{1,0:T(8,128)(2,1)S(1)} %pad_maximum_fusion.16.kv1, bf16[512,640]{1,0:T(8,128)(2,1)} %collective-permute-done.42.kv2, ...), custom_call_target="tpu_custom_call" | custom-call | flops 12000000000 | bytes 5000000 | tf_op jit(solution)/shard_map/pallas_call | solution.py:200
  376.6 5.9 multiply_convert_fusion.6
  385.0 4.6 collective-permute-start.45
  389.7 5.4 collective-permute-done.46
  395.1 6.6 collective-permute-done.45
  410.5 4.6 copy-done
  415.0 10.0 shard_map.225
  437.7 15.7 %shard_map.226 = (bf16[6144,960]{1,0:T(8,128)(2,1)S(1)}, bf16[1024,960]{1,0:T(8,128)(2,1)S(1)}) custom-call(s32[256,1]{1,0:T(8,128)S(1)} %copy.557.rows_ref, s32[1,1024]{1,0:T(1,128)S(1)} %bitcast.577, s32[256,1]{1,0:T(8,128)S(1)} %copy.558.target_ref, f32[256,1]{1,0:T(8,128)S(1)} %fusion.97.norm_ref, f32[256,6144]{1,0:T(8,128)S(1)} %get-tuple-element.94.logit_ref, ...), custom_call_target="tpu_custom_call" | custom-call | tf_op jit(solution)/shard_map/pallas_call | solution.py:339
  453.4 4.5 copy-done.7
  470.5 4.8 collective-permute-done.55
  478.4 6.7 collective-permute-done.53
  488.0 5.5 multiply_convert_fusion.4
  504.4 12.9 %shard_map.227 = (f32[128,960]{1,0:T(8,128)S(1)}, bf16[512,640]{1,0:T(8,128)(2,1)S(1)}, bf16[512,640]{1,0:T(8,128)(2,1)S(1)}, bf16[512,640]{1,0:T(8,128)(2,1)}, bf16[512,640]{1,0:T(8,128)(2,1)S(1)}) custom-call(bf16[128,960]{1,0:T(8,128)(2,1)S(1)} %copy-done.41, bf16[512,640]{1,0:T(8,128)(2,1)} %constant_dynamic-update-slice_fusion.8.kv0, ...), custom_call_target="tpu_custom_call" | custom-call | flops 20000000000 | bytes 9000000 | tf_op jit(solution)/shard_map/pallas_call | solution.py:245
  535.9 5.7 collective-permute-done.61
  553.6 4.9 multiply_convert_fusion.2
  565.2 13.2 %shard_map.228 = (f32[128,960]{1,0:T(8,128)S(1)}, bf16[512,640]{1,0:T(8,128)(2,1)S(1)}, bf16[512,640]{1,0:T(8,128)(2,1)S(1)}, bf16[512,640]{1,0:T(8,128)(2,1)}, bf16[512,640]{1,0:T(8,128)(2,1)}) custom-call(bf16[128,960]{1,0:T(8,128)(2,1)S(1)} %copy-done.39, bf16[512,640]{1,0:T(8,128)(2,1)} %constant_dynamic-update-slice_fusion.4.kv0, ...), custom_call_target="tpu_custom_call" | custom-call | flops 20000000000 | bytes 9000000 | tf_op jit(solution)/shard_map/pallas_call | solution.py:245
  599.6 6.5 collective-permute-done.70
  624.8 5.9 shard_map.229
  641.2 10.3 %copy.587 = bf16[3,1280,960]{1,2,0:T(8,128)(2,1)} copy(bf16[3,1280,960]{2,1,0:T(8,128)(2,1)} %copy-done.1) | data formatting | bytes 14745600 | tf_op jit(solution)/shard_map/optimization_barrier | solution.py:127
  682.3 12.5 %shard_map.230 = (f32[128,960]{1,0:T(8,128)S(1)}, bf16[512,640]{1,0:T(8,128)(2,1)S(1)}, bf16[512,640]{1,0:T(8,128)(2,1)S(1)}, bf16[512,640]{1,0:T(8,128)(2,1)S(1)}, bf16[512,640]{1,0:T(8,128)(2,1)S(1)}) custom-call(bf16[128,960]{1,0:T(8,128)(2,1)S(1)} %copy-done.37, bf16[512,640]{1,0:T(8,128)(2,1)} %constant_dynamic-update-slice_fusion.kv0, ...), custom_call_target="tpu_custom_call" | custom-call | flops 20000000000 | bytes 9000000 | tf_op jit(solution)/shard_map/pallas_call | solution.py:245
  707.2 10.6 %copy.595.refs_6_ = bf16[3,1280,960]{2,1,0:T(8,128)(2,1)} copy(bf16[3,1280,960]{1,2,0:T(8,128)(2,1)} %collective-permute-done.74) | data formatting | bytes 14745600 | tf_op jit(solution)/shard_map/optimization_barrier | solution.py:127
  720.9 7.8 shard_map.232
  752.8 15.3 %collective-permute-start.114 = (bf16[4,3,80,448]{3,2,1,0:T(8,128)(2,1)}, bf16[4,3,80,448]{3,2,1,0:T(8,128)(2,1)}, u32[]{:S(2)}, u32[]{:S(2)}) collective-permute-start(bf16[4,3,80,448]{3,2,1,0:T(8,128)(2,1)} %bitcast.563), channel_id=1, source_target_pairs={{0,12},{4,0},{8,4},{12,8},{1,13},{5,1},{9,5},{13,9},{2,14},{6,2},{... | collective-permute-start | bytes 2580488 | tf_op jit(solution)/shard_map/ppermute | solution.py:48
  778.6 30.6 %collective-permute-done.114 = bf16[4,3,80,448]{3,2,1,0:T(8,128)(2,1)} collective-permute-done((bf16[4,3,80,448]{3,2,1,0:T(8,128)(2,1)}, bf16[4,3,80,448]{3,2,1,0:T(8,128)(2,1)}, u32[]{:S(2)}, u32[]{:S(2)}) %collective-permute-start.114) | collective-permute-done | bytes 860192 | tf_op jit(solution)/shard_map/ppermute | solution.py:48
  818.6 7.8 shard_map.231
  826.4 4.6 collective-permute-start.122
  870.9 4.1 collective-permute-start.118
  892.7 5.6 all-to-all-done.2
  911.1 4.7 collective-permute-done.96
  917.3 10.1 collective-permute-done.94
  938.6 5.5 collective-permute-done.87
  947.0 10.5 %collective-permute-done.85 = bf16[4,112,512]{2,1,0:T(8,128)(2,1)S(1)} collective-permute-done((bf16[4,112,512]{2,1,0:T(8,128)(2,1)S(1)}, bf16[4,112,512]{2,1,0:T(8,128)(2,1)S(1)}, u32[]{:S(2)}, u32[]{:S(2)}) %collective-permute-start.85) | collective-permute-done | bytes 458784 | tf_op jit(solution)/shard_map/ppermute | solution.py:48
  997.1 5.3 multiply_subtract_fusion
  (1162 shorter events, 568.7 us)
Async XLA Ops:
  11.0 22.3 %collective-permute-start = (f32[1,128]{1,0:T(1,128)S(1)}, f32[1,128]{1,0:T(1,128)S(1)}, u32[]{:S(2)}, u32[]{:S(2)}) collective-permute-start(f32[1,128]{1,0:T(1,128)S(1)} %broadcast_in_dim.130), channel_id=1, source_target_pairs={{0,16},{16,0},{1,17},{17,1},{2,18},{18,2},{3,19},{19,3},{4,20},{20... | collective-permute-start | bytes 1544 | tf_op jit(solution)/shard_map/ppermute | solution.py:52
  29.7 26.2 %all-to-all-start.1 = ((bf16[16,24,960]{2,1,0:T(8,128)(2,1)}), bf16[16,24,960]{2,1,0:T(8,128)(2,1)S(1)}, u32[]{:S(2)}, u32[]{:S(2)}) async-start(bf16[16,24,960]{2,1,0:T(8,128)(2,1)} %bitcast.23), calls=%async_computation.2 | async-start | bytes 1572864 | tf_op jit(solution)/shard_map/all_to_all | solution.py:549
  63.7 75.9 %all-gather.7.cloned.1.call-start = ((), (), s32[]{:S(2)}) async-start(), calls=%async_computation.7 | async-start | bytes 6340608 | tf_op jit(solution)/shard_map/all_gather | solution.py:513
  64.2 165.8 %all-gather.9.cloned.1.call-start = ((), (), s32[]{:S(2)}) async-start(), calls=%async_computation.8 | async-start | bytes 16220160 | tf_op jit(solution)/shard_map/all_gather | solution.py:516
  73.0 337.4 %all-gather.11.cloned.1.call-start = ((), (), s32[]{:S(2)}) async-start(), calls=%async_computation.9 | async-start | bytes 13369344 | tf_op jit(solution)/shard_map/all_gather | solution.py:517
  73.6 567.6 %reduce-scatter.5.cloned.1.call-start = ((), (), s32[]{:S(2)}) async-start(), calls=%async_computation.10 | async-start | bytes 13369344 | tf_op jit(solution)/shard_map/reduce_scatter | solution.py:675
  142.0 14.3 %collective-permute-start.10 = (bf16[4,128,960]{1,2,0:T(8,128)(2,1)}, bf16[4,128,960]{1,2,0:T(8,128)(2,1)S(1)}, u32[]{:S(2)}, u32[]{:S(2)}) collective-permute-start(bf16[4,128,960]{1,2,0:T(8,128)(2,1)} %copy.529), channel_id=1, source_target_pairs={{0,16},{16,0},{1,17},{17,1},{2,18},{18,2},{3,19},{19,3},{4,20},{20... | collective-permute-start | bytes 2949128 | tf_op jit(solution)/shard_map/ppermute | solution.py:52
  159.6 14.8 %collective-permute-start.11 = (bf16[128,960]{1,0:T(8,128)(2,1)}, bf16[128,960]{1,0:T(8,128)(2,1)}, u32[]{:S(2)}, u32[]{:S(2)}) collective-permute-start(bf16[128,960]{1,0:T(8,128)(2,1)} %get-tuple-element.323), channel_id=1, source_target_pairs={{0,32},{32,64},{64,96},{96,0},{1,33},{33,65},{65,97},{97,1},{2,34}... | collective-permute-start | bytes 737288 | tf_op jit(solution)/shard_map/ppermute | solution.py:48
  180.9 14.4 %collective-permute-start.14 = (bf16[128,640]{1,0:T(8,128)(2,1)S(1)}, bf16[128,640]{1,0:T(8,128)(2,1)S(1)}, u32[]{:S(2)}, u32[]{:S(2)}) collective-permute-start(bf16[128,640]{1,0:T(8,128)(2,1)S(1)} %pad_maximum_fusion.28), channel_id=1, source_target_pairs={{0,1},{1,2},{2,3},{3,4},{4,5},{5,6},{6,7},{7,8},{8,9},{9,10},{10,1... | collective-permute-start | bytes 491528 | tf_op jit(solution)/shard_map/ppermute | solution.py:140
  183.8 16.8 %collective-permute-start.15 = (bf16[128,640]{1,0:T(8,128)(2,1)S(1)}, bf16[128,640]{1,0:T(8,128)(2,1)S(1)}, u32[]{:S(2)}, u32[]{:S(2)}) collective-permute-start(bf16[128,640]{1,0:T(8,128)(2,1)S(1)} %pad_maximum_fusion.28), channel_id=1, source_target_pairs={{32,1},{33,2},{34,3},{35,4},{36,5},{37,6},{38,7},{39,8},{40,9},{41... | collective-permute-start | bytes 491528 | tf_op jit(solution)/shard_map/ppermute | solution.py:140
  184.8 17.7 %collective-permute-start.16 = (bf16[128,640]{1,0:T(8,128)(2,1)S(1)}, bf16[128,640]{1,0:T(8,128)(2,1)S(1)}, u32[]{:S(2)}, u32[]{:S(2)}) collective-permute-start(bf16[128,640]{1,0:T(8,128)(2,1)S(1)} %pad_maximum_fusion.28), channel_id=1, source_target_pairs={{64,1},{65,2},{66,3},{67,4},{68,5},{69,6},{70,7},{71,8},{72,9},{73... | collective-permute-start | bytes 491528 | tf_op jit(solution)/shard_map/ppermute | solution.py:140
  189.6 15.3 %collective-permute-start.17 = (bf16[128,640]{1,0:T(8,128)(2,1)S(1)}, bf16[128,640]{1,0:T(8,128)(2,1)S(1)}, u32[]{:S(2)}, u32[]{:S(2)}) collective-permute-start(bf16[128,640]{1,0:T(8,128)(2,1)S(1)} %pad_maximum_fusion.28), channel_id=1, source_target_pairs={{96,1},{97,2},{98,3},{99,4},{100,5},{101,6},{102,7},{103,8},{104,9... | collective-permute-start | bytes 491528 | tf_op jit(solution)/shard_map/ppermute | solution.py:140
  192.2 15.0 %collective-permute-start.20 = (bf16[128,640]{1,0:T(8,128)(2,1)S(1)}, bf16[128,640]{1,0:T(8,128)(2,1)S(1)}, u32[]{:S(2)}, u32[]{:S(2)}) collective-permute-start(bf16[128,640]{1,0:T(8,128)(2,1)S(1)} %pad_maximum_fusion.28), channel_id=1, source_target_pairs={{0,32},{32,64},{64,96},{1,33},{33,65},{65,97},{2,34},{34,66},{66,9... | collective-permute-start | bytes 491528 | tf_op jit(solution)/shard_map/ppermute | solution.py:133
  255.2 21.7 %collective-permute-start.26 = (bf16[128,640]{1,0:T(8,128)(2,1)S(1)}, bf16[128,640]{1,0:T(8,128)(2,1)S(1)}, u32[]{:S(2)}, u32[]{:S(2)}) collective-permute-start(bf16[128,640]{1,0:T(8,128)(2,1)S(1)} %pad_maximum_fusion.29), channel_id=1, source_target_pairs={{0,1},{1,2},{2,3},{3,4},{4,5},{5,6},{6,7},{7,8},{8,9},{9,10},{10,1... | collective-permute-start | bytes 491528 | tf_op jit(solution)/shard_map/ppermute | solution.py:140
  262.4 21.0 %collective-permute-start.27 = (bf16[128,640]{1,0:T(8,128)(2,1)S(1)}, bf16[128,640]{1,0:T(8,128)(2,1)S(1)}, u32[]{:S(2)}, u32[]{:S(2)}) collective-permute-start(bf16[128,640]{1,0:T(8,128)(2,1)S(1)} %pad_maximum_fusion.29), channel_id=1, source_target_pairs={{32,1},{33,2},{34,3},{35,4},{36,5},{37,6},{38,7},{39,8},{40,9},{41... | collective-permute-start | bytes 491528 | tf_op jit(solution)/shard_map/ppermute | solution.py:140
  263.1 22.3 %collective-permute-start.28 = (bf16[128,640]{1,0:T(8,128)(2,1)S(1)}, bf16[128,640]{1,0:T(8,128)(2,1)S(1)}, u32[]{:S(2)}, u32[]{:S(2)}) collective-permute-start(bf16[128,640]{1,0:T(8,128)(2,1)S(1)} %pad_maximum_fusion.29), channel_id=1, source_target_pairs={{64,1},{65,2},{66,3},{67,4},{68,5},{69,6},{70,7},{71,8},{72,9},{73... | collective-permute-start | bytes 491528 | tf_op jit(solution)/shard_map/ppermute | solution.py:140
  266.8 19.2 %collective-permute-start.29 = (bf16[128,640]{1,0:T(8,128)(2,1)S(1)}, bf16[128,640]{1,0:T(8,128)(2,1)S(1)}, u32[]{:S(2)}, u32[]{:S(2)}) collective-permute-start(bf16[128,640]{1,0:T(8,128)(2,1)S(1)} %pad_maximum_fusion.29), channel_id=1, source_target_pairs={{96,1},{97,2},{98,3},{99,4},{100,5},{101,6},{102,7},{103,8},{104,9... | collective-permute-start | bytes 491528 | tf_op jit(solution)/shard_map/ppermute | solution.py:140
  270.5 18.5 %collective-permute-start.32 = (bf16[128,640]{1,0:T(8,128)(2,1)S(1)}, bf16[128,640]{1,0:T(8,128)(2,1)S(1)}, u32[]{:S(2)}, u32[]{:S(2)}) collective-permute-start(bf16[128,640]{1,0:T(8,128)(2,1)S(1)} %pad_maximum_fusion.29), channel_id=1, source_target_pairs={{0,32},{32,64},{64,96},{1,33},{33,65},{65,97},{2,34},{34,66},{66,9... | collective-permute-start | bytes 491528 | tf_op jit(solution)/shard_map/ppermute | solution.py:133
  325.5 17.4 %collective-permute-start.35 = (bf16[128,640]{1,0:T(8,128)(2,1)S(1)}, bf16[128,640]{1,0:T(8,128)(2,1)S(1)}, u32[]{:S(2)}, u32[]{:S(2)}) collective-permute-start(bf16[128,640]{1,0:T(8,128)(2,1)S(1)} %pad_maximum_fusion.30), channel_id=1, source_target_pairs={{0,1},{1,2},{2,3},{3,4},{4,5},{5,6},{6,7},{7,8},{8,9},{9,10},{10,1... | collective-permute-start | bytes 491528 | tf_op jit(solution)/shard_map/ppermute | solution.py:140
  327.8 23.1 %collective-permute-start.36 = (bf16[128,640]{1,0:T(8,128)(2,1)S(1)}, bf16[128,640]{1,0:T(8,128)(2,1)S(1)}, u32[]{:S(2)}, u32[]{:S(2)}) collective-permute-start(bf16[128,640]{1,0:T(8,128)(2,1)S(1)} %pad_maximum_fusion.30), channel_id=1, source_target_pairs={{32,1},{33,2},{34,3},{35,4},{36,5},{37,6},{38,7},{39,8},{40,9},{41... | collective-permute-start | bytes 491528 | tf_op jit(solution)/shard_map/ppermute | solution.py:140
  328.4 24.4 %collective-permute-start.37 = (bf16[128,640]{1,0:T(8,128)(2,1)S(1)}, bf16[128,640]{1,0:T(8,128)(2,1)S(1)}, u32[]{:S(2)}, u32[]{:S(2)}) collective-permute-start(bf16[128,640]{1,0:T(8,128)(2,1)S(1)} %pad_maximum_fusion.30), channel_id=1, source_target_pairs={{64,1},{65,2},{66,3},{67,4},{68,5},{69,6},{70,7},{71,8},{72,9},{73... | collective-permute-start | bytes 491528 | tf_op jit(solution)/shard_map/ppermute | solution.py:140
  333.8 19.8 %collective-permute-start.38 = (bf16[128,640]{1,0:T(8,128)(2,1)S(1)}, bf16[128,640]{1,0:T(8,128)(2,1)S(1)}, u32[]{:S(2)}, u32[]{:S(2)}) collective-permute-start(bf16[128,640]{1,0:T(8,128)(2,1)S(1)} %pad_maximum_fusion.30), channel_id=1, source_target_pairs={{96,1},{97,2},{98,3},{99,4},{100,5},{101,6},{102,7},{103,8},{104,9... | collective-permute-start | bytes 491528 | tf_op jit(solution)/shard_map/ppermute | solution.py:140
  336.5 19.9 %collective-permute-start.41 = (bf16[128,640]{1,0:T(8,128)(2,1)S(1)}, bf16[128,640]{1,0:T(8,128)(2,1)S(1)}, u32[]{:S(2)}, u32[]{:S(2)}) collective-permute-start(bf16[128,640]{1,0:T(8,128)(2,1)S(1)} %pad_maximum_fusion.30), channel_id=1, source_target_pairs={{0,32},{32,64},{64,96},{1,33},{33,65},{65,97},{2,34},{34,66},{66,9... | collective-permute-start | bytes 491528 | tf_op jit(solution)/shard_map/ppermute | solution.py:133
  385.0 16.7 %collective-permute-start.45 = (bf16[128,960]{1,0:T(8,128)(2,1)S(1)}, bf16[128,960]{1,0:T(8,128)(2,1)S(1)}, u32[]{:S(2)}, u32[]{:S(2)}) collective-permute-start(bf16[128,960]{1,0:T(8,128)(2,1)S(1)} %multiply_convert_fusion.12), channel_id=1, source_target_pairs={{0,64},{32,96},{64,0},{96,32},{1,65},{33,97},{65,1},{97,33},{2,66}... | collective-permute-start | bytes 737288 | tf_op jit(solution)/shard_map/ppermute | solution.py:48
  470.0 15.1 %collective-permute-start.53 = (bf16[128,960]{1,0:T(8,128)(2,1)S(1)}, bf16[128,960]{1,0:T(8,128)(2,1)S(1)}, u32[]{:S(2)}, u32[]{:S(2)}) collective-permute-start(bf16[128,960]{1,0:T(8,128)(2,1)S(1)} %get-tuple-element.318), channel_id=1, source_target_pairs={{0,32},{32,64},{64,96},{96,0},{1,33},{33,65},{65,97},{97,1},{2,34}... | collective-permute-start | bytes 737288 | tf_op jit(solution)/shard_map/ppermute | solution.py:48
  527.0 14.6 %collective-permute-start.61 = (bf16[128,640]{1,0:T(8,128)(2,1)S(1)}, bf16[128,640]{1,0:T(8,128)(2,1)S(1)}, u32[]{:S(2)}, u32[]{:S(2)}) collective-permute-start(bf16[128,640]{1,0:T(8,128)(2,1)S(1)} %get-tuple-element.349), channel_id=1, source_target_pairs={{1,0},{2,1},{3,2},{4,3},{5,4},{6,5},{7,6},{8,7},{9,8},{10,9},{11,1... | collective-permute-start | bytes 491528 | tf_op jit(solution)/shard_map/ppermute | solution.py:158
  589.5 16.6 %collective-permute-start.70 = (bf16[128,640]{1,0:T(8,128)(2,1)S(1)}, bf16[128,640]{1,0:T(8,128)(2,1)S(1)}, u32[]{:S(2)}, u32[]{:S(2)}) collective-permute-start(bf16[128,640]{1,0:T(8,128)(2,1)S(1)} %get-tuple-element.342), channel_id=1, source_target_pairs={{1,0},{2,1},{3,2},{4,3},{5,4},{6,5},{7,6},{8,7},{9,8},{10,9},{11,1... | collective-permute-start | bytes 491528 | tf_op jit(solution)/shard_map/ppermute | solution.py:158
  651.4 49.5 %collective-permute-start.74 = (bf16[3,1280,960]{1,2,0:T(8,128)(2,1)}, bf16[3,1280,960]{1,2,0:T(8,128)(2,1)}, u32[]{:S(2)}, u32[]{:S(2)}) collective-permute-start(bf16[3,1280,960]{1,2,0:T(8,128)(2,1)} %copy.587), channel_id=1, source_target_pairs={{0,16},{16,0},{1,17},{17,1},{2,18},{18,2},{3,19},{19,3},{4,20},{20... | collective-permute-start | bytes 22118408 | tf_op jit(solution)/shard_map/ppermute | solution.py:52
  701.0 33.9 %collective-permute-start.79 = (bf16[512,640]{1,0:T(8,128)(2,1)}, bf16[512,640]{1,0:T(8,128)(2,1)}, u32[]{:S(2)}, u32[]{:S(2)}) collective-permute-start(bf16[512,640]{1,0:T(8,128)(2,1)} %copy-done.51), channel_id=1, source_target_pairs={{0,16},{16,0},{1,17},{17,1},{2,18},{18,2},{3,19},{19,3},{4,20},{20... | collective-permute-start | bytes 1966088 | tf_op jit(solution)/shard_map/ppermute | solution.py:52
  739.5 28.6 %collective-permute-start.80 = (bf16[128,640]{1,0:T(8,128)(2,1)S(1)}, bf16[128,640]{1,0:T(8,128)(2,1)S(1)}, u32[]{:S(2)}, u32[]{:S(2)}) collective-permute-start(bf16[128,640]{1,0:T(8,128)(2,1)S(1)} %get-tuple-element.335), channel_id=1, source_target_pairs={{1,0},{2,1},{3,2},{4,3},{5,4},{6,5},{7,6},{8,7},{9,8},{10,9},{11,1... | collective-permute-start | bytes 491528 | tf_op jit(solution)/shard_map/ppermute | solution.py:158
  741.1 27.1 %collective-permute-start.78 = (bf16[128,640]{1,0:T(8,128)(2,1)S(1)}, bf16[128,640]{1,0:T(8,128)(2,1)S(1)}, u32[]{:S(2)}, u32[]{:S(2)}) collective-permute-start(bf16[128,640]{1,0:T(8,128)(2,1)S(1)} %get-tuple-element.333), channel_id=1, source_target_pairs={{32,0},{64,32},{96,64},{33,1},{65,33},{97,65},{34,2},{66,34},{98,6... | collective-permute-start | bytes 491528 | tf_op jit(solution)/shard_map/ppermute | solution.py:152
  744.4 24.4 %collective-permute-start.77 = (bf16[128,640]{1,0:T(8,128)(2,1)S(1)}, bf16[128,640]{1,0:T(8,128)(2,1)S(1)}, u32[]{:S(2)}, u32[]{:S(2)}) collective-permute-start(bf16[128,640]{1,0:T(8,128)(2,1)S(1)} %get-tuple-element.334), channel_id=1, source_target_pairs={{64,0},{96,32},{65,1},{97,33},{66,2},{98,34},{67,3},{99,35},{68,4}... | collective-permute-start | bytes 491528 | tf_op jit(solution)/shard_map/ppermute | solution.py:152
  747.2 23.6 %collective-permute-start.76 = (bf16[128,640]{1,0:T(8,128)(2,1)S(1)}, bf16[128,640]{1,0:T(8,128)(2,1)S(1)}, u32[]{:S(2)}, u32[]{:S(2)}) collective-permute-start(bf16[128,640]{1,0:T(8,128)(2,1)S(1)} %get-tuple-element.332), channel_id=1, source_target_pairs={{96,0},{97,1},{98,2},{99,3},{100,4},{101,5},{102,6},{103,7},{104,8... | collective-permute-start | bytes 491528 | tf_op jit(solution)/shard_map/ppermute | solution.py:152
  752.8 56.4 %collective-permute-start.114 = (bf16[4,3,80,448]{3,2,1,0:T(8,128)(2,1)}, bf16[4,3,80,448]{3,2,1,0:T(8,128)(2,1)}, u32[]{:S(2)}, u32[]{:S(2)}) collective-permute-start(bf16[4,3,80,448]{3,2,1,0:T(8,128)(2,1)} %bitcast.563), channel_id=1, source_target_pairs={{0,12},{4,0},{8,4},{12,8},{1,13},{5,1},{9,5},{13,9},{2,14},{6,2},{... | collective-permute-start | bytes 2580488 | tf_op jit(solution)/shard_map/ppermute | solution.py:48
  768.1 41.7 %collective-permute-start.113 = (bf16[4,3,80,448]{3,2,1,0:T(8,128)(2,1)}, bf16[4,3,80,448]{3,2,1,0:T(8,128)(2,1)}, u32[]{:S(2)}, u32[]{:S(2)}) collective-permute-start(bf16[4,3,80,448]{3,2,1,0:T(8,128)(2,1)} %bitcast.564), channel_id=1, source_target_pairs={{0,8},{4,12},{8,0},{12,4},{1,9},{5,13},{9,1},{13,5},{2,10},{6,14},... | collective-permute-start | bytes 2580488 | tf_op jit(solution)/shard_map/ppermute | solution.py:48
  768.1 58.3 %collective-permute-start.112 = (bf16[4,3,80,448]{3,2,1,0:T(8,128)(2,1)}, bf16[4,3,80,448]{3,2,1,0:T(8,128)(2,1)}, u32[]{:S(2)}, u32[]{:S(2)}) collective-permute-start(bf16[4,3,80,448]{3,2,1,0:T(8,128)(2,1)} %bitcast.565), channel_id=1, source_target_pairs={{0,4},{4,8},{8,12},{12,0},{1,5},{5,9},{9,13},{13,1},{2,6},{6,10},{... | collective-permute-start | bytes 2580488 | tf_op jit(solution)/shard_map/ppermute | solution.py:48
  768.8 76.6 %collective-permute-start.105 = (bf16[4,3,80,512]{3,2,1,0:T(8,128)(2,1)}, bf16[4,3,80,512]{3,2,1,0:T(8,128)(2,1)}, u32[]{:S(2)}, u32[]{:S(2)}) collective-permute-start(bf16[4,3,80,512]{3,2,1,0:T(8,128)(2,1)} %bitcast.566), channel_id=1, source_target_pairs={{0,3},{1,0},{2,1},{3,2},{4,7},{5,4},{6,5},{7,6},{8,11},{9,8},{10,9... | collective-permute-start | bytes 2949128 | tf_op jit(solution)/shard_map/ppermute | solution.py:48
  770.7 75.7 %collective-permute-start.104 = (bf16[4,3,80,512]{3,2,1,0:T(8,128)(2,1)}, bf16[4,3,80,512]{3,2,1,0:T(8,128)(2,1)}, u32[]{:S(2)}, u32[]{:S(2)}) collective-permute-start(bf16[4,3,80,512]{3,2,1,0:T(8,128)(2,1)} %bitcast.567), channel_id=1, source_target_pairs={{0,2},{1,3},{2,0},{3,1},{4,6},{5,7},{6,4},{7,5},{8,10},{9,11},{10,... | collective-permute-start | bytes 2949128 | tf_op jit(solution)/shard_map/ppermute | solution.py:48
  809.3 37.2 %collective-permute-start.103 = (bf16[4,3,80,512]{3,2,1,0:T(8,128)(2,1)}, bf16[4,3,80,512]{3,2,1,0:T(8,128)(2,1)}, u32[]{:S(2)}, u32[]{:S(2)}) collective-permute-start(bf16[4,3,80,512]{3,2,1,0:T(8,128)(2,1)} %bitcast.568), channel_id=1, source_target_pairs={{0,1},{1,2},{2,3},{3,0},{4,5},{5,6},{6,7},{7,4},{8,9},{9,10},{10,1... | collective-permute-start | bytes 2949128 | tf_op jit(solution)/shard_map/ppermute | solution.py:48
  809.8 21.1 %collective-permute-start.123 = (bf16[128,960]{1,0:T(8,128)(2,1)S(1)}, bf16[128,960]{1,0:T(8,128)(2,1)}, u32[]{:S(2)}, u32[]{:S(2)}) collective-permute-start(bf16[128,960]{1,0:T(8,128)(2,1)S(1)} %fusion.56), channel_id=1, source_target_pairs={{0,32},{32,64},{64,96},{96,0},{1,33},{33,65},{65,97},{97,1},{2,34}... | collective-permute-start | bytes 737288 | tf_op jit(solution)/shard_map/ppermute | solution.py:48
  834.7 70.3 %collective-permute-start.84 = (bf16[4,352,960]{2,1,0:T(8,128)(2,1)}, bf16[4,352,960]{2,1,0:T(8,128)(2,1)}, u32[]{:S(2)}, u32[]{:S(2)}) collective-permute-start(bf16[4,352,960]{2,1,0:T(8,128)(2,1)} %get-tuple-element.122), channel_id=1, source_target_pairs={{0,16},{16,0},{1,17},{17,1},{2,18},{18,2},{3,19},{19,3},{4,20},{20... | collective-permute-start | bytes 8110088 | tf_op jit(solution)/shard_map/ppermute | solution.py:52
  846.5 29.7 %collective-permute-start.124 = (bf16[4,128,960]{1,2,0:T(8,128)(2,1)}, bf16[4,128,960]{1,2,0:T(8,128)(2,1)}, u32[]{:S(2)}, u32[]{:S(2)}) collective-permute-start(bf16[4,128,960]{1,2,0:T(8,128)(2,1)} %copy.602), channel_id=1, source_target_pairs={{0,16},{16,0},{1,17},{17,1},{2,18},{18,2},{3,19},{19,3},{4,20},{20... | collective-permute-start | bytes 2949128 | tf_op jit(solution)/shard_map/ppermute | solution.py:52
  863.3 23.2 %collective-permute-start.120 = (bf16[3,20,448]{2,1,0:T(8,128)(2,1)}, bf16[3,20,448]{2,1,0:T(8,128)(2,1)S(1)}, u32[]{:S(2)}, u32[]{:S(2)}) collective-permute-start(bf16[3,20,448]{2,1,0:T(8,128)(2,1)} %get-tuple-element.383), channel_id=1, source_target_pairs={{0,32},{32,64},{64,96},{96,0},{1,33},{33,65},{65,97},{97,1},{2,34}... | collective-permute-start | bytes 161288 | tf_op jit(solution)/shard_map/ppermute | solution.py:48
  863.4 23.6 %collective-permute-start.119 = (bf16[3,20,448]{2,1,0:T(8,128)(2,1)S(1)}, bf16[3,20,448]{2,1,0:T(8,128)(2,1)S(1)}, u32[]{:S(2)}, u32[]{:S(2)}) collective-permute-start(bf16[3,20,448]{2,1,0:T(8,128)(2,1)S(1)} %get-tuple-element.384), channel_id=1, source_target_pairs={{0,64},{32,96},{64,0},{96,32},{1,65},{33,97},{65,1},{97,33},{2,66}... | collective-permute-start | bytes 161288 | tf_op jit(solution)/shard_map/ppermute | solution.py:48
  870.9 18.2 %collective-permute-start.118 = (bf16[3,20,448]{2,1,0:T(8,128)(2,1)S(1)}, bf16[3,20,448]{2,1,0:T(8,128)(2,1)}, u32[]{:S(2)}, u32[]{:S(2)}) collective-permute-start(bf16[3,20,448]{2,1,0:T(8,128)(2,1)S(1)} %get-tuple-element.382), channel_id=1, source_target_pairs={{0,96},{32,0},{64,32},{96,64},{1,97},{33,1},{65,33},{97,65},{2,98}... | collective-permute-start | bytes 161288 | tf_op jit(solution)/shard_map/ppermute | solution.py:48
  881.9 16.4 %all-to-all-start.2 = ((bf16[16,24,960]{2,1,0:T(8,128)(2,1)}), bf16[16,24,960]{2,1,0:T(8,128)(2,1)S(1)}, u32[]{:S(2)}, u32[]{:S(2)}) async-start(bf16[16,24,960]{2,1,0:T(8,128)(2,1)} %bitcast.203), calls=%async_computation.4 | async-start | bytes 1572864 | tf_op jit(solution)/shard_map/all_to_all | solution.py:830
  910.6 16.8 %collective-permute-start.94 = (bf16[352,448]{1,0:T(8,128)(2,1)S(1)}, bf16[352,448]{1,0:T(8,128)(2,1)S(1)}, u32[]{:S(2)}, u32[]{:S(2)}) collective-permute-start(bf16[352,448]{1,0:T(8,128)(2,1)S(1)} %get-tuple-element.313), channel_id=1, source_target_pairs={{0,32},{32,64},{64,96},{96,0},{1,33},{33,65},{65,97},{97,1},{2,34}... | collective-permute-start | bytes 946184 | tf_op jit(solution)/shard_map/ppermute | solution.py:48
  933.9 23.5 %collective-permute-start.85 = (bf16[4,112,512]{2,1,0:T(8,128)(2,1)S(1)}, bf16[4,112,512]{2,1,0:T(8,128)(2,1)S(1)}, u32[]{:S(2)}, u32[]{:S(2)}) collective-permute-start(bf16[4,112,512]{2,1,0:T(8,128)(2,1)S(1)} %get-tuple-element.310), channel_id=1, source_target_pairs={{0,4},{4,8},{8,12},{12,0},{1,5},{5,9},{9,13},{13,1},{2,6},{6,10},{... | collective-permute-start | bytes 1376264 | tf_op jit(solution)/shard_map/ppermute | solution.py:48
  (363 other events, 3089.0 us)
Sparse Core Ops, SparseCore 1:
  67.7 71.7 all-gather.6
  141.7 77.5 all-gather.8
  221.2 98.7 all-gather.10
  458.0 100.0 reduce-scatter.4

commit v2 on v1

--- a/solution.py
+++ b/solution.py
@@ -4,6 +4,7 @@
 import jax.numpy as jnp
 from jax import lax
 from jax.experimental import pallas as pl
+from jax.experimental.layout import Layout, with_layout_constraint
 from jax.experimental.pallas import tpu as pltpu
 from jax.sharding import Mesh
 from jax.sharding import PartitionSpec as P
@@ -52,11 +53,6 @@
     return lax.ppermute(value, "core", [(0, 1), (1, 0)])
 
 
-def shift_group(value, steps):
-    pairs = [(i, i + steps) for i in range(DP) if 0 <= i + steps < DP]
-    return lax.ppermute(value, DP_AXES, pairs)
-
-
 def gather_group(value):
     parts = jnp.stack([value] + [shift(value, "z", -k) for k in (1, 2, 3)])
     return jnp.stack([parts, swap(parts)])
@@ -90,22 +86,6 @@
     return (grad_values, jnp.sum(grad_out * values * inverse, axis=0))
 
 
-def rotation(positions):
-    half = HEAD_DIM // 2
-    freqs = ROPE_BASE ** (-jnp.arange(half, dtype=FLOAT) / half)
-    angles = positions.astype(FLOAT)[:, None] * freqs[None, :]
-    return jnp.cos(angles)[:, None, :], jnp.sin(angles)[:, None, :]
-
-
-def rotate(values, cosine, sine):
-    half = HEAD_DIM // 2
-    first = values[..., :half]
-    second = values[..., half:]
-    return jnp.concatenate(
-        [first * cosine - second * sine, second * cosine + first * sine], axis=-1
-    )
-
-
 def mm(left, right):
     return jnp.dot(left, right, preferred_element_type=FLOAT)
 
@@ -121,6 +101,14 @@
 def reorder(blocks, order):
     hit = order[:, None] == jnp.arange(MP)[None, :]
     return jnp.sum(jnp.where(hit[:, :, None], blocks[..., None, :, :], 0), axis=-2)
+
+
+def by_rows(value):
+    return with_layout_constraint(value, Layout(tuple(range(value.ndim))))
+
+
+def by_cols(value):
+    return with_layout_constraint(value, Layout((1, 0)))
 
 
 def tie(*values):
@@ -169,15 +157,44 @@
     )
 
 
+def head_lanes(ref, head):
+    return jnp.concatenate(
+        [ref[64 * (3 * head + i) : 64 * (3 * head + i) + 64, :] for i in range(3)], axis=1
+    )
+
+
+def turn(value, cosine, sine):
+    parts = []
+    for head in range(value.shape[0] // 64):
+        first = value[64 * head : 64 * head + 32]
+        second = value[64 * head + 32 : 64 * head + 64]
+        parts.append(first * cosine - second * sine)
+        parts.append(second * cosine + first * sine)
+    return jnp.concatenate(parts, axis=0)
+
+
+def normalize(values, weight):
+    return values * lax.rsqrt(jnp.mean(values * values, axis=-1, keepdims=True) + EPS_NORM) * weight
+
+
+def normalize_back(values, weight, grad_out):
+    inverse = lax.rsqrt(jnp.mean(values * values, axis=-1, keepdims=True) + EPS_NORM)
+    weighted = grad_out * weight
+    grad_values = inverse * weighted - values * (inverse * inverse * inverse) * jnp.mean(
+        weighted * values, axis=-1, keepdims=True
+    )
+    return grad_values, jnp.sum(grad_out * values * inverse, axis=0, keepdims=True)
+
+
 def attend_kernel(query_ref, kv0, kv1, kv2, kv3, bias_ref, out_ref, log_ref):
     for head in range(KV_HEADS):
-        queries = head_rows(query_ref, head)
+        queries = head_lanes(query_ref, head)
         top = None
         for part, kv_ref in enumerate((kv0, kv1, kv2, kv3)):
             keys = kv_ref[:, 64 * head : 64 * head + 64]
             values = kv_ref[:, 320 + 64 * head : 320 + 64 * head + 64]
             bias = bias_ref[512 * part : 512 * part + 512, :]
-            scores = contract_cols(keys, queries) + jnp.concatenate([bias, bias, bias], axis=1)
+            scores = nn(keys, queries) + jnp.concatenate([bias, bias, bias], axis=1)
             part_top = jnp.max(scores, axis=0, keepdims=True)
             new_top = part_top if top is None else jnp.maximum(top, part_top)
             expo = jnp.exp(scores - new_top)
@@ -196,25 +213,37 @@
         log_ref[head : head + 1, :] = top + jnp.log(total)
 
 
+def params(mib):
+    return pltpu.CompilerParams(vmem_limit_bytes=mib * 1024 * 1024)
+
+
+def whole(*shape):
+    return pl.BlockSpec(shape, lambda i: (0,) * len(shape))
+
+
+def struct(kind, *shape):
+    return jax.ShapeDtypeStruct(shape, kind)
+
+
 def attend(queries, pairs, bias):
     return pl.pallas_call(
         attend_kernel,
-        out_shape=(
-            jax.ShapeDtypeStruct((TOK_DEV, HEADS * HEAD_DIM), BFLOAT),
-            jax.ShapeDtypeStruct((8, 3 * TOK_DEV), FLOAT),
-        ),
+        out_shape=(struct(BFLOAT, TOK_DEV, D), struct(FLOAT, 8, 3 * TOK_DEV)),
         cost_estimate=pl.CostEstimate(
             flops=12_000_000_000, bytes_accessed=5_000_000, transcendentals=4_000_000
         ),
-        compiler_params=pltpu.CompilerParams(vmem_limit_bytes=32 * 1024 * 1024),
+        compiler_params=params(24),
     )(queries, *pairs, bias)
 
 
 def attend_back_kernel(
-    query_ref, kv0, kv1, kv2, kv3, bias_ref, log_ref, att_ref, grad_ref, dq_ref, d0, d1, d2, d3
+    query_ref, kv0, kv1, kv2, kv3, bias_ref, log_ref, att_ref, grad_ref, cos_ref, sin_ref,
+    dq_ref, d0, d1, d2, d3
 ):
+    cosine = jnp.concatenate([cos_ref[...]] * 3, axis=1)
+    sine = jnp.concatenate([sin_ref[...]] * 3, axis=1)
     for head in range(KV_HEADS):
-        queries = head_rows(query_ref, head)
+        queries = head_lanes(query_ref, head)
         grads = head_rows(grad_ref, head)
         outs = head_rows(att_ref, head)
         delta = jnp.sum((grads.astype(FLOAT) * outs.astype(FLOAT)).T, axis=0, keepdims=True)
@@ -225,31 +254,258 @@
             values = kv_ref[:, 320 + 64 * head : 320 + 64 * head + 64]
             bias = bias_ref[512 * part : 512 * part + 512, :]
             probs = jnp.exp(
-                contract_cols(keys, queries) + jnp.concatenate([bias, bias, bias], axis=1) - log_total
+                nn(keys, queries) + jnp.concatenate([bias, bias, bias], axis=1) - log_total
             )
             grad_scores = (probs * (contract_cols(values, grads) - delta)).astype(BFLOAT)
-            d_ref[:, 64 * head : 64 * head + 64] = nn(grad_scores, queries).astype(BFLOAT)
+            d_ref[:, 64 * head : 64 * head + 64] = contract_cols(grad_scores, queries).astype(BFLOAT)
             d_ref[:, 320 + 64 * head : 320 + 64 * head + 64] = nn(
                 probs.astype(BFLOAT), grads
             ).astype(BFLOAT)
             part_back = contract_rows(keys, grad_scores)
             back = part_back if back is None else back + part_back
-        back = back.T * (HEAD_DIM**-0.5)
+        back = turn(back * (HEAD_DIM**-0.5), cosine, -sine).T.astype(BFLOAT)
         for i in range(3):
             place = 64 * (3 * head + i)
             dq_ref[:, place : place + 64] = back[128 * i : 128 * i + 128]
 
 
-def attend_back(queries, pairs, bias, log_total, attended, grads):
-    side = jax.ShapeDtypeStruct((4 * TOK_DEV, 640), BFLOAT)
+def attend_back(queries, pairs, bias, log_total, attended, grads, cosine, sine):
+    side = struct(BFLOAT, 4 * TOK_DEV, 640)
     return pl.pallas_call(
         attend_back_kernel,
-        out_shape=(jax.ShapeDtypeStruct((TOK_DEV, HEADS * HEAD_DIM), FLOAT), side, side, side, side),
+        out_shape=(struct(BFLOAT, TOK_DEV, D), side, side, side, side),
         cost_estimate=pl.CostEstimate(
             flops=20_000_000_000, bytes_accessed=9_000_000, transcendentals=4_000_000
         ),
-        compiler_params=pltpu.CompilerParams(vmem_limit_bytes=32 * 1024 * 1024),
-    )(queries, *pairs, bias, log_total, attended, grads)
+        compiler_params=params(24),
+    )(queries, *pairs, bias, log_total, attended, grads, cosine, sine)
+
+
+def project(hidden, gain, wq_ref, wk_ref, wv_ref, cos_ref, sin_ref, normed_ref, query_ref, pair_ref):
+    normed = normalize(hidden, gain).astype(BFLOAT)
+    normed_ref[...] = normed
+    cosine, sine = cos_ref[...], sin_ref[...]
+    keys = turn(nn(normed, wk_ref[...]).T, cosine, sine).T
+    pair_ref[:, 0:320] = keys.astype(BFLOAT)
+    pair_ref[:, 320:640] = nn(normed, wv_ref[...]).astype(BFLOAT)
+    queries = turn(nn(normed, wq_ref[...]).T, cosine, sine)
+    query_ref[...] = (queries * (HEAD_DIM**-0.5)).astype(BFLOAT)
+
+
+PROJECTED = (
+    struct(BFLOAT, TOK_DEV, D),
+    struct(BFLOAT, D, TOK_DEV),
+    struct(BFLOAT, TOK_DEV, 640),
+)
+
+
+def enter_kernel(hidden_ref, gain_ref, *refs):
+    project(hidden_ref[...], gain_ref[0:1, :], *refs)
+
+
+def enter(hidden, gains, wq, wk, wv, cosine, sine):
+    return pl.pallas_call(enter_kernel, out_shape=PROJECTED, compiler_params=params(24))(
+        hidden, gains, wq, wk, wv, cosine, sine
+    )
+
+
+FF_BLOCK = 640
+FF_STEPS = FF // FF_BLOCK
+
+
+def block_kernel(
+    more, att_ref, hidden_ref, sel_ref, gain_ref, router_ref, wo_ref, weight_ref, *refs
+):
+    proj_in, refs = (refs[:5], refs[5:]) if more else ((), refs)
+    mixed_ref, input_ref, gate_ref, up_ref, inner_ref, branch_ref, logit_ref, new_ref = refs[:8]
+    acc_ref = refs[-1]
+    step = pl.program_id(0)
+
+    @pl.when(step == 0)
+    def first():
+        mixed = hidden_ref[...] + nn(att_ref[...], wo_ref[...])
+        mixed_ref[...] = mixed
+        input_ref[...] = normalize(mixed, gain_ref[1:2, :]).astype(BFLOAT)
+        acc_ref[...] = mixed
+
+    rows = input_ref[...]
+    gate = contract_cols(rows, weight_ref[0])
+    up = contract_cols(rows, weight_ref[1])
+    gate_ref[...] = gate
+    up_ref[...] = up
+    inner = (gate * jax.nn.sigmoid(gate) * up).astype(BFLOAT)
+    inner_ref[...] = inner
+    acc_ref[...] += nn(inner, weight_ref[2])
+
+    @pl.when(step == FF_STEPS - 1)
+    def last():
+        hidden = hidden_ref[...]
+        branch = acc_ref[...]
+        branch_ref[...] = branch
+        logit = jnp.sum(hidden * router_ref[...], axis=1, keepdims=True)
+        logit_ref[...] = logit
+        new = hidden + sel_ref[...] * jax.nn.sigmoid(logit) * (branch - hidden)
+        new_ref[...] = new
+        if more:
+            project(new, gain_ref[0:1, :], *proj_in, *refs[8:11])
+
+
+def block(att, hidden, sel, gains, router, wo, weights, projections):
+    more = projections is not None
+    proj_specs = [whole(D, D), whole(D, 320), whole(D, 320), whole(32, 128), whole(32, 128)]
+    rows = pl.BlockSpec((TOK_DEV, FF_BLOCK), lambda i: (0, i))
+    return pl.pallas_call(
+        functools.partial(block_kernel, more),
+        grid=(FF_STEPS,),
+        in_specs=[
+            whole(TOK_DEV, D),
+            whole(TOK_DEV, D),
+            whole(TOK_DEV, 1),
+            whole(8, D),
+            whole(1, D),
+            whole(D, D),
+            pl.BlockSpec((3, FF_BLOCK, D), lambda i: (0, i, 0)),
+        ]
+        + proj_specs * more,
+        out_specs=[
+            whole(TOK_DEV, D),
+            whole(TOK_DEV, D),
+            rows,
+            rows,
+            rows,
+            whole(TOK_DEV, D),
+            whole(TOK_DEV, 1),
+            whole(TOK_DEV, D),
+        ]
+        + [whole(TOK_DEV, D), whole(D, TOK_DEV), whole(TOK_DEV, 640)] * more,
+        out_shape=(
+            struct(FLOAT, TOK_DEV, D),
+            struct(BFLOAT, TOK_DEV, D),
+            struct(FLOAT, TOK_DEV, FF),
+            struct(FLOAT, TOK_DEV, FF),
+            struct(BFLOAT, TOK_DEV, FF),
+            struct(FLOAT, TOK_DEV, D),
+            struct(FLOAT, TOK_DEV, 1),
+            struct(FLOAT, TOK_DEV, D),
+        )
+        + (PROJECTED if more else ()),
+        scratch_shapes=[pltpu.VMEM((TOK_DEV, D), FLOAT)],
+        cost_estimate=pl.CostEstimate(
+            flops=4_000_000_000, bytes_accessed=20_000_000, transcendentals=400_000
+        ),
+        compiler_params=params(32),
+    )(att, hidden, sel, gains, router, wo, weights, *(projections if more else ()))
+
+
+def block_back_kernel(
+    new_ref, sel_ref, logit_ref, hidden_ref, branch_ref, mixed_ref, gain_ref, router_ref, wo_ref,
+    gate_ref, up_ref, weight_ref,
+    rows_ref, dgate_ref, dup_ref, in_ref, attn_ref, back_ref, small_ref, acc_ref
+):
+    step = pl.program_id(0)
+    sigma = jax.nn.sigmoid(logit_ref[...])
+    weight = sel_ref[...] * sigma
+
+    @pl.when(step == 0)
+    def first():
+        rows_ref[...] = (weight * new_ref[...]).astype(BFLOAT)
+        acc_ref[...] = jnp.zeros_like(acc_ref)
+
+    inner = contract_cols(rows_ref[...], weight_ref[2])
+    gate = gate_ref[...]
+    shape = jax.nn.sigmoid(gate)
+    dgate = (inner * up_ref[...] * shape * (1.0 + gate * (1.0 - shape))).astype(BFLOAT)
+    dup = (inner * gate * shape).astype(BFLOAT)
+    dgate_ref[...] = dgate
+    dup_ref[...] = dup
+    acc_ref[...] += nn(dgate, weight_ref[0]) + nn(dup, weight_ref[1])
+
+    @pl.when(step == FF_STEPS - 1)
+    def last():
+        grad_new = new_ref[...]
+        hidden = hidden_ref[...]
+        grad_branch = weight * grad_new
+        grad_weight = jnp.sum(grad_new * (branch_ref[...] - hidden), axis=1, keepdims=True)
+        grad_logit = grad_weight * sel_ref[...] * sigma * (1.0 - sigma) + ROUTER_LOSS / TOK_DEV * (
+            sigma - sel_ref[...]
+        )
+        grad_norm, gain_row = normalize_back(mixed_ref[...], gain_ref[1:2, :], acc_ref[...])
+        grad_mixed = grad_branch + grad_norm
+        in_ref[...] = grad_new - grad_branch + grad_logit * router_ref[...] + grad_mixed
+        attn = grad_mixed.astype(BFLOAT)
+        attn_ref[...] = attn
+        back_ref[...] = contract_cols(attn, wo_ref[...]).astype(BFLOAT)
+        small_ref[0:1, :] = gain_row
+        small_ref[1:2, :] = jnp.sum(grad_logit * hidden, axis=0, keepdims=True)
+        small_ref[2:8, :] = jnp.zeros((6, D), FLOAT)
+
+
+def block_back(new, sel, logit, hidden, branch, mixed, gains, router, wo, gate, up, weights):
+    rows = pl.BlockSpec((TOK_DEV, FF_BLOCK), lambda i: (0, i))
+    full = whole(TOK_DEV, D)
+    return pl.pallas_call(
+        block_back_kernel,
+        grid=(FF_STEPS,),
+        in_specs=[
+            full,
+            whole(TOK_DEV, 1),
+            whole(TOK_DEV, 1),
+            full,
+            full,
+            full,
+            whole(8, D),
+            whole(1, D),
+            whole(D, D),
+            rows,
+            rows,
+            pl.BlockSpec((3, FF_BLOCK, D), lambda i: (0, i, 0)),
+        ],
+        out_specs=[full, rows, rows, full, full, full, whole(8, D)],
+        out_shape=(
+            struct(BFLOAT, TOK_DEV, D),
+            struct(BFLOAT, TOK_DEV, FF),
+            struct(BFLOAT, TOK_DEV, FF),
+            struct(FLOAT, TOK_DEV, D),
+            struct(BFLOAT, TOK_DEV, D),
+            struct(BFLOAT, TOK_DEV, D),
+            struct(FLOAT, 8, D),
+        ),
+        scratch_shapes=[pltpu.VMEM((TOK_DEV, D), FLOAT)],
+        cost_estimate=pl.CostEstimate(
+            flops=4_000_000_000, bytes_accessed=20_000_000, transcendentals=400_000
+        ),
+        compiler_params=params(32),
+    )(new, sel, logit, hidden, branch, mixed, gains, router, wo, gate, up, weights)
+
+
+def enter_back_kernel(
+    in_ref, dq_ref, own_ref, hidden_ref, gain_ref, wq_ref, wk_ref, wv_ref, cos_ref, sin_ref,
+    pair_ref, out_ref, small_ref
+):
+    keys = turn(own_ref[:, 0:320].T, cos_ref[...], -sin_ref[...]).T.astype(BFLOAT)
+    values = own_ref[:, 320:640].astype(BFLOAT)
+    pair_ref[:, 0:320] = keys
+    pair_ref[:, 320:640] = values
+    grad_normed = (
+        contract_cols(dq_ref[...], wq_ref[...])
+        + contract_cols(keys, wk_ref[...])
+        + contract_cols(values, wv_ref[...])
+    )
+    grad_hidden, gain_row = normalize_back(hidden_ref[...], gain_ref[0:1, :], grad_normed)
+    out_ref[...] = in_ref[...] + grad_hidden
+    small_ref[...] = jnp.concatenate([gain_row, jnp.zeros((7, D), FLOAT)], axis=0)
+
+
+def enter_back(grad_in, dq, own, hidden, gains, wq, wk, wv, cosine, sine):
+    return pl.pallas_call(
+        enter_back_kernel,
+        out_shape=(
+            struct(BFLOAT, TOK_DEV, 640),
+            struct(FLOAT, TOK_DEV, D),
+            struct(FLOAT, 8, D),
+        ),
+        compiler_params=params(24),
+    )(grad_in, dq, own, hidden, gains, wq, wk, wv, cosine, sine)
 
 
 HEAD_BLOCK = 512
@@ -280,23 +536,20 @@
 
 
 def head(loss_rows, near_rows, final_rows, local_targets, table):
-    def whole(shape):
-        return pl.BlockSpec(shape, lambda i: (0, 0))
-
     return pl.pallas_call(
         head_kernel,
         grid=(VOCAB_MP // HEAD_BLOCK,),
         in_specs=[
-            whole((256, 1)),
-            whole((1, ROWS)),
-            whole((ROWS, D)),
-            whole((256, 1)),
+            whole(256, 1),
+            whole(1, ROWS),
+            whole(ROWS, D),
+            whole(256, 1),
             pl.BlockSpec((HEAD_BLOCK, D), lambda i: (i, 0)),
         ],
         out_specs=[
             pl.BlockSpec((256, HEAD_BLOCK), lambda i: (0, i)),
-            whole((256, D)),
-            whole((256, 128)),
+            whole(256, D),
+            whole(256, 128),
         ],
         out_shape=(
             jax.ShapeDtypeStruct((256, VOCAB_MP), FLOAT),
@@ -333,22 +586,19 @@
 
 
 def head_back(loss_rows, near_rows, local_targets, log_norm, logits, picked, table):
-    def whole(shape):
-        return pl.BlockSpec(shape, lambda i: (0, 0))
-
     return pl.pallas_call(
         head_back_kernel,
         grid=(VOCAB_MP // HEAD_BLOCK,),
         in_specs=[
-            whole((256, 1)),
-            whole((1, ROWS)),
-            whole((256, 1)),
-            whole((256, 1)),
+            whole(256, 1),
+            whole(1, ROWS),
+            whole(256, 1),
+            whole(256, 1),
             pl.BlockSpec((256, HEAD_BLOCK), lambda i: (0, i)),
-            whole((256, D)),
+            whole(256, D),
             pl.BlockSpec((HEAD_BLOCK, D), lambda i: (i, 0)),
         ],
-        out_specs=[pl.BlockSpec((HEAD_BLOCK, D), lambda i: (i, 0)), whole((ROWS, D))],
+        out_specs=[pl.BlockSpec((HEAD_BLOCK, D), lambda i: (i, 0)), whole(ROWS, D)],
         out_shape=(
             jax.ShapeDtypeStruct((VOCAB_MP, D), BFLOAT),
             jax.ShapeDtypeStruct((ROWS, D), BFLOAT),
@@ -361,30 +611,28 @@
 def mlp_grad_kernel(added, which_ref, *refs):
     lefts, rights, refs = refs[0:3], refs[3:6], refs[6:]
     for i in range(3):
-        total = contract_rows(lefts[i][...], rights[i][...])
+        total = contract_rows(lefts[i][...], rights[i][...]).reshape(8, 80, D)
         if added:
-            total = total + refs[0][i].astype(FLOAT)
-        refs[-1][i] = total.astype(BFLOAT)
+            total = total + refs[0][:, i].astype(FLOAT)
+        refs[-1][:, i] = total.astype(BFLOAT)
 
 
 def mlp_grads(which, lefts, rights, received=None):
     added = received is not None
-    block = 256
     rows = lefts[0].shape[0]
-    steps = FF // 2 // block
-    out_spec = pl.BlockSpec((3, block, D), lambda i, half: (0, i, 0))
+    out_spec = pl.BlockSpec((8, 3, 80, D), lambda i, half: (i, 0, 0, 0))
     return pl.pallas_call(
         functools.partial(mlp_grad_kernel, added),
         grid_spec=pltpu.PrefetchScalarGridSpec(
             num_scalar_prefetch=1,
-            grid=(steps,),
-            in_specs=[pl.BlockSpec((rows, block), lambda i, half: (0, half[0] * steps + i))] * 3
+            grid=(2,),
+            in_specs=[pl.BlockSpec((rows, 640), lambda i, half: (0, half[0] * 2 + i))] * 3
             + [pl.BlockSpec((rows, D), lambda i, half: (0, 0))] * 3
             + [out_spec] * added,
             out_specs=out_spec,
         ),
-        out_shape=jax.ShapeDtypeStruct((3, FF // 2, D), BFLOAT),
-        compiler_params=pltpu.CompilerParams(vmem_limit_bytes=32 * 1024 * 1024),
+        out_shape=struct(BFLOAT, 16, 3, 80, D),
+        compiler_params=params(40),
     )(which.reshape(1), *lefts, *rights, *([received] if added else []))
 
 
@@ -499,8 +747,6 @@
     model_index = z * 2 + core
     data_index = y * 4 + x
     device = model_index * DP + data_index
-    groups_per = HEADS // KV_HEADS
-    scale = HEAD_DIM ** (-0.5)
     own_table = table_master.astype(BFLOAT)
 
     near = jnp.stack([((z + k) % 4) * 2 + (core ^ j) for j in (0, 1) for k in range(4)])
@@ -556,8 +802,8 @@
         rows = jnp.take(full, jnp.clip(local_ids, 0, VOCAB_MP - 1), axis=0)
         return jnp.where(inside[:, None], rows, jnp.zeros_like(rows))
 
+    asked_rows, pack_blocks = tie(asked_rows, pack_blocks)
     looked = lax.cond(over, looked_dense, looked_sparse)
-    looked, pack_blocks = tie(looked, pack_blocks)
     hidden = scatter_group(looked.reshape(2, 4, TOK_DEV, D), FLOAT)
 
     pack_weights = join_pack(pack_blocks)
@@ -565,18 +811,16 @@
     w_key = pack_weights[960:1280].reshape(D, KV_HEADS * HEAD_DIM)
     w_value = pack_weights[1280:1600].reshape(D, KV_HEADS * HEAD_DIM)
     w_out = pack_weights[1600:2560]
-    gains = pack_weights[2560:2563].astype(FLOAT)
+    gains = jnp.concatenate([pack_weights[2560:2563].astype(FLOAT), jnp.zeros((5, D), FLOAT)])
     router = pack_weights[2563:2566].astype(FLOAT)
-    mlp_weights = (
-        mlp_blocks.reshape(2, 4, 4, 3, 80, D).transpose(3, 0, 2, 1, 4, 5).reshape(3, FF, D)
-    )
-    gate_w = mlp_weights[0]
-    up_w = mlp_weights[1]
-    down_w = mlp_weights[2]
-
+    mlp_weights = mlp_blocks.reshape(32, 3, 80, D).transpose(1, 0, 2, 3).reshape(3, FF, D)
+
+    half_dim = HEAD_DIM // 2
+    freqs = ROPE_BASE ** (-jnp.arange(half_dim, dtype=FLOAT) / half_dim)
     first_row = data_index * ROWS + model_index * TOK_DEV
-    query_rows = first_row + jnp.arange(TOK_DEV, dtype=jnp.int32)
-    cosine, sine = rotation(query_rows)
+    angles = freqs[:, None] * (first_row + jnp.arange(TOK_DEV, dtype=jnp.int32)).astype(FLOAT)[None, :]
+    turns = (jnp.cos(angles), jnp.sin(angles))
+    projections = (w_query, w_key, w_value) + turns
     group_sel = selections.reshape(RECUR, DP, MP, TOK_DEV)
     prev_index = jnp.maximum(data_index - 1, 0)
     here_sel = lax.dynamic_index_in_dim(group_sel, data_index, 1, False)
@@ -601,47 +845,46 @@
     )
     biases = jnp.where(biases, 0.0, MASKED)
 
+    sel_cols = own_sel.astype(FLOAT)[:, :, None]
     saves = []
-    penalty_total = jnp.zeros((), FLOAT)
+    logits_all = []
+    normed, queries, pair = enter(hidden, gains, *projections)
     for step in range(RECUR):
-        normed = rms_scale(hidden, gains[0]).astype(BFLOAT)
-        keys_own = rotate(mm(normed, w_key).reshape(TOK_DEV, KV_HEADS, HEAD_DIM), cosine, sine)
-        values_own = mm(normed, w_value)
-        pair = jnp.concatenate([keys_own.reshape(TOK_DEV, -1), values_own], axis=1).astype(BFLOAT)
         pairs = group_gather(pair)
-        queries = (
-            rotate(mm(normed, w_query).reshape(TOK_DEV, HEADS, HEAD_DIM), cosine, sine) * scale
-        ).astype(BFLOAT)
-        attended, log_total = attend(queries.reshape(TOK_DEV, -1), pairs, biases[step])
-        mixed = hidden + mm(attended, w_out)
-        mlp_input = rms_scale(mixed, gains[1]).astype(BFLOAT)
-        gate_pre = contract_cols(mlp_input, gate_w)
-        up_pre = contract_cols(mlp_input, up_w)
-        inner = (jax.nn.silu(gate_pre) * up_pre).astype(BFLOAT)
-        branch = mixed + mm(inner, down_w)
-        logit = jnp.dot(hidden, router[step], precision=HIGHEST)
-        chosen = own_sel[step].astype(FLOAT)
-        weight_sel = chosen * jax.nn.sigmoid(logit)
-        new_hidden = hidden + weight_sel[:, None] * (branch - hidden)
-        penalty_total = penalty_total + jnp.sum(jax.nn.softplus(logit) - chosen * logit)
+        attended, log_total = attend(queries, pairs, biases[step])
+        mixed, mlp_input, gate, up, inner, branch, logit, new_hidden, *nexts = block(
+            attended,
+            hidden,
+            sel_cols[step],
+            gains,
+            router[step : step + 1],
+            w_out,
+            mlp_weights,
+            projections if step < RECUR - 1 else None,
+        )
+        logits_all.append(logit[:, 0])
         saves.append(
             (
                 hidden,
                 normed,
                 queries,
                 pairs,
+                attended,
                 log_total,
-                attended,
                 mixed,
                 mlp_input,
-                gate_pre,
-                up_pre,
+                gate,
+                up,
                 inner,
                 branch,
                 logit,
             )
         )
         hidden = new_hidden
+        if nexts:
+            normed, queries, pair = nexts
+    logits_all = jnp.stack(logits_all)
+    penalty_total = jnp.sum(jax.nn.softplus(logits_all) - own_sel.astype(FLOAT) * logits_all)
 
     normed_final = rms_scale(hidden, gains[2]).astype(BFLOAT)
     final_rows = gather_group(normed_final).reshape(ROWS, D)
@@ -677,119 +920,74 @@
     kept = []
     mlp_parts = []
     router_rows = [None] * RECUR
-    gain_one = jnp.zeros((D,), FLOAT)
-    gain_two = jnp.zeros((D,), FLOAT)
+    gain_one = jnp.zeros((1, D), FLOAT)
+    gain_two = jnp.zeros((1, D), FLOAT)
     for step in reversed(range(RECUR)):
-        grad_new = grad_hidden
         (
             hidden_in,
             normed,
             queries,
             pairs,
+            attended,
             log_total,
-            attended,
             mixed,
             mlp_input,
-            gate_pre,
-            up_pre,
+            gate,
+            up,
             inner,
             branch,
             logit,
         ) = saves[step]
-        chosen = own_sel[step].astype(FLOAT)
-        sigma = jax.nn.sigmoid(logit)
-        weight_sel = chosen * sigma
-        grad_branch = weight_sel[:, None] * grad_new
-        grad_weight = jnp.sum(grad_new * (branch - hidden_in), axis=-1)
-        grad_logit = grad_weight * chosen * sigma * (1.0 - sigma) + ROUTER_LOSS / TOK_DEV * (
-            sigma - chosen
+        grad_rows, grad_gate, grad_up, grad_in, grad_attn, grad_attended, small = block_back(
+            grad_hidden,
+            sel_cols[step],
+            logit,
+            hidden_in,
+            branch,
+            mixed,
+            gains,
+            router[step : step + 1],
+            w_out,
+            gate,
+            up,
+            mlp_weights,
         )
-        grad_in = (
-            grad_new - weight_sel[:, None] * grad_new + grad_logit[:, None] * router[step][None, :]
-        )
-        router_rows[step] = jnp.dot(grad_logit, hidden_in, precision=HIGHEST)
-        grad_rows = grad_branch.astype(BFLOAT)
-        grad_inner = contract_cols(grad_rows, down_w)
-        sigma_gate = jax.nn.sigmoid(gate_pre)
-        grad_gate = (
-            grad_inner * up_pre * sigma_gate * (1.0 + gate_pre * (1.0 - sigma_gate))
-        ).astype(BFLOAT)
-        grad_up = (grad_inner * gate_pre * sigma_gate).astype(BFLOAT)
+        gain_two = gain_two + small[0:1]
+        router_rows[step] = small[1:2]
         mlp_parts.append((grad_gate, grad_up, inner, mlp_input, mlp_input, grad_rows))
-        grad_normed_two = mm(grad_gate, gate_w) + mm(grad_up, up_w)
-        grad_mixed_norm, part_two = rms_back(mixed, gains[1], grad_normed_two)
-        gain_two = gain_two + part_two
-        grad_mixed = grad_branch + grad_mixed_norm
-        grad_in = grad_in + grad_mixed
-        grad_attn = grad_mixed.astype(BFLOAT)
-        grad_attended = (
-            contract_cols(grad_attn, w_out).astype(BFLOAT)
-        )
         if step == 0:
             mlp_kept = [jnp.concatenate(parts, axis=0) for parts in zip(*mlp_parts)]
             far = mlp_grads(1 - core, mlp_kept[:3], mlp_kept[3:])
-            grad_attended, far, head_grad = tie(grad_attended, far, head_grad)
-            far = swap(far)
-        grad_queries, *grad_sides = attend_back(
-            queries.reshape(TOK_DEV, -1), pairs, biases[step], log_total, attended, grad_attended
+            far, grad_attended, head_grad = tie(by_rows(far), grad_attended, head_grad)
+            far = by_rows(swap(far))
+        grad_query, *grad_sides = attend_back(
+            queries, pairs, biases[step], log_total, attended, grad_attended, *turns
         )
         if step == 0:
             far, *grad_sides = tie(far, *grad_sides)
             mlp_half = mlp_grads(core, mlp_kept[:3], mlp_kept[3:], far)
+            mlp_sum = lax.psum_scatter(
+                mlp_half.reshape(16 * 240, D), DP_AXES, scatter_dimension=0, tiled=True
+            )
         grad_own = group_scatter(*grad_sides)
-        grad_query_pre = (
-            rotate(grad_queries.reshape(TOK_DEV, HEADS, HEAD_DIM), cosine, -sine)
-            .reshape(TOK_DEV, -1)
-            .astype(BFLOAT)
+        grad_pair, grad_hidden, small = enter_back(
+            grad_in, grad_query, grad_own, hidden_in, gains, *projections
         )
-        grad_key_pre = (
-            rotate(grad_own[:, :320].reshape(TOK_DEV, KV_HEADS, HEAD_DIM), cosine, -sine)
-            .reshape(TOK_DEV, -1)
-            .astype(BFLOAT)
-        )
-        grad_value_pre = grad_own[:, 320:].astype(BFLOAT)
-        grad_normed = (
-            contract_cols(grad_query_pre, w_query)
-            + contract_cols(grad_key_pre, w_key)
-            + contract_cols(grad_value_pre, w_value)
-        )
-        grad_hidden_norm, part_one = rms_back(hidden_in, gains[0], grad_normed)
-        gain_one = gain_one + part_one
-        grad_hidden = grad_in + grad_hidden_norm
-        kept.append(
-            (
-                normed,
-                grad_query_pre,
-                grad_key_pre,
-                grad_value_pre,
-                attended,
-                grad_attn,
-            )
-        )
-    (
-        normed_all,
-        grad_query_all,
-        grad_key_all,
-        grad_value_all,
-        attended_all,
-        grad_attn_all,
-    ) = [jnp.concatenate(parts, axis=0) for parts in zip(*kept)]
-
-    mlp_half = mlp_half.reshape(3, 4, 4, 80, D)
-    cols = mlp_half[..., :512].transpose(1, 2, 0, 3, 4)
-    part = stage(stage(cols, "x", x).astype(BFLOAT), "y", y).astype(BFLOAT)
-    left = stage_near(part.reshape(3, 4, UNITS, -1).transpose(1, 0, 2, 3), "z")
-    cols = mlp_half[..., 512:].transpose(2, 1, 0, 3, 4)
-    part = stage(stage(cols, "y", y).astype(BFLOAT), "x", x).astype(BFLOAT)
-    right = stage_near(part.reshape(3, 4, UNITS, -1).transpose(1, 0, 2, 3), "z")
-    mlp_grad = jnp.concatenate([left, right], axis=-1)
+        gain_one = gain_one + small[0:1]
+        kept.append((normed, grad_query, grad_pair, attended, grad_attn))
+    normed_all, grad_query_all, grad_pair_all, attended_all, grad_attn_all = [
+        jnp.concatenate(parts, axis=0) for parts in zip(*kept)
+    ]
 
     def aligned_row(which):
         return (pack_row(which) // 16) * 16
 
     small = jnp.concatenate(
         [
-            jnp.stack([gain_one, gain_two, grad_gain_final] + router_rows),
+            gain_one,
+            gain_two,
+            grad_gain_final[None],
+            *router_rows,
             jnp.zeros((10, D), FLOAT),
         ]
     )
@@ -800,8 +998,8 @@
         starts,
         normed_all,
         grad_query_all,
-        grad_key_all,
-        grad_value_all,
+        grad_pair_all[:, :320],
+        grad_pair_all[:, 320:],
         attended_all,
         grad_attn_all,
         small,
@@ -814,13 +1012,9 @@
     def x_windows(value):
         return jnp.stack([value[..., i : i + 48, :] for i in (0, 16, 40, 56)])
 
-    part = stage(y_windows(half[..., :512]), "y", y).astype(BFLOAT)
-    part = stage(part, "z", z).astype(BFLOAT)
-    left = stage(x_windows(part), "x", x)
-    part = stage(half[..., 512:], "z", z).astype(BFLOAT)
+    part = stage(half, "z", z).astype(BFLOAT)
     part = stage(y_windows(part), "y", y).astype(BFLOAT)
-    right = stage(x_windows(part), "x", x)
-    part = jnp.concatenate([left, right], axis=-1).reshape(-1)
+    part = stage(x_windows(part), "x", x).reshape(-1)
     begin = aligned_row(DP * model_index) + 80 * y + (20 * x) // 8 * 8
     pack_grad = lax.dynamic_slice(part, (PACK_DEV * device - D * begin,), (PACK_DEV,))
 
@@ -829,8 +1023,10 @@
     unique = contract_rows(place_hot, grad_embed).astype(BFLOAT)
     unique = lax.all_to_all(unique, DP_AXES, 0, 0, tiled=True)
 
-    def embed_sparse():
-        return contract_rows(owner_hot, unique)
+    sparse = contract_rows(owner_hot, unique)
+
+    mlp_sum = mlp_sum.reshape(3, 4, UNITS, D).transpose(1, 0, 2, 3)
+    mlp_grad = stage_near(mlp_sum, "z")
 
     def embed_dense():
         kept_rows = grad_embed.astype(FLOAT) * inside.astype(FLOAT)[:, None]
@@ -841,7 +1037,9 @@
             sums.astype(BFLOAT), DP_AXES, scatter_dimension=0, tiled=True
         ).astype(FLOAT)
 
-    table_grad = head_grad.astype(FLOAT) + lax.cond(over, embed_dense, embed_sparse)
+    sparse, mlp_grad, pack_grad = tie(sparse, mlp_grad, pack_grad)
+    table_grad = head_grad.astype(FLOAT) + lax.cond(over, embed_dense, lambda: sparse)
+    table_grad = by_cols(table_grad)
 
     squares = (
         jnp.sum(pack_grad * pack_grad)

time: 1040 us -> 853 us (0.82)
  matrix products: 109 us -> 6.8 us
  Pallas kernels: 124 us -> 186 us
  waiting for transfers between devices: 257 us -> 198 us
  other arithmetic: 106 us -> 58.8 us
  starting transfers between devices: 228 us -> 204 us
  local copies, waits for them, and re-layouts: 170 us -> 153 us
    dot_general x27 -> x0, matrix products: 64.1 us -> none  [the longest x21 54.1 us: contract_cols(): lax.dot_general(left, right, (((1,), (1,)), ((), ())), preferred_element_...]
    ppermute x72 -> x48, waiting for transfers between devices: 153 us -> 91.9 us  [shift(): return lax.ppermute(value, axis, [(i, (i + steps) % 4) for i in range(4)])]
    pallas_call x6 -> x16, Pallas kernels: 71.5 us -> 131 us  [the longest x3 34.6 us: attend_back(): pl.pallas_call(attend_back_kernel, out_shape=(struct(BFLOAT, TOK_DEV, D),...]
    all_gather x1, waiting for transfers between devices: 59.8 us -> 23.4 us  [shards(): pack_blocks = lax.all_gather(pack_block, ALL_AXES, axis=0, tiled=True)]
    dot_general x25 -> x4, matrix products: 39.7 us -> 4.29 us  [mm(): return jnp.dot(left, right, preferred_element_type=FLOAT)]
    ppermute x12, waiting for transfers between devices: 20.6 us -> 42.2 us  [group_scatter(): total = total + lax.ppermute(prev[k], ('z',) + DP_AXES, pairs).astype(FLOAT)]
    optimization_barrier x2 -> x1, local copies, waits for them, and re-layouts: 20.9 us -> 2.29 us  [tie(): return lax.optimization_barrier(values)]
    ppermute x72 -> x48, starting transfers between devices: 91.6 us -> 74 us  [shift(): return lax.ppermute(value, axis, [(i, (i + steps) % 4) for i in range(4)])]
  transfers between devices with their start and end apart: 142 -> 119, of which waited for: 62 -> 53; matrix products, arithmetic and copies ran while one was open for 29% -> 15% of each run, Pallas kernels for 10% -> 18%
where the time goes in v2:
time: 853 us; the launch traced here: 839 us
  starting transfers between devices  204 us (24%)
  waiting for transfers between devices  198 us (23%)
  Pallas kernels  186 us (22%)
  local copies, waits for them, and re-layouts  153 us (18%)
  other arithmetic  58.8 us (7%)
  between operations  24.6 us (3%)
    ppermute x48, waiting for transfers between devices, shift(): return lax.ppermute(value, axis, [(i, (i + steps) % 4) for i in range(4)])  91.9 us
    unnamed x446, local copies, waits for them, and re-layouts  83.1 us
    ppermute x48, starting transfers between devices, shift(): return lax.ppermute(value, axis, [(i, (i + steps) % 4) for i in range(4)])  74 us
    ppermute x12, waiting for transfers between devices, group_scatter(): total = total + lax.ppermute(prev[k], ('z',) + DP_AXES, pairs).astype(FLOAT)  42.2 us
    pallas_call x3, Pallas kernels, attend_back(): pl.pallas_call(attend_back_kernel, out_shape=(struct(BFLOAT, TOK_DEV, D),...  34.6 us
    pallas_call x3, Pallas kernels, block_back(): pl.pallas_call(block_back_kernel, grid=(FF_STEPS,), in_specs=[full, whole...  31.5 us
    ppermute x12, starting transfers between devices, group_gather(): prev.append(lax.ppermute(pair, ('z',) + DP_AXES, pairs))  31.1 us
    ppermute x9, starting transfers between devices, group_gather(): lax.ppermute(pair, 'z', [((i + k) % 4, i) for i in range(4) if (i + k) %...  30.2 us
  transfers between devices with their start and end apart: 119, of which 53 were waited for; matrix products, arithmetic and copies ran while one was open for 15% of the time, Pallas kernels for 18%

profile of v2, /device:TPU:1, one launch (start us, length us, event | category | flops | bytes accessed | tf_op | source)
XLA Modules:
  0.0 838.9 jit_solution(468032266806935406)
XLA Ops:
  20.2 6.8 all-to-all-start
  54.9 6.3 collective-permute-done.7
  66.1 23.4 %all-gather.7.cloned.1.call-done.blocks_ref = bf16[3072,960]{1,0:T(8,128)(2,1)} async-done(((bf16[24,960]{1,0:T(8,128)(2,1)}), bf16[3072,960]{1,0:T(8,128)(2,1)}) %all-gather.7.cloned.1.call-update) | async-done | bytes 5898256 | tf_op jit(solution)/shard_map/all_gather | solution.py:759
  89.5 11.9 %conditional.2 = (bf16[1024,960]{1,0:T(8,128)(2,1)}) conditional(s32[]{:T(128)} %bitcast.12, (bf16[1024,384]{1,0:T(8,128)(2,1)}, bf16[384,960]{1,0:T(8,128)(2,1)S(1)}) %tuple.143, (pred[1024]{0:T(1024)(128)(4,1)S(1)}, s32[1024]{0:T(1024)S(1)}, bf16[384,960]{1,0:T(8,128)(2,1)S(1)}) %tuple.26), branch_computations={%region_4.5_spmd, %region_5.6_spmd} | conditional | flops 755957760 | bytes 49269836 | solution.py:806
  117.8 5.2 shard_map.221
  134.8 5.0 fusion.73
  139.8 6.4 collective-permute-done.11
  149.4 5.8 collective-permute-start.18
  162.6 6.0 collective-permute-start.16
  181.6 8.8 %shard_map.223 = (bf16[128,960]{1,0:T(8,128)(2,1)S(1)}, f32[8,384]{1,0:T(8,128)S(1)}) custom-call(bf16[960,128]{1,0:T(8,128)(2,1)S(1)} %copy-done.150, bf16[512,640]{1,0:T(8,128)(2,1)S(1)} %constant_dynamic-update-slice_fusion.kv0, bf16[512,640]{1,0:T(8,128)(2,1)S(1)} %constant_dynamic-update-slice_fusion.4.kv1, ...), custom_call_target="tpu_custom_call" | custom-call | flops 12000000000 | bytes 5000000 | tf_op jit(solution)/shard_map/pallas_call | solution.py:229
  194.6 13.7 %copy.168 = bf16[3,32,80,960]{3,2,1,0:T(8,128)(2,1)} copy(bf16[3,32,80,960]{3,2,0,1:T(8,128)(2,1)} %bitcast.321) | data formatting | bytes 29491200 | tf_op jit(solution)/shard_map/transpose | solution.py:816
  208.3 10.1 %shard_map.224 = (f32[128,960]{1,0:T(8,128)S(1)}, bf16[128,960]{1,0:T(8,128)(2,1)S(1)}, f32[128,2560]{1,0:T(8,128)S(1)}, f32[128,2560]{1,0:T(8,128)S(1)}, bf16[1...) custom-call(bf16[128,960]{1,0:T(8,128)(2,1)S(1)} %copy-done.56, ...), custom_call_target="tpu_custom_call" | custom-call | flops 4000000000 | bytes 20000000 | tf_op jit(solution)/shard_map/pallas_call | solution.py:357
  225.8 8.4 %collective-permute-start.30 = (bf16[128,640]{1,0:T(8,128)(2,1)S(1)}, bf16[128,640]{1,0:T(8,128)(2,1)S(1)}, u32[]{:S(2)}, u32[]{:S(2)}) collective-permute-start(bf16[128,640]{1,0:T(8,128)(2,1)S(1)} %get-tuple-element.152), channel_id=1, source_target_pairs={{0,96},{1,97},{2,98},{3,99},{4,100},{5,101},{6,102},{7,103},{8,104... | collective-permute-start | bytes 491528 | tf_op jit(solution)/shard_map/ppermute | solution.py:121
  241.8 6.0 collective-permute-start.28
  256.0 6.3 collective-permute-done.29
  268.4 10.6 %shard_map.225 = (bf16[128,960]{1,0:T(8,128)(2,1)S(1)}, f32[8,384]{1,0:T(8,128)S(1)}) custom-call(bf16[960,128]{1,0:T(8,128)(2,1)S(1)} %copy-done.153, bf16[512,640]{1,0:T(8,128)(2,1)} %constant_dynamic-update-slice_fusion.8.kv0, bf16[512,640]{1,0:T(8,128)(2,1)} %constant_dynamic-update-slice_fusion.12.kv1, bf16[512,640]{1,0:T(8,128)(2,1)} %collective-permute-done.33.kv2, ...), custom_call_target="tpu_custom_call" | custom-call | flops 12000000000 | bytes 5000000 | tf_op jit(solution)/shard_map/pallas_call | solution.py:229
  279.6 10.2 %shard_map.226 = (f32[128,960]{1,0:T(8,128)S(1)}, bf16[128,960]{1,0:T(8,128)(2,1)S(1)}, f32[128,2560]{1,0:T(8,128)S(1)}, f32[128,2560]{1,0:T(8,128)S(1)}, bf16[1...) custom-call(bf16[128,960]{1,0:T(8,128)(2,1)S(1)} %get-tuple-element., ...), custom_call_target="tpu_custom_call" | custom-call | flops 4000000000 | bytes 20000000 | tf_op jit(solution)/shard_map/pallas_call | solution.py:357
  297.2 5.4 collective-permute-start.39
  330.0 10.6 %shard_map.227 = (bf16[128,960]{1,0:T(8,128)(2,1)S(1)}, f32[8,384]{1,0:T(8,128)S(1)}) custom-call(bf16[960,128]{1,0:T(8,128)(2,1)S(1)} %copy-done.156, bf16[512,640]{1,0:T(8,128)(2,1)} %constant_dynamic-update-slice_fusion.16.kv0, bf16[512,640]{1,0:T(8,128)(2,1)} %constant_dynamic-update-slice_fusion.20.kv1, bf16[512,640]{1,0:T(8,128)(2,1)} %collective-permute-done.42.kv2, ...), custom_call_target="tpu_custom_call" | custom-call | flops 12000000000 | bytes 5000000 | tf_op jit(solution)/shard_map/pallas_call | solution.py:229
  341.2 9.3 %shard_map.228 = (f32[128,960]{1,0:T(8,128)S(1)}, bf16[128,960]{1,0:T(8,128)(2,1)S(1)}, f32[128,2560]{1,0:T(8,128)S(1)}, f32[128,2560]{1,0:T(8,128)S(1)}, bf16[1...) custom-call(bf16[128,960]{1,0:T(8,128)(2,1)S(1)} %get-tuple-element.157.att_ref, ...), custom_call_target="tpu_custom_call" | custom-call | flops 4000000000 | bytes 20000000 | tf_op jit(solution)/shard_map/pallas_call | solution.py:357
  350.8 5.5 collective-permute-start.44
  357.1 10.4 %collective-permute-done.44 = bf16[128,960]{1,0:T(8,128)(2,1)S(1)} collective-permute-done((bf16[128,960]{1,0:T(8,128)(2,1)S(1)}, bf16[128,960]{1,0:T(8,128)(2,1)S(1)}, u32[]{:S(2)}, u32[]{:S(2)}) %collective-permute-start.44) | collective-permute-done | bytes 245792 | tf_op jit(solution)/shard_map/ppermute | solution.py:49
  391.8 10.0 %shard_map.229 = (f32[256,6144]{1,0:T(8,128)S(1)}, bf16[256,960]{1,0:T(8,128)(2,1)S(1)}, f32[256,128]{1,0:T(8,128)S(1)}) custom-call(s32[256,1]{1,0:T(8,128)S(1)} %copy-done.54, s32[1,1024]{1,0:T(1,128)S(1)} %bitcast.312, bf16[1024,960]{1,0:T(8,128)(2,1)S(1)} %bitcast.311, s32[256,1]{1,0:T(8,128)S(1)} %copy-done.53, bf16[6144,960]{1,0:T(8,128)(2,1)S(1)} %copy-done.4), custom_call_target="tpu_custom_call" | custom-call | tf_op jit(solution)/shard_map/pallas_call | solution.py:539
  413.7 15.7 %shard_map.230 = (bf16[6144,960]{1,0:T(8,128)(2,1)S(1)}, bf16[1024,960]{1,0:T(8,128)(2,1)S(1)}) custom-call(s32[256,1]{1,0:T(8,128)S(1)} %copy-done.54, s32[1,1024]{1,0:T(1,128)S(1)} %bitcast.313, s32[256,1]{1,0:T(8,128)S(1)} %copy-done.53, f32[256,1]{1,0:T(8,128)S(1)} %fusion.43.norm_ref, f32[256,6144]{1,0:T(8,128)S(1)} %get-tuple-element.161.logit_ref, ...), custom_call_target="tpu_custom_call" | custom-call | tf_op jit(solution)/shard_map/pallas_call | solution.py:589
  452.7 5.5 collective-permute-done.53
  458.2 6.1 collective-permute-done.54
  464.9 10.8 %shard_map.231 = (bf16[128,960]{1,0:T(8,128)(2,1)S(1)}, bf16[128,2560]{1,0:T(8,128)(2,1)S(1)}, bf16[128,2560]{1,0:T(8,128)(2,1)S(1)}, f32[128,960]{1,0:T(8,128)S...) custom-call(f32[128,960]{1,0:T(8,128)S(1)} %multiply_subtract_fusion.1.new_ref, ...), custom_call_target="tpu_custom_call" | custom-call | flops 4000000000 | bytes 20000000 | tf_op jit(solution)/shard_map/pallas_call | solution.py:446
  475.8 12.2 %shard_map.232 = (bf16[128,960]{1,0:T(8,128)(2,1)S(1)}, bf16[512,640]{1,0:T(8,128)(2,1)S(1)}, bf16[512,640]{1,0:T(8,128)(2,1)S(1)}, bf16[512,640]{1,0:T(8,128)(2,1)S(1)}, bf16[512,640]{1,0:T(8,128)(2,1)S(1)}) custom-call(bf16[960,128]{1,0:T(8,128)(2,1)S(1)} %copy-done.157, bf16[512,640]{1,0:T(8,128)(2,1)} %constant_dynamic-update-slice_fusion.16.kv0, ...), custom_call_target="tpu_custom_call" | custom-call | flops 20000000000 | bytes 9000000 | tf_op jit(solution)/shard_map/pallas_call | solution.py:274
  497.6 6.0 collective-permute-done.57
  506.4 9.2 %collective-permute-done.63 = bf16[128,640]{1,0:T(8,128)(2,1)S(1)} collective-permute-done((bf16[128,640]{1,0:T(8,128)(2,1)S(1)}, bf16[128,640]{1,0:T(8,128)(2,1)S(1)}, u32[]{:S(2)}, u32[]{:S(2)}) %collective-permute-start.63) | collective-permute-done | bytes 163872 | tf_op jit(solution)/shard_map/ppermute | solution.py:146
  520.0 10.4 %shard_map.234 = (bf16[128,960]{1,0:T(8,128)(2,1)S(1)}, bf16[128,2560]{1,0:T(8,128)(2,1)S(1)}, bf16[128,2560]{1,0:T(8,128)(2,1)S(1)}, f32[128,960]{1,0:T(8,128)S...) custom-call(f32[128,960]{1,0:T(8,128)S(1)} %get-tuple-element.177.new_ref, ...), custom_call_target="tpu_custom_call" | custom-call | flops 4000000000 | bytes 20000000 | tf_op jit(solution)/shard_map/pallas_call | solution.py:446
  531.2 12.1 %shard_map.235 = (bf16[128,960]{1,0:T(8,128)(2,1)S(1)}, bf16[512,640]{1,0:T(8,128)(2,1)S(1)}, bf16[512,640]{1,0:T(8,128)(2,1)S(1)}, bf16[512,640]{1,0:T(8,128)(2,1)S(1)}, bf16[512,640]{1,0:T(8,128)(2,1)S(1)}) custom-call(bf16[960,128]{1,0:T(8,128)(2,1)S(1)} %copy-done.154, bf16[512,640]{1,0:T(8,128)(2,1)} %constant_dynamic-update-slice_fusion.8.kv0, ...), custom_call_target="tpu_custom_call" | custom-call | flops 20000000000 | bytes 9000000 | tf_op jit(solution)/shard_map/pallas_call | solution.py:274
  552.3 5.9 collective-permute-done.66
  561.3 7.1 collective-permute-done.72
  573.8 10.3 %shard_map.237 = (bf16[128,960]{1,0:T(8,128)(2,1)S(1)}, bf16[128,2560]{1,0:T(8,128)(2,1)S(1)}, bf16[128,2560]{1,0:T(8,128)(2,1)S(1)}, f32[128,960]{1,0:T(8,128)S...) custom-call(f32[128,960]{1,0:T(8,128)S(1)} %get-tuple-element.191.new_ref, ...), custom_call_target="tpu_custom_call" | custom-call | flops 4000000000 | bytes 20000000 | tf_op jit(solution)/shard_map/pallas_call | solution.py:446
  585.3 6.7 shard_map.238
  606.5 10.3 %shard_map.239 = (bf16[128,960]{1,0:T(8,128)(2,1)S(1)}, bf16[512,640]{1,0:T(8,128)(2,1)S(1)}, bf16[512,640]{1,0:T(8,128)(2,1)S(1)}, bf16[512,640]{1,0:T(8,128)(2,1)S(1)}, bf16[512,640]{1,0:T(8,128)(2,1)S(1)}) custom-call(bf16[960,128]{1,0:T(8,128)(2,1)S(1)} %copy-done.151, bf16[512,640]{1,0:T(8,128)(2,1)S(1)} %copy-done.135, ...), custom_call_target="tpu_custom_call" | custom-call | flops 20000000000 | bytes 9000000 | tf_op jit(solution)/shard_map/pallas_call | solution.py:274
  616.8 9.4 %shard_map.241 = bf16[16,3,80,960]{3,2,1,0:T(8,128)(2,1)} custom-call(s32[1]{0:T(128)} %bitcast.74.which_ref, bf16[384,2560]{1,0:T(8,128)(2,1)S(1)} %copy-done.18, bf16[384,2560]{1,0:T(8,128)(2,1)S(1)} %copy-done.16, bf16[384,2560]{1,0:T(8,128)(2,1)S(1)} %copy-done.21, bf16[384,960]{1,0:T(8,128)(2,1)S(1)} %copy-done.7, bf16[384,960]{1,0:T(8,128)(2,1)S(1)} %copy-done.7, ...), custom_call_target="tpu_custom_call" | custom-call | tf_op jit(solution)/shard_map/pallas_call | solution.py:624
  640.7 6.1 collective-permute-done.76
  650.5 16.9 %collective-permute-done.82 = bf16[128,640]{1,0:T(8,128)(2,1)S(1)} collective-permute-done((bf16[128,640]{1,0:T(8,128)(2,1)S(1)}, bf16[128,640]{1,0:T(8,128)(2,1)S(1)}, u32[]{:S(2)}, u32[]{:S(2)}) %collective-permute-start.82) | collective-permute-done | bytes 163872 | tf_op jit(solution)/shard_map/ppermute | solution.py:146
  667.3 4.7 collective-permute-done.83
  681.6 7.8 shard_map.242
  702.9 6.0 collective-permute-done.86
  731.6 9.8 %all-to-all-start.2 = ((bf16[16,24,960]{2,1,0:T(8,128)(2,1)}), bf16[16,24,960]{2,1,0:T(8,128)(2,1)S(1)}, u32[]{:S(2)}, u32[]{:S(2)}) async-start(bf16[16,24,960]{2,1,0:T(8,128)(2,1)} %bitcast.72), calls=%async_computation.3 | async-start | bytes 1572864 | tf_op jit(solution)/shard_map/all_to_all | solution.py:1024
  741.4 13.9 %collective-permute-done.92 = bf16[352,960]{1,0:T(8,128)(2,1)} collective-permute-done((bf16[352,960]{1,0:T(8,128)(2,1)}, bf16[352,960]{1,0:T(8,128)(2,1)}, u32[]{:S(2)}, u32[]{:S(2)}) %collective-permute-start.92) | collective-permute-done | bytes 675872 | tf_op jit(solution)/shard_map/ppermute | solution.py:49
  768.2 5.8 collective-permute-done.96
  776.1 5.5 collective-permute-start.100
  822.9 5.2 multiply_subtract_fusion
  (844 shorter events, 397.9 us)
Async XLA Ops:
  8.0 81.5 %all-gather.7.cloned.1.call-start = ((), (), s32[]{:S(2)}) async-start(), calls=%async_computation.8 | async-start | bytes 6340608 | tf_op jit(solution)/shard_map/all_gather | solution.py:759
  11.4 51.8 %collective-permute-start.23 = (bf16[3,20,960]{2,1,0:T(8,128)(2,1)S(1)}, bf16[3,20,960]{2,1,0:T(8,128)(2,1)S(1)}, u32[]{:S(2)}, u32[]{:S(2)}) collective-permute-start(bf16[3,20,960]{2,1,0:T(8,128)(2,1)S(1)} %convert_element_type.371), channel_id=1, source_target_pairs={{0,32},{32,64},{64,96},{96,0},{1,33},{33,65},{65,97},{97,1},{2,34}... | collective-permute-start | bytes 345608 | tf_op jit(solution)/shard_map/ppermute | solution.py:49
  13.9 49.3 %collective-permute-start.24 = (bf16[3,20,960]{2,1,0:T(8,128)(2,1)S(1)}, bf16[3,20,960]{2,1,0:T(8,128)(2,1)S(1)}, u32[]{:S(2)}, u32[]{:S(2)}) collective-permute-start(bf16[3,20,960]{2,1,0:T(8,128)(2,1)S(1)} %convert_element_type.371), channel_id=1, source_target_pairs={{0,64},{32,96},{64,0},{96,32},{1,65},{33,97},{65,1},{97,33},{2,66}... | collective-permute-start | bytes 345608 | tf_op jit(solution)/shard_map/ppermute | solution.py:49
  20.2 21.2 %all-to-all-start = ((f32[16,1,24]{2,1,0:T(1,128)}), f32[16,1,24]{2,1,0:T(1,128)S(1)}, u32[]{:S(2)}, u32[]{:S(2)}) async-start(f32[16,1,24]{2,1,0:T(1,128)} %bitcast.11), calls=%async_computation.1 | async-start | bytes 16384 | tf_op jit(solution)/shard_map/all_to_all | solution.py:790
  36.2 12.6 %collective-permute-start.4 = (f32[1,128]{1,0:T(1,128)S(1)}, f32[1,128]{1,0:T(1,128)S(1)}, u32[]{:S(2)}, u32[]{:S(2)}) collective-permute-start(f32[1,128]{1,0:T(1,128)S(1)} %add_add_fusion.5), channel_id=1, source_target_pairs={{0,4},{4,8},{8,12},{12,0},{1,5},{5,9},{9,13},{13,1},{2,6},{6,10},{... | collective-permute-start | bytes 1544 | tf_op jit(solution)/shard_map/ppermute | solution.py:49
  44.6 21.5 %all-to-all-start.1 = ((bf16[16,24,960]{2,1,0:T(8,128)(2,1)}), bf16[16,24,960]{2,1,0:T(8,128)(2,1)S(1)}, u32[]{:S(2)}, u32[]{:S(2)}) async-start(bf16[16,24,960]{2,1,0:T(8,128)(2,1)} %bitcast.13), calls=%async_computation.2 | async-start | bytes 1572864 | tf_op jit(solution)/shard_map/all_to_all | solution.py:795
  48.8 12.4 %collective-permute-start.7 = (f32[1,128]{1,0:T(1,128)S(1)}, f32[1,128]{1,0:T(1,128)S(1)}, u32[]{:S(2)}, u32[]{:S(2)}) collective-permute-start(f32[1,128]{1,0:T(1,128)S(1)} %add_add_fusion.4), channel_id=1, source_target_pairs={{0,1},{1,2},{2,3},{3,0},{4,5},{5,6},{6,7},{7,4},{8,9},{9,10},{10,1... | collective-permute-start | bytes 1544 | tf_op jit(solution)/shard_map/ppermute | solution.py:49
  50.2 12.9 %collective-permute-start.8 = (f32[1,128]{1,0:T(1,128)S(1)}, f32[1,128]{1,0:T(1,128)S(1)}, u32[]{:S(2)}, u32[]{:S(2)}) collective-permute-start(f32[1,128]{1,0:T(1,128)S(1)} %add_add_fusion.4), channel_id=1, source_target_pairs={{0,2},{1,3},{2,0},{3,1},{4,6},{5,7},{6,4},{7,5},{8,10},{9,11},{10,... | collective-permute-start | bytes 1544 | tf_op jit(solution)/shard_map/ppermute | solution.py:49
  101.4 93.1 %all-gather.9.cloned.1.call-start = ((), (), s32[]{:S(2)}) async-start(), calls=%async_computation.9 | async-start | bytes 16220160 | tf_op jit(solution)/shard_map/all_gather | solution.py:762
  102.0 281.8 %all-gather.11.cloned.1.call-start = ((), (), s32[]{:S(2)}) async-start(), calls=%async_computation.10 | async-start | bytes 13369344 | tf_op jit(solution)/shard_map/all_gather | solution.py:763
  102.6 492.0 %reduce-scatter.10.cloned.1.call-start = ((), (), s32[]{:S(2)}) async-start(), calls=%async_computation.12 | async-start | bytes 13369344
  112.4 15.9 %collective-permute-start.10 = (bf16[4,128,960]{1,2,0:T(8,128)(2,1)S(1)}, bf16[4,128,960]{1,2,0:T(8,128)(2,1)}, u32[]{:S(2)}, u32[]{:S(2)}) collective-permute-start(bf16[4,128,960]{1,2,0:T(8,128)(2,1)S(1)} %copy.166), channel_id=1, source_target_pairs={{0,16},{16,0},{1,17},{17,1},{2,18},{18,2},{3,19},{19,3},{4,20},{20... | collective-permute-start | bytes 2949128 | tf_op jit(solution)/shard_map/ppermute | solution.py:53
  131.5 14.7 %collective-permute-start.11 = (bf16[128,960]{1,0:T(8,128)(2,1)S(1)}, bf16[128,960]{1,0:T(8,128)(2,1)S(1)}, u32[]{:S(2)}, u32[]{:S(2)}) collective-permute-start(bf16[128,960]{1,0:T(8,128)(2,1)S(1)} %get-tuple-element.306), channel_id=1, source_target_pairs={{0,32},{32,64},{64,96},{96,0},{1,33},{33,65},{65,97},{97,1},{2,34}... | collective-permute-start | bytes 737288 | tf_op jit(solution)/shard_map/ppermute | solution.py:49
  131.6 14.6 %collective-permute-start.12 = (bf16[128,960]{1,0:T(8,128)(2,1)S(1)}, bf16[128,960]{1,0:T(8,128)(2,1)S(1)}, u32[]{:S(2)}, u32[]{:S(2)}) collective-permute-start(bf16[128,960]{1,0:T(8,128)(2,1)S(1)} %get-tuple-element.308), channel_id=1, source_target_pairs={{0,64},{32,96},{64,0},{96,32},{1,65},{33,97},{65,1},{97,33},{2,66}... | collective-permute-start | bytes 737288 | tf_op jit(solution)/shard_map/ppermute | solution.py:49
  133.4 13.1 %collective-permute-start.13 = (bf16[128,960]{1,0:T(8,128)(2,1)S(1)}, bf16[128,960]{1,0:T(8,128)(2,1)S(1)}, u32[]{:S(2)}, u32[]{:S(2)}) collective-permute-start(bf16[128,960]{1,0:T(8,128)(2,1)S(1)} %get-tuple-element.307), channel_id=1, source_target_pairs={{0,96},{32,0},{64,32},{96,64},{1,97},{33,1},{65,33},{97,65},{2,98}... | collective-permute-start | bytes 737288 | tf_op jit(solution)/shard_map/ppermute | solution.py:49
  149.4 13.2 %collective-permute-start.18 = (bf16[128,640]{1,0:T(8,128)(2,1)}, bf16[128,640]{1,0:T(8,128)(2,1)}, u32[]{:S(2)}, u32[]{:S(2)}) collective-permute-start(bf16[128,640]{1,0:T(8,128)(2,1)} %get-tuple-element.149), channel_id=1, source_target_pairs={{0,96},{1,97},{2,98},{3,99},{4,100},{5,101},{6,102},{7,103},{8,104... | collective-permute-start | bytes 491528 | tf_op jit(solution)/shard_map/ppermute | solution.py:121
  155.9 13.7 %collective-permute-start.19 = (bf16[128,640]{1,0:T(8,128)(2,1)}, bf16[128,640]{1,0:T(8,128)(2,1)S(1)}, u32[]{:S(2)}, u32[]{:S(2)}) collective-permute-start(bf16[128,640]{1,0:T(8,128)(2,1)} %get-tuple-element.149), channel_id=1, source_target_pairs={{0,64},{32,96},{1,65},{33,97},{2,66},{34,98},{3,67},{35,99},{4,68}... | collective-permute-start | bytes 491528 | tf_op jit(solution)/shard_map/ppermute | solution.py:121
  158.3 12.7 %collective-permute-start.20 = (bf16[128,640]{1,0:T(8,128)(2,1)}, bf16[128,640]{1,0:T(8,128)(2,1)S(1)}, u32[]{:S(2)}, u32[]{:S(2)}) collective-permute-start(bf16[128,640]{1,0:T(8,128)(2,1)} %get-tuple-element.149), channel_id=1, source_target_pairs={{0,32},{32,64},{64,96},{1,33},{33,65},{65,97},{2,34},{34,66},{66,9... | collective-permute-start | bytes 491528 | tf_op jit(solution)/shard_map/ppermute | solution.py:121
  160.0 12.5 %collective-permute-start.14 = (bf16[128,640]{1,0:T(8,128)(2,1)}, bf16[128,640]{1,0:T(8,128)(2,1)S(1)}, u32[]{:S(2)}, u32[]{:S(2)}) collective-permute-start(bf16[128,640]{1,0:T(8,128)(2,1)} %get-tuple-element.149), channel_id=1, source_target_pairs={{0,1},{1,2},{2,3},{3,4},{4,5},{5,6},{6,7},{7,8},{8,9},{9,10},{10,1... | collective-permute-start | bytes 491528 | tf_op jit(solution)/shard_map/ppermute | solution.py:128
  225.8 15.9 %collective-permute-start.30 = (bf16[128,640]{1,0:T(8,128)(2,1)S(1)}, bf16[128,640]{1,0:T(8,128)(2,1)S(1)}, u32[]{:S(2)}, u32[]{:S(2)}) collective-permute-start(bf16[128,640]{1,0:T(8,128)(2,1)S(1)} %get-tuple-element.152), channel_id=1, source_target_pairs={{0,96},{1,97},{2,98},{3,99},{4,100},{5,101},{6,102},{7,103},{8,104... | collective-permute-start | bytes 491528 | tf_op jit(solution)/shard_map/ppermute | solution.py:121
  234.2 14.2 %collective-permute-start.31 = (bf16[128,640]{1,0:T(8,128)(2,1)S(1)}, bf16[128,640]{1,0:T(8,128)(2,1)S(1)}, u32[]{:S(2)}, u32[]{:S(2)}) collective-permute-start(bf16[128,640]{1,0:T(8,128)(2,1)S(1)} %get-tuple-element.152), channel_id=1, source_target_pairs={{0,64},{32,96},{1,65},{33,97},{2,66},{34,98},{3,67},{35,99},{4,68}... | collective-permute-start | bytes 491528 | tf_op jit(solution)/shard_map/ppermute | solution.py:121
  236.2 14.2 %collective-permute-start.32 = (bf16[128,640]{1,0:T(8,128)(2,1)S(1)}, bf16[128,640]{1,0:T(8,128)(2,1)S(1)}, u32[]{:S(2)}, u32[]{:S(2)}) collective-permute-start(bf16[128,640]{1,0:T(8,128)(2,1)S(1)} %get-tuple-element.152), channel_id=1, source_target_pairs={{0,32},{32,64},{64,96},{1,33},{33,65},{65,97},{2,34},{34,66},{66,9... | collective-permute-start | bytes 491528 | tf_op jit(solution)/shard_map/ppermute | solution.py:121
  238.7 13.1 %collective-permute-start.26 = (bf16[128,640]{1,0:T(8,128)(2,1)S(1)}, bf16[128,640]{1,0:T(8,128)(2,1)S(1)}, u32[]{:S(2)}, u32[]{:S(2)}) collective-permute-start(bf16[128,640]{1,0:T(8,128)(2,1)S(1)} %get-tuple-element.152), channel_id=1, source_target_pairs={{0,1},{1,2},{2,3},{3,4},{4,5},{5,6},{6,7},{7,8},{8,9},{9,10},{10,1... | collective-permute-start | bytes 491528 | tf_op jit(solution)/shard_map/ppermute | solution.py:128
  241.8 13.6 %collective-permute-start.28 = (bf16[128,640]{1,0:T(8,128)(2,1)S(1)}, bf16[128,640]{1,0:T(8,128)(2,1)S(1)}, u32[]{:S(2)}, u32[]{:S(2)}) collective-permute-start(bf16[128,640]{1,0:T(8,128)(2,1)S(1)} %get-tuple-element.152), channel_id=1, source_target_pairs={{64,1},{65,2},{66,3},{67,4},{68,5},{69,6},{70,7},{71,8},{72,9},{73... | collective-permute-start | bytes 491528 | tf_op jit(solution)/shard_map/ppermute | solution.py:128
  248.4 13.9 %collective-permute-start.29 = (bf16[128,640]{1,0:T(8,128)(2,1)S(1)}, bf16[128,640]{1,0:T(8,128)(2,1)S(1)}, u32[]{:S(2)}, u32[]{:S(2)}) collective-permute-start(bf16[128,640]{1,0:T(8,128)(2,1)S(1)} %get-tuple-element.152), channel_id=1, source_target_pairs={{96,1},{97,2},{98,3},{99,4},{100,5},{101,6},{102,7},{103,8},{104,9... | collective-permute-start | bytes 491528 | tf_op jit(solution)/shard_map/ppermute | solution.py:128
  251.1 13.8 %collective-permute-start.34 = (bf16[512,640]{1,0:T(8,128)(2,1)}, bf16[512,640]{1,0:T(8,128)(2,1)}, u32[]{:S(2)}, u32[]{:S(2)}) collective-permute-start(bf16[512,640]{1,0:T(8,128)(2,1)} %constant_dynamic-update-slice_fusion.12.kv1), channel_id=1, source_target_pairs={{0,16},{16,0},{1,17},{17,1},{2,18},{18,2},{3,19},{19,3},{4,20},{20... | collective-permute-start | bytes 1966088 | tf_op jit(solution)/shard_map/ppermute | solution.py:53
  297.2 14.9 %collective-permute-start.39 = (bf16[128,640]{1,0:T(8,128)(2,1)S(1)}, bf16[128,640]{1,0:T(8,128)(2,1)S(1)}, u32[]{:S(2)}, u32[]{:S(2)}) collective-permute-start(bf16[128,640]{1,0:T(8,128)(2,1)S(1)} %get-tuple-element.156), channel_id=1, source_target_pairs={{0,96},{1,97},{2,98},{3,99},{4,100},{5,101},{6,102},{7,103},{8,104... | collective-permute-start | bytes 491528 | tf_op jit(solution)/shard_map/ppermute | solution.py:121
  302.6 14.9 %collective-permute-start.40 = (bf16[128,640]{1,0:T(8,128)(2,1)S(1)}, bf16[128,640]{1,0:T(8,128)(2,1)S(1)}, u32[]{:S(2)}, u32[]{:S(2)}) collective-permute-start(bf16[128,640]{1,0:T(8,128)(2,1)S(1)} %get-tuple-element.156), channel_id=1, source_target_pairs={{0,64},{32,96},{1,65},{33,97},{2,66},{34,98},{3,67},{35,99},{4,68}... | collective-permute-start | bytes 491528 | tf_op jit(solution)/shard_map/ppermute | solution.py:121
  304.6 14.8 %collective-permute-start.41 = (bf16[128,640]{1,0:T(8,128)(2,1)S(1)}, bf16[128,640]{1,0:T(8,128)(2,1)S(1)}, u32[]{:S(2)}, u32[]{:S(2)}) collective-permute-start(bf16[128,640]{1,0:T(8,128)(2,1)S(1)} %get-tuple-element.156), channel_id=1, source_target_pairs={{0,32},{32,64},{64,96},{1,33},{33,65},{65,97},{2,34},{34,66},{66,9... | collective-permute-start | bytes 491528 | tf_op jit(solution)/shard_map/ppermute | solution.py:121
  307.1 14.5 %collective-permute-start.35 = (bf16[128,640]{1,0:T(8,128)(2,1)S(1)}, bf16[128,640]{1,0:T(8,128)(2,1)S(1)}, u32[]{:S(2)}, u32[]{:S(2)}) collective-permute-start(bf16[128,640]{1,0:T(8,128)(2,1)S(1)} %get-tuple-element.156), channel_id=1, source_target_pairs={{0,1},{1,2},{2,3},{3,4},{4,5},{5,6},{6,7},{7,8},{8,9},{9,10},{10,1... | collective-permute-start | bytes 491528 | tf_op jit(solution)/shard_map/ppermute | solution.py:128
  350.8 16.7 %collective-permute-start.44 = (bf16[128,960]{1,0:T(8,128)(2,1)S(1)}, bf16[128,960]{1,0:T(8,128)(2,1)S(1)}, u32[]{:S(2)}, u32[]{:S(2)}) collective-permute-start(bf16[128,960]{1,0:T(8,128)(2,1)S(1)} %multiply_convert_fusion), channel_id=1, source_target_pairs={{0,96},{32,0},{64,32},{96,64},{1,97},{33,1},{65,33},{97,65},{2,98}... | collective-permute-start | bytes 737288 | tf_op jit(solution)/shard_map/ppermute | solution.py:49
  356.3 14.8 %collective-permute-start.46 = (bf16[128,960]{1,0:T(8,128)(2,1)S(1)}, bf16[128,960]{1,0:T(8,128)(2,1)S(1)}, u32[]{:S(2)}, u32[]{:S(2)}) collective-permute-start(bf16[128,960]{1,0:T(8,128)(2,1)S(1)} %multiply_convert_fusion), channel_id=1, source_target_pairs={{0,32},{32,64},{64,96},{96,0},{1,33},{33,65},{65,97},{97,1},{2,34}... | collective-permute-start | bytes 737288 | tf_op jit(solution)/shard_map/ppermute | solution.py:49
  435.4 347.3 %reduce-scatter.8.cloned.1.call-start = ((), (), s32[]{:S(2)}) async-start(), calls=%async_computation.11 | async-start | bytes 8355840 | tf_op jit(solution)/shard_map/reduce_scatter | solution.py:969
  449.5 14.8 %collective-permute-start.54 = (bf16[128,960]{1,0:T(8,128)(2,1)S(1)}, bf16[128,960]{1,0:T(8,128)(2,1)S(1)}, u32[]{:S(2)}, u32[]{:S(2)}) collective-permute-start(bf16[128,960]{1,0:T(8,128)(2,1)S(1)} %get-tuple-element.303), channel_id=1, source_target_pairs={{0,64},{32,96},{64,0},{96,32},{1,65},{33,97},{65,1},{97,33},{2,66}... | collective-permute-start | bytes 737288 | tf_op jit(solution)/shard_map/ppermute | solution.py:49
  504.9 12.7 %collective-permute-start.64 = (bf16[128,640]{1,0:T(8,128)(2,1)S(1)}, bf16[128,640]{1,0:T(8,128)(2,1)S(1)}, u32[]{:S(2)}, u32[]{:S(2)}) collective-permute-start(bf16[128,640]{1,0:T(8,128)(2,1)S(1)} %get-tuple-element.334), channel_id=1, source_target_pairs={{1,96},{2,97},{3,98},{4,99},{5,100},{6,101},{7,102},{8,103},{9,104... | collective-permute-start | bytes 491528 | tf_op jit(solution)/shard_map/ppermute | solution.py:146
  548.7 12.5 %collective-permute-start.68 = (bf16[128,640]{1,0:T(8,128)(2,1)S(1)}, bf16[128,640]{1,0:T(8,128)(2,1)S(1)}, u32[]{:S(2)}, u32[]{:S(2)}) collective-permute-start(bf16[128,640]{1,0:T(8,128)(2,1)S(1)} %get-tuple-element.324), channel_id=1, source_target_pairs={{32,0},{64,32},{96,64},{33,1},{65,33},{97,65},{34,2},{66,34},{98,6... | collective-permute-start | bytes 491528 | tf_op jit(solution)/shard_map/ppermute | solution.py:140
  596.9 19.8 %collective-permute-start.74 = (bf16[16,3,80,960]{3,2,1,0:T(8,128)(2,1)}, bf16[16,3,80,960]{3,2,1,0:T(8,128)(2,1)}, u32[]{:S(2)}, u32[]{:S(2)}) collective-permute-start(bf16[16,3,80,960]{3,2,1,0:T(8,128)(2,1)} %shard_map.238), channel_id=1, source_target_pairs={{0,16},{16,0},{1,17},{17,1},{2,18},{18,2},{3,19},{19,3},{4,20},{20... | collective-permute-start | bytes 22118408 | tf_op jit(solution)/shard_map/ppermute | solution.py:53
  634.2 12.5 %collective-permute-start.76 = (bf16[128,640]{1,0:T(8,128)(2,1)S(1)}, bf16[128,640]{1,0:T(8,128)(2,1)S(1)}, u32[]{:S(2)}, u32[]{:S(2)}) collective-permute-start(bf16[128,640]{1,0:T(8,128)(2,1)S(1)} %get-tuple-element.316), channel_id=1, source_target_pairs={{96,0},{97,1},{98,2},{99,3},{100,4},{101,5},{102,6},{103,7},{104,8... | collective-permute-start | bytes 491528 | tf_op jit(solution)/shard_map/ppermute | solution.py:140
  637.0 13.5 %collective-permute-start.78 = (bf16[128,640]{1,0:T(8,128)(2,1)S(1)}, bf16[128,640]{1,0:T(8,128)(2,1)S(1)}, u32[]{:S(2)}, u32[]{:S(2)}) collective-permute-start(bf16[128,640]{1,0:T(8,128)(2,1)S(1)} %get-tuple-element.317), channel_id=1, source_target_pairs={{32,0},{64,32},{96,64},{33,1},{65,33},{97,65},{34,2},{66,34},{98,6... | collective-permute-start | bytes 491528 | tf_op jit(solution)/shard_map/ppermute | solution.py:140
  646.8 20.6 %collective-permute-start.82 = (bf16[128,640]{1,0:T(8,128)(2,1)S(1)}, bf16[128,640]{1,0:T(8,128)(2,1)S(1)}, u32[]{:S(2)}, u32[]{:S(2)}) collective-permute-start(bf16[128,640]{1,0:T(8,128)(2,1)S(1)} %get-tuple-element.321), channel_id=1, source_target_pairs={{1,64},{2,65},{3,66},{4,67},{5,68},{6,69},{7,70},{8,71},{9,72},{10... | collective-permute-start | bytes 491528 | tf_op jit(solution)/shard_map/ppermute | solution.py:146
  648.1 24.0 %collective-permute-start.83 = (bf16[128,640]{1,0:T(8,128)(2,1)S(1)}, bf16[128,640]{1,0:T(8,128)(2,1)S(1)}, u32[]{:S(2)}, u32[]{:S(2)}) collective-permute-start(bf16[128,640]{1,0:T(8,128)(2,1)S(1)} %get-tuple-element.320), channel_id=1, source_target_pairs={{1,96},{2,97},{3,98},{4,99},{5,100},{6,101},{7,102},{8,103},{9,104... | collective-permute-start | bytes 491528 | tf_op jit(solution)/shard_map/ppermute | solution.py:146
  691.0 24.0 %collective-permute-start.91 = (bf16[4,352,960]{2,1,0:T(8,128)(2,1)}, bf16[4,352,960]{2,1,0:T(8,128)(2,1)}, u32[]{:S(2)}, u32[]{:S(2)}) collective-permute-start(bf16[4,352,960]{2,1,0:T(8,128)(2,1)} %get-tuple-element.245), channel_id=1, source_target_pairs={{0,16},{16,0},{1,17},{17,1},{2,18},{18,2},{3,19},{19,3},{4,20},{20... | collective-permute-start | bytes 8110088 | tf_op jit(solution)/shard_map/ppermute | solution.py:53
  696.4 12.5 %collective-permute-start.86 = (bf16[128,960]{1,0:T(8,128)(2,1)S(1)}, bf16[128,960]{1,0:T(8,128)(2,1)S(1)}, u32[]{:S(2)}, u32[]{:S(2)}) collective-permute-start(bf16[128,960]{1,0:T(8,128)(2,1)S(1)} %convert_element_type.424), channel_id=1, source_target_pairs={{0,32},{32,64},{64,96},{96,0},{1,33},{33,65},{65,97},{97,1},{2,34}... | collective-permute-start | bytes 737288 | tf_op jit(solution)/shard_map/ppermute | solution.py:49
  712.8 13.2 %collective-permute-start.87 = (bf16[4,128,960]{1,2,0:T(8,128)(2,1)}, bf16[4,128,960]{1,2,0:T(8,128)(2,1)}, u32[]{:S(2)}, u32[]{:S(2)}) collective-permute-start(bf16[4,128,960]{1,2,0:T(8,128)(2,1)} %copy.184), channel_id=1, source_target_pairs={{0,16},{16,0},{1,17},{17,1},{2,18},{18,2},{3,19},{19,3},{4,20},{20... | collective-permute-start | bytes 2949128 | tf_op jit(solution)/shard_map/ppermute | solution.py:53
  720.6 34.7 %collective-permute-start.92 = (bf16[352,960]{1,0:T(8,128)(2,1)}, bf16[352,960]{1,0:T(8,128)(2,1)}, u32[]{:S(2)}, u32[]{:S(2)}) collective-permute-start(bf16[352,960]{1,0:T(8,128)(2,1)} %get-tuple-element.292), channel_id=1, source_target_pairs={{0,32},{32,64},{64,96},{96,0},{1,33},{33,65},{65,97},{97,1},{2,34}... | collective-permute-start | bytes 2027528 | tf_op jit(solution)/shard_map/ppermute | solution.py:49
  722.1 33.2 %collective-permute-start.93 = (bf16[352,960]{1,0:T(8,128)(2,1)}, bf16[352,960]{1,0:T(8,128)(2,1)}, u32[]{:S(2)}, u32[]{:S(2)}) collective-permute-start(bf16[352,960]{1,0:T(8,128)(2,1)} %get-tuple-element.294), channel_id=1, source_target_pairs={{0,64},{32,96},{64,0},{96,32},{1,65},{33,97},{65,1},{97,33},{2,66}... | collective-permute-start | bytes 2027528 | tf_op jit(solution)/shard_map/ppermute | solution.py:49
  722.5 33.1 %collective-permute-start.94 = (bf16[352,960]{1,0:T(8,128)(2,1)}, bf16[352,960]{1,0:T(8,128)(2,1)}, u32[]{:S(2)}, u32[]{:S(2)}) collective-permute-start(bf16[352,960]{1,0:T(8,128)(2,1)} %get-tuple-element.293), channel_id=1, source_target_pairs={{0,96},{32,0},{64,32},{96,64},{1,97},{33,1},{65,33},{97,65},{2,98}... | collective-permute-start | bytes 2027528 | tf_op jit(solution)/shard_map/ppermute | solution.py:49
  731.6 34.4 %all-to-all-start.2 = ((bf16[16,24,960]{2,1,0:T(8,128)(2,1)}), bf16[16,24,960]{2,1,0:T(8,128)(2,1)S(1)}, u32[]{:S(2)}, u32[]{:S(2)}) async-start(bf16[16,24,960]{2,1,0:T(8,128)(2,1)} %bitcast.72), calls=%async_computation.3 | async-start | bytes 1572864 | tf_op jit(solution)/shard_map/all_to_all | solution.py:1024
  (277 other events, 2453.9 us)
Sparse Core Ops, SparseCore 0:
  12.4 77.0 all-gather.6
Sparse Core Ops, SparseCore 1:
  104.7 71.6 all-gather.8
  178.5 102.9 all-gather.10
  435.5 98.8 reduce-scatter.9
  626.4 90.5 reduce-scatter.7

commit v3 on v2

--- a/solution.py
+++ b/solution.py
@@ -54,16 +54,17 @@
 
 
 def gather_group(value):
-    parts = jnp.stack([value] + [shift(value, "z", -k) for k in (1, 2, 3)])
-    return jnp.stack([parts, swap(parts)])
-
-
-def scatter_group(blocks, kind=BFLOAT):
-    half = (blocks[0].astype(FLOAT) + swap(blocks[1].astype(BFLOAT)).astype(FLOAT)).astype(BFLOAT)
+    near = by_rows(jnp.concatenate([value] + [shift(value, "z", -k) for k in (1, 2, 3)], axis=0))
+    return near, by_rows(swap(near))
+
+
+def scatter_group(near, far):
+    half = (near.astype(FLOAT) + by_rows(swap(by_rows(far))).astype(FLOAT)).astype(BFLOAT)
+    half = half.reshape(4, TOK_DEV, -1)
     total = half[0].astype(FLOAT)
     for k in (1, 2, 3):
         total = total + shift(half[k], "z", k).astype(FLOAT)
-    return total.astype(kind)
+    return total
 
 
 def sum_all(value):
@@ -299,6 +300,37 @@
 )
 
 
+def spread_kernel(place_ref, rows_ref, near_ref, far_ref):
+    place = lax.broadcasted_iota(jnp.int32, (512, DP * CAP), 1)
+    for part, ref in enumerate((near_ref, far_ref)):
+        hot = (place_ref[512 * part : 512 * part + 512, :] == place).astype(FLOAT).astype(BFLOAT)
+        ref[...] = nn(hot, rows_ref[...]).astype(BFLOAT)
+
+
+def spread(place, rows):
+    return pl.pallas_call(
+        spread_kernel,
+        out_shape=(struct(BFLOAT, 512, D), struct(BFLOAT, 512, D)),
+        compiler_params=params(24),
+    )(place, rows)
+
+
+def collect_kernel(place_ref, near_ref, far_ref, out_ref):
+    place = lax.broadcasted_iota(jnp.int32, (512, DP * CAP), 1)
+    total = None
+    for part, ref in enumerate((near_ref, far_ref)):
+        hot = (place_ref[512 * part : 512 * part + 512, :] == place).astype(FLOAT).astype(BFLOAT)
+        sums = contract_rows(hot, ref[...])
+        total = sums if total is None else total + sums
+    out_ref[...] = total.astype(BFLOAT)
+
+
+def collect(place, near, far):
+    return pl.pallas_call(
+        collect_kernel, out_shape=struct(BFLOAT, DP * CAP, D), compiler_params=params(24)
+    )(place, near, far)
+
+
 def enter_kernel(hidden_ref, gain_ref, *refs):
     project(hidden_ref[...], gain_ref[0:1, :], *refs)
 
@@ -309,8 +341,13 @@
     )
 
 
+BIG = 56
 FF_BLOCK = 640
 FF_STEPS = FF // FF_BLOCK
+
+
+def weight(ref, which):
+    return ref[:, which].reshape(FF_BLOCK, D)
 
 
 def block_kernel(
@@ -318,24 +355,31 @@
 ):
     proj_in, refs = (refs[:5], refs[5:]) if more else ((), refs)
     mixed_ref, input_ref, gate_ref, up_ref, inner_ref, branch_ref, logit_ref, new_ref = refs[:8]
-    acc_ref = refs[-1]
+    proj_out, refs = (refs[8:11], refs[11:]) if more else ((), refs[8:])
+    acc_ref = refs[0]
     step = pl.program_id(0)
+    copies = [
+        pltpu.make_async_copy(source, target, refs[4].at[i])
+        for i, (source, target) in enumerate(zip(proj_in[:3], refs[1:4]))
+    ]
 
     @pl.when(step == 0)
     def first():
+        for copy in copies:
+            copy.start()
         mixed = hidden_ref[...] + nn(att_ref[...], wo_ref[...])
         mixed_ref[...] = mixed
         input_ref[...] = normalize(mixed, gain_ref[1:2, :]).astype(BFLOAT)
         acc_ref[...] = mixed
 
     rows = input_ref[...]
-    gate = contract_cols(rows, weight_ref[0])
-    up = contract_cols(rows, weight_ref[1])
+    gate = contract_cols(rows, weight(weight_ref, 0))
+    up = contract_cols(rows, weight(weight_ref, 1))
     gate_ref[...] = gate
     up_ref[...] = up
     inner = (gate * jax.nn.sigmoid(gate) * up).astype(BFLOAT)
     inner_ref[...] = inner
-    acc_ref[...] += nn(inner, weight_ref[2])
+    acc_ref[...] += nn(inner, weight(weight_ref, 2))
 
     @pl.when(step == FF_STEPS - 1)
     def last():
@@ -346,13 +390,18 @@
         logit_ref[...] = logit
         new = hidden + sel_ref[...] * jax.nn.sigmoid(logit) * (branch - hidden)
         new_ref[...] = new
+        for copy in copies:
+            copy.wait()
         if more:
-            project(new, gain_ref[0:1, :], *proj_in, *refs[8:11])
+            project(new, gain_ref[0:1, :], *refs[1:4], *proj_in[3:], *proj_out)
+
+
+WEIGHT_SPEC = pl.BlockSpec((FF_BLOCK // 80, 3, 80, D), lambda i: (i, 0, 0, 0))
 
 
 def block(att, hidden, sel, gains, router, wo, weights, projections):
     more = projections is not None
-    proj_specs = [whole(D, D), whole(D, 320), whole(D, 320), whole(32, 128), whole(32, 128)]
+    proj_specs = [pl.BlockSpec(memory_space=pl.ANY)] * 3 + [whole(32, 128), whole(32, 128)]
     rows = pl.BlockSpec((TOK_DEV, FF_BLOCK), lambda i: (0, i))
     return pl.pallas_call(
         functools.partial(block_kernel, more),
@@ -364,7 +413,7 @@
             whole(8, D),
             whole(1, D),
             whole(D, D),
-            pl.BlockSpec((3, FF_BLOCK, D), lambda i: (0, i, 0)),
+            WEIGHT_SPEC,
         ]
         + proj_specs * more,
         out_specs=[
@@ -389,42 +438,51 @@
             struct(FLOAT, TOK_DEV, D),
         )
         + (PROJECTED if more else ()),
-        scratch_shapes=[pltpu.VMEM((TOK_DEV, D), FLOAT)],
+        scratch_shapes=[pltpu.VMEM((TOK_DEV, D), FLOAT)]
+        + [
+            pltpu.VMEM((D, D), BFLOAT),
+            pltpu.VMEM((D, 320), BFLOAT),
+            pltpu.VMEM((D, 320), BFLOAT),
+            pltpu.SemaphoreType.DMA((3,)),
+        ]
+        * more,
         cost_estimate=pl.CostEstimate(
             flops=4_000_000_000, bytes_accessed=20_000_000, transcendentals=400_000
         ),
-        compiler_params=params(32),
+        compiler_params=params(BIG),
     )(att, hidden, sel, gains, router, wo, weights, *(projections if more else ()))
 
 
 def block_back_kernel(
     new_ref, sel_ref, logit_ref, hidden_ref, branch_ref, mixed_ref, gain_ref, router_ref, wo_ref,
     gate_ref, up_ref, weight_ref,
-    rows_ref, dgate_ref, dup_ref, in_ref, attn_ref, back_ref, small_ref, acc_ref
+    rows_ref, dgate_ref, dup_ref, in_ref, attn_ref, back_ref, small_ref, acc_ref, held_ref, sem
 ):
     step = pl.program_id(0)
     sigma = jax.nn.sigmoid(logit_ref[...])
-    weight = sel_ref[...] * sigma
+    chosen = sel_ref[...] * sigma
+    copy = pltpu.make_async_copy(wo_ref, held_ref, sem)
 
     @pl.when(step == 0)
     def first():
-        rows_ref[...] = (weight * new_ref[...]).astype(BFLOAT)
+        copy.start()
+        rows_ref[...] = (chosen * new_ref[...]).astype(BFLOAT)
         acc_ref[...] = jnp.zeros_like(acc_ref)
 
-    inner = contract_cols(rows_ref[...], weight_ref[2])
+    inner = contract_cols(rows_ref[...], weight(weight_ref, 2))
     gate = gate_ref[...]
     shape = jax.nn.sigmoid(gate)
     dgate = (inner * up_ref[...] * shape * (1.0 + gate * (1.0 - shape))).astype(BFLOAT)
     dup = (inner * gate * shape).astype(BFLOAT)
     dgate_ref[...] = dgate
     dup_ref[...] = dup
-    acc_ref[...] += nn(dgate, weight_ref[0]) + nn(dup, weight_ref[1])
+    acc_ref[...] += nn(dgate, weight(weight_ref, 0)) + nn(dup, weight(weight_ref, 1))
 
     @pl.when(step == FF_STEPS - 1)
     def last():
         grad_new = new_ref[...]
         hidden = hidden_ref[...]
-        grad_branch = weight * grad_new
+        grad_branch = chosen * grad_new
         grad_weight = jnp.sum(grad_new * (branch_ref[...] - hidden), axis=1, keepdims=True)
         grad_logit = grad_weight * sel_ref[...] * sigma * (1.0 - sigma) + ROUTER_LOSS / TOK_DEV * (
             sigma - sel_ref[...]
@@ -434,7 +492,8 @@
         in_ref[...] = grad_new - grad_branch + grad_logit * router_ref[...] + grad_mixed
         attn = grad_mixed.astype(BFLOAT)
         attn_ref[...] = attn
-        back_ref[...] = contract_cols(attn, wo_ref[...]).astype(BFLOAT)
+        copy.wait()
+        back_ref[...] = contract_cols(attn, held_ref[...]).astype(BFLOAT)
         small_ref[0:1, :] = gain_row
         small_ref[1:2, :] = jnp.sum(grad_logit * hidden, axis=0, keepdims=True)
         small_ref[2:8, :] = jnp.zeros((6, D), FLOAT)
@@ -455,10 +514,10 @@
             full,
             whole(8, D),
             whole(1, D),
-            whole(D, D),
+            pl.BlockSpec(memory_space=pl.ANY),
             rows,
             rows,
-            pl.BlockSpec((3, FF_BLOCK, D), lambda i: (0, i, 0)),
+            WEIGHT_SPEC,
         ],
         out_specs=[full, rows, rows, full, full, full, whole(8, D)],
         out_shape=(
@@ -470,11 +529,15 @@
             struct(BFLOAT, TOK_DEV, D),
             struct(FLOAT, 8, D),
         ),
-        scratch_shapes=[pltpu.VMEM((TOK_DEV, D), FLOAT)],
+        scratch_shapes=[
+            pltpu.VMEM((TOK_DEV, D), FLOAT),
+            pltpu.VMEM((D, D), BFLOAT),
+            pltpu.SemaphoreType.DMA,
+        ],
         cost_estimate=pl.CostEstimate(
             flops=4_000_000_000, bytes_accessed=20_000_000, transcendentals=400_000
         ),
-        compiler_params=params(32),
+        compiler_params=params(BIG),
     )(new, sel, logit, hidden, branch, mixed, gains, router, wo, gate, up, weights)
 
 
@@ -511,13 +574,15 @@
 HEAD_BLOCK = 512
 
 
-def head_kernel(rows_ref, near_ref, final_ref, target_ref, table_ref, logit_ref, pick_ref, stat_ref):
+def head_kernel(rows_ref, near_ref, side_ref, far_ref, target_ref, table_ref, logit_ref, pick_ref, stat_ref):
     step = pl.program_id(0)
 
     @pl.when(step == 0)
     def first():
         hot = (rows_ref[...] == near_ref[...]).astype(FLOAT).astype(BFLOAT)
-        pick_ref[...] = nn(hot, final_ref[...]).astype(BFLOAT)
+        pick_ref[...] = (nn(hot[:, :512], side_ref[...]) + nn(hot[:, 512:], far_ref[...])).astype(
+            BFLOAT
+        )
         lane = lax.broadcasted_iota(jnp.int32, (256, 128), 1)
         stat_ref[...] = jnp.where(lane == 0, MASKED, 0.0)
 
@@ -535,14 +600,15 @@
     stat_ref[:, 0:1] = top
 
 
-def head(loss_rows, near_rows, final_rows, local_targets, table):
+def head(loss_rows, near_rows, near, far, local_targets, table):
     return pl.pallas_call(
         head_kernel,
         grid=(VOCAB_MP // HEAD_BLOCK,),
         in_specs=[
             whole(256, 1),
             whole(1, ROWS),
-            whole(ROWS, D),
+            whole(512, D),
+            whole(512, D),
             whole(256, 1),
             pl.BlockSpec((HEAD_BLOCK, D), lambda i: (i, 0)),
         ],
@@ -556,12 +622,12 @@
             jax.ShapeDtypeStruct((256, D), BFLOAT),
             jax.ShapeDtypeStruct((256, 128), FLOAT),
         ),
-        compiler_params=pltpu.CompilerParams(vmem_limit_bytes=32 * 1024 * 1024),
-    )(loss_rows, near_rows, final_rows, local_targets, table)
+        compiler_params=params(BIG),
+    )(loss_rows, near_rows, near, far, local_targets, table)
 
 
 def head_back_kernel(
-    rows_ref, near_ref, target_ref, norm_ref, logit_ref, pick_ref, table_ref, grad_ref, out_ref, sum_ref
+    rows_ref, near_ref, target_ref, norm_ref, logit_ref, pick_ref, table_ref, grad_ref, side_ref, far_ref, sum_ref
 ):
     step = pl.program_id(0)
     place = step * HEAD_BLOCK + lax.broadcasted_iota(jnp.int32, (256, HEAD_BLOCK), 1)
@@ -582,7 +648,9 @@
     @pl.when(step == pl.num_programs(0) - 1)
     def last():
         hot = (rows_ref[...] == near_ref[...]).astype(FLOAT).astype(BFLOAT)
-        out_ref[...] = contract_rows(hot, sum_ref[...].astype(BFLOAT)).astype(BFLOAT)
+        total = sum_ref[...].astype(BFLOAT)
+        side_ref[...] = contract_rows(hot[:, :512], total).astype(BFLOAT)
+        far_ref[...] = contract_rows(hot[:, 512:], total).astype(BFLOAT)
 
 
 def head_back(loss_rows, near_rows, local_targets, log_norm, logits, picked, table):
@@ -598,75 +666,129 @@
             whole(256, D),
             pl.BlockSpec((HEAD_BLOCK, D), lambda i: (i, 0)),
         ],
-        out_specs=[pl.BlockSpec((HEAD_BLOCK, D), lambda i: (i, 0)), whole(ROWS, D)],
+        out_specs=[pl.BlockSpec((HEAD_BLOCK, D), lambda i: (i, 0)), whole(512, D), whole(512, D)],
         out_shape=(
-            jax.ShapeDtypeStruct((VOCAB_MP, D), BFLOAT),
-            jax.ShapeDtypeStruct((ROWS, D), BFLOAT),
+            struct(BFLOAT, VOCAB_MP, D),
+            struct(BFLOAT, 512, D),
+            struct(BFLOAT, 512, D),
         ),
         scratch_shapes=[pltpu.VMEM((256, D), FLOAT)],
-        compiler_params=pltpu.CompilerParams(vmem_limit_bytes=32 * 1024 * 1024),
+        compiler_params=params(BIG),
     )(loss_rows, near_rows, local_targets, log_norm, logits, picked, table)
 
 
-def mlp_grad_kernel(added, which_ref, *refs):
-    lefts, rights, refs = refs[0:3], refs[3:6], refs[6:]
+def mlp_grad_kernel(which_ref, *refs):
+    out_ref = refs[-1]
+
+    def joined(first):
+        return jnp.concatenate([ref[...] for ref in refs[first:-1:10]], axis=0)
+
+    def both(first):
+        return jnp.concatenate([joined(first), joined(first + 5)], axis=0)
+
+    rights = both(3), both(3), both(4)
     for i in range(3):
-        total = contract_rows(lefts[i][...], rights[i][...]).reshape(8, 80, D)
-        if added:
-            total = total + refs[0][:, i].astype(FLOAT)
-        refs[-1][:, i] = total.astype(BFLOAT)
-
-
-def mlp_grads(which, lefts, rights, received=None):
-    added = received is not None
-    rows = lefts[0].shape[0]
-    out_spec = pl.BlockSpec((8, 3, 80, D), lambda i, half: (i, 0, 0, 0))
+        out_ref[:, i] = contract_rows(both(i), rights[i]).reshape(8, 80, D).astype(BFLOAT)
+
+
+def mlp_grads(which, kept, received):
+    def cols(width, place):
+        return pl.BlockSpec((TOK_DEV, width), place)
+
+    own = [cols(640, lambda i, half: (0, half[0] * 2 + i))] * 3 + [cols(D, lambda i, half: (0, 0))] * 2
+    far = [cols(640, lambda i, half, n=n: (0, 2 * n + i)) for n in range(3)] + [
+        cols(D, lambda i, half, n=n: (n, 0)) for n in (0, 1)
+    ]
+    args = []
+    for parts, other in zip(kept, received):
+        args += [*parts, *[other[0]] * 3, *[other[1]] * 2]
     return pl.pallas_call(
-        functools.partial(mlp_grad_kernel, added),
+        mlp_grad_kernel,
         grid_spec=pltpu.PrefetchScalarGridSpec(
             num_scalar_prefetch=1,
             grid=(2,),
-            in_specs=[pl.BlockSpec((rows, 640), lambda i, half: (0, half[0] * 2 + i))] * 3
-            + [pl.BlockSpec((rows, D), lambda i, half: (0, 0))] * 3
-            + [out_spec] * added,
-            out_specs=out_spec,
+            in_specs=(own + far) * RECUR,
+            out_specs=pl.BlockSpec((8, 3, 80, D), lambda i, half: (i, 0, 0, 0)),
         ),
         out_shape=struct(BFLOAT, 16, 3, 80, D),
         compiler_params=params(40),
-    )(which.reshape(1), *lefts, *rights, *([received] if added else []))
-
-
-def pack_grad_kernel(
-    starts_ref, normed_ref, dq_ref, dk_ref, dv_ref, att_ref, grad_ref, rows_ref, mine_ref, other_ref, buf
-):
-    buf[0:960, :] = contract_rows(normed_ref[...], dq_ref[...]).astype(BFLOAT)
-    buf[1600:2560, :] = contract_rows(att_ref[...], grad_ref[...]).astype(BFLOAT)
+    )(which.reshape(1), *args)
+
+
+def square_grad_kernel(*refs):
+    wq_ref, wo_ref = refs[-2:]
+    ins = refs[:-2]
+
+    def joined(first):
+        return jnp.concatenate([ref[...] for ref in ins[first::8]], axis=0)
+
+    def both(first):
+        return jnp.concatenate([joined(first), joined(first + 4)], axis=0)
+
+    wq_ref[...] = contract_rows(both(2), both(3)).astype(BFLOAT)
+    wo_ref[...] = contract_rows(both(0), both(1)).astype(BFLOAT)
+
+
+def square_grads(kept, received, queries):
+    full = whole(TOK_DEV, D)
+    far = [pl.BlockSpec((TOK_DEV, D), lambda i, n=n: (n, 0)) for n in (2, 3, 4)] + [full]
+    args = []
+    for parts, other, query in zip(kept, received, queries):
+        args += [*parts, *[other[1]] * 3, query]
+    return pl.pallas_call(
+        square_grad_kernel,
+        grid=(1,),
+        in_specs=([full] * 4 + far) * RECUR,
+        out_specs=[whole(D, D), whole(D, D)],
+        out_shape=(struct(BFLOAT, D, D), struct(BFLOAT, D, D)),
+        compiler_params=params(40),
+    )(*args)
+
+
+def pack_grad_kernel(starts_ref, *refs):
+    wq_ref, wo_ref, rows_ref = refs[:3]
+    ins = refs[3:-3]
+    left_ref, right_ref, buf = refs[-3:]
+    buf[0:960, :] = wq_ref[...]
+    buf[1600:2560, :] = wo_ref[...]
     buf[2560:2576, :] = rows_ref[...].astype(BFLOAT)
     buf[2576:2688, :] = jnp.zeros((112, D), BFLOAT)
+    normed = jnp.concatenate([ref[...] for ref in ins[0::4] + ins[1::4]], axis=0)
+    grads = jnp.concatenate([ref[...] for ref in ins[2::4] + ins[3::4]], axis=0)
     line = lax.broadcasted_iota(jnp.int32, (960, 320), 0)
     place = lax.broadcasted_iota(jnp.int32, (960, 320), 1)
-    for first, ref in ((960, dk_ref), (1280, dv_ref)):
-        full = contract_rows(normed_ref[...], ref[...]).astype(BFLOAT)
-        for i in range(3):
-            chosen = (line == 3 * place + i).astype(FLOAT).astype(BFLOAT)
-            buf[first : first + 320, 320 * i : 320 * i + 320] = contract_rows(chosen, full).astype(
-                BFLOAT
-            )
+    full = contract_rows(normed, grads).astype(BFLOAT)
+    for i in range(3):
+        chosen = (line == 3 * place + i).astype(FLOAT).astype(BFLOAT)
+        rows = contract_rows(chosen, full).astype(BFLOAT)
+        buf[960:1280, 320 * i : 320 * i + 320] = rows[:, 0:320]
+        buf[1280:1600, 320 * i : 320 * i + 320] = rows[:, 320:640]
     for i in range(4):
-        mine_ref[i] = buf[pl.ds(pl.multiple_of(starts_ref[i], 16), 352), :]
-        other_ref[i] = buf[pl.ds(pl.multiple_of(starts_ref[4 + i], 16), 352), :]
-
-
-def pack_grads(starts, *parts):
-    side = jax.ShapeDtypeStruct((4, 352, D), BFLOAT)
+        start = pl.multiple_of(starts_ref[i], 16)
+        left_ref[i] = buf[pl.ds(start, 352), 0:512]
+        right_ref[i] = buf[pl.ds(start, 352), 512:960]
+
+
+def pack_grads(starts, wq, wo, small, kept, received, pairs):
+    args = []
+    for (normed, pair), other, far in zip(kept, received, pairs):
+        args += [normed, other[1], pair, far]
+    specs = [
+        whole(TOK_DEV, D),
+        pl.BlockSpec((TOK_DEV, D), lambda i: (4, 0)),
+        whole(TOK_DEV, 640),
+        whole(TOK_DEV, 640),
+    ]
     return pl.pallas_call(
         pack_grad_kernel,
-        in_specs=[pl.BlockSpec(memory_space=pltpu.SMEM)]
-        + [pl.BlockSpec(memory_space=pltpu.VMEM)] * len(parts),
-        out_shape=(side, side),
+        grid=(1,),
+        in_specs=[pl.BlockSpec(memory_space=pltpu.SMEM), whole(D, D), whole(D, D), whole(16, D)]
+        + specs * RECUR,
+        out_specs=[whole(4, 352, 512), whole(4, 352, 448)],
+        out_shape=(struct(BFLOAT, 4, 352, 512), struct(BFLOAT, 4, 352, 448)),
         scratch_shapes=[pltpu.VMEM((PACK_PAD, D), BFLOAT)],
-        compiler_params=pltpu.CompilerParams(vmem_limit_bytes=40 * 1024 * 1024),
-    )(starts, *parts)
+        compiler_params=params(40),
+    )(starts, wq, wo, small, *args)
 
 
 def adam_update(master, first, second, grad, clip):
@@ -724,21 +846,16 @@
     return total
 
 
-def shards(
+def gradients(
+    dense,
     token_ids,
     targets,
     loss_rows,
     selections,
     boundary,
     pack_master,
-    pack_first,
-    pack_second,
     mlp_master,
-    mlp_first,
-    mlp_second,
     table_master,
-    table_first,
-    table_second,
 ):
     z = lax.axis_index("z")
     core = lax.axis_index("core")
@@ -756,11 +873,21 @@
     pack_block = lax.dynamic_update_slice(
         jnp.zeros((24 * D,), BFLOAT), pack_master.astype(BFLOAT), (pack_offset,)
     ).reshape(24, D)
-    pack_blocks = lax.all_gather(pack_block, ALL_AXES, axis=0, tiled=True)
-    mlp_own = mlp_master.astype(BFLOAT)
-    mlp_quad = jnp.concatenate([mlp_own] + [shift(mlp_own, "z", k) for k in (1, 2, 3)], axis=1)
-    mlp_blocks = lax.all_gather(mlp_quad.reshape(3 * 80, D), ("core", "y", "x"), axis=0, tiled=True)
-    table = lax.all_gather(own_table, DP_AXES, axis=0, tiled=True)
+    own = jnp.concatenate([pack_block, mlp_master.astype(BFLOAT).reshape(3 * UNITS, D)], axis=0)
+    ring = [own] + [shift(own, "z", k) for k in (1, 2, 3)]
+    pack_quad = []
+    for i in range(4):
+        part = ring[3][:24]
+        for k in (2, 1, 0):
+            part = jnp.where(z == (i + k) % 4, ring[k][:24], part)
+        pack_quad.append(part)
+    pack_quad = jnp.concatenate(pack_quad, axis=0)
+    mlp_quad = jnp.concatenate([part[24:].reshape(3, UNITS, D) for part in ring], axis=1)
+    near_axes = ("core", "y", "x")
+    pack_blocks = lax.all_gather(pack_quad, near_axes, axis=0, tiled=True)
+    pack_blocks = (
+        pack_blocks.reshape(2, DP, 4, 24, D).transpose(2, 0, 1, 3, 4).reshape(128 * 24, D)
+    )
 
     group_ids = token_ids[0]
     near_ids = reorder(group_ids.reshape(MP, TOK_DEV), near).reshape(-1)
@@ -775,36 +902,36 @@
     slots = mm(present.astype(BFLOAT), before)
     asked = present & (slots < CAP)
     over = jnp.max(jnp.where(present & (slots >= CAP), 1.0, 0.0))
-    over = sum_all(jnp.full((1, 128), over, FLOAT))[0, 0] > 0
     slot_table = jnp.where(asked, slots, 255.0).reshape(48, 128).astype(BFLOAT)
     token_slot = jnp.sum(mm(high_hot, slot_table) * low_hot.astype(FLOAT), axis=-1)
     token_place = jnp.where(
         inside & (token_slot < CAP), (high // 3) * CAP + token_slot.astype(jnp.int32), -1
     )
-    place_hot = (token_place[:, None] == jnp.arange(DP * CAP)[None, :]).astype(BFLOAT)
+    token_place = token_place[:, None]
     match = asked[:, None, :] & (slots[:, None, :] == jnp.arange(CAP, dtype=FLOAT)[None, :, None])
     request = (
         jnp.sum(jnp.where(match, jnp.arange(1, VOCAB_DEV + 1, dtype=FLOAT)[None, None, :], 0.0), axis=-1)
         - 1.0
     )
+    request = jnp.concatenate([request, jnp.full((DP, 8), over, FLOAT)], axis=1)
     request = lax.all_to_all(request, DP_AXES, 0, 0, tiled=True)
+    over = jnp.max(request[:, CAP:])
     owner_hot = (
-        request.reshape(-1)[:, None] == jnp.arange(VOCAB_DEV, dtype=FLOAT)[None, :]
+        request[:, :CAP].reshape(-1)[:, None] == jnp.arange(VOCAB_DEV, dtype=FLOAT)[None, :]
     ).astype(BFLOAT)
-    sent_rows = mm(owner_hot, own_table).astype(BFLOAT)
-    asked_rows = lax.all_to_all(sent_rows, DP_AXES, 0, 0, tiled=True)
-
-    def looked_sparse():
-        return mm(place_hot, asked_rows).astype(BFLOAT)
-
-    def looked_dense():
-        full = lax.all_gather(own_table, DP_AXES, axis=0, tiled=True)
-        rows = jnp.take(full, jnp.clip(local_ids, 0, VOCAB_MP - 1), axis=0)
-        return jnp.where(inside[:, None], rows, jnp.zeros_like(rows))
-
-    asked_rows, pack_blocks = tie(asked_rows, pack_blocks)
-    looked = lax.cond(over, looked_dense, looked_sparse)
-    hidden = scatter_group(looked.reshape(2, 4, TOK_DEV, D), FLOAT)
+    mlp_quad, owner_hot = tie(mlp_quad, owner_hot)
+    mlp_weights = lax.all_gather(mlp_quad.reshape(3 * 80, D), near_axes, axis=0, tiled=True)
+    mlp_weights = mlp_weights.reshape(32, 3, 80, D)
+    asked_rows = lax.all_to_all(mm(owner_hot, own_table).astype(BFLOAT), DP_AXES, 0, 0, tiled=True)
+    own_table, asked_rows = tie(own_table, asked_rows)
+    table = lax.all_gather(own_table, DP_AXES, axis=0, tiled=True)
+    if dense:
+        rows = jnp.take(table, jnp.clip(local_ids, 0, VOCAB_MP - 1), axis=0)
+        looked = jnp.where(inside[:, None], rows, jnp.zeros_like(rows))
+        looked = looked[:512], looked[512:]
+    else:
+        looked = spread(token_place, asked_rows)
+    hidden = scatter_group(*looked)
 
     pack_weights = join_pack(pack_blocks)
     w_query = pack_weights[:960]
@@ -813,8 +940,6 @@
     w_out = pack_weights[1600:2560]
     gains = jnp.concatenate([pack_weights[2560:2563].astype(FLOAT), jnp.zeros((5, D), FLOAT)])
     router = pack_weights[2563:2566].astype(FLOAT)
-    mlp_weights = mlp_blocks.reshape(32, 3, 80, D).transpose(1, 0, 2, 3).reshape(3, FF, D)
-
     half_dim = HEAD_DIM // 2
     freqs = ROPE_BASE ** (-jnp.arange(half_dim, dtype=FLOAT) / half_dim)
     first_row = data_index * ROWS + model_index * TOK_DEV
@@ -830,20 +955,23 @@
     prev_sel = prev_sel.reshape(RECUR, ROWS)
     start = lax.dynamic_index_in_dim(boundary, data_index, 0, False)
     prev_start = lax.dynamic_index_in_dim(boundary, prev_index, 0, False)
-    place = (model_index * TOK_DEV + jnp.arange(TOK_DEV, dtype=jnp.int32))[None, None, :]
-    key_place = near_rows[None, :, None]
-    own_seen = (
-        (key_place <= place)
-        & ((key_place < start) == (place < start))
-        & ((near_sel[:, :, None] > 0) | (key_place == place))
-    )
-    prev_seen = (
-        (data_index > 0) & (place < start) & (key_place >= prev_start) & (prev_sel[:, :, None] > 0)
-    )
-    biases = jnp.concatenate(
-        [prev_seen[:, :512], own_seen[:, :512], prev_seen[:, 512:], own_seen[:, 512:]], axis=1
-    )
-    biases = jnp.where(biases, 0.0, MASKED)
+    place = (model_index * TOK_DEV + jnp.arange(TOK_DEV, dtype=jnp.int32))[None, :]
+    key_place = near_rows[:, None]
+    biases = []
+    for step in range(RECUR):
+        own_seen = (
+            (key_place <= place)
+            & ((key_place < start) == (place < start))
+            & ((near_sel[step][:, None] > 0) | (key_place == place))
+        )
+        prev_seen = (
+            (data_index > 0)
+            & (place < start)
+            & (key_place >= prev_start)
+            & (prev_sel[step][:, None] > 0)
+        )
+        seen = [prev_seen[:512], own_seen[:512], prev_seen[512:], own_seen[512:]]
+        biases.append(jnp.where(jnp.concatenate(seen, axis=0), 0.0, MASKED))
 
     sel_cols = own_sel.astype(FLOAT)[:, :, None]
     saves = []
@@ -887,19 +1015,22 @@
     penalty_total = jnp.sum(jax.nn.softplus(logits_all) - own_sel.astype(FLOAT) * logits_all)
 
     normed_final = rms_scale(hidden, gains[2]).astype(BFLOAT)
-    final_rows = gather_group(normed_final).reshape(ROWS, D)
+    final_rows = gather_group(normed_final)
     row_targets = lax.dynamic_index_in_dim(targets, data_index, 0, keepdims=False)
     head_args = (loss_rows[0][:, None], near_rows[None, :])
     local_targets = (row_targets - model_index * VOCAB_MP)[:, None]
-    logits, picked, stats = head(*head_args, final_rows, local_targets, table)
-    stats = stats[:, :3].T
+    logits, picked, stats = head(*head_args, *final_rows, local_targets, table)
+    stats = jnp.concatenate([stats[:, :3].T, jnp.full((1, 256), over)])
 
     def join_stats(parts):
         top = parts[0][0]
         for part in parts[1:]:
             top = jnp.maximum(top, part[0])
         total = sum(part[1] * jnp.exp(part[0] - top) for part in parts)
-        return jnp.stack([top, total, sum(part[2] for part in parts)])
+        over = parts[0][3]
+        for part in parts[1:]:
+            over = jnp.maximum(over, part[3])
+        return jnp.stack([top, total, sum(part[2] for part in parts), over])
 
     stats = join_stats([stats, swap(stats)])
     stats = join_stats([stats] + [shift(stats, "z", k) for k in (1, 2, 3)])
@@ -910,15 +1041,15 @@
         jnp.sum(lax.dynamic_slice_in_dim(cross, model_index * per_device, per_device))
         + ROUTER_LOSS * penalty_total
     )
-    head_grad, scattered = head_back(
+    head_grad, *scattered = head_back(
         *head_args, local_targets, log_norm[:, None], logits, picked, table
     )
-    grad_final = scatter_group(scattered.reshape(2, 4, TOK_DEV, D), FLOAT)
+    grad_final = scatter_group(*scattered)
     grad_hidden, grad_gain_final = rms_back(hidden, gains[2], grad_final)
-    head_grad = lax.psum_scatter(head_grad, DP_AXES, scatter_dimension=0, tiled=True)
-
-    kept = []
-    mlp_parts = []
+    if not dense:
+        head_grad = lax.psum_scatter(head_grad, DP_AXES, scatter_dimension=0, tiled=True)
+
+    mlp_kept, far_kept, square_kept, far_queries, pack_kept, far_pairs = [], [], [], [], [], []
     router_rows = [None] * RECUR
     gain_one = jnp.zeros((1, D), FLOAT)
     gain_two = jnp.zeros((1, D), FLOAT)
@@ -954,30 +1085,33 @@
         )
         gain_two = gain_two + small[0:1]
         router_rows[step] = small[1:2]
-        mlp_parts.append((grad_gate, grad_up, inner, mlp_input, mlp_input, grad_rows))
-        if step == 0:
-            mlp_kept = [jnp.concatenate(parts, axis=0) for parts in zip(*mlp_parts)]
-            far = mlp_grads(1 - core, mlp_kept[:3], mlp_kept[3:])
-            far, grad_attended, head_grad = tie(by_rows(far), grad_attended, head_grad)
-            far = by_rows(swap(far))
+        mlp_kept.append((grad_gate, grad_up, inner, mlp_input, grad_rows))
+
+        def far_half(value):
+            return lax.dynamic_slice_in_dim(value, (1 - core) * (FF // 2), FF // 2, 1)
+
+        sent = jnp.concatenate([far_half(grad_gate), far_half(grad_up), far_half(inner)], axis=1)
+        rows = jnp.concatenate([mlp_input, grad_rows, attended, grad_attn, normed], axis=0)
+        far_kept.append((swap(sent), by_rows(swap(by_rows(rows)))))
         grad_query, *grad_sides = attend_back(
             queries, pairs, biases[step], log_total, attended, grad_attended, *turns
         )
+        square_kept.append((attended, grad_attn, normed, grad_query))
+        far_queries.append(by_rows(swap(grad_query)))
+        grad_own = group_scatter(*grad_sides)
         if step == 0:
-            far, *grad_sides = tie(far, *grad_sides)
-            mlp_half = mlp_grads(core, mlp_kept[:3], mlp_kept[3:], far)
+            mlp_half = mlp_grads(core.astype(jnp.int32), mlp_kept, far_kept)
             mlp_sum = lax.psum_scatter(
                 mlp_half.reshape(16 * 240, D), DP_AXES, scatter_dimension=0, tiled=True
             )
-        grad_own = group_scatter(*grad_sides)
+            squares = square_grads(square_kept, far_kept, far_queries)
+            grad_own, mlp_half, *squares = tie(grad_own, mlp_half, *squares)
         grad_pair, grad_hidden, small = enter_back(
             grad_in, grad_query, grad_own, hidden_in, gains, *projections
         )
         gain_one = gain_one + small[0:1]
-        kept.append((normed, grad_query, grad_pair, attended, grad_attn))
-    normed_all, grad_query_all, grad_pair_all, attended_all, grad_attn_all = [
-        jnp.concatenate(parts, axis=0) for parts in zip(*kept)
-    ]
+        pack_kept.append((normed, grad_pair))
+        far_pairs.append(swap(grad_pair))
 
     def aligned_row(which):
         return (pack_row(which) // 16) * 16
@@ -991,20 +1125,9 @@
             jnp.zeros((10, D), FLOAT),
         ]
     )
-    starts = jnp.stack(
-        [aligned_row(DP * (2 * i + c)) for c in (core, 1 - core) for i in range(4)]
-    ).astype(jnp.int32)
-    mine, other = pack_grads(
-        starts,
-        normed_all,
-        grad_query_all,
-        grad_pair_all[:, :320],
-        grad_pair_all[:, 320:],
-        attended_all,
-        grad_attn_all,
-        small,
-    )
-    half = (mine.astype(FLOAT) + swap(other).astype(FLOAT)).astype(BFLOAT)
+    small = small + swap(small)
+    starts = jnp.stack([aligned_row(DP * (2 * i + core)) for i in range(4)]).astype(jnp.int32)
+    left, right = pack_grads(starts, *squares, small, pack_kept, far_kept, far_pairs)
 
     def y_windows(value):
         return jnp.stack([value[..., 80 * i : 80 * i + 112, :] for i in range(4)])
@@ -1012,35 +1135,68 @@
     def x_windows(value):
         return jnp.stack([value[..., i : i + 48, :] for i in (0, 16, 40, 56)])
 
-    part = stage(half, "z", z).astype(BFLOAT)
-    part = stage(y_windows(part), "y", y).astype(BFLOAT)
+    left = stage(y_windows(left), "y", y).astype(BFLOAT)
+    right = stage(right, "z", z).astype(BFLOAT)
+    left = stage(left, "z", z).astype(BFLOAT)
+    right = stage(y_windows(right), "y", y).astype(BFLOAT)
+    part = jnp.concatenate([left, right], axis=-1)
+    part, mlp_sum = tie(part, mlp_sum)
     part = stage(x_windows(part), "x", x).reshape(-1)
     begin = aligned_row(DP * model_index) + 80 * y + (20 * x) // 8 * 8
     pack_grad = lax.dynamic_slice(part, (PACK_DEV * device - D * begin,), (PACK_DEV,))
 
-    grad_embed = gather_group(grad_hidden.astype(BFLOAT)).reshape(ROWS, D)
-
-    unique = contract_rows(place_hot, grad_embed).astype(BFLOAT)
-    unique = lax.all_to_all(unique, DP_AXES, 0, 0, tiled=True)
-
-    sparse = contract_rows(owner_hot, unique)
-
     mlp_sum = mlp_sum.reshape(3, 4, UNITS, D).transpose(1, 0, 2, 3)
     mlp_grad = stage_near(mlp_sum, "z")
 
-    def embed_dense():
-        kept_rows = grad_embed.astype(FLOAT) * inside.astype(FLOAT)[:, None]
+    grad_embed = gather_group(grad_hidden.astype(BFLOAT))
+    if dense:
+        kept_rows = jnp.concatenate(grad_embed).astype(FLOAT) * inside.astype(FLOAT)[:, None]
         sums = jax.ops.segment_sum(
             kept_rows, jnp.clip(local_ids, 0, VOCAB_MP - 1), num_segments=VOCAB_MP
         )
-        return lax.psum_scatter(
-            sums.astype(BFLOAT), DP_AXES, scatter_dimension=0, tiled=True
+        table_grad = lax.psum_scatter(
+            (head_grad.astype(FLOAT) + sums).astype(BFLOAT),
+            DP_AXES,
+            scatter_dimension=0,
+            tiled=True,
         ).astype(FLOAT)
-
-    sparse, mlp_grad, pack_grad = tie(sparse, mlp_grad, pack_grad)
-    table_grad = head_grad.astype(FLOAT) + lax.cond(over, embed_dense, lambda: sparse)
-    table_grad = by_cols(table_grad)
-
+    else:
+        unique = collect(token_place, *grad_embed)
+        unique = lax.all_to_all(unique, DP_AXES, 0, 0, tiled=True)
+        table_grad = head_grad.astype(FLOAT) + contract_rows(owner_hot, unique)
+    return pack_grad, mlp_grad, by_cols(table_grad), loss_part, stats[3, 0]
+
+
+def shards(
+    token_ids,
+    targets,
+    loss_rows,
+    selections,
+    boundary,
+    pack_master,
+    pack_first,
+    pack_second,
+    mlp_master,
+    mlp_first,
+    mlp_second,
+    table_master,
+    table_first,
+    table_second,
+):
+    args = (
+        token_ids,
+        targets,
+        loss_rows,
+        selections,
+        boundary,
+        pack_master,
+        mlp_master,
+        table_master,
+    )
+    *found, over = gradients(False, *args)
+    pack_grad, mlp_grad, table_grad, loss_part = lax.cond(
+        over > 0, lambda: gradients(True, *args)[:4], lambda: tuple(found)
+    )
     squares = (
         jnp.sum(pack_grad * pack_grad)
         + jnp.sum(mlp_grad * mlp_grad)

time: 853 us -> 885 us (1.038)
  blocking collectives: 0 us -> 26.7 us
  Pallas kernels: 186 us -> 211 us
  starting transfers between devices: 204 us -> 182 us
  other arithmetic: 58.8 us -> 71.9 us
  waiting for transfers between devices: 198 us -> 186 us
    all_to_all x0 -> x2, blocking collectives: none -> 26.7 us  [the longest x1 13.7 us: gradients(): lax.all_to_all(mm(owner_hot, own_table).astype(BFLOAT), DP_AXES, 0, 0, ti...]
    all_gather x3, waiting for transfers between devices: 23.4 us -> 0.01 us  [the longest x1 0.01 us: gradients(): pack_blocks = lax.all_gather(pack_quad, near_axes, axis=0, tiled=True)]
    another operation x5 -> x26, local copies, waits for them, and re-layouts: 5.61 us -> 26.1 us  [the longest x7 13.8 us: by_rows(): return with_layout_constraint(value, Layout(tuple(range(value.ndim))))]
    unnamed x6, waiting for transfers between devices: 1.11 us -> 18.8 us
    ppermute x12, waiting for transfers between devices: 42.2 us -> 25.4 us  [group_scatter(): total = total + lax.ppermute(prev[k], ('z',) + DP_AXES, pairs).astype(FLOAT)]
    ppermute x12, waiting for transfers between devices: 12.5 us -> 27.8 us  [group_gather(): prev.append(lax.ppermute(pair, ('z',) + DP_AXES, pairs))]
    all_to_all x3 -> x1, starting transfers between devices: 20.6 us -> 5.43 us  [gradients(): unique = lax.all_to_all(unique, DP_AXES, 0, 0, tiled=True)]
    ppermute x48 -> x45, starting transfers between devices: 74 us -> 60.5 us  [shift(): return lax.ppermute(value, axis, [(i, (i + steps) % 4) for i in range(4)])]
  transfers between devices with their start and end apart: 119 -> 124, of which waited for: 53 -> 44; matrix products, arithmetic and copies ran while one was open for 15% -> 14% of each run, Pallas kernels for 18% -> 13%
where the time goes in v3:
time: 885 us; the launch traced here: 868 us
  Pallas kernels  211 us (24%)
  waiting for transfers between devices  186 us (21%)
  starting transfers between devices  182 us (21%)
  local copies, waits for them, and re-layouts  157 us (18%)
  other arithmetic  71.9 us (8%)
  blocking collectives  26.7 us (3%)
  between operations  22.7 us (3%)
    ppermute x45, waiting for transfers between devices, shift(): return lax.ppermute(value, axis, [(i, (i + steps) % 4) for i in range(4)])  95.2 us
    unnamed x443, local copies, waits for them, and re-layouts  73.5 us
    ppermute x45, starting transfers between devices, shift(): return lax.ppermute(value, axis, [(i, (i + steps) % 4) for i in range(4)])  60.5 us
    pallas_call x3, Pallas kernels, block_back(): pl.pallas_call(block_back_kernel, grid=(FF_STEPS,), in_specs=[full, whole...  39.4 us
    pallas_call x3, Pallas kernels, block(): pl.pallas_call(functools.partial(block_kernel, more), grid=(FF_STEPS,), i...  39 us
    ppermute x31, starting transfers between devices, swap(): return lax.ppermute(value, 'core', [(0, 1), (1, 0)])  32.5 us
    pallas_call x3, Pallas kernels, attend_back(): pl.pallas_call(attend_back_kernel, out_shape=(struct(BFLOAT, TOK_DEV, D),...  31.4 us
    ppermute x12, starting transfers between devices, group_gather(): prev.append(lax.ppermute(pair, ('z',) + DP_AXES, pairs))  29.8 us
  transfers between devices with their start and end apart: 124, of which 44 were waited for; matrix products, arithmetic and copies ran while one was open for 14% of the time, Pallas kernels for 13%

profile of v3, /device:TPU:1, one launch (start us, length us, event | category | flops | bytes accessed | tf_op | source)
XLA Modules:
  0.0 868.0 jit_solution(8637363501161061476)
XLA Ops:
  18.8 4.7 collective-permute-done.109
  26.8 13.0 %all_to_all.46 = f32[16,1,32]{2,1,0:T(1,128)S(1)} all-to-all(f32[16,1,32]{2,1,0:T(1,128)S(1)} %bitcast.621), channel_id=1, replica_groups=mesh['z'=4,'core'=2,'y'=4,'x'=4] {'y','x'}, dimensions={0} | all-to-all | bytes 4096 | tf_op jit(solution)/shard_map/all_to_all | solution.py:917
  43.3 13.7 %all_to_all.47 = bf16[16,24,960]{2,1,0:T(8,128)(2,1)S(1)} all-to-all(bf16[16,24,960]{2,1,0:T(8,128)(2,1)S(1)} %bitcast.594), channel_id=1, replica_groups=mesh['z'=4,'core'=2,'y'=4,'x'=4] {'y','x'}, dimensions={0} | all-to-all | bytes 1474560 | tf_op jit(solution)/shard_map/all_to_all | solution.py:925
  85.4 7.0 collective-permute-done.113
  96.9 10.4 %shard_map.222 = bf16[2688,960]{1,0:T(8,128)(2,1)} custom-call(bf16[3072,960]{1,0:T(8,128)(2,1)S(1)} %bitcast.575), custom_call_target="tpu_custom_call" | custom-call | tf_op jit(solution)/shard_map/pallas_call | solution.py:824
  117.9 4.9 collective-permute-start.119
  131.4 4.5 collective-permute-start.117
  139.0 6.0 collective-permute-done.117
  145.0 6.8 collective-permute-done.118
  155.0 8.8 %shard_map.224 = (bf16[128,960]{1,0:T(8,128)(2,1)S(1)}, f32[8,384]{1,0:T(8,128)S(1)}) custom-call(bf16[960,128]{1,0:T(8,128)(2,1)S(1)} %copy-done.278, bf16[512,640]{1,0:T(8,128)(2,1)S(1)} %constant_dynamic-update-slice_fusion.43.kv0, bf16[512,640]{1,0:T(8,128)(2,1)S(1)} %constant_dynamic-update-slice_fusion.47.kv1, ...), custom_call_target="tpu_custom_call" | custom-call | flops 12000000000 | bytes 5000000 | tf_op jit(solution)/shard_map/pallas_call | solution.py:230
  167.8 13.7 %shard_map.225 = (f32[128,960]{1,0:T(8,128)}, bf16[128,960]{1,0:T(8,128)(2,1)}, f32[128,2560]{1,0:T(8,128)}, f32[128,2560]{1,0:T(8,128)}, bf16[128,2560]{1,0:T(8...) custom-call(bf16[128,960]{1,0:T(8,128)(2,1)} %copy-done.46, ...), custom_call_target="tpu_custom_call" | custom-call | flops 4000000000 | bytes 20000000 | tf_op jit(solution)/shard_map/pallas_call | solution.py:406
  181.5 4.6 collective-permute-start.128
  194.6 5.6 collective-permute-start.126
  203.0 5.1 collective-permute-done.126
  208.2 7.0 collective-permute-done.127
  218.8 8.8 %shard_map.226 = (bf16[128,960]{1,0:T(8,128)(2,1)S(1)}, f32[8,384]{1,0:T(8,128)S(1)}) custom-call(bf16[960,128]{1,0:T(8,128)(2,1)S(1)} %copy-done.285, bf16[512,640]{1,0:T(8,128)(2,1)S(1)} %constant_dynamic-update-slice_fusion.51.kv0, bf16[512,640]{1,0:T(8,128)(2,1)S(1)} %constant_dynamic-update-slice_fusion.55.kv1, ...), custom_call_target="tpu_custom_call" | custom-call | flops 12000000000 | bytes 5000000 | tf_op jit(solution)/shard_map/pallas_call | solution.py:230
  228.4 13.2 %shard_map.227 = (f32[128,960]{1,0:T(8,128)}, bf16[128,960]{1,0:T(8,128)(2,1)}, f32[128,2560]{1,0:T(8,128)}, f32[128,2560]{1,0:T(8,128)}, bf16[128,2560]{1,0:T(8...) custom-call(bf16[128,960]{1,0:T(8,128)(2,1)} %copy-done.48, ...), custom_call_target="tpu_custom_call" | custom-call | flops 4000000000 | bytes 20000000 | tf_op jit(solution)/shard_map/pallas_call | solution.py:406
  241.6 5.4 collective-permute-start.137
  255.6 6.6 collective-permute-start.135
  272.5 8.8 %shard_map.228 = (bf16[128,960]{1,0:T(8,128)(2,1)S(1)}, f32[8,384]{1,0:T(8,128)S(1)}) custom-call(bf16[960,128]{1,0:T(8,128)(2,1)S(1)} %copy-done.288, bf16[512,640]{1,0:T(8,128)(2,1)S(1)} %constant_dynamic-update-slice_fusion.59.kv0, bf16[512,640]{1,0:T(8,128)(2,1)S(1)} %constant_dynamic-update-slice_fusion.63.kv1, ...), custom_call_target="tpu_custom_call" | custom-call | flops 12000000000 | bytes 5000000 | tf_op jit(solution)/shard_map/pallas_call | solution.py:230
  282.0 12.1 %shard_map.229 = (f32[128,960]{1,0:T(8,128)}, bf16[128,960]{1,0:T(8,128)(2,1)}, f32[128,2560]{1,0:T(8,128)}, f32[128,2560]{1,0:T(8,128)}, bf16[128,2560]{1,0:T(8...) custom-call(bf16[128,960]{1,0:T(8,128)(2,1)} %copy-done.51, ...), custom_call_target="tpu_custom_call" | custom-call | flops 4000000000 | bytes 20000000 | tf_op jit(solution)/shard_map/pallas_call | solution.py:406
  299.5 5.2 collective-permute-done.142
  307.6 6.6 collective-permute-done.144
  321.8 15.1 %shard_map.230 = (f32[256,6144]{1,0:T(8,128)}, bf16[256,960]{1,0:T(8,128)(2,1)}, f32[256,128]{1,0:T(8,128)}) custom-call(s32[256,1]{1,0:T(8,128)} %copy.339.rows_ref, s32[1,1024]{1,0:T(1,128)} %bitcast.618, bf16[512,960]{1,0:T(8,128)(2,1)} %copy-done.298, bf16[512,960]{1,0:T(8,128)(2,1)} %copy.338.far_ref, s32[256,1]{1,0:T(8,128)} %copy.340.target_ref, ...), custom_call_target="tpu_custom_call" | custom-call | tf_op jit(solution)/shard_map/pallas_call | solution.py:604
  344.6 6.3 collective-permute-done.147
  352.1 20.8 %shard_map.231 = (bf16[6144,960]{1,0:T(8,128)(2,1)}, bf16[512,960]{1,0:T(8,128)(2,1)}, bf16[512,960]{1,0:T(8,128)(2,1)}) custom-call(s32[256,1]{1,0:T(8,128)} %copy.339.rows_ref, s32[1,1024]{1,0:T(1,128)} %bitcast.619, s32[256,1]{1,0:T(8,128)} %copy.340.target_ref, f32[256,1]{1,0:T(8,128)} %fusion.104.norm_ref, f32[256,6144]{1,0:T(8,128)} %get-tuple-element.558.logit_ref, ...), custom_call_target="tpu_custom_call" | custom-call | tf_op jit(solution)/shard_map/pallas_call | solution.py:657
  386.8 5.2 collective-permute-done.151
  392.0 6.2 collective-permute-done.152
  400.1 13.1 %shard_map.232 = (bf16[128,960]{1,0:T(8,128)(2,1)}, bf16[128,2560]{1,0:T(8,128)(2,1)}, bf16[128,2560]{1,0:T(8,128)(2,1)}, f32[128,960]{1,0:T(8,128)}, bf16[128,9...) custom-call(f32[128,960]{1,0:T(8,128)} %multiply_subtract_fusion.2.new_ref, f32[128,1]{1,0:T(8,128)} %copy.336.sel_ref, ...), custom_call_target="tpu_custom_call" | custom-call | flops 4000000000 | bytes 20000000 | tf_op jit(solution)/shard_map/pallas_call | solution.py:505
  414.3 10.3 %shard_map.233 = (bf16[128,960]{1,0:T(8,128)(2,1)S(1)}, bf16[512,640]{1,0:T(8,128)(2,1)S(1)}, bf16[512,640]{1,0:T(8,128)(2,1)S(1)}, bf16[512,640]{1,0:T(8,128)(2,1)S(1)}, bf16[512,640]{1,0:T(8,128)(2,1)S(1)}) custom-call(bf16[960,128]{1,0:T(8,128)(2,1)S(1)} %copy-done.288, bf16[512,640]{1,0:T(8,128)(2,1)S(1)} %copy-done.233, ...), custom_call_target="tpu_custom_call" | custom-call | flops 20000000000 | bytes 9000000 | tf_op jit(solution)/shard_map/pallas_call | solution.py:275
  447.7 5.5 collective-permute-done.161
  461.4 13.4 %shard_map.235 = (bf16[128,960]{1,0:T(8,128)(2,1)}, bf16[128,2560]{1,0:T(8,128)(2,1)}, bf16[128,2560]{1,0:T(8,128)(2,1)}, f32[128,960]{1,0:T(8,128)}, bf16[128,9...) custom-call(f32[128,960]{1,0:T(8,128)} %copy-done.205, f32[128,1]{1,0:T(8,128)} %copy.335.sel_ref, ...), custom_call_target="tpu_custom_call" | custom-call | flops 4000000000 | bytes 20000000 | tf_op jit(solution)/shard_map/pallas_call | solution.py:505
  477.9 10.3 %shard_map.236 = (bf16[128,960]{1,0:T(8,128)(2,1)S(1)}, bf16[512,640]{1,0:T(8,128)(2,1)S(1)}, bf16[512,640]{1,0:T(8,128)(2,1)S(1)}, bf16[512,640]{1,0:T(8,128)(2,1)S(1)}, bf16[512,640]{1,0:T(8,128)(2,1)S(1)}) custom-call(bf16[960,128]{1,0:T(8,128)(2,1)S(1)} %copy-done.286, bf16[512,640]{1,0:T(8,128)(2,1)S(1)} %copy-done.231, ...), custom_call_target="tpu_custom_call" | custom-call | flops 20000000000 | bytes 9000000 | tf_op jit(solution)/shard_map/pallas_call | solution.py:275
  524.6 12.8 %shard_map.238 = (bf16[128,960]{1,0:T(8,128)(2,1)}, bf16[128,2560]{1,0:T(8,128)(2,1)}, bf16[128,2560]{1,0:T(8,128)(2,1)}, f32[128,960]{1,0:T(8,128)}, bf16[128,9...) custom-call(f32[128,960]{1,0:T(8,128)} %copy-done.203, f32[128,1]{1,0:T(8,128)} %copy.334.sel_ref, ...), custom_call_target="tpu_custom_call" | custom-call | flops 4000000000 | bytes 20000000 | tf_op jit(solution)/shard_map/pallas_call | solution.py:505
  571.6 10.0 %shard_map.240 = bf16[16,3,80,960]{3,2,1,0:T(8,128)(2,1)} custom-call(s32[1]{0:T(128)} %bitcast.167.which_ref, bf16[128,2560]{1,0:T(8,128)(2,1)S(1)} %copy-done.103, bf16[128,2560]{1,0:T(8,128)(2,1)S(1)} %copy-done.105, bf16[128,2560]{1,0:T(8,128)(2,1)S(1)} %copy-done.101, bf16[128,960]{1,0:T(8,128)(2,1)S(1)} %copy-done.157, ...), custom_call_target="tpu_custom_call" | custom-call | tf_op jit(solution)/shard_map/pallas_call | solution.py:705
  591.4 10.9 %shard_map.239 = (bf16[128,960]{1,0:T(8,128)(2,1)S(1)}, bf16[512,640]{1,0:T(8,128)(2,1)S(1)}, bf16[512,640]{1,0:T(8,128)(2,1)S(1)}, bf16[512,640]{1,0:T(8,128)(2,1)S(1)}, bf16[512,640]{1,0:T(8,128)(2,1)}) custom-call(bf16[960,128]{1,0:T(8,128)(2,1)S(1)} %copy-done.279, bf16[512,640]{1,0:T(8,128)(2,1)S(1)} %copy-done.229, bf16[512,640]{1,0:T(8,128)(2,1)S(1)} %copy-done.217, ...), custom_call_target="tpu_custom_call" | custom-call | flops 20000000000 | bytes 9000000 | tf_op jit(solution)/shard_map/pallas_call | solution.py:275
  625.8 5.1 collective-permute-done.173
  636.7 14.7 %collective-permute-done.179 = bf16[128,640]{1,0:T(8,128)(2,1)S(1)} collective-permute-done((bf16[128,640]{1,0:T(8,128)(2,1)S(1)}, bf16[128,640]{1,0:T(8,128)(2,1)S(1)}, u32[]{:S(2)}, u32[]{:S(2)}) %collective-permute-start.179) | collective-permute-done | bytes 163872 | tf_op jit(solution)/shard_map/ppermute | solution.py:147
  681.5 4.9 shard_map.243
  701.3 5.5 collective-permute-done.201
  712.5 4.4 collective-permute-done.194
  718.6 16.5 %collective-permute-done.195 = bf16[4,112,512]{2,1,0:T(8,128)(2,1)} collective-permute-done((bf16[4,112,512]{2,1,0:T(8,128)(2,1)}, bf16[4,112,512]{2,1,0:T(8,128)(2,1)}, u32[]{:S(2)}, u32[]{:S(2)}) %collective-permute-start.195) | collective-permute-done | bytes 458784 | tf_op jit(solution)/shard_map/ppermute | solution.py:49
  738.1 6.2 collective-permute-done.204
  752.0 5.4 all-to-all-start.3
  766.8 6.6 collective-permute-done.206
  781.3 18.4 %reduce-scatter.15.cloned.1.call-done = bf16[384,960]{1,0:T(8,128)(2,1)} async-done(((bf16[6144,960]{1,0:T(8,128)(2,1)}), bf16[384,960]{1,0:T(8,128)(2,1)}) %reduce-scatter.15.cloned.1.call-update) | async-done | bytes 737296
  804.6 26.5 %conditional.1 = (f32[19245]{0:T(1024)S(1)}, f32[3,20,960]{2,1,0:T(8,128)}, f32[384,960]{0,1:T(8,128)S(1)}, f32[]{:T(128)}, f32[]{:T(128)}, /*index=5*/f32[]{:T(128)}) conditional(s32[]{:T(128)} %bitcast.152, (s32[]{:T(128)}, bf16[4,48,960]{2,1,0:T(8,128)(2,1)}, f32[48,960]{1,0:T(8,128)}, f32[48,960]{1,0:T(8,128)}, f32[48,960]{1,0:T(8,128)}, ...), branch_computations={%region_12.17_spmd, %region_17.34_spmd} | conditional | flops 120092434432 | bytes 1076539904 | solution.py:1197
  853.1 5.1 multiply_subtract_fusion.1
  (914 shorter events, 422.5 us)
Async XLA Ops:
  7.2 86.1 %all-gather.13.cloned.1.call-start = ((), (), s32[]{:S(2)}) async-start(), calls=%async_computation.13 | async-start | bytes 6488064 | tf_op jit(solution)/shard_map/all_gather | solution.py:887
  24.3 143.5 %all-gather.15.cloned.1.call-start = ((), (), s32[]{:S(2)}) async-start(), calls=%async_computation.14 | async-start | bytes 16220160 | tf_op jit(solution)/shard_map/all_gather | solution.py:923
  41.4 280.4 %all-gather.17.cloned.1.call-start = ((), (), s32[]{:S(2)}) async-start(), calls=%async_computation.15 | async-start | bytes 13369344 | tf_op jit(solution)/shard_map/all_gather | solution.py:927
  57.1 700.4 %reduce-scatter.13.cloned.1.call-start = ((), (), s32[]{:S(2)}) async-start(), calls=%async_computation.16 | async-start | bytes 8355840 | tf_op jit(solution)/shard_map/reduce_scatter | solution.py:1104
  77.9 14.5 %collective-permute-start.113 = (bf16[128,960]{1,0:T(8,128)(2,1)S(1)}, bf16[128,960]{1,0:T(8,128)(2,1)S(1)}, u32[]{:S(2)}, u32[]{:S(2)}) collective-permute-start(bf16[128,960]{1,0:T(8,128)(2,1)S(1)} %get-tuple-element.1097), channel_id=1, source_target_pairs={{0,64},{32,96},{64,0},{96,32},{1,65},{33,97},{65,1},{97,33},{2,66}... | collective-permute-start | bytes 737288 | tf_op jit(solution)/shard_map/ppermute | solution.py:49
  131.4 13.6 %collective-permute-start.117 = (bf16[128,640]{1,0:T(8,128)(2,1)}, bf16[128,640]{1,0:T(8,128)(2,1)S(1)}, u32[]{:S(2)}, u32[]{:S(2)}) collective-permute-start(bf16[128,640]{1,0:T(8,128)(2,1)} %get-tuple-element.543), channel_id=1, source_target_pairs={{64,1},{65,2},{66,3},{67,4},{68,5},{69,6},{70,7},{71,8},{72,9},{73... | collective-permute-start | bytes 491528 | tf_op jit(solution)/shard_map/ppermute | solution.py:129
  135.9 15.8 %collective-permute-start.118 = (bf16[128,640]{1,0:T(8,128)(2,1)}, bf16[128,640]{1,0:T(8,128)(2,1)S(1)}, u32[]{:S(2)}, u32[]{:S(2)}) collective-permute-start(bf16[128,640]{1,0:T(8,128)(2,1)} %get-tuple-element.543), channel_id=1, source_target_pairs={{96,1},{97,2},{98,3},{99,4},{100,5},{101,6},{102,7},{103,8},{104,9... | collective-permute-start | bytes 491528 | tf_op jit(solution)/shard_map/ppermute | solution.py:129
  137.3 16.4 %collective-permute-start.123 = (bf16[512,640]{1,0:T(8,128)(2,1)S(1)}, bf16[512,640]{1,0:T(8,128)(2,1)S(1)}, u32[]{:S(2)}, u32[]{:S(2)}) collective-permute-start(bf16[512,640]{1,0:T(8,128)(2,1)S(1)} %constant_dynamic-update-slice_fusion.47.kv1), channel_id=1, source_target_pairs={{0,16},{16,0},{1,17},{17,1},{2,18},{18,2},{3,19},{19,3},{4,20},{20... | collective-permute-start | bytes 1966088 | tf_op jit(solution)/shard_map/ppermute | solution.py:53
  194.6 13.6 %collective-permute-start.126 = (bf16[128,640]{1,0:T(8,128)(2,1)}, bf16[128,640]{1,0:T(8,128)(2,1)S(1)}, u32[]{:S(2)}, u32[]{:S(2)}) collective-permute-start(bf16[128,640]{1,0:T(8,128)(2,1)} %get-tuple-element.547), channel_id=1, source_target_pairs={{64,1},{65,2},{66,3},{67,4},{68,5},{69,6},{70,7},{71,8},{72,9},{73... | collective-permute-start | bytes 491528 | tf_op jit(solution)/shard_map/ppermute | solution.py:129
  200.3 14.9 %collective-permute-start.127 = (bf16[128,640]{1,0:T(8,128)(2,1)}, bf16[128,640]{1,0:T(8,128)(2,1)S(1)}, u32[]{:S(2)}, u32[]{:S(2)}) collective-permute-start(bf16[128,640]{1,0:T(8,128)(2,1)} %get-tuple-element.547), channel_id=1, source_target_pairs={{96,1},{97,2},{98,3},{99,4},{100,5},{101,6},{102,7},{103,8},{104,9... | collective-permute-start | bytes 491528 | tf_op jit(solution)/shard_map/ppermute | solution.py:129
  201.7 15.6 %collective-permute-start.132 = (bf16[512,640]{1,0:T(8,128)(2,1)S(1)}, bf16[512,640]{1,0:T(8,128)(2,1)S(1)}, u32[]{:S(2)}, u32[]{:S(2)}) collective-permute-start(bf16[512,640]{1,0:T(8,128)(2,1)S(1)} %constant_dynamic-update-slice_fusion.55.kv1), channel_id=1, source_target_pairs={{0,16},{16,0},{1,17},{17,1},{2,18},{18,2},{3,19},{19,3},{4,20},{20... | collective-permute-start | bytes 1966088 | tf_op jit(solution)/shard_map/ppermute | solution.py:53
  241.6 14.0 %collective-permute-start.137 = (bf16[128,640]{1,0:T(8,128)(2,1)}, bf16[128,640]{1,0:T(8,128)(2,1)S(1)}, u32[]{:S(2)}, u32[]{:S(2)}) collective-permute-start(bf16[128,640]{1,0:T(8,128)(2,1)} %get-tuple-element.551), channel_id=1, source_target_pairs={{0,96},{1,97},{2,98},{3,99},{4,100},{5,101},{6,102},{7,103},{8,104... | collective-permute-start | bytes 491528 | tf_op jit(solution)/shard_map/ppermute | solution.py:122
  247.7 14.6 %collective-permute-start.138 = (bf16[128,640]{1,0:T(8,128)(2,1)}, bf16[128,640]{1,0:T(8,128)(2,1)S(1)}, u32[]{:S(2)}, u32[]{:S(2)}) collective-permute-start(bf16[128,640]{1,0:T(8,128)(2,1)} %get-tuple-element.551), channel_id=1, source_target_pairs={{0,64},{32,96},{1,65},{33,97},{2,66},{34,98},{3,67},{35,99},{4,68}... | collective-permute-start | bytes 491528 | tf_op jit(solution)/shard_map/ppermute | solution.py:122
  250.0 13.7 %collective-permute-start.139 = (bf16[128,640]{1,0:T(8,128)(2,1)}, bf16[128,640]{1,0:T(8,128)(2,1)S(1)}, u32[]{:S(2)}, u32[]{:S(2)}) collective-permute-start(bf16[128,640]{1,0:T(8,128)(2,1)} %get-tuple-element.551), channel_id=1, source_target_pairs={{0,32},{32,64},{64,96},{1,33},{33,65},{65,97},{2,34},{34,66},{66,9... | collective-permute-start | bytes 491528 | tf_op jit(solution)/shard_map/ppermute | solution.py:122
  299.3 14.9 %collective-permute-start.144 = (bf16[128,960]{1,0:T(8,128)(2,1)S(1)}, bf16[128,960]{1,0:T(8,128)(2,1)S(1)}, u32[]{:S(2)}, u32[]{:S(2)}) collective-permute-start(bf16[128,960]{1,0:T(8,128)(2,1)S(1)} %multiply_convert_fusion.1), channel_id=1, source_target_pairs={{0,32},{32,64},{64,96},{96,0},{1,33},{33,65},{65,97},{97,1},{2,34}... | collective-permute-start | bytes 737288 | tf_op jit(solution)/shard_map/ppermute | solution.py:49
  382.9 15.3 %collective-permute-start.152 = (bf16[128,960]{1,0:T(8,128)(2,1)S(1)}, bf16[128,960]{1,0:T(8,128)(2,1)S(1)}, u32[]{:S(2)}, u32[]{:S(2)}) collective-permute-start(bf16[128,960]{1,0:T(8,128)(2,1)S(1)} %get-tuple-element.1094), channel_id=1, source_target_pairs={{0,64},{32,96},{64,0},{96,32},{1,65},{33,97},{65,1},{97,33},{2,66}... | collective-permute-start | bytes 737288 | tf_op jit(solution)/shard_map/ppermute | solution.py:49
  431.7 16.0 %collective-permute-start.157 = (bf16[128,640]{1,0:T(8,128)(2,1)}, bf16[128,640]{1,0:T(8,128)(2,1)}, u32[]{:S(2)}, u32[]{:S(2)}) collective-permute-start(bf16[128,640]{1,0:T(8,128)(2,1)} %get-tuple-element.1113), channel_id=1, source_target_pairs={{32,0},{64,32},{96,64},{33,1},{65,33},{97,65},{34,2},{66,34},{98,6... | collective-permute-start | bytes 491528 | tf_op jit(solution)/shard_map/ppermute | solution.py:141
  434.1 13.6 %collective-permute-start.159 = (bf16[128,640]{1,0:T(8,128)(2,1)}, bf16[128,640]{1,0:T(8,128)(2,1)}, u32[]{:S(2)}, u32[]{:S(2)}) collective-permute-start(bf16[128,640]{1,0:T(8,128)(2,1)} %get-tuple-element.1115), channel_id=1, source_target_pairs={{1,0},{2,1},{3,2},{4,3},{5,4},{6,5},{7,6},{8,7},{9,8},{10,9},{11,1... | collective-permute-start | bytes 491528 | tf_op jit(solution)/shard_map/ppermute | solution.py:147
  495.9 15.6 %collective-permute-start.166 = (bf16[128,640]{1,0:T(8,128)(2,1)}, bf16[128,640]{1,0:T(8,128)(2,1)}, u32[]{:S(2)}, u32[]{:S(2)}) collective-permute-start(bf16[128,640]{1,0:T(8,128)(2,1)} %get-tuple-element.1106), channel_id=1, source_target_pairs={{32,0},{64,32},{96,64},{33,1},{65,33},{97,65},{34,2},{66,34},{98,6... | collective-permute-start | bytes 491528 | tf_op jit(solution)/shard_map/ppermute | solution.py:141
  498.3 15.0 %collective-permute-start.168 = (bf16[128,640]{1,0:T(8,128)(2,1)}, bf16[128,640]{1,0:T(8,128)(2,1)}, u32[]{:S(2)}, u32[]{:S(2)}) collective-permute-start(bf16[128,640]{1,0:T(8,128)(2,1)} %get-tuple-element.1108), channel_id=1, source_target_pairs={{1,0},{2,1},{3,2},{4,3},{5,4},{6,5},{7,6},{8,7},{9,8},{10,9},{11,1... | collective-permute-start | bytes 491528 | tf_op jit(solution)/shard_map/ppermute | solution.py:147
  499.6 13.8 %collective-permute-start.169 = (bf16[128,640]{1,0:T(8,128)(2,1)}, bf16[128,640]{1,0:T(8,128)(2,1)}, u32[]{:S(2)}, u32[]{:S(2)}) collective-permute-start(bf16[128,640]{1,0:T(8,128)(2,1)} %get-tuple-element.1111), channel_id=1, source_target_pairs={{1,32},{2,33},{3,34},{4,35},{5,36},{6,37},{7,38},{8,39},{9,40},{10... | collective-permute-start | bytes 491528 | tf_op jit(solution)/shard_map/ppermute | solution.py:147
  511.5 35.3 %collective-permute-start.182 = (bf16[640,960]{0,1:T(8,128)(2,1)}, bf16[640,960]{0,1:T(8,128)(2,1)}, u32[]{:S(2)}, u32[]{:S(2)}) collective-permute-start(bf16[640,960]{0,1:T(8,128)(2,1)} %copy.348), channel_id=1, source_target_pairs={{0,16},{16,0},{1,17},{17,1},{2,18},{18,2},{3,19},{19,3},{4,20},{20... | collective-permute-start | bytes 3686408 | tf_op jit(solution)/shard_map/ppermute | solution.py:53
  513.3 40.2 %collective-permute-start.181 = (bf16[128,3840]{1,0:T(8,128)(2,1)}, bf16[128,3840]{1,0:T(8,128)(2,1)}, u32[]{:S(2)}, u32[]{:S(2)}) collective-permute-start(bf16[128,3840]{1,0:T(8,128)(2,1)} %pad_maximum_fusion.16), channel_id=1, source_target_pairs={{0,16},{16,0},{1,17},{17,1},{2,18},{18,2},{3,19},{19,3},{4,20},{20... | collective-permute-start | bytes 2949128 | tf_op jit(solution)/shard_map/ppermute | solution.py:53
  513.4 35.2 %collective-permute-start.184 = (bf16[640,960]{0,1:T(8,128)(2,1)}, bf16[640,960]{0,1:T(8,128)(2,1)}, u32[]{:S(2)}, u32[]{:S(2)}) collective-permute-start(bf16[640,960]{0,1:T(8,128)(2,1)} %copy.350), channel_id=1, source_target_pairs={{0,16},{16,0},{1,17},{17,1},{2,18},{18,2},{3,19},{19,3},{4,20},{20... | collective-permute-start | bytes 3686408 | tf_op jit(solution)/shard_map/ppermute | solution.py:53
  516.2 37.3 %collective-permute-start.183 = (bf16[128,3840]{1,0:T(8,128)(2,1)}, bf16[128,3840]{1,0:T(8,128)(2,1)}, u32[]{:S(2)}, u32[]{:S(2)}) collective-permute-start(bf16[128,3840]{1,0:T(8,128)(2,1)} %pad_maximum_fusion.17), channel_id=1, source_target_pairs={{0,16},{16,0},{1,17},{17,1},{2,18},{18,2},{3,19},{19,3},{4,20},{20... | collective-permute-start | bytes 2949128 | tf_op jit(solution)/shard_map/ppermute | solution.py:53
  581.7 218.1 %reduce-scatter.15.cloned.1.call-start = ((), (), s32[]{:S(2)}) async-start(), calls=%async_computation.17 | async-start | bytes 13369344
  630.9 20.5 %collective-permute-start.179 = (bf16[128,640]{1,0:T(8,128)(2,1)S(1)}, bf16[128,640]{1,0:T(8,128)(2,1)S(1)}, u32[]{:S(2)}, u32[]{:S(2)}) collective-permute-start(bf16[128,640]{1,0:T(8,128)(2,1)S(1)} %get-tuple-element.1103), channel_id=1, source_target_pairs={{1,64},{2,65},{3,66},{4,67},{5,68},{6,69},{7,70},{8,71},{9,72},{10... | collective-permute-start | bytes 491528 | tf_op jit(solution)/shard_map/ppermute | solution.py:147
  632.2 21.4 %collective-permute-start.180 = (bf16[128,640]{1,0:T(8,128)(2,1)S(1)}, bf16[128,640]{1,0:T(8,128)(2,1)S(1)}, u32[]{:S(2)}, u32[]{:S(2)}) collective-permute-start(bf16[128,640]{1,0:T(8,128)(2,1)S(1)} %get-tuple-element.1102), channel_id=1, source_target_pairs={{1,96},{2,97},{3,98},{4,99},{5,100},{6,101},{7,102},{8,103},{9,104... | collective-permute-start | bytes 491528 | tf_op jit(solution)/shard_map/ppermute | solution.py:147
  635.0 19.5 %collective-permute-start.187 = (bf16[128,960]{1,0:T(8,128)(2,1)S(1)}, bf16[128,960]{1,0:T(8,128)(2,1)S(1)}, u32[]{:S(2)}, u32[]{:S(2)}) collective-permute-start(bf16[128,960]{1,0:T(8,128)(2,1)S(1)} %copy-done.129), channel_id=1, source_target_pairs={{0,16},{16,0},{1,17},{17,1},{2,18},{18,2},{3,19},{19,3},{4,20},{20... | collective-permute-start | bytes 737288 | tf_op jit(solution)/shard_map/ppermute | solution.py:53
  636.1 18.3 %collective-permute-start.188 = (bf16[128,960]{1,0:T(8,128)(2,1)S(1)}, bf16[128,960]{1,0:T(8,128)(2,1)S(1)}, u32[]{:S(2)}, u32[]{:S(2)}) collective-permute-start(bf16[128,960]{1,0:T(8,128)(2,1)S(1)} %copy-done.132), channel_id=1, source_target_pairs={{0,16},{16,0},{1,17},{17,1},{2,18},{18,2},{3,19},{19,3},{4,20},{20... | collective-permute-start | bytes 737288 | tf_op jit(solution)/shard_map/ppermute | solution.py:53
  636.3 39.7 %collective-permute-start.191 = (bf16[128,640]{1,0:T(8,128)(2,1)}, bf16[128,640]{1,0:T(8,128)(2,1)}, u32[]{:S(2)}, u32[]{:S(2)}) collective-permute-start(bf16[128,640]{1,0:T(8,128)(2,1)} %get-tuple-element.634.refs_5_), channel_id=1, source_target_pairs={{0,16},{16,0},{1,17},{17,1},{2,18},{18,2},{3,19},{19,3},{4,20},{20... | collective-permute-start | bytes 491528 | tf_op jit(solution)/shard_map/ppermute | solution.py:53
  653.6 22.5 %collective-permute-start.192 = (bf16[128,640]{1,0:T(8,128)(2,1)}, bf16[128,640]{1,0:T(8,128)(2,1)}, u32[]{:S(2)}, u32[]{:S(2)}) collective-permute-start(bf16[128,640]{1,0:T(8,128)(2,1)} %get-tuple-element.635.refs_9_), channel_id=1, source_target_pairs={{0,16},{16,0},{1,17},{17,1},{2,18},{18,2},{3,19},{19,3},{4,20},{20... | collective-permute-start | bytes 491528 | tf_op jit(solution)/shard_map/ppermute | solution.py:53
  672.8 18.7 %collective-permute-start.212 = (bf16[128,960]{1,0:T(8,128)(2,1)S(1)}, bf16[128,960]{1,0:T(8,128)(2,1)S(1)}, u32[]{:S(2)}, u32[]{:S(2)}) collective-permute-start(bf16[128,960]{1,0:T(8,128)(2,1)S(1)} %convert_element_type.786), channel_id=1, source_target_pairs={{0,96},{32,0},{64,32},{96,64},{1,97},{33,1},{65,33},{97,65},{2,98}... | collective-permute-start | bytes 737288 | tf_op jit(solution)/shard_map/ppermute | solution.py:49
  674.1 19.2 %collective-permute-start.213 = (bf16[128,960]{1,0:T(8,128)(2,1)S(1)}, bf16[128,960]{1,0:T(8,128)(2,1)S(1)}, u32[]{:S(2)}, u32[]{:S(2)}) collective-permute-start(bf16[128,960]{1,0:T(8,128)(2,1)S(1)} %convert_element_type.786), channel_id=1, source_target_pairs={{0,64},{32,96},{64,0},{96,32},{1,65},{33,97},{65,1},{97,33},{2,66}... | collective-permute-start | bytes 737288 | tf_op jit(solution)/shard_map/ppermute | solution.py:49
  676.0 19.7 %collective-permute-start.214 = (bf16[128,960]{1,0:T(8,128)(2,1)S(1)}, bf16[128,960]{1,0:T(8,128)(2,1)S(1)}, u32[]{:S(2)}, u32[]{:S(2)}) collective-permute-start(bf16[128,960]{1,0:T(8,128)(2,1)S(1)} %convert_element_type.786), channel_id=1, source_target_pairs={{0,32},{32,64},{64,96},{96,0},{1,33},{33,65},{65,97},{97,1},{2,34}... | collective-permute-start | bytes 737288 | tf_op jit(solution)/shard_map/ppermute | solution.py:49
  688.2 18.6 %collective-permute-start.201 = (bf16[352,448]{1,0:T(8,128)(2,1)}, bf16[352,448]{1,0:T(8,128)(2,1)}, u32[]{:S(2)}, u32[]{:S(2)}) collective-permute-start(bf16[352,448]{1,0:T(8,128)(2,1)} %get-tuple-element.1091), channel_id=1, source_target_pairs={{0,64},{32,96},{64,0},{96,32},{1,65},{33,97},{65,1},{97,33},{2,66}... | collective-permute-start | bytes 946184 | tf_op jit(solution)/shard_map/ppermute | solution.py:49
  691.5 17.2 %collective-permute-start.202 = (bf16[352,448]{1,0:T(8,128)(2,1)}, bf16[352,448]{1,0:T(8,128)(2,1)}, u32[]{:S(2)}, u32[]{:S(2)}) collective-permute-start(bf16[352,448]{1,0:T(8,128)(2,1)} %get-tuple-element.1090), channel_id=1, source_target_pairs={{0,96},{32,0},{64,32},{96,64},{1,97},{33,1},{65,33},{97,65},{2,98}... | collective-permute-start | bytes 946184 | tf_op jit(solution)/shard_map/ppermute | solution.py:49
  693.3 23.6 %collective-permute-start.194 = (bf16[4,112,512]{2,1,0:T(8,128)(2,1)}, bf16[4,112,512]{2,1,0:T(8,128)(2,1)S(1)}, u32[]{:S(2)}, u32[]{:S(2)}) collective-permute-start(bf16[4,112,512]{2,1,0:T(8,128)(2,1)} %get-tuple-element.1082), channel_id=1, source_target_pairs={{0,4},{4,8},{8,12},{12,0},{1,5},{5,9},{9,13},{13,1},{2,6},{6,10},{... | collective-permute-start | bytes 1376264 | tf_op jit(solution)/shard_map/ppermute | solution.py:49
  695.7 39.4 %collective-permute-start.195 = (bf16[4,112,512]{2,1,0:T(8,128)(2,1)}, bf16[4,112,512]{2,1,0:T(8,128)(2,1)}, u32[]{:S(2)}, u32[]{:S(2)}) collective-permute-start(bf16[4,112,512]{2,1,0:T(8,128)(2,1)} %get-tuple-element.1084), channel_id=1, source_target_pairs={{0,8},{4,12},{8,0},{12,4},{1,9},{5,13},{9,1},{13,5},{2,10},{6,14},... | collective-permute-start | bytes 1376264 | tf_op jit(solution)/shard_map/ppermute | solution.py:49
  699.0 36.1 %collective-permute-start.196 = (bf16[4,112,512]{2,1,0:T(8,128)(2,1)}, bf16[4,112,512]{2,1,0:T(8,128)(2,1)S(1)}, u32[]{:S(2)}, u32[]{:S(2)}) collective-permute-start(bf16[4,112,512]{2,1,0:T(8,128)(2,1)} %get-tuple-element.1083), channel_id=1, source_target_pairs={{0,12},{4,0},{8,4},{12,8},{1,13},{5,1},{9,5},{13,9},{2,14},{6,2},{... | collective-permute-start | bytes 1376264 | tf_op jit(solution)/shard_map/ppermute | solution.py:49
  706.9 41.6 %collective-permute-start.215 = (bf16[512,960]{0,1:T(8,128)(2,1)}, bf16[512,960]{0,1:T(8,128)(2,1)}, u32[]{:S(2)}, u32[]{:S(2)}) collective-permute-start(bf16[512,960]{0,1:T(8,128)(2,1)} %copy.355), channel_id=1, source_target_pairs={{0,16},{16,0},{1,17},{17,1},{2,18},{18,2},{3,19},{19,3},{4,20},{20... | collective-permute-start | bytes 2949128 | tf_op jit(solution)/shard_map/ppermute | solution.py:53
  710.4 27.3 %collective-permute-start.203 = (bf16[112,448]{1,0:T(8,128)(2,1)S(1)}, bf16[112,448]{1,0:T(8,128)(2,1)S(1)}, u32[]{:S(2)}, u32[]{:S(2)}) collective-permute-start(bf16[112,448]{1,0:T(8,128)(2,1)S(1)} %get-tuple-element.1129), channel_id=1, source_target_pairs={{0,4},{4,8},{8,12},{12,0},{1,5},{5,9},{9,13},{13,1},{2,6},{6,10},{... | collective-permute-start | bytes 301064 | tf_op jit(solution)/shard_map/ppermute | solution.py:49
  716.9 27.4 %collective-permute-start.204 = (bf16[112,448]{1,0:T(8,128)(2,1)S(1)}, bf16[112,448]{1,0:T(8,128)(2,1)S(1)}, u32[]{:S(2)}, u32[]{:S(2)}) collective-permute-start(bf16[112,448]{1,0:T(8,128)(2,1)S(1)} %get-tuple-element.1131), channel_id=1, source_target_pairs={{0,8},{4,12},{8,0},{12,4},{1,9},{5,13},{9,1},{13,5},{2,10},{6,14},... | collective-permute-start | bytes 301064 | tf_op jit(solution)/shard_map/ppermute | solution.py:49
  752.0 22.2 %all-to-all-start.3 = ((bf16[16,24,960]{2,1,0:T(8,128)(2,1)}), bf16[16,24,960]{2,1,0:T(8,128)(2,1)S(1)}, u32[]{:S(2)}, u32[]{:S(2)}) async-start(bf16[16,24,960]{2,1,0:T(8,128)(2,1)} %bitcast.205), calls=%async_computation.6 | async-start | bytes 1572864 | tf_op jit(solution)/shard_map/all_to_all | solution.py:1165
  759.5 13.9 %collective-permute-start.206 = (bf16[48,960]{1,0:T(8,128)(2,1)S(1)}, bf16[48,960]{1,0:T(8,128)(2,1)S(1)}, u32[]{:S(2)}, u32[]{:S(2)}) collective-permute-start(bf16[48,960]{1,0:T(8,128)(2,1)S(1)} %get-tuple-element.1134), channel_id=1, source_target_pairs={{0,1},{1,2},{2,3},{3,0},{4,5},{5,6},{6,7},{7,4},{8,9},{9,10},{10,1... | collective-permute-start | bytes 276488 | tf_op jit(solution)/shard_map/ppermute | solution.py:49
  760.9 18.2 %collective-permute-start.209 = (bf16[3,20,960]{2,1,0:T(8,128)(2,1)S(1)}, bf16[3,20,960]{2,1,0:T(8,128)(2,1)S(1)}, u32[]{:S(2)}, u32[]{:S(2)}) collective-permute-start(bf16[3,20,960]{2,1,0:T(8,128)(2,1)S(1)} %get-tuple-element.1121), channel_id=1, source_target_pairs={{0,96},{32,0},{64,32},{96,64},{1,97},{33,1},{65,33},{97,65},{2,98}... | collective-permute-start | bytes 345608 | tf_op jit(solution)/shard_map/ppermute | solution.py:49
  763.7 16.1 %collective-permute-start.210 = (bf16[3,20,960]{2,1,0:T(8,128)(2,1)S(1)}, bf16[3,20,960]{2,1,0:T(8,128)(2,1)S(1)}, u32[]{:S(2)}, u32[]{:S(2)}) collective-permute-start(bf16[3,20,960]{2,1,0:T(8,128)(2,1)S(1)} %get-tuple-element.1120), channel_id=1, source_target_pairs={{0,64},{32,96},{64,0},{96,32},{1,65},{33,97},{65,1},{97,33},{2,66}... | collective-permute-start | bytes 345608 | tf_op jit(solution)/shard_map/ppermute | solution.py:49
  763.7 16.8 %collective-permute-start.211 = (bf16[3,20,960]{2,1,0:T(8,128)(2,1)S(1)}, bf16[3,20,960]{2,1,0:T(8,128)(2,1)S(1)}, u32[]{:S(2)}, u32[]{:S(2)}) collective-permute-start(bf16[3,20,960]{2,1,0:T(8,128)(2,1)S(1)} %get-tuple-element.1119), channel_id=1, source_target_pairs={{0,32},{32,64},{64,96},{96,0},{1,33},{33,65},{65,97},{97,1},{2,34}... | collective-permute-start | bytes 345608 | tf_op jit(solution)/shard_map/ppermute | solution.py:49
  (285 other events, 2422.4 us)
Sparse Core Ops, SparseCore 0:
  24.4 50.8 all-gather.12
  78.4 79.2 all-gather.14
  160.1 99.1 all-gather.16
  581.8 89.0 reduce-scatter.12
  674.2 125.5 reduce-scatter.14

commit v4 on v3

--- a/solution.py
+++ b/solution.py
@@ -54,16 +54,15 @@
 
 
 def gather_group(value):
-    near = by_rows(jnp.concatenate([value] + [shift(value, "z", -k) for k in (1, 2, 3)], axis=0))
-    return near, by_rows(swap(near))
-
-
-def scatter_group(near, far):
-    half = (near.astype(FLOAT) + by_rows(swap(by_rows(far))).astype(FLOAT)).astype(BFLOAT)
-    half = half.reshape(4, TOK_DEV, -1)
-    total = half[0].astype(FLOAT)
+    near = [value] + [shift(value, "z", -k) for k in (1, 2, 3)]
+    return near + [swap(part) for part in near]
+
+
+def scatter_group(blocks):
+    half = [near.astype(FLOAT) + swap(far).astype(FLOAT) for near, far in zip(blocks[:4], blocks[4:])]
+    total = half[0]
     for k in (1, 2, 3):
-        total = total + shift(half[k], "z", k).astype(FLOAT)
+        total = total + shift(half[k].astype(BFLOAT), "z", k).astype(FLOAT)
     return total
 
 
@@ -102,10 +101,6 @@
 def reorder(blocks, order):
     hit = order[:, None] == jnp.arange(MP)[None, :]
     return jnp.sum(jnp.where(hit[:, :, None], blocks[..., None, :, :], 0), axis=-2)
-
-
-def by_rows(value):
-    return with_layout_constraint(value, Layout(tuple(range(value.ndim))))
 
 
 def by_cols(value):
@@ -127,9 +122,7 @@
             for g in range(1, DP):
                 pairs.append((((i + k) % 4) * DP + g - 1, i * DP + g))
         prev.append(lax.ppermute(pair, ("z",) + DP_AXES, pairs))
-    own = jnp.concatenate(own, axis=0)
-    prev = jnp.concatenate(prev, axis=0)
-    return prev, own, swap(prev), swap(own)
+    return prev + own + [swap(part) for part in prev] + [swap(part) for part in own]
 
 
 def group_scatter(prev, own, prev_far, own_far):
@@ -187,13 +180,20 @@
     return grad_values, jnp.sum(grad_out * values * inverse, axis=0, keepdims=True)
 
 
-def attend_kernel(query_ref, kv0, kv1, kv2, kv3, bias_ref, out_ref, log_ref):
+def joined(refs, part, first):
+    return jnp.concatenate(
+        [ref[:, first : first + 64] for ref in refs[4 * part : 4 * part + 4]], axis=0
+    )
+
+
+def attend_kernel(query_ref, *refs):
+    kv_refs, (bias_ref, out_ref, log_ref) = refs[:16], refs[16:]
     for head in range(KV_HEADS):
         queries = head_lanes(query_ref, head)
         top = None
-        for part, kv_ref in enumerate((kv0, kv1, kv2, kv3)):
-            keys = kv_ref[:, 64 * head : 64 * head + 64]
-            values = kv_ref[:, 320 + 64 * head : 320 + 64 * head + 64]
+        for part in range(4):
+            keys = joined(kv_refs, part, 64 * head)
+            values = joined(kv_refs, part, 320 + 64 * head)
             bias = bias_ref[512 * part : 512 * part + 512, :]
             scores = nn(keys, queries) + jnp.concatenate([bias, bias, bias], axis=1)
             part_top = jnp.max(scores, axis=0, keepdims=True)
@@ -233,14 +233,14 @@
         cost_estimate=pl.CostEstimate(
             flops=12_000_000_000, bytes_accessed=5_000_000, transcendentals=4_000_000
         ),
-        compiler_params=params(24),
+        compiler_params=params(BIG),
     )(queries, *pairs, bias)
 
 
-def attend_back_kernel(
-    query_ref, kv0, kv1, kv2, kv3, bias_ref, log_ref, att_ref, grad_ref, cos_ref, sin_ref,
-    dq_ref, d0, d1, d2, d3
-):
+def attend_back_kernel(query_ref, *refs):
+    kv_refs, refs = refs[:16], refs[16:]
+    bias_ref, log_ref, att_ref, grad_ref, cos_ref, sin_ref, dq_ref = refs[:7]
+    d_refs = refs[7:]
     cosine = jnp.concatenate([cos_ref[...]] * 3, axis=1)
     sine = jnp.concatenate([sin_ref[...]] * 3, axis=1)
     for head in range(KV_HEADS):
@@ -250,9 +250,9 @@
         delta = jnp.sum((grads.astype(FLOAT) * outs.astype(FLOAT)).T, axis=0, keepdims=True)
         log_total = log_ref[head : head + 1, :]
         back = None
-        for part, (kv_ref, d_ref) in enumerate(((kv0, d0), (kv1, d1), (kv2, d2), (kv3, d3))):
-            keys = kv_ref[:, 64 * head : 64 * head + 64]
-            values = kv_ref[:, 320 + 64 * head : 320 + 64 * head + 64]
+        for part, d_ref in enumerate(d_refs):
+            keys = joined(kv_refs, part, 64 * head)
+            values = joined(kv_refs, part, 320 + 64 * head)
             bias = bias_ref[512 * part : 512 * part + 512, :]
             probs = jnp.exp(
                 nn(keys, queries) + jnp.concatenate([bias, bias, bias], axis=1) - log_total
@@ -278,7 +278,7 @@
         cost_estimate=pl.CostEstimate(
             flops=20_000_000_000, bytes_accessed=9_000_000, transcendentals=4_000_000
         ),
-        compiler_params=params(24),
+        compiler_params=params(BIG),
     )(queries, *pairs, bias, log_total, attended, grads, cosine, sine)
 
 
@@ -300,35 +300,35 @@
 )
 
 
-def spread_kernel(place_ref, rows_ref, near_ref, far_ref):
-    place = lax.broadcasted_iota(jnp.int32, (512, DP * CAP), 1)
-    for part, ref in enumerate((near_ref, far_ref)):
-        hot = (place_ref[512 * part : 512 * part + 512, :] == place).astype(FLOAT).astype(BFLOAT)
+def spread_kernel(place_ref, rows_ref, *out_refs):
+    place = lax.broadcasted_iota(jnp.int32, (TOK_DEV, DP * CAP), 1)
+    for part, ref in enumerate(out_refs):
+        hot = (place_ref[128 * part : 128 * part + 128, :] == place).astype(FLOAT).astype(BFLOAT)
         ref[...] = nn(hot, rows_ref[...]).astype(BFLOAT)
 
 
 def spread(place, rows):
     return pl.pallas_call(
         spread_kernel,
-        out_shape=(struct(BFLOAT, 512, D), struct(BFLOAT, 512, D)),
-        compiler_params=params(24),
+        out_shape=[struct(BFLOAT, TOK_DEV, D)] * MP,
+        compiler_params=params(BIG),
     )(place, rows)
 
 
-def collect_kernel(place_ref, near_ref, far_ref, out_ref):
-    place = lax.broadcasted_iota(jnp.int32, (512, DP * CAP), 1)
+def collect_kernel(place_ref, *refs):
+    place = lax.broadcasted_iota(jnp.int32, (TOK_DEV, DP * CAP), 1)
     total = None
-    for part, ref in enumerate((near_ref, far_ref)):
-        hot = (place_ref[512 * part : 512 * part + 512, :] == place).astype(FLOAT).astype(BFLOAT)
+    for part, ref in enumerate(refs[:-1]):
+        hot = (place_ref[128 * part : 128 * part + 128, :] == place).astype(FLOAT).astype(BFLOAT)
         sums = contract_rows(hot, ref[...])
         total = sums if total is None else total + sums
-    out_ref[...] = total.astype(BFLOAT)
-
-
-def collect(place, near, far):
+    refs[-1][...] = total.astype(BFLOAT)
+
+
+def collect(place, blocks):
     return pl.pallas_call(
-        collect_kernel, out_shape=struct(BFLOAT, DP * CAP, D), compiler_params=params(24)
-    )(place, near, far)
+        collect_kernel, out_shape=struct(BFLOAT, DP * CAP, D), compiler_params=params(BIG)
+    )(place, *blocks)
 
 
 def enter_kernel(hidden_ref, gain_ref, *refs):
@@ -336,7 +336,7 @@
 
 
 def enter(hidden, gains, wq, wk, wv, cosine, sine):
-    return pl.pallas_call(enter_kernel, out_shape=PROJECTED, compiler_params=params(24))(
+    return pl.pallas_call(enter_kernel, out_shape=PROJECTED, compiler_params=params(BIG))(
         hidden, gains, wq, wk, wv, cosine, sine
     )
 
@@ -567,22 +567,25 @@
             struct(FLOAT, TOK_DEV, D),
             struct(FLOAT, 8, D),
         ),
-        compiler_params=params(24),
+        compiler_params=params(BIG),
     )(grad_in, dq, own, hidden, gains, wq, wk, wv, cosine, sine)
 
 
-HEAD_BLOCK = 512
-
-
-def head_kernel(rows_ref, near_ref, side_ref, far_ref, target_ref, table_ref, logit_ref, pick_ref, stat_ref):
+HEAD_BLOCK = 1024
+
+
+def head_kernel(rows_ref, near_ref, *refs):
+    block_refs, (target_ref, table_ref, logit_ref, pick_ref, out_ref, stat_ref) = refs[:8], refs[8:]
     step = pl.program_id(0)
 
     @pl.when(step == 0)
     def first():
-        hot = (rows_ref[...] == near_ref[...]).astype(FLOAT).astype(BFLOAT)
-        pick_ref[...] = (nn(hot[:, :512], side_ref[...]) + nn(hot[:, 512:], far_ref[...])).astype(
-            BFLOAT
-        )
+        picked = None
+        for i, ref in enumerate(block_refs):
+            hot = rows_ref[...] == near_ref[:, 128 * i : 128 * i + 128]
+            part = nn(hot.astype(FLOAT).astype(BFLOAT), ref[...])
+            picked = part if picked is None else picked + part
+        pick_ref[...] = picked.astype(BFLOAT)
         lane = lax.broadcasted_iota(jnp.int32, (256, 128), 1)
         stat_ref[...] = jnp.where(lane == 0, MASKED, 0.0)
 
@@ -599,61 +602,61 @@
     stat_ref[:, 2:3] = stat_ref[:, 2:3] + hit
     stat_ref[:, 0:1] = top
 
-
-def head(loss_rows, near_rows, near, far, local_targets, table):
+    @pl.when(step == pl.num_programs(0) - 1)
+    def last():
+        out_ref[...] = stat_ref[...].T[0:8]
+
+
+def head(loss_rows, near_rows, blocks, local_targets, table):
     return pl.pallas_call(
         head_kernel,
         grid=(VOCAB_MP // HEAD_BLOCK,),
-        in_specs=[
-            whole(256, 1),
-            whole(1, ROWS),
-            whole(512, D),
-            whole(512, D),
-            whole(256, 1),
-            pl.BlockSpec((HEAD_BLOCK, D), lambda i: (i, 0)),
-        ],
+        in_specs=[whole(256, 1), whole(1, ROWS)]
+        + [whole(TOK_DEV, D)] * MP
+        + [whole(256, 1), pl.BlockSpec((HEAD_BLOCK, D), lambda i: (i, 0))],
         out_specs=[
             pl.BlockSpec((256, HEAD_BLOCK), lambda i: (0, i)),
             whole(256, D),
-            whole(256, 128),
+            whole(8, 256),
         ],
         out_shape=(
-            jax.ShapeDtypeStruct((256, VOCAB_MP), FLOAT),
-            jax.ShapeDtypeStruct((256, D), BFLOAT),
-            jax.ShapeDtypeStruct((256, 128), FLOAT),
+            struct(FLOAT, 256, VOCAB_MP),
+            struct(BFLOAT, 256, D),
+            struct(FLOAT, 8, 256),
         ),
+        scratch_shapes=[pltpu.VMEM((256, 128), FLOAT)],
         compiler_params=params(BIG),
-    )(loss_rows, near_rows, near, far, local_targets, table)
+    )(loss_rows, near_rows, *blocks, local_targets, table)
 
 
 def head_back_kernel(
-    rows_ref, near_ref, target_ref, norm_ref, logit_ref, pick_ref, table_ref, grad_ref, side_ref, far_ref, sum_ref
+    rows_ref, near_ref, target_ref, stat_ref, logit_ref, pick_ref, table_ref, grad_ref, *refs
 ):
+    block_refs, (sum_ref, norm_ref) = refs[:8], refs[8:]
     step = pl.program_id(0)
+
+    @pl.when(step == 0)
+    def first():
+        norm = stat_ref[0:1, :] + jnp.log(stat_ref[1:2, :])
+        norm_ref[:, 0:8] = jnp.concatenate([norm] * 8, axis=0).T
+        sum_ref[...] = jnp.zeros((256, D), FLOAT)
+
     place = step * HEAD_BLOCK + lax.broadcasted_iota(jnp.int32, (256, HEAD_BLOCK), 1)
-    probs = jnp.exp(logit_ref[...] - norm_ref[...])
+    probs = jnp.exp(logit_ref[...] - norm_ref[:, 0:1])
     hit = jnp.where(place == target_ref[...], 1.0, 0.0)
     grads = ((probs - hit) * (1.0 / TOK_DEV)).astype(BFLOAT)
     grad_ref[...] = contract_rows(grads, pick_ref[...]).astype(BFLOAT)
-    part = nn(grads, table_ref[...])
-
-    @pl.when(step == 0)
-    def first():
-        sum_ref[...] = part
-
-    @pl.when(step > 0)
-    def later():
-        sum_ref[...] += part
+    sum_ref[...] += nn(grads, table_ref[...])
 
     @pl.when(step == pl.num_programs(0) - 1)
     def last():
-        hot = (rows_ref[...] == near_ref[...]).astype(FLOAT).astype(BFLOAT)
         total = sum_ref[...].astype(BFLOAT)
-        side_ref[...] = contract_rows(hot[:, :512], total).astype(BFLOAT)
-        far_ref[...] = contract_rows(hot[:, 512:], total).astype(BFLOAT)
-
-
-def head_back(loss_rows, near_rows, local_targets, log_norm, logits, picked, table):
+        for i, ref in enumerate(block_refs):
+            hot = rows_ref[...] == near_ref[:, 128 * i : 128 * i + 128]
+            ref[...] = contract_rows(hot.astype(FLOAT).astype(BFLOAT), total).astype(BFLOAT)
+
+
+def head_back(loss_rows, near_rows, local_targets, stats, logits, picked, table):
     return pl.pallas_call(
         head_back_kernel,
         grid=(VOCAB_MP // HEAD_BLOCK,),
@@ -661,20 +664,16 @@
             whole(256, 1),
             whole(1, ROWS),
             whole(256, 1),
-            whole(256, 1),
+            whole(8, 256),
             pl.BlockSpec((256, HEAD_BLOCK), lambda i: (0, i)),
             whole(256, D),
             pl.BlockSpec((HEAD_BLOCK, D), lambda i: (i, 0)),
         ],
-        out_specs=[pl.BlockSpec((HEAD_BLOCK, D), lambda i: (i, 0)), whole(512, D), whole(512, D)],
-        out_shape=(
-            struct(BFLOAT, VOCAB_MP, D),
-            struct(BFLOAT, 512, D),
-            struct(BFLOAT, 512, D),
-        ),
-        scratch_shapes=[pltpu.VMEM((256, D), FLOAT)],
+        out_specs=[pl.BlockSpec((HEAD_BLOCK, D), lambda i: (i, 0))] + [whole(TOK_DEV, D)] * MP,
+        out_shape=[struct(BFLOAT, VOCAB_MP, D)] + [struct(BFLOAT, TOK_DEV, D)] * MP,
+        scratch_shapes=[pltpu.VMEM((256, D), FLOAT), pltpu.VMEM((256, 128), FLOAT)],
         compiler_params=params(BIG),
-    )(loss_rows, near_rows, local_targets, log_norm, logits, picked, table)
+    )(loss_rows, near_rows, local_targets, stats, logits, picked, table)
 
 
 def mlp_grad_kernel(which_ref, *refs):
@@ -695,13 +694,12 @@
     def cols(width, place):
         return pl.BlockSpec((TOK_DEV, width), place)
 
-    own = [cols(640, lambda i, half: (0, half[0] * 2 + i))] * 3 + [cols(D, lambda i, half: (0, 0))] * 2
-    far = [cols(640, lambda i, half, n=n: (0, 2 * n + i)) for n in range(3)] + [
-        cols(D, lambda i, half, n=n: (n, 0)) for n in (0, 1)
-    ]
+    rights = [cols(D, lambda i, half: (0, 0))] * 2
+    own = [cols(640, lambda i, half: (0, half[0] * 2 + i))] * 3 + rights
+    far = [cols(640, lambda i, half: (0, i))] * 3 + rights
     args = []
     for parts, other in zip(kept, received):
-        args += [*parts, *[other[0]] * 3, *[other[1]] * 2]
+        args += [*parts, *other]
     return pl.pallas_call(
         mlp_grad_kernel,
         grid_spec=pltpu.PrefetchScalarGridSpec(
@@ -711,7 +709,7 @@
             out_specs=pl.BlockSpec((8, 3, 80, D), lambda i, half: (i, 0, 0, 0)),
         ),
         out_shape=struct(BFLOAT, 16, 3, 80, D),
-        compiler_params=params(40),
+        compiler_params=params(BIG),
     )(which.reshape(1), *args)
 
 
@@ -729,19 +727,17 @@
     wo_ref[...] = contract_rows(both(0), both(1)).astype(BFLOAT)
 
 
-def square_grads(kept, received, queries):
-    full = whole(TOK_DEV, D)
-    far = [pl.BlockSpec((TOK_DEV, D), lambda i, n=n: (n, 0)) for n in (2, 3, 4)] + [full]
+def square_grads(kept, received):
     args = []
-    for parts, other, query in zip(kept, received, queries):
-        args += [*parts, *[other[1]] * 3, query]
+    for parts, other in zip(kept, received):
+        args += [*parts, *other]
     return pl.pallas_call(
         square_grad_kernel,
         grid=(1,),
-        in_specs=([full] * 4 + far) * RECUR,
+        in_specs=[whole(TOK_DEV, D)] * (8 * RECUR),
         out_specs=[whole(D, D), whole(D, D)],
         out_shape=(struct(BFLOAT, D, D), struct(BFLOAT, D, D)),
-        compiler_params=params(40),
+        compiler_params=params(BIG),
     )(*args)
 
 
@@ -769,16 +765,11 @@
         right_ref[i] = buf[pl.ds(start, 352), 512:960]
 
 
-def pack_grads(starts, wq, wo, small, kept, received, pairs):
+def pack_grads(starts, wq, wo, small, kept, received):
     args = []
-    for (normed, pair), other, far in zip(kept, received, pairs):
-        args += [normed, other[1], pair, far]
-    specs = [
-        whole(TOK_DEV, D),
-        pl.BlockSpec((TOK_DEV, D), lambda i: (4, 0)),
-        whole(TOK_DEV, 640),
-        whole(TOK_DEV, 640),
-    ]
+    for (normed, pair), (far_normed, far_pair) in zip(kept, received):
+        args += [normed, far_normed, pair, far_pair]
+    specs = [whole(TOK_DEV, D)] * 2 + [whole(TOK_DEV, 640)] * 2
     return pl.pallas_call(
         pack_grad_kernel,
         grid=(1,),
@@ -787,7 +778,7 @@
         out_specs=[whole(4, 352, 512), whole(4, 352, 448)],
         out_shape=(struct(BFLOAT, 4, 352, 512), struct(BFLOAT, 4, 352, 448)),
         scratch_shapes=[pltpu.VMEM((PACK_PAD, D), BFLOAT)],
-        compiler_params=params(40),
+        compiler_params=params(BIG),
     )(starts, wq, wo, small, *args)
 
 
@@ -928,10 +919,10 @@
     if dense:
         rows = jnp.take(table, jnp.clip(local_ids, 0, VOCAB_MP - 1), axis=0)
         looked = jnp.where(inside[:, None], rows, jnp.zeros_like(rows))
-        looked = looked[:512], looked[512:]
+        looked = [looked[128 * i : 128 * i + 128] for i in range(MP)]
     else:
         looked = spread(token_place, asked_rows)
-    hidden = scatter_group(*looked)
+    hidden = scatter_group(looked)
 
     pack_weights = join_pack(pack_blocks)
     w_query = pack_weights[:960]
@@ -1019,8 +1010,9 @@
     row_targets = lax.dynamic_index_in_dim(targets, data_index, 0, keepdims=False)
     head_args = (loss_rows[0][:, None], near_rows[None, :])
     local_targets = (row_targets - model_index * VOCAB_MP)[:, None]
-    logits, picked, stats = head(*head_args, *final_rows, local_targets, table)
-    stats = jnp.concatenate([stats[:, :3].T, jnp.full((1, 256), over)])
+    logits, picked, stats = head(*head_args, final_rows, local_targets, table)
+    flag_row = lax.broadcasted_iota(jnp.int32, (8, 256), 0) == 3
+    stats = jnp.where(flag_row, over, stats)
 
     def join_stats(parts):
         top = parts[0][0]
@@ -1030,7 +1022,8 @@
         over = parts[0][3]
         for part in parts[1:]:
             over = jnp.maximum(over, part[3])
-        return jnp.stack([top, total, sum(part[2] for part in parts), over])
+        rest = [jnp.zeros_like(top)] * 4
+        return jnp.stack([top, total, sum(part[2] for part in parts), over] + rest)
 
     stats = join_stats([stats, swap(stats)])
     stats = join_stats([stats] + [shift(stats, "z", k) for k in (1, 2, 3)])
@@ -1041,15 +1034,14 @@
         jnp.sum(lax.dynamic_slice_in_dim(cross, model_index * per_device, per_device))
         + ROUTER_LOSS * penalty_total
     )
-    head_grad, *scattered = head_back(
-        *head_args, local_targets, log_norm[:, None], logits, picked, table
-    )
-    grad_final = scatter_group(*scattered)
+    head_grad, *scattered = head_back(*head_args, local_targets, stats, logits, picked, table)
+    grad_final = scatter_group(scattered)
     grad_hidden, grad_gain_final = rms_back(hidden, gains[2], grad_final)
     if not dense:
         head_grad = lax.psum_scatter(head_grad, DP_AXES, scatter_dimension=0, tiled=True)
 
-    mlp_kept, far_kept, square_kept, far_queries, pack_kept, far_pairs = [], [], [], [], [], []
+    mlp_kept, mlp_far, square_kept, square_far, pack_kept, pack_far = [], [], [], [], [], []
+    loss_part, flag, grad_hidden = tie(loss_part, stats[3, 0], grad_hidden)
     router_rows = [None] * RECUR
     gain_one = jnp.zeros((1, D), FLOAT)
     gain_two = jnp.zeros((1, D), FLOAT)
@@ -1090,28 +1082,35 @@
         def far_half(value):
             return lax.dynamic_slice_in_dim(value, (1 - core) * (FF // 2), FF // 2, 1)
 
-        sent = jnp.concatenate([far_half(grad_gate), far_half(grad_up), far_half(inner)], axis=1)
-        rows = jnp.concatenate([mlp_input, grad_rows, attended, grad_attn, normed], axis=0)
-        far_kept.append((swap(sent), by_rows(swap(by_rows(rows)))))
+        mlp_far.append(
+            [swap(far_half(part)) for part in (grad_gate, grad_up, inner)]
+            + [swap(mlp_input), swap(grad_rows)]
+        )
         grad_query, *grad_sides = attend_back(
             queries, pairs, biases[step], log_total, attended, grad_attended, *turns
         )
+        far_normed = swap(normed)
         square_kept.append((attended, grad_attn, normed, grad_query))
-        far_queries.append(by_rows(swap(grad_query)))
+        square_far.append((swap(attended), swap(grad_attn), far_normed, swap(grad_query)))
+        if step == 0:
+            tied = tie(*grad_sides, *mlp_kept[-1])
+            grad_sides, mlp_kept[-1] = tied[:4], tied[4:]
         grad_own = group_scatter(*grad_sides)
         if step == 0:
-            mlp_half = mlp_grads(core.astype(jnp.int32), mlp_kept, far_kept)
+            mlp_half = mlp_grads(core.astype(jnp.int32), mlp_kept, mlp_far)
             mlp_sum = lax.psum_scatter(
                 mlp_half.reshape(16 * 240, D), DP_AXES, scatter_dimension=0, tiled=True
             )
-            squares = square_grads(square_kept, far_kept, far_queries)
+            squares = square_grads(square_kept, square_far)
             grad_own, mlp_half, *squares = tie(grad_own, mlp_half, *squares)
         grad_pair, grad_hidden, small = enter_back(
             grad_in, grad_query, grad_own, hidden_in, gains, *projections
         )
         gain_one = gain_one + small[0:1]
         pack_kept.append((normed, grad_pair))
-        far_pairs.append(swap(grad_pair))
+        pack_far.append((far_normed, swap(grad_pair)))
+        if step == 1 and not dense:
+            head_grad, grad_hidden = tie(head_grad, grad_hidden)
 
     def aligned_row(which):
         return (pack_row(which) // 16) * 16
@@ -1127,7 +1126,7 @@
     )
     small = small + swap(small)
     starts = jnp.stack([aligned_row(DP * (2 * i + core)) for i in range(4)]).astype(jnp.int32)
-    left, right = pack_grads(starts, *squares, small, pack_kept, far_kept, far_pairs)
+    left, right = pack_grads(starts, *squares, small, pack_kept, pack_far)
 
     def y_windows(value):
         return jnp.stack([value[..., 80 * i : 80 * i + 112, :] for i in range(4)])
@@ -1161,10 +1160,10 @@
             tiled=True,
         ).astype(FLOAT)
     else:
-        unique = collect(token_place, *grad_embed)
+        unique = collect(token_place, grad_embed)
         unique = lax.all_to_all(unique, DP_AXES, 0, 0, tiled=True)
         table_grad = head_grad.astype(FLOAT) + contract_rows(owner_hot, unique)
-    return pack_grad, mlp_grad, by_cols(table_grad), loss_part, stats[3, 0]
+    return pack_grad, mlp_grad, by_cols(table_grad), loss_part, flag
 
 
 def shards(
@@ -1193,7 +1192,7 @@
         mlp_master,
         table_master,
     )
-    *found, over = gradients(False, *args)
+    *found, over = tie(*gradients(False, *args))
     pack_grad, mlp_grad, table_grad, loss_part = lax.cond(
         over > 0, lambda: gradients(True, *args)[:4], lambda: tuple(found)
     )

time: 885 us -> 773 us (0.87)
  local copies, waits for them, and re-layouts: 157 us -> 45.5 us
  waiting for transfers between devices: 186 us -> 113 us
  starting transfers between devices: 182 us -> 234 us
  Pallas kernels: 211 us -> 246 us
  other arithmetic: 71.9 us -> 59.5 us
    unnamed x443 -> x312, local copies, waits for them, and re-layouts: 73.5 us -> 9.97 us
    ppermute x45, waiting for transfers between devices: 95.2 us -> 63.8 us  [shift(): return lax.ppermute(value, axis, [(i, (i + steps) % 4) for i in range(4)])]
    ppermute x31 -> x79, starting transfers between devices: 32.5 us -> 63.2 us  [swap(): return lax.ppermute(value, 'core', [(0, 1), (1, 0)])]
    another operation x24 -> x5, local copies, waits for them, and re-layouts: 25.2 us -> 0.65 us  [the longest x2 0.64 us: join_stats(): jnp.stack([top, total, sum((part[2] for part in parts)), over] + rest)]
    ppermute x12, waiting for transfers between devices: 27.8 us -> 4.3 us  [group_gather(): prev.append(lax.ppermute(pair, ('z',) + DP_AXES, pairs))]
    unnamed x6, waiting for transfers between devices: 18.8 us -> 0.09 us
    ppermute x7 -> x0, local copies, waits for them, and re-layouts: 13 us -> none  [swap(): return lax.ppermute(value, 'core', [(0, 1), (1, 0)])]
    ppermute x45, starting transfers between devices: 60.5 us -> 72.9 us  [shift(): return lax.ppermute(value, axis, [(i, (i + steps) % 4) for i in range(4)])]
  transfers between devices with their start and end apart: 124 -> 172, of which waited for: 44 -> 47; matrix products, arithmetic and copies ran while one was open for 14% -> 10% of each run, Pallas kernels for 13% -> 27%
where the time goes in v4:
time: 773 us; the launch traced here: 759 us
  Pallas kernels  246 us (32%)
  starting transfers between devices  234 us (30%)
  waiting for transfers between devices  113 us (15%)
  other arithmetic  59.5 us (8%)
  local copies, waits for them, and re-layouts  45.5 us (6%)
  blocking collectives  28.6 us (4%)
  between operations  22.4 us (3%)
    ppermute x45, starting transfers between devices, shift(): return lax.ppermute(value, axis, [(i, (i + steps) % 4) for i in range(4)])  72.9 us
    ppermute x45, waiting for transfers between devices, shift(): return lax.ppermute(value, axis, [(i, (i + steps) % 4) for i in range(4)])  63.8 us
    ppermute x79, starting transfers between devices, swap(): return lax.ppermute(value, 'core', [(0, 1), (1, 0)])  63.2 us
    pallas_call x3, Pallas kernels, attend_back(): pl.pallas_call(attend_back_kernel, out_shape=(struct(BFLOAT, TOK_DEV, D),...  41.6 us
    pallas_call x3, Pallas kernels, block_back(): pl.pallas_call(block_back_kernel, grid=(FF_STEPS,), in_specs=[full, whole...  39.7 us
    pallas_call x3, Pallas kernels, block(): pl.pallas_call(functools.partial(block_kernel, more), grid=(FF_STEPS,), i...  38.9 us
    pallas_call x3, Pallas kernels, attend(): pl.pallas_call(attend_kernel, out_shape=(struct(BFLOAT, TOK_DEV, D), stru...  35.3 us
    ppermute x9, starting transfers between devices, group_gather(): lax.ppermute(pair, 'z', [((i + k) % 4, i) for i in range(4) if (i + k) %...  33.5 us
  transfers between devices with their start and end apart: 172, of which 47 were waited for; matrix products, arithmetic and copies ran while one was open for 10% of the time, Pallas kernels for 27%

profile of v4, /device:TPU:1, one launch (start us, length us, event | category | flops | bytes accessed | tf_op | source)
XLA Modules:
  0.0 759.1 jit_solution(4544537494186659928)
XLA Ops:
  9.9 4.7 collective-permute-start.158
  15.2 6.6 collective-permute-done.158
  29.1 13.0 %all_to_all.46 = f32[16,1,32]{2,1,0:T(1,128)S(1)} all-to-all(f32[16,1,32]{2,1,0:T(1,128)S(1)} %bitcast.437), channel_id=1, replica_groups=mesh['z'=4,'core'=2,'y'=4,'x'=4] {'y','x'}, dimensions={0} | all-to-all | bytes 4096 | tf_op jit(solution)/shard_map/all_to_all | solution.py:908
  44.7 15.6 %all_to_all.47 = bf16[16,24,960]{2,1,0:T(8,128)(2,1)} all-to-all(bf16[16,24,960]{2,1,0:T(8,128)(2,1)S(1)} %bitcast.409), channel_id=1, replica_groups=mesh['z'=4,'core'=2,'y'=4,'x'=4] {'y','x'}, dimensions={0} | all-to-all | bytes 1474560 | tf_op jit(solution)/shard_map/all_to_all | solution.py:916
  88.2 6.4 collective-permute-done.161
  99.1 5.3 shard_map.222
  111.5 4.5 fusion.115
  128.2 5.9 collective-permute-start.170
  140.4 4.3 collective-permute-done.169.refs_3_
  150.6 11.8 %shard_map.224 = (bf16[128,960]{1,0:T(8,128)(2,1)}, f32[8,384]{1,0:T(8,128)}) custom-call(bf16[960,128]{1,0:T(8,128)(2,1)} %get-tuple-element.320.query_ref, bf16[128,640]{1,0:T(8,128)(2,1)} %copy-done.187, bf16[128,640]{1,0:T(8,128)(2,1)} %copy-done.189, bf16[128,640]{1,0:T(8,128)(2,1)} %copy-done.191, bf16[128,640]{1,0:T(8,128)(2,1)} %copy-done.193, ...), custom_call_target="tpu_custom_call" | custom-call | flops 12000000000 | bytes 5000000 | tf_op jit(solution)/shard_map/pallas_call | solution.py:230
  162.4 13.5 %shard_map.225 = (f32[128,960]{1,0:T(8,128)}, bf16[128,960]{1,0:T(8,128)(2,1)}, f32[128,2560]{1,0:T(8,128)}, f32[128,2560]{1,0:T(8,128)}, bf16[128,2560]{1,0:T(8...) custom-call(bf16[128,960]{1,0:T(8,128)(2,1)} %get-tuple-element.323., ...), custom_call_target="tpu_custom_call" | custom-call | flops 4000000000 | bytes 20000000 | tf_op jit(solution)/shard_map/pallas_call | solution.py:406
  175.9 5.1 collective-permute-start.181
  181.7 5.1 collective-permute-start.183
  189.1 7.4 collective-permute-start.185
  208.7 11.8 %shard_map.226 = (bf16[128,960]{1,0:T(8,128)(2,1)}, f32[8,384]{1,0:T(8,128)}) custom-call(bf16[960,128]{1,0:T(8,128)(2,1)} %get-tuple-element.325.query_ref, bf16[128,640]{1,0:T(8,128)(2,1)} %copy-done.220, bf16[128,640]{1,0:T(8,128)(2,1)} %copy-done.222, bf16[128,640]{1,0:T(8,128)(2,1)} %copy-done.224, bf16[128,640]{1,0:T(8,128)(2,1)} %copy-done.225, ...), custom_call_target="tpu_custom_call" | custom-call | flops 12000000000 | bytes 5000000 | tf_op jit(solution)/shard_map/pallas_call | solution.py:230
  220.6 13.4 %shard_map.227 = (f32[128,960]{1,0:T(8,128)}, bf16[128,960]{1,0:T(8,128)(2,1)}, f32[128,2560]{1,0:T(8,128)}, f32[128,2560]{1,0:T(8,128)}, bf16[128,2560]{1,0:T(8...) custom-call(bf16[128,960]{1,0:T(8,128)(2,1)} %get-tuple-element.327., ...), custom_call_target="tpu_custom_call" | custom-call | flops 4000000000 | bytes 20000000 | tf_op jit(solution)/shard_map/pallas_call | solution.py:406
  236.4 7.2 collective-permute-start.198
  244.9 8.9 %collective-permute-start.200 = (bf16[128,640]{1,0:T(8,128)(2,1)}, bf16[128,640]{1,0:T(8,128)(2,1)S(1)}, u32[]{:S(2)}, u32[]{:S(2)}) collective-permute-start(bf16[128,640]{1,0:T(8,128)(2,1)} %get-tuple-element.330.refs_4_), channel_id=1, source_target_pairs={{0,96},{1,97},{2,98},{3,99},{4,100},{5,101},{6,102},{7,103},{8,104... | collective-permute-start | bytes 491528 | tf_op jit(solution)/shard_map/ppermute | solution.py:117
  266.3 11.7 %shard_map.228 = (bf16[128,960]{1,0:T(8,128)(2,1)}, f32[8,384]{1,0:T(8,128)}) custom-call(bf16[960,128]{1,0:T(8,128)(2,1)} %get-tuple-element.329.query_ref, bf16[128,640]{1,0:T(8,128)(2,1)} %copy-done.249, bf16[128,640]{1,0:T(8,128)(2,1)} %copy-done.251, bf16[128,640]{1,0:T(8,128)(2,1)} %copy-done.253, bf16[128,640]{1,0:T(8,128)(2,1)} %copy-done.255, ...), custom_call_target="tpu_custom_call" | custom-call | flops 12000000000 | bytes 5000000 | tf_op jit(solution)/shard_map/pallas_call | solution.py:230
  278.0 12.0 %shard_map.229 = (f32[128,960]{1,0:T(8,128)}, bf16[128,960]{1,0:T(8,128)(2,1)}, f32[128,2560]{1,0:T(8,128)}, f32[128,2560]{1,0:T(8,128)}, bf16[128,2560]{1,0:T(8...) custom-call(bf16[128,960]{1,0:T(8,128)(2,1)} %get-tuple-element.331.att_ref.refs_18_.refs_0_, ...), custom_call_target="tpu_custom_call" | custom-call | flops 4000000000 | bytes 20000000 | tf_op jit(solution)/shard_map/pallas_call | solution.py:406
  300.9 6.1 collective-permute-start.215
  314.7 13.4 %shard_map.230 = (f32[256,6144]{1,0:T(8,128)}, bf16[256,960]{1,0:T(8,128)(2,1)}, f32[8,256]{1,0:T(8,128)}) custom-call(s32[256,1]{1,0:T(8,128)} %copy.193.rows_ref, s32[1,1024]{1,0:T(1,128)} %bitcast.434, bf16[128,960]{1,0:T(8,128)(2,1)} %copy-done.38, bf16[128,960]{1,0:T(8,128)(2,1)} %copy-done.112, bf16[128,960]{1,0:T(8,128)(2,1)} %copy-done.113, ...), custom_call_target="tpu_custom_call" | custom-call | tf_op jit(solution)/shard_map/pallas_call | solution.py:611
  337.1 17.6 %shard_map.231 = (bf16[6144,960]{1,0:T(8,128)(2,1)}, bf16[128,960]{1,0:T(8,128)(2,1)}, bf16[128,960]{1,0:T(8,128)(2,1)}, bf16[128,960]{1,0:T(8,128)(2,1)}, bf16[...) custom-call(s32[256,1]{1,0:T(8,128)} %copy.193.rows_ref, ...), custom_call_target="tpu_custom_call" | custom-call | tf_op jit(solution)/shard_map/pallas_call | solution.py:660
  370.1 6.7 collective-permute-done.224
  378.1 13.7 %shard_map.232 = (bf16[128,960]{1,0:T(8,128)(2,1)}, bf16[128,2560]{1,0:T(8,128)(2,1)}, bf16[128,2560]{1,0:T(8,128)(2,1)}, f32[128,960]{1,0:T(8,128)}, bf16[128,9...) custom-call(f32[128,960]{1,0:T(8,128)} %multiply_subtract_fusion.2.new_ref, f32[128,1]{1,0:T(8,128)} %copy.190.sel_ref, ...), custom_call_target="tpu_custom_call" | custom-call | flops 4000000000 | bytes 20000000 | tf_op jit(solution)/shard_map/pallas_call | solution.py:505
  391.8 14.1 %shard_map.233 = (bf16[128,960]{1,0:T(8,128)(2,1)}, bf16[512,640]{1,0:T(8,128)(2,1)}, bf16[512,640]{1,0:T(8,128)(2,1)}, bf16[512,640]{1,0:T(8,128)(2,1)}, bf16[512,640]{1,0:T(8,128)(2,1)}) custom-call(bf16[960,128]{1,0:T(8,128)(2,1)} %get-tuple-element.329.query_ref, bf16[128,640]{1,0:T(8,128)(2,1)} %copy-done.249, bf16[128,640]{1,0:T(8,128)(2,1)} %copy-done.251, ...), custom_call_target="tpu_custom_call" | custom-call | flops 20000000000 | bytes 9000000 | tf_op jit(solution)/shard_map/pallas_call | solution.py:275
  415.9 5.8 collective-permute-done.237
  423.0 4.4 collective-permute-done.236
  429.5 4.3 collective-permute-done.234
  439.0 5.3 shard_map.234
  444.4 13.1 %shard_map.235 = (bf16[128,960]{1,0:T(8,128)(2,1)}, bf16[128,2560]{1,0:T(8,128)(2,1)}, bf16[128,2560]{1,0:T(8,128)(2,1)}, f32[128,960]{1,0:T(8,128)}, bf16[128,9...) custom-call(f32[128,960]{1,0:T(8,128)} %get-tuple-element.363.new_ref, f32[128,1]{1,0:T(8,128)} %copy.189.sel_ref, ...), custom_call_target="tpu_custom_call" | custom-call | flops 4000000000 | bytes 20000000 | tf_op jit(solution)/shard_map/pallas_call | solution.py:505
  457.5 13.8 %shard_map.236 = (bf16[128,960]{1,0:T(8,128)(2,1)}, bf16[512,640]{1,0:T(8,128)(2,1)}, bf16[512,640]{1,0:T(8,128)(2,1)}, bf16[512,640]{1,0:T(8,128)(2,1)}, bf16[512,640]{1,0:T(8,128)(2,1)}) custom-call(bf16[960,128]{1,0:T(8,128)(2,1)} %get-tuple-element.325.query_ref, bf16[128,640]{1,0:T(8,128)(2,1)} %copy-done.220, bf16[128,640]{1,0:T(8,128)(2,1)} %copy-done.222, ...), custom_call_target="tpu_custom_call" | custom-call | flops 20000000000 | bytes 9000000 | tf_op jit(solution)/shard_map/pallas_call | solution.py:275
  498.4 4.7 shard_map.237
  504.7 12.8 %shard_map.238 = (bf16[128,960]{1,0:T(8,128)(2,1)}, bf16[128,2560]{1,0:T(8,128)(2,1)}, bf16[128,2560]{1,0:T(8,128)(2,1)}, f32[128,960]{1,0:T(8,128)}, bf16[128,9...) custom-call(f32[128,960]{1,0:T(8,128)} %get-tuple-element.377.new_ref, f32[128,1]{1,0:T(8,128)} %copy.188.sel_ref, ...), custom_call_target="tpu_custom_call" | custom-call | flops 4000000000 | bytes 20000000 | tf_op jit(solution)/shard_map/pallas_call | solution.py:505
  522.9 13.6 %shard_map.239 = (bf16[128,960]{1,0:T(8,128)(2,1)}, bf16[512,640]{1,0:T(8,128)(2,1)}, bf16[512,640]{1,0:T(8,128)(2,1)}, bf16[512,640]{1,0:T(8,128)(2,1)}, bf16[512,640]{1,0:T(8,128)(2,1)}) custom-call(bf16[960,128]{1,0:T(8,128)(2,1)} %get-tuple-element.320.query_ref, bf16[128,640]{1,0:T(8,128)(2,1)} %copy-done.187, bf16[128,640]{1,0:T(8,128)(2,1)} %copy-done.189, ...), custom_call_target="tpu_custom_call" | custom-call | flops 20000000000 | bytes 9000000 | tf_op jit(solution)/shard_map/pallas_call | solution.py:275
  537.8 11.7 %shard_map.240 = bf16[16,3,80,960]{3,2,1,0:T(8,128)(2,1)} custom-call(s32[1]{0:T(128)} %bitcast.153.which_ref, bf16[128,2560]{1,0:T(8,128)(2,1)} %get-tuple-element.396.refs_0_, bf16[128,2560]{1,0:T(8,128)(2,1)} %get-tuple-element.397.refs_1_, bf16[128,2560]{1,0:T(8,128)(2,1)} %get-tuple-element.398.refs_2_, bf16[128,960]{1,0:T(8,128)(2,1)} %get-tuple-element.399.refs_3_, ...), custom_call_target="tpu_custom_call" | custom-call | tf_op jit(solution)/shard_map/pallas_call | solution.py:703
  573.9 7.4 shard_map.241
  583.9 4.6 collective-permute-done.252
  591.3 4.9 shard_map.242
  604.1 8.2 %shard_map.243 = (bf16[4,352,512]{2,1,0:T(8,128)(2,1)}, bf16[4,352,448]{2,1,0:T(8,128)(2,1)}) custom-call(s32[4]{0:T(128)} %pad_add_fusion.1.starts_ref, bf16[960,960]{1,0:T(8,128)(2,1)} %get-tuple-element.420.refs_0_, bf16[960,960]{1,0:T(8,128)(2,1)} %get-tuple-element.421.refs_1_, f32[16,960]{1,0:T(8,128)} %add.1368.refs_2_, ...), custom_call_target="tpu_custom_call" | custom-call | tf_op jit(solution)/shard_map/pallas_call | solution.py:773
  625.7 9.0 %collective-permute-start.289 = (bf16[4,112,512]{2,1,0:T(8,128)(2,1)}, bf16[4,112,512]{2,1,0:T(8,128)(2,1)}, u32[]{:S(2)}, u32[]{:S(2)}) collective-permute-start(bf16[4,112,512]{2,1,0:T(8,128)(2,1)} %get-tuple-element.678), channel_id=1, source_target_pairs={{0,12},{4,0},{8,4},{12,8},{1,13},{5,1},{9,5},{13,9},{2,14},{6,2},{... | collective-permute-start | bytes 1376264 | tf_op jit(solution)/shard_map/ppermute | solution.py:49
  638.4 5.9 collective-permute-start.288
  652.5 4.4 shard_map.244
  657.0 6.3 all-to-all-start.3
  671.9 5.7 collective-permute-done.296
  682.4 6.0 collective-permute-start.301
  701.3 6.7 conditional.1
  713.5 5.7 collective-permute-start.312
  (818 shorter events, 327.9 us)
Async XLA Ops:
  7.2 88.4 %all-gather.13.cloned.1.call-start = ((), (), s32[]{:S(2)}) async-start(), calls=%async_computation.13 | async-start | bytes 6488064 | tf_op jit(solution)/shard_map/all_gather | solution.py:878
  26.5 135.9 %all-gather.15.cloned.1.call-start = ((), (), s32[]{:S(2)}) async-start(), calls=%async_computation.14 | async-start | bytes 16220160 | tf_op jit(solution)/shard_map/all_gather | solution.py:914
  43.4 270.4 %all-gather.17.cloned.1.call-start = ((), (), s32[]{:S(2)}) async-start(), calls=%async_computation.15 | async-start | bytes 13369344 | tf_op jit(solution)/shard_map/all_gather | solution.py:918
  60.4 442.7 %reduce-scatter.15.cloned.1.call-start = ((), (), s32[]{:S(2)}) async-start(), calls=%async_computation.17 | async-start | bytes 13369344
  126.1 18.6 %collective-permute-start.169 = (bf16[128,640]{1,0:T(8,128)(2,1)}, bf16[128,640]{1,0:T(8,128)(2,1)S(1)}, u32[]{:S(2)}, u32[]{:S(2)}) collective-permute-start(bf16[128,640]{1,0:T(8,128)(2,1)} %get-tuple-element.321.refs_4_), channel_id=1, source_target_pairs={{96,1},{97,2},{98,3},{99,4},{100,5},{101,6},{102,7},{103,8},{104,9... | collective-permute-start | bytes 491528 | tf_op jit(solution)/shard_map/ppermute | solution.py:124
  128.2 17.4 %collective-permute-start.170 = (bf16[128,640]{1,0:T(8,128)(2,1)}, bf16[128,640]{1,0:T(8,128)(2,1)S(1)}, u32[]{:S(2)}, u32[]{:S(2)}) collective-permute-start(bf16[128,640]{1,0:T(8,128)(2,1)} %get-tuple-element.321.refs_4_), channel_id=1, source_target_pairs={{0,96},{1,97},{2,98},{3,99},{4,100},{5,101},{6,102},{7,103},{8,104... | collective-permute-start | bytes 491528 | tf_op jit(solution)/shard_map/ppermute | solution.py:117
  175.9 20.6 %collective-permute-start.181 = (bf16[128,640]{1,0:T(8,128)(2,1)}, bf16[128,640]{1,0:T(8,128)(2,1)S(1)}, u32[]{:S(2)}, u32[]{:S(2)}) collective-permute-start(bf16[128,640]{1,0:T(8,128)(2,1)} %get-tuple-element.326.refs_4_), channel_id=1, source_target_pairs={{0,1},{1,2},{2,3},{3,4},{4,5},{5,6},{6,7},{7,8},{8,9},{9,10},{10,1... | collective-permute-start | bytes 491528 | tf_op jit(solution)/shard_map/ppermute | solution.py:124
  181.0 16.9 %collective-permute-start.182 = (bf16[128,640]{1,0:T(8,128)(2,1)}, bf16[128,640]{1,0:T(8,128)(2,1)S(1)}, u32[]{:S(2)}, u32[]{:S(2)}) collective-permute-start(bf16[128,640]{1,0:T(8,128)(2,1)} %get-tuple-element.326.refs_4_), channel_id=1, source_target_pairs={{32,1},{33,2},{34,3},{35,4},{36,5},{37,6},{38,7},{39,8},{40,9},{41... | collective-permute-start | bytes 491528 | tf_op jit(solution)/shard_map/ppermute | solution.py:124
  181.7 18.7 %collective-permute-start.183 = (bf16[128,640]{1,0:T(8,128)(2,1)}, bf16[128,640]{1,0:T(8,128)(2,1)S(1)}, u32[]{:S(2)}, u32[]{:S(2)}) collective-permute-start(bf16[128,640]{1,0:T(8,128)(2,1)} %get-tuple-element.326.refs_4_), channel_id=1, source_target_pairs={{64,1},{65,2},{66,3},{67,4},{68,5},{69,6},{70,7},{71,8},{72,9},{73... | collective-permute-start | bytes 491528 | tf_op jit(solution)/shard_map/ppermute | solution.py:124
  186.8 15.6 %collective-permute-start.184 = (bf16[128,640]{1,0:T(8,128)(2,1)}, bf16[128,640]{1,0:T(8,128)(2,1)S(1)}, u32[]{:S(2)}, u32[]{:S(2)}) collective-permute-start(bf16[128,640]{1,0:T(8,128)(2,1)} %get-tuple-element.326.refs_4_), channel_id=1, source_target_pairs={{96,1},{97,2},{98,3},{99,4},{100,5},{101,6},{102,7},{103,8},{104,9... | collective-permute-start | bytes 491528 | tf_op jit(solution)/shard_map/ppermute | solution.py:124
  234.0 19.9 %collective-permute-start.196 = (bf16[128,640]{1,0:T(8,128)(2,1)}, bf16[128,640]{1,0:T(8,128)(2,1)S(1)}, u32[]{:S(2)}, u32[]{:S(2)}) collective-permute-start(bf16[128,640]{1,0:T(8,128)(2,1)} %get-tuple-element.330.refs_4_), channel_id=1, source_target_pairs={{0,1},{1,2},{2,3},{3,4},{4,5},{5,6},{6,7},{7,8},{8,9},{9,10},{10,1... | collective-permute-start | bytes 491528 | tf_op jit(solution)/shard_map/ppermute | solution.py:124
  235.7 19.5 %collective-permute-start.197 = (bf16[128,640]{1,0:T(8,128)(2,1)}, bf16[128,640]{1,0:T(8,128)(2,1)S(1)}, u32[]{:S(2)}, u32[]{:S(2)}) collective-permute-start(bf16[128,640]{1,0:T(8,128)(2,1)} %get-tuple-element.330.refs_4_), channel_id=1, source_target_pairs={{32,1},{33,2},{34,3},{35,4},{36,5},{37,6},{38,7},{39,8},{40,9},{41... | collective-permute-start | bytes 491528 | tf_op jit(solution)/shard_map/ppermute | solution.py:124
  236.4 21.3 %collective-permute-start.198 = (bf16[128,640]{1,0:T(8,128)(2,1)}, bf16[128,640]{1,0:T(8,128)(2,1)S(1)}, u32[]{:S(2)}, u32[]{:S(2)}) collective-permute-start(bf16[128,640]{1,0:T(8,128)(2,1)} %get-tuple-element.330.refs_4_), channel_id=1, source_target_pairs={{64,1},{65,2},{66,3},{67,4},{68,5},{69,6},{70,7},{71,8},{72,9},{73... | collective-permute-start | bytes 491528 | tf_op jit(solution)/shard_map/ppermute | solution.py:124
  243.6 16.3 %collective-permute-start.199 = (bf16[128,640]{1,0:T(8,128)(2,1)}, bf16[128,640]{1,0:T(8,128)(2,1)S(1)}, u32[]{:S(2)}, u32[]{:S(2)}) collective-permute-start(bf16[128,640]{1,0:T(8,128)(2,1)} %get-tuple-element.330.refs_4_), channel_id=1, source_target_pairs={{96,1},{97,2},{98,3},{99,4},{100,5},{101,6},{102,7},{103,8},{104,9... | collective-permute-start | bytes 491528 | tf_op jit(solution)/shard_map/ppermute | solution.py:124
  244.9 15.1 %collective-permute-start.200 = (bf16[128,640]{1,0:T(8,128)(2,1)}, bf16[128,640]{1,0:T(8,128)(2,1)S(1)}, u32[]{:S(2)}, u32[]{:S(2)}) collective-permute-start(bf16[128,640]{1,0:T(8,128)(2,1)} %get-tuple-element.330.refs_4_), channel_id=1, source_target_pairs={{0,96},{1,97},{2,98},{3,99},{4,100},{5,101},{6,102},{7,103},{8,104... | collective-permute-start | bytes 491528 | tf_op jit(solution)/shard_map/ppermute | solution.py:117
  296.6 17.1 %collective-permute-start.214 = (bf16[128,960]{1,0:T(8,128)(2,1)S(1)}, bf16[128,960]{1,0:T(8,128)(2,1)S(1)}, u32[]{:S(2)}, u32[]{:S(2)}) collective-permute-start(bf16[128,960]{1,0:T(8,128)(2,1)S(1)} %multiply_convert_fusion.1.refs_0_), channel_id=1, source_target_pairs={{0,16},{16,0},{1,17},{17,1},{2,18},{18,2},{3,19},{19,3},{4,20},{20... | collective-permute-start | bytes 737288 | tf_op jit(solution)/shard_map/ppermute | solution.py:53
  354.8 326.8 %reduce-scatter.13.cloned.1.call-start = ((), (), s32[]{:S(2)}) async-start(), calls=%async_computation.16 | async-start | bytes 8355840 | tf_op jit(solution)/shard_map/reduce_scatter | solution.py:1101
  362.1 14.7 %collective-permute-start.224 = (bf16[128,960]{1,0:T(8,128)(2,1)S(1)}, bf16[128,960]{1,0:T(8,128)(2,1)S(1)}, u32[]{:S(2)}, u32[]{:S(2)}) collective-permute-start(bf16[128,960]{1,0:T(8,128)(2,1)S(1)} %add_convert_fusion.21), channel_id=1, source_target_pairs={{0,32},{32,64},{64,96},{96,0},{1,33},{33,65},{65,97},{97,1},{2,34}... | collective-permute-start | bytes 737288 | tf_op jit(solution)/shard_map/ppermute | solution.py:49
  411.1 16.4 %collective-permute-start.236 = (bf16[128,640]{1,0:T(8,128)(2,1)S(1)}, bf16[128,640]{1,0:T(8,128)(2,1)S(1)}, u32[]{:S(2)}, u32[]{:S(2)}) collective-permute-start(bf16[128,640]{1,0:T(8,128)(2,1)S(1)} %get-tuple-element.706), channel_id=1, source_target_pairs={{1,64},{2,65},{3,66},{4,67},{5,68},{6,69},{7,70},{8,71},{9,72},{10... | collective-permute-start | bytes 491528 | tf_op jit(solution)/shard_map/ppermute | solution.py:140
  412.4 17.1 %collective-permute-start.235 = (bf16[128,640]{1,0:T(8,128)(2,1)S(1)}, bf16[128,640]{1,0:T(8,128)(2,1)S(1)}, u32[]{:S(2)}, u32[]{:S(2)}) collective-permute-start(bf16[128,640]{1,0:T(8,128)(2,1)S(1)} %get-tuple-element.707), channel_id=1, source_target_pairs={{1,32},{2,33},{3,34},{4,35},{5,36},{6,37},{7,38},{8,39},{9,40},{10... | collective-permute-start | bytes 491528 | tf_op jit(solution)/shard_map/ppermute | solution.py:140
  413.1 20.8 %collective-permute-start.234 = (bf16[128,640]{1,0:T(8,128)(2,1)S(1)}, bf16[128,640]{1,0:T(8,128)(2,1)S(1)}, u32[]{:S(2)}, u32[]{:S(2)}) collective-permute-start(bf16[128,640]{1,0:T(8,128)(2,1)S(1)} %get-tuple-element.704), channel_id=1, source_target_pairs={{1,0},{2,1},{3,2},{4,3},{5,4},{6,5},{7,6},{8,7},{9,8},{10,9},{11,1... | collective-permute-start | bytes 491528 | tf_op jit(solution)/shard_map/ppermute | solution.py:140
  414.6 19.2 %collective-permute-start.232 = (bf16[128,640]{1,0:T(8,128)(2,1)S(1)}, bf16[128,640]{1,0:T(8,128)(2,1)S(1)}, u32[]{:S(2)}, u32[]{:S(2)}) collective-permute-start(bf16[128,640]{1,0:T(8,128)(2,1)S(1)} %get-tuple-element.702), channel_id=1, source_target_pairs={{32,0},{64,32},{96,64},{33,1},{65,33},{97,65},{34,2},{66,34},{98,6... | collective-permute-start | bytes 491528 | tf_op jit(solution)/shard_map/ppermute | solution.py:134
  487.2 30.4 %collective-permute-start.268 = (bf16[128,1280]{1,0:T(8,128)(2,1)S(1)}, bf16[128,1280]{1,0:T(8,128)(2,1)S(1)}, u32[]{:S(2)}, u32[]{:S(2)}) collective-permute-start(bf16[128,1280]{1,0:T(8,128)(2,1)S(1)} %constant_dynamic-slice_fusion.11), channel_id=1, source_target_pairs={{0,16},{16,0},{1,17},{17,1},{2,18},{18,2},{3,19},{19,3},{4,20},{20... | collective-permute-start | bytes 983048 | tf_op jit(solution)/shard_map/ppermute | solution.py:53
  492.3 25.2 %collective-permute-start.269 = (bf16[128,960]{1,0:T(8,128)(2,1)S(1)}, bf16[128,960]{1,0:T(8,128)(2,1)}, u32[]{:S(2)}, u32[]{:S(2)}) collective-permute-start(bf16[128,960]{1,0:T(8,128)(2,1)S(1)} %copy-done.93), channel_id=1, source_target_pairs={{0,16},{16,0},{1,17},{17,1},{2,18},{18,2},{3,19},{19,3},{4,20},{20... | collective-permute-start | bytes 737288 | tf_op jit(solution)/shard_map/ppermute | solution.py:53
  493.4 25.0 %collective-permute-start.263 = (bf16[128,1280]{1,0:T(8,128)(2,1)S(1)}, bf16[128,1280]{1,0:T(8,128)(2,1)S(1)}, u32[]{:S(2)}, u32[]{:S(2)}) collective-permute-start(bf16[128,1280]{1,0:T(8,128)(2,1)S(1)} %constant_dynamic-slice_fusion.14), channel_id=1, source_target_pairs={{0,16},{16,0},{1,17},{17,1},{2,18},{18,2},{3,19},{19,3},{4,20},{20... | collective-permute-start | bytes 983048 | tf_op jit(solution)/shard_map/ppermute | solution.py:53
  493.4 24.8 %collective-permute-start.264 = (bf16[128,960]{1,0:T(8,128)(2,1)}, bf16[128,960]{1,0:T(8,128)(2,1)S(1)}, u32[]{:S(2)}, u32[]{:S(2)}) collective-permute-start(bf16[128,960]{1,0:T(8,128)(2,1)} %get-tuple-element.404.refs_13_), channel_id=1, source_target_pairs={{0,16},{16,0},{1,17},{17,1},{2,18},{18,2},{3,19},{19,3},{4,20},{20... | collective-permute-start | bytes 737288 | tf_op jit(solution)/shard_map/ppermute | solution.py:53
  496.4 22.4 %collective-permute-start.259 = (bf16[128,960]{1,0:T(8,128)(2,1)}, bf16[128,960]{1,0:T(8,128)(2,1)}, u32[]{:S(2)}, u32[]{:S(2)}) collective-permute-start(bf16[128,960]{1,0:T(8,128)(2,1)} %get-tuple-element.399.refs_3_), channel_id=1, source_target_pairs={{0,16},{16,0},{1,17},{17,1},{2,18},{18,2},{3,19},{19,3},{4,20},{20... | collective-permute-start | bytes 737288 | tf_op jit(solution)/shard_map/ppermute | solution.py:53
  521.0 15.6 %collective-permute-start.261 = (bf16[128,1280]{1,0:T(8,128)(2,1)S(1)}, bf16[128,1280]{1,0:T(8,128)(2,1)S(1)}, u32[]{:S(2)}, u32[]{:S(2)}) collective-permute-start(bf16[128,1280]{1,0:T(8,128)(2,1)S(1)} %copy-done.71), channel_id=1, source_target_pairs={{0,16},{16,0},{1,17},{17,1},{2,18},{18,2},{3,19},{19,3},{4,20},{20... | collective-permute-start | bytes 983048 | tf_op jit(solution)/shard_map/ppermute | solution.py:53
  521.5 15.1 %collective-permute-start.262 = (bf16[128,1280]{1,0:T(8,128)(2,1)S(1)}, bf16[128,1280]{1,0:T(8,128)(2,1)S(1)}, u32[]{:S(2)}, u32[]{:S(2)}) collective-permute-start(bf16[128,1280]{1,0:T(8,128)(2,1)S(1)} %constant_dynamic-slice_fusion.15), channel_id=1, source_target_pairs={{0,16},{16,0},{1,17},{17,1},{2,18},{18,2},{3,19},{19,3},{4,20},{20... | collective-permute-start | bytes 983048 | tf_op jit(solution)/shard_map/ppermute | solution.py:53
  521.6 15.1 %collective-permute-start.266 = (bf16[128,1280]{1,0:T(8,128)(2,1)S(1)}, bf16[128,1280]{1,0:T(8,128)(2,1)S(1)}, u32[]{:S(2)}, u32[]{:S(2)}) collective-permute-start(bf16[128,1280]{1,0:T(8,128)(2,1)S(1)} %constant_dynamic-slice_fusion.13), channel_id=1, source_target_pairs={{0,16},{16,0},{1,17},{17,1},{2,18},{18,2},{3,19},{19,3},{4,20},{20... | collective-permute-start | bytes 983048 | tf_op jit(solution)/shard_map/ppermute | solution.py:53
  522.0 14.7 %collective-permute-start.267 = (bf16[128,1280]{1,0:T(8,128)(2,1)S(1)}, bf16[128,1280]{1,0:T(8,128)(2,1)S(1)}, u32[]{:S(2)}, u32[]{:S(2)}) collective-permute-start(bf16[128,1280]{1,0:T(8,128)(2,1)S(1)} %constant_dynamic-slice_fusion.12), channel_id=1, source_target_pairs={{0,16},{16,0},{1,17},{17,1},{2,18},{18,2},{3,19},{19,3},{4,20},{20... | collective-permute-start | bytes 983048 | tf_op jit(solution)/shard_map/ppermute | solution.py:53
  560.6 20.7 %collective-permute-start.253 = (bf16[128,640]{1,0:T(8,128)(2,1)S(1)}, bf16[128,640]{1,0:T(8,128)(2,1)S(1)}, u32[]{:S(2)}, u32[]{:S(2)}) collective-permute-start(bf16[128,640]{1,0:T(8,128)(2,1)S(1)} %get-tuple-element.693), channel_id=1, source_target_pairs={{1,32},{2,33},{3,34},{4,35},{5,36},{6,37},{7,38},{8,39},{9,40},{10... | collective-permute-start | bytes 491528 | tf_op jit(solution)/shard_map/ppermute | solution.py:140
  561.3 27.2 %collective-permute-start.252 = (bf16[128,640]{1,0:T(8,128)(2,1)S(1)}, bf16[128,640]{1,0:T(8,128)(2,1)S(1)}, u32[]{:S(2)}, u32[]{:S(2)}) collective-permute-start(bf16[128,640]{1,0:T(8,128)(2,1)S(1)} %get-tuple-element.690), channel_id=1, source_target_pairs={{1,0},{2,1},{3,2},{4,3},{5,4},{6,5},{7,6},{8,7},{9,8},{10,9},{11,1... | collective-permute-start | bytes 491528 | tf_op jit(solution)/shard_map/ppermute | solution.py:140
  562.7 27.7 %collective-permute-start.250 = (bf16[128,640]{1,0:T(8,128)(2,1)S(1)}, bf16[128,640]{1,0:T(8,128)(2,1)S(1)}, u32[]{:S(2)}, u32[]{:S(2)}) collective-permute-start(bf16[128,640]{1,0:T(8,128)(2,1)S(1)} %get-tuple-element.688), channel_id=1, source_target_pairs={{32,0},{64,32},{96,64},{33,1},{65,33},{97,65},{34,2},{66,34},{98,6... | collective-permute-start | bytes 491528 | tf_op jit(solution)/shard_map/ppermute | solution.py:134
  567.2 23.2 %collective-permute-start.249 = (bf16[128,640]{1,0:T(8,128)(2,1)S(1)}, bf16[128,640]{1,0:T(8,128)(2,1)S(1)}, u32[]{:S(2)}, u32[]{:S(2)}) collective-permute-start(bf16[128,640]{1,0:T(8,128)(2,1)S(1)} %get-tuple-element.689), channel_id=1, source_target_pairs={{64,0},{96,32},{65,1},{97,33},{66,2},{98,34},{67,3},{99,35},{68,4}... | collective-permute-start | bytes 491528 | tf_op jit(solution)/shard_map/ppermute | solution.py:134
  571.7 18.7 %collective-permute-start.248 = (bf16[128,640]{1,0:T(8,128)(2,1)S(1)}, bf16[128,640]{1,0:T(8,128)(2,1)S(1)}, u32[]{:S(2)}, u32[]{:S(2)}) collective-permute-start(bf16[128,640]{1,0:T(8,128)(2,1)S(1)} %get-tuple-element.687), channel_id=1, source_target_pairs={{96,0},{97,1},{98,2},{99,3},{100,4},{101,5},{102,6},{103,7},{104,8... | collective-permute-start | bytes 491528 | tf_op jit(solution)/shard_map/ppermute | solution.py:134
  581.4 21.3 %collective-permute-start.284 = (bf16[128,640]{1,0:T(8,128)(2,1)S(1)}, bf16[128,640]{1,0:T(8,128)(2,1)S(1)}, u32[]{:S(2)}, u32[]{:S(2)}) collective-permute-start(bf16[128,640]{1,0:T(8,128)(2,1)S(1)} %copy-done.164), channel_id=1, source_target_pairs={{0,16},{16,0},{1,17},{17,1},{2,18},{18,2},{3,19},{19,3},{4,20},{20... | collective-permute-start | bytes 491528 | tf_op jit(solution)/shard_map/ppermute | solution.py:53
  599.5 17.7 %collective-permute-start.305 = (bf16[128,960]{1,0:T(8,128)(2,1)S(1)}, bf16[128,960]{1,0:T(8,128)(2,1)S(1)}, u32[]{:S(2)}, u32[]{:S(2)}) collective-permute-start(bf16[128,960]{1,0:T(8,128)(2,1)S(1)} %convert_element_type.881.refs_0_), channel_id=1, source_target_pairs={{0,96},{32,0},{64,32},{96,64},{1,97},{33,1},{65,33},{97,65},{2,98}... | collective-permute-start | bytes 737288 | tf_op jit(solution)/shard_map/ppermute | solution.py:49
  599.6 38.8 %collective-permute-start.306 = (bf16[128,960]{1,0:T(8,128)(2,1)S(1)}, bf16[128,960]{1,0:T(8,128)(2,1)S(1)}, u32[]{:S(2)}, u32[]{:S(2)}) collective-permute-start(bf16[128,960]{1,0:T(8,128)(2,1)S(1)} %convert_element_type.881.refs_0_), channel_id=1, source_target_pairs={{0,64},{32,96},{64,0},{96,32},{1,65},{33,97},{65,1},{97,33},{2,66}... | collective-permute-start | bytes 737288 | tf_op jit(solution)/shard_map/ppermute | solution.py:49
  615.0 19.7 %collective-permute-start.293 = (bf16[352,448]{1,0:T(8,128)(2,1)S(1)}, bf16[352,448]{1,0:T(8,128)(2,1)S(1)}, u32[]{:S(2)}, u32[]{:S(2)}) collective-permute-start(bf16[352,448]{1,0:T(8,128)(2,1)S(1)} %get-tuple-element.684), channel_id=1, source_target_pairs={{0,32},{32,64},{64,96},{96,0},{1,33},{33,65},{65,97},{97,1},{2,34}... | collective-permute-start | bytes 946184 | tf_op jit(solution)/shard_map/ppermute | solution.py:49
  617.2 27.1 %collective-permute-start.307 = (bf16[128,960]{1,0:T(8,128)(2,1)S(1)}, bf16[128,960]{1,0:T(8,128)(2,1)S(1)}, u32[]{:S(2)}, u32[]{:S(2)}) collective-permute-start(bf16[128,960]{1,0:T(8,128)(2,1)S(1)} %convert_element_type.881.refs_0_), channel_id=1, source_target_pairs={{0,32},{32,64},{64,96},{96,0},{1,33},{33,65},{65,97},{97,1},{2,34}... | collective-permute-start | bytes 737288 | tf_op jit(solution)/shard_map/ppermute | solution.py:49
  623.4 22.6 %collective-permute-start.308 = (bf16[128,960]{1,0:T(8,128)(2,1)S(1)}, bf16[128,960]{1,0:T(8,128)(2,1)S(1)}, u32[]{:S(2)}, u32[]{:S(2)}) collective-permute-start(bf16[128,960]{1,0:T(8,128)(2,1)S(1)} %convert_element_type.881.refs_0_), channel_id=1, source_target_pairs={{0,16},{16,0},{1,17},{17,1},{2,18},{18,2},{3,19},{19,3},{4,20},{20... | collective-permute-start | bytes 737288 | tf_op jit(solution)/shard_map/ppermute | solution.py:53
  625.7 37.6 %collective-permute-start.289 = (bf16[4,112,512]{2,1,0:T(8,128)(2,1)}, bf16[4,112,512]{2,1,0:T(8,128)(2,1)}, u32[]{:S(2)}, u32[]{:S(2)}) collective-permute-start(bf16[4,112,512]{2,1,0:T(8,128)(2,1)} %get-tuple-element.678), channel_id=1, source_target_pairs={{0,12},{4,0},{8,4},{12,8},{1,13},{5,1},{9,5},{13,9},{2,14},{6,2},{... | collective-permute-start | bytes 1376264 | tf_op jit(solution)/shard_map/ppermute | solution.py:49
  638.4 26.3 %collective-permute-start.288 = (bf16[4,112,512]{2,1,0:T(8,128)(2,1)}, bf16[4,112,512]{2,1,0:T(8,128)(2,1)}, u32[]{:S(2)}, u32[]{:S(2)}) collective-permute-start(bf16[4,112,512]{2,1,0:T(8,128)(2,1)} %get-tuple-element.679), channel_id=1, source_target_pairs={{0,8},{4,12},{8,0},{12,4},{1,9},{5,13},{9,1},{13,5},{2,10},{6,14},... | collective-permute-start | bytes 1376264 | tf_op jit(solution)/shard_map/ppermute | solution.py:49
  644.3 21.3 %collective-permute-start.287 = (bf16[4,112,512]{2,1,0:T(8,128)(2,1)}, bf16[4,112,512]{2,1,0:T(8,128)(2,1)}, u32[]{:S(2)}, u32[]{:S(2)}) collective-permute-start(bf16[4,112,512]{2,1,0:T(8,128)(2,1)} %get-tuple-element.677), channel_id=1, source_target_pairs={{0,4},{4,8},{8,12},{12,0},{1,5},{5,9},{9,13},{13,1},{2,6},{6,10},{... | collective-permute-start | bytes 1376264 | tf_op jit(solution)/shard_map/ppermute | solution.py:49
  648.0 23.3 %collective-permute-start.298 = (bf16[112,448]{1,0:T(8,128)(2,1)}, bf16[112,448]{1,0:T(8,128)(2,1)}, u32[]{:S(2)}, u32[]{:S(2)}) collective-permute-start(bf16[112,448]{1,0:T(8,128)(2,1)} %get-tuple-element.719), channel_id=1, source_target_pairs={{0,12},{4,0},{8,4},{12,8},{1,13},{5,1},{9,5},{13,9},{2,14},{6,2},{... | collective-permute-start | bytes 301064 | tf_op jit(solution)/shard_map/ppermute | solution.py:49
  650.4 21.6 %collective-permute-start.297 = (bf16[112,448]{1,0:T(8,128)(2,1)}, bf16[112,448]{1,0:T(8,128)(2,1)}, u32[]{:S(2)}, u32[]{:S(2)}) collective-permute-start(bf16[112,448]{1,0:T(8,128)(2,1)} %get-tuple-element.720), channel_id=1, source_target_pairs={{0,8},{4,12},{8,0},{12,4},{1,9},{5,13},{9,1},{13,5},{2,10},{6,14},... | collective-permute-start | bytes 301064 | tf_op jit(solution)/shard_map/ppermute | solution.py:49
  657.0 21.9 %all-to-all-start.3 = ((bf16[16,24,960]{2,1,0:T(8,128)(2,1)}), bf16[16,24,960]{2,1,0:T(8,128)(2,1)S(1)}, u32[]{:S(2)}, u32[]{:S(2)}) async-start(bf16[16,24,960]{2,1,0:T(8,128)(2,1)} %bitcast.411), calls=%async_computation.6 | async-start | bytes 1572864 | tf_op jit(solution)/shard_map/all_to_all | solution.py:1164
  (277 other events, 2083.7 us)
Sparse Core Ops, SparseCore 0:
  26.6 49.7 all-gather.12
  79.5 78.3 all-gather.14
  160.2 104.6 all-gather.16
  354.9 103.6 reduce-scatter.14
  549.6 95.3 reduce-scatter.12

commit v5 on v4

--- a/solution.py
+++ b/solution.py
@@ -58,19 +58,15 @@
     return near + [swap(part) for part in near]
 
 
-def scatter_group(blocks):
+def scatter_group(blocks, other=None):
     half = [near.astype(FLOAT) + swap(far).astype(FLOAT) for near, far in zip(blocks[:4], blocks[4:])]
     total = half[0]
+    sent = [part.astype(BFLOAT) for part in half[1:]]
+    if other is not None:
+        *sent, other = tie(*sent, other)
     for k in (1, 2, 3):
-        total = total + shift(half[k].astype(BFLOAT), "z", k).astype(FLOAT)
-    return total
-
-
-def sum_all(value):
-    value = value + swap(value)
-    for axis in ("z", "y", "x"):
-        value = value + shift(value, axis, 1) + shift(value, axis, 2) + shift(value, axis, 3)
-    return value
+        total = total + shift(sent[k - 1], "z", k).astype(FLOAT)
+    return total if other is None else (total, other)
 
 
 def rms_scale(values, weight):
@@ -233,7 +229,7 @@
         cost_estimate=pl.CostEstimate(
             flops=12_000_000_000, bytes_accessed=5_000_000, transcendentals=4_000_000
         ),
-        compiler_params=params(BIG),
+        compiler_params=params(24),
     )(queries, *pairs, bias)
 
 
@@ -278,7 +274,7 @@
         cost_estimate=pl.CostEstimate(
             flops=20_000_000_000, bytes_accessed=9_000_000, transcendentals=4_000_000
         ),
-        compiler_params=params(BIG),
+        compiler_params=params(24),
     )(queries, *pairs, bias, log_total, attended, grads, cosine, sine)
 
 
@@ -311,7 +307,7 @@
     return pl.pallas_call(
         spread_kernel,
         out_shape=[struct(BFLOAT, TOK_DEV, D)] * MP,
-        compiler_params=params(BIG),
+        compiler_params=params(24),
     )(place, rows)
 
 
@@ -327,7 +323,7 @@
 
 def collect(place, blocks):
     return pl.pallas_call(
-        collect_kernel, out_shape=struct(BFLOAT, DP * CAP, D), compiler_params=params(BIG)
+        collect_kernel, out_shape=struct(BFLOAT, DP * CAP, D), compiler_params=params(24)
     )(place, *blocks)
 
 
@@ -336,7 +332,7 @@
 
 
 def enter(hidden, gains, wq, wk, wv, cosine, sine):
-    return pl.pallas_call(enter_kernel, out_shape=PROJECTED, compiler_params=params(BIG))(
+    return pl.pallas_call(enter_kernel, out_shape=PROJECTED, compiler_params=params(24))(
         hidden, gains, wq, wk, wv, cosine, sine
     )
 
@@ -567,7 +563,7 @@
             struct(FLOAT, TOK_DEV, D),
             struct(FLOAT, 8, D),
         ),
-        compiler_params=params(BIG),
+        compiler_params=params(24),
     )(grad_in, dq, own, hidden, gains, wq, wk, wv, cosine, sine)
 
 
@@ -743,8 +739,8 @@
 
 def pack_grad_kernel(starts_ref, *refs):
     wq_ref, wo_ref, rows_ref = refs[:3]
-    ins = refs[3:-3]
-    left_ref, right_ref, buf = refs[-3:]
+    ins = refs[3:-2]
+    out_ref, buf = refs[-2:]
     buf[0:960, :] = wq_ref[...]
     buf[1600:2560, :] = wo_ref[...]
     buf[2560:2576, :] = rows_ref[...].astype(BFLOAT)
@@ -761,8 +757,7 @@
         buf[1280:1600, 320 * i : 320 * i + 320] = rows[:, 320:640]
     for i in range(4):
         start = pl.multiple_of(starts_ref[i], 16)
-        left_ref[i] = buf[pl.ds(start, 352), 0:512]
-        right_ref[i] = buf[pl.ds(start, 352), 512:960]
+        out_ref[i] = buf[pl.ds(start, 352), :]
 
 
 def pack_grads(starts, wq, wo, small, kept, received):
@@ -775,8 +770,8 @@
         grid=(1,),
         in_specs=[pl.BlockSpec(memory_space=pltpu.SMEM), whole(D, D), whole(D, D), whole(16, D)]
         + specs * RECUR,
-        out_specs=[whole(4, 352, 512), whole(4, 352, 448)],
-        out_shape=(struct(BFLOAT, 4, 352, 512), struct(BFLOAT, 4, 352, 448)),
+        out_specs=whole(4, 352, D),
+        out_shape=struct(BFLOAT, 4, 352, D),
         scratch_shapes=[pltpu.VMEM((PACK_PAD, D), BFLOAT)],
         compiler_params=params(BIG),
     )(starts, wq, wo, small, *args)
@@ -798,27 +793,43 @@
     return (1283 * device) // 64
 
 
-def join_kernel(blocks_ref, out_ref):
-    step = pl.program_id(0)
-    first = jnp.minimum((step * (128 * 64)) // 1283, 118)
-    first = (first // 2) * 2
-    window = blocks_ref[pl.ds(pl.multiple_of(first * 24, 48), 240), :]
-    row = step * 128 + lax.broadcasted_iota(jnp.int32, (128, 240), 0)
+def join_kernel(blocks_ref, wq_ref, wk_ref, wv_ref, wo_ref, small_ref, buf):
+    row = lax.broadcasted_iota(jnp.int32, (128, 240), 0)
     place = lax.broadcasted_iota(jnp.int32, (128, 240), 1)
     device = (place * 2731) >> 16
-    source = ((1283 * (first + device)) >> 6) + place - 24 * device
-    chosen = (source == row).astype(FLOAT).astype(BFLOAT)
-    out_ref[...] = jnp.dot(chosen, window, preferred_element_type=FLOAT).astype(BFLOAT)
+    for step in range(PACK_PAD // 128):
+        first = min(step * 128 * 64 // 1283, 118) // 2 * 2
+        source = ((1283 * (first + device)) >> 6) + place - 24 * device
+        chosen = (source == row + 128 * step).astype(FLOAT).astype(BFLOAT)
+        buf[128 * step : 128 * step + 128, :] = nn(
+            chosen, blocks_ref[24 * first : 24 * first + 240, :]
+        ).astype(BFLOAT)
+    wq_ref[...] = buf[0:960, :]
+    wo_ref[...] = buf[1600:2560, :]
+    small_ref[...] = buf[2560:2576, :]
+    line = lax.broadcasted_iota(jnp.int32, (960, 320), 0)
+    place = lax.broadcasted_iota(jnp.int32, (960, 320), 1)
+    for first, ref in ((960, wk_ref), (1280, wv_ref)):
+        total = None
+        for i in range(3):
+            chosen = (line == 3 * place + i).astype(FLOAT).astype(BFLOAT)
+            part = nn(chosen, buf[first : first + 320, 320 * i : 320 * i + 320])
+            total = part if total is None else total + part
+        ref[...] = total.astype(BFLOAT)
 
 
 def join_pack(blocks):
     return pl.pallas_call(
         join_kernel,
-        grid=(PACK_PAD // 128,),
-        in_specs=[pl.BlockSpec((128 * 24, D), lambda i: (0, 0))],
-        out_specs=pl.BlockSpec((128, D), lambda i: (i, 0)),
-        out_shape=jax.ShapeDtypeStruct((PACK_PAD, D), BFLOAT),
-        compiler_params=pltpu.CompilerParams(vmem_limit_bytes=32 * 1024 * 1024),
+        out_shape=(
+            struct(BFLOAT, D, D),
+            struct(BFLOAT, D, 320),
+            struct(BFLOAT, D, 320),
+            struct(BFLOAT, D, D),
+            struct(BFLOAT, 16, D),
+        ),
+        scratch_shapes=[pltpu.VMEM((PACK_PAD, D), BFLOAT)],
+        compiler_params=params(32),
     )(blocks)
 
 
@@ -827,13 +838,6 @@
     for k in (1, 2, 3):
         sent = lax.dynamic_index_in_dim(value, (index + k) % 4, 0, False)
         total = total + shift(sent, axis, k).astype(FLOAT)
-    return total
-
-
-def stage_near(value, axis):
-    total = value[0].astype(FLOAT)
-    for k in (1, 2, 3):
-        total = total + shift(value[k], axis, -k).astype(FLOAT)
     return total
 
 
@@ -864,21 +868,18 @@
     pack_block = lax.dynamic_update_slice(
         jnp.zeros((24 * D,), BFLOAT), pack_master.astype(BFLOAT), (pack_offset,)
     ).reshape(24, D)
-    own = jnp.concatenate([pack_block, mlp_master.astype(BFLOAT).reshape(3 * UNITS, D)], axis=0)
-    ring = [own] + [shift(own, "z", k) for k in (1, 2, 3)]
-    pack_quad = []
+    pack_quad = [pack_block] + [shift(pack_block, "x", k) for k in (1, 2, 3)]
+    pack_rows = []
     for i in range(4):
-        part = ring[3][:24]
+        part = pack_quad[3]
         for k in (2, 1, 0):
-            part = jnp.where(z == (i + k) % 4, ring[k][:24], part)
-        pack_quad.append(part)
-    pack_quad = jnp.concatenate(pack_quad, axis=0)
-    mlp_quad = jnp.concatenate([part[24:].reshape(3, UNITS, D) for part in ring], axis=1)
-    near_axes = ("core", "y", "x")
-    pack_blocks = lax.all_gather(pack_quad, near_axes, axis=0, tiled=True)
-    pack_blocks = (
-        pack_blocks.reshape(2, DP, 4, 24, D).transpose(2, 0, 1, 3, 4).reshape(128 * 24, D)
-    )
+            part = jnp.where(x == (i + k) % 4, pack_quad[k], part)
+        pack_rows.append(part)
+    pack_blocks = lax.all_gather(
+        jnp.concatenate(pack_rows, axis=0), ("z", "core", "y"), axis=0, tiled=True
+    )
+    mlp_own = mlp_master.astype(BFLOAT)
+    mlp_quad = jnp.concatenate([mlp_own] + [shift(mlp_own, "x", k) for k in (1, 2, 3)], axis=1)
 
     group_ids = token_ids[0]
     near_ids = reorder(group_ids.reshape(MP, TOK_DEV), near).reshape(-1)
@@ -911,7 +912,9 @@
         request[:, :CAP].reshape(-1)[:, None] == jnp.arange(VOCAB_DEV, dtype=FLOAT)[None, :]
     ).astype(BFLOAT)
     mlp_quad, owner_hot = tie(mlp_quad, owner_hot)
-    mlp_weights = lax.all_gather(mlp_quad.reshape(3 * 80, D), near_axes, axis=0, tiled=True)
+    mlp_weights = lax.all_gather(
+        mlp_quad.reshape(3 * 80, D), ("core", "z", "y"), axis=0, tiled=True
+    )
     mlp_weights = mlp_weights.reshape(32, 3, 80, D)
     asked_rows = lax.all_to_all(mm(owner_hot, own_table).astype(BFLOAT), DP_AXES, 0, 0, tiled=True)
     own_table, asked_rows = tie(own_table, asked_rows)
@@ -922,15 +925,12 @@
         looked = [looked[128 * i : 128 * i + 128] for i in range(MP)]
     else:
         looked = spread(token_place, asked_rows)
-    hidden = scatter_group(looked)
-
-    pack_weights = join_pack(pack_blocks)
-    w_query = pack_weights[:960]
-    w_key = pack_weights[960:1280].reshape(D, KV_HEADS * HEAD_DIM)
-    w_value = pack_weights[1280:1600].reshape(D, KV_HEADS * HEAD_DIM)
-    w_out = pack_weights[1600:2560]
-    gains = jnp.concatenate([pack_weights[2560:2563].astype(FLOAT), jnp.zeros((5, D), FLOAT)])
-    router = pack_weights[2563:2566].astype(FLOAT)
+    hidden, pack_blocks = scatter_group(looked, pack_blocks)
+
+    w_query, w_key, w_value, w_out, last_rows = join_pack(pack_blocks)
+    gains = jnp.concatenate([last_rows[:3].astype(FLOAT), jnp.zeros((5, D), FLOAT)])
+    router = last_rows[3:6].astype(FLOAT)
+
     half_dim = HEAD_DIM // 2
     freqs = ROPE_BASE ** (-jnp.arange(half_dim, dtype=FLOAT) / half_dim)
     first_row = data_index * ROWS + model_index * TOK_DEV
@@ -1099,7 +1099,7 @@
         if step == 0:
             mlp_half = mlp_grads(core.astype(jnp.int32), mlp_kept, mlp_far)
             mlp_sum = lax.psum_scatter(
-                mlp_half.reshape(16 * 240, D), DP_AXES, scatter_dimension=0, tiled=True
+                mlp_half.reshape(16 * 240, D), ("z", "y"), scatter_dimension=0, tiled=True
             )
             squares = square_grads(square_kept, square_far)
             grad_own, mlp_half, *squares = tie(grad_own, mlp_half, *squares)
@@ -1126,7 +1126,7 @@
     )
     small = small + swap(small)
     starts = jnp.stack([aligned_row(DP * (2 * i + core)) for i in range(4)]).astype(jnp.int32)
-    left, right = pack_grads(starts, *squares, small, pack_kept, pack_far)
+    part = pack_grads(starts, *squares, small, pack_kept, pack_far)
 
     def y_windows(value):
         return jnp.stack([value[..., 80 * i : 80 * i + 112, :] for i in range(4)])
@@ -1134,18 +1134,22 @@
     def x_windows(value):
         return jnp.stack([value[..., i : i + 48, :] for i in (0, 16, 40, 56)])
 
-    left = stage(y_windows(left), "y", y).astype(BFLOAT)
-    right = stage(right, "z", z).astype(BFLOAT)
-    left = stage(left, "z", z).astype(BFLOAT)
-    right = stage(y_windows(right), "y", y).astype(BFLOAT)
-    part = jnp.concatenate([left, right], axis=-1)
-    part, mlp_sum = tie(part, mlp_sum)
-    part = stage(x_windows(part), "x", x).reshape(-1)
+    part = stage(part, "z", z).astype(BFLOAT)
+    part = stage(y_windows(part), "y", y).astype(BFLOAT)
+    part, mlp_sum = tie(x_windows(part), mlp_sum)
+    mlp_sum = mlp_sum.reshape(3, 4, UNITS, D).transpose(1, 0, 2, 3).reshape(4, 3 * UNITS, D)
+
+    def toward(k):
+        mine = lax.dynamic_index_in_dim(part, (x + k) % 4, 0, False)
+        return jnp.concatenate([mine, mlp_sum[(4 - k) % 4]], axis=0)
+
+    total = toward(0).astype(FLOAT)
+    for k in (1, 2, 3):
+        total = total + shift(toward(k), "x", k).astype(FLOAT)
+    part = total[:48].reshape(-1)
+    mlp_grad = total[48:].reshape(3, UNITS, D)
     begin = aligned_row(DP * model_index) + 80 * y + (20 * x) // 8 * 8
     pack_grad = lax.dynamic_slice(part, (PACK_DEV * device - D * begin,), (PACK_DEV,))
-
-    mlp_sum = mlp_sum.reshape(3, 4, UNITS, D).transpose(1, 0, 2, 3)
-    mlp_grad = stage_near(mlp_sum, "z")
 
     grad_embed = gather_group(grad_hidden.astype(BFLOAT))
     if dense:
@@ -1163,7 +1167,13 @@
         unique = collect(token_place, grad_embed)
         unique = lax.all_to_all(unique, DP_AXES, 0, 0, tiled=True)
         table_grad = head_grad.astype(FLOAT) + contract_rows(owner_hot, unique)
-    return pack_grad, mlp_grad, by_cols(table_grad), loss_part, flag
+    table_grad = by_cols(table_grad)
+    squares = (
+        jnp.sum(pack_grad * pack_grad)
+        + jnp.sum(mlp_grad * mlp_grad)
+        + jnp.sum(table_grad * table_grad)
+    )
+    return pack_grad, mlp_grad, table_grad, squares, loss_part, flag
 
 
 def shards(
@@ -1193,16 +1203,14 @@
         table_master,
     )
     *found, over = tie(*gradients(False, *args))
-    pack_grad, mlp_grad, table_grad, loss_part = lax.cond(
-        over > 0, lambda: gradients(True, *args)[:4], lambda: tuple(found)
-    )
-    squares = (
-        jnp.sum(pack_grad * pack_grad)
-        + jnp.sum(mlp_grad * mlp_grad)
-        + jnp.sum(table_grad * table_grad)
-    )
-    lane = lax.broadcasted_iota(jnp.int32, (1, 128), 1)
-    sums = sum_all(jnp.where(lane == 0, squares, loss_part))
+    pack_grad, mlp_grad, table_grad, squares, loss_part = lax.cond(
+        over > 0, lambda: gradients(True, *args)[:5], lambda: tuple(found)
+    )
+    lane = lax.broadcasted_iota(jnp.int32, (128, 128), 1)
+    sums = lax.all_to_all(
+        jnp.where(lane == 0, squares, loss_part), ALL_AXES, 0, 0, tiled=True
+    )
+    sums = jnp.sum(sums, axis=0, keepdims=True)
     total_squares = sums[0, 0]
     loss_sum = sums[0, 1]
     grad_norm = jnp.sqrt(total_squares)

time: 773 us -> 780 us (level)
  waiting for transfers between devices: 113 us -> 153 us
  local copies, waits for them, and re-layouts: 45.5 us -> 84.5 us
  Pallas kernels: 246 us -> 210 us
  starting transfers between devices: 234 us -> 215 us
  other arithmetic: 59.5 us -> 44.6 us
    unnamed x312 -> x475, local copies, waits for them, and re-layouts: 9.97 us -> 55.2 us
    ppermute x45 -> x30, waiting for transfers between devices: 63.8 us -> 101 us  [shift(): return lax.ppermute(value, axis, [(i, (i + steps) % 4) for i in range(4)])]
    ppermute x45 -> x30, starting transfers between devices: 72.9 us -> 46.5 us  [shift(): return lax.ppermute(value, axis, [(i, (i + steps) % 4) for i in range(4)])]
    ppermute x12, waiting for transfers between devices: 32 us -> 21.9 us  [group_scatter(): total = total + lax.ppermute(prev[k], ('z',) + DP_AXES, pairs).astype(FLOAT)]
    pallas_call x3, Pallas kernels: 41.6 us -> 31.5 us  [attend_back(): pl.pallas_call(attend_back_kernel, out_shape=(struct(BFLOAT, TOK_DEV, D),...]
    all_gather x2, waiting for transfers between devices: 0.01 us -> 9.99 us  [the longest x1 8.55 us: gradients(): lax.all_gather(mlp_quad.reshape(3 * 80, D), ('core', 'z', 'y'), axis=0, t...]
    pallas_call x3, Pallas kernels: 15 us -> 6.13 us  [enter_back(): pl.pallas_call(enter_back_kernel, out_shape=(struct(BFLOAT, TOK_DEV, 640)...]
    pallas_call x3, Pallas kernels: 35.3 us -> 26.5 us  [attend(): pl.pallas_call(attend_kernel, out_shape=(struct(BFLOAT, TOK_DEV, D), stru...]
  transfers between devices with their start and end apart: 172 -> 157, of which waited for: 47 -> 53; matrix products, arithmetic and copies ran while one was open for 10% -> 8% of each run, Pallas kernels for 27% -> 22%
where the time goes in v5:
time: 780 us; the launch traced here: 769 us
  starting transfers between devices  215 us (28%)
  Pallas kernels  210 us (27%)
  waiting for transfers between devices  153 us (20%)
  local copies, waits for them, and re-layouts  84.5 us (11%)
  other arithmetic  44.6 us (6%)
  blocking collectives  30.4 us (4%)
  between operations  23.4 us (3%)
    ppermute x30, waiting for transfers between devices, shift(): return lax.ppermute(value, axis, [(i, (i + steps) % 4) for i in range(4)])  101 us
    ppermute x78, starting transfers between devices, swap(): return lax.ppermute(value, 'core', [(0, 1), (1, 0)])  62.5 us
    unnamed x475, local copies, waits for them, and re-layouts  55.2 us
    ppermute x30, starting transfers between devices, shift(): return lax.ppermute(value, axis, [(i, (i + steps) % 4) for i in range(4)])  46.5 us
    pallas_call x3, Pallas kernels, block_back(): pl.pallas_call(block_back_kernel, grid=(FF_STEPS,), in_specs=[full, whole...  40.1 us
    pallas_call x3, Pallas kernels, block(): pl.pallas_call(functools.partial(block_kernel, more), grid=(FF_STEPS,), i...  38.3 us
    ppermute x12, starting transfers between devices, group_gather(): prev.append(lax.ppermute(pair, ('z',) + DP_AXES, pairs))  37.2 us
    pallas_call x3, Pallas kernels, attend_back(): pl.pallas_call(attend_back_kernel, out_shape=(struct(BFLOAT, TOK_DEV, D),...  31.5 us
  transfers between devices with their start and end apart: 157, of which 53 were waited for; matrix products, arithmetic and copies ran while one was open for 8% of the time, Pallas kernels for 22%

profile of v5, /device:TPU:1, one launch (start us, length us, event | category | flops | bytes accessed | tf_op | source)
XLA Modules:
  0.0 768.9 jit_solution(17121306673916792404)
XLA Ops:
  20.4 6.2 all-to-all-start.1
  38.9 14.9 %all_to_all.52 = bf16[16,24,960]{2,1,0:T(8,128)(2,1)S(1)} all-to-all(bf16[16,24,960]{2,1,0:T(8,128)(2,1)S(1)} %bitcast.327), channel_id=1, replica_groups=mesh['z'=4,'core'=2,'y'=4,'x'=4] {'y','x'}, dimensions={0} | all-to-all | bytes 1474560 | tf_op jit(solution)/shard_map/all_to_all | solution.py:919
  63.7 5.1 collective-permute-start.154
  81.3 4.6 shard_map.222
  86.3 6.6 collective-permute-done.160
  96.1 3.6 collective-permute-start.165
  99.7 3.4 collective-permute-start.166
  103.1 4.3 collective-permute-start.167
  117.7 5.3 collective-permute-start.173
  125.4 9.0 %shard_map.224 = (bf16[128,960]{1,0:T(8,128)(2,1)S(1)}, f32[8,384]{1,0:T(8,128)S(1)}) custom-call(bf16[960,128]{1,0:T(8,128)(2,1)S(1)} %get-tuple-element.335.query_ref, bf16[128,640]{1,0:T(8,128)(2,1)S(1)} %collective-permute-done.163.refs_0_, bf16[128,640]{1,0:T(8,128)(2,1)S(1)} %collective-permute-done.164.refs_1_, ...), custom_call_target="tpu_custom_call" | custom-call | flops 12000000000 | bytes 5000000 | tf_op jit(solution)/shard_map/pallas_call | solution.py:226
  142.7 8.6 %all-gather.15.cloned.1.call-done = bf16[7680,960]{1,0:T(8,128)(2,1)} async-done(((bf16[240,960]{1,0:T(8,128)(2,1)}), bf16[7680,960]{1,0:T(8,128)(2,1)}) %all-gather.15.cloned.1.call-update) | async-done | bytes 14745616 | tf_op jit(solution)/shard_map/all_gather | solution.py:915
  151.3 13.0 %shard_map.225 = (f32[128,960]{1,0:T(8,128)}, bf16[128,960]{1,0:T(8,128)(2,1)}, f32[128,2560]{1,0:T(8,128)}, f32[128,2560]{1,0:T(8,128)}, bf16[128,2560]{1,0:T(8...) custom-call(bf16[128,960]{1,0:T(8,128)(2,1)} %copy-done.34, ...), custom_call_target="tpu_custom_call" | custom-call | flops 4000000000 | bytes 20000000 | tf_op jit(solution)/shard_map/pallas_call | solution.py:402
  168.2 7.2 collective-permute-start.180
  176.7 6.2 collective-permute-start.182
  194.5 8.8 %shard_map.226 = (bf16[128,960]{1,0:T(8,128)(2,1)S(1)}, f32[8,384]{1,0:T(8,128)S(1)}) custom-call(bf16[960,128]{1,0:T(8,128)(2,1)S(1)} %copy-done.125, bf16[128,640]{1,0:T(8,128)(2,1)S(1)} %collective-permute-done.178.refs_0_, bf16[128,640]{1,0:T(8,128)(2,1)S(1)} %collective-permute-done.179.refs_1_, bf16[128,640]{1,0:T(8,128)(2,1)S(1)} %collective-permute-done.180.refs_2_, ...), custom_call_target="tpu_custom_call" | custom-call | flops 12000000000 | bytes 5000000 | tf_op jit(solution)/shard_map/pallas_call | solution.py:226
  204.2 13.3 %shard_map.227 = (f32[128,960]{1,0:T(8,128)}, bf16[128,960]{1,0:T(8,128)(2,1)}, f32[128,2560]{1,0:T(8,128)}, f32[128,2560]{1,0:T(8,128)}, bf16[128,2560]{1,0:T(8...) custom-call(bf16[128,960]{1,0:T(8,128)(2,1)} %copy-done.36, ...), custom_call_target="tpu_custom_call" | custom-call | flops 4000000000 | bytes 20000000 | tf_op jit(solution)/shard_map/pallas_call | solution.py:402
  217.5 5.5 collective-permute-start.193
  223.7 8.4 %collective-permute-start.195 = (bf16[128,640]{1,0:T(8,128)(2,1)}, bf16[128,640]{1,0:T(8,128)(2,1)S(1)}, u32[]{:S(2)}, u32[]{:S(2)}) collective-permute-start(bf16[128,640]{1,0:T(8,128)(2,1)} %get-tuple-element.346.refs_4_), channel_id=1, source_target_pairs={{64,1},{65,2},{66,3},{67,4},{68,5},{69,6},{70,7},{71,8},{72,9},{73... | collective-permute-start | bytes 491528 | tf_op jit(solution)/shard_map/ppermute | solution.py:120
  233.5 7.7 %collective-permute-start.197 = (bf16[128,640]{1,0:T(8,128)(2,1)}, bf16[128,640]{1,0:T(8,128)(2,1)S(1)}, u32[]{:S(2)}, u32[]{:S(2)}) collective-permute-start(bf16[128,640]{1,0:T(8,128)(2,1)} %get-tuple-element.346.refs_4_), channel_id=1, source_target_pairs={{0,96},{1,97},{2,98},{3,99},{4,100},{5,101},{6,102},{7,103},{8,104... | collective-permute-start | bytes 491528 | tf_op jit(solution)/shard_map/ppermute | solution.py:113
  252.7 8.8 %shard_map.228 = (bf16[128,960]{1,0:T(8,128)(2,1)S(1)}, f32[8,384]{1,0:T(8,128)S(1)}) custom-call(bf16[960,128]{1,0:T(8,128)(2,1)S(1)} %copy-done.129, bf16[128,640]{1,0:T(8,128)(2,1)S(1)} %collective-permute-done.193.refs_0_, bf16[128,640]{1,0:T(8,128)(2,1)S(1)} %collective-permute-done.194.refs_1_, bf16[128,640]{1,0:T(8,128)(2,1)S(1)} %collective-permute-done.195.refs_2_, ...), custom_call_target="tpu_custom_call" | custom-call | flops 12000000000 | bytes 5000000 | tf_op jit(solution)/shard_map/pallas_call | solution.py:226
  262.4 11.9 %shard_map.229 = (f32[128,960]{1,0:T(8,128)}, bf16[128,960]{1,0:T(8,128)(2,1)}, f32[128,2560]{1,0:T(8,128)}, f32[128,2560]{1,0:T(8,128)}, bf16[128,2560]{1,0:T(8...) custom-call(bf16[128,960]{1,0:T(8,128)(2,1)} %copy-done.39, ...), custom_call_target="tpu_custom_call" | custom-call | flops 4000000000 | bytes 20000000 | tf_op jit(solution)/shard_map/pallas_call | solution.py:402
  285.9 6.1 collective-permute-start.212
  300.0 13.4 %shard_map.230 = (f32[256,6144]{1,0:T(8,128)}, bf16[256,960]{1,0:T(8,128)(2,1)}, f32[8,256]{1,0:T(8,128)}) custom-call(s32[256,1]{1,0:T(8,128)} %copy.198.rows_ref, s32[1,1024]{1,0:T(1,128)} %bitcast.350, bf16[128,960]{1,0:T(8,128)(2,1)} %copy-done.338, bf16[128,960]{1,0:T(8,128)(2,1)} %copy-done.384, bf16[128,960]{1,0:T(8,128)(2,1)} %copy-done.385, ...), custom_call_target="tpu_custom_call" | custom-call | tf_op jit(solution)/shard_map/pallas_call | solution.py:607
  322.8 17.5 %shard_map.231 = (bf16[6144,960]{1,0:T(8,128)(2,1)}, bf16[128,960]{1,0:T(8,128)(2,1)}, bf16[128,960]{1,0:T(8,128)(2,1)}, bf16[128,960]{1,0:T(8,128)(2,1)}, bf16[...) custom-call(s32[256,1]{1,0:T(8,128)} %copy.198.rows_ref, ...), custom_call_target="tpu_custom_call" | custom-call | tf_op jit(solution)/shard_map/pallas_call | solution.py:656
  356.8 6.7 collective-permute-done.221
  366.7 13.9 %shard_map.232 = (bf16[128,960]{1,0:T(8,128)(2,1)}, bf16[128,2560]{1,0:T(8,128)(2,1)}, bf16[128,2560]{1,0:T(8,128)(2,1)}, f32[128,960]{1,0:T(8,128)}, bf16[128,9...) custom-call(f32[128,960]{1,0:T(8,128)} %multiply_subtract_fusion.2.new_ref, f32[128,1]{1,0:T(8,128)} %copy.195.sel_ref, ...), custom_call_target="tpu_custom_call" | custom-call | flops 4000000000 | bytes 20000000 | tf_op jit(solution)/shard_map/pallas_call | solution.py:501
  381.8 10.9 %shard_map.233 = (bf16[128,960]{1,0:T(8,128)(2,1)S(1)}, bf16[512,640]{1,0:T(8,128)(2,1)S(1)}, bf16[512,640]{1,0:T(8,128)(2,1)S(1)}, bf16[512,640]{1,0:T(8,128)(2,1)}, bf16[512,640]{1,0:T(8,128)(2,1)S(1)}) custom-call(bf16[960,128]{1,0:T(8,128)(2,1)S(1)} %copy-done.130, bf16[128,640]{1,0:T(8,128)(2,1)S(1)} %copy-done.266, bf16[128,640]{1,0:T(8,128)(2,1)S(1)} %copy-done.270, ...), custom_call_target="tpu_custom_call" | custom-call | flops 20000000000 | bytes 9000000 | tf_op jit(solution)/shard_map/pallas_call | solution.py:271
  404.1 4.6 collective-permute-done.234
  410.0 3.8 collective-permute-done.233
  415.8 3.9 collective-permute-done.231
  421.0 3.8 collective-permute-done.227
  428.0 13.3 %shard_map.235 = (bf16[128,960]{1,0:T(8,128)(2,1)}, bf16[128,2560]{1,0:T(8,128)(2,1)}, bf16[128,2560]{1,0:T(8,128)(2,1)}, f32[128,960]{1,0:T(8,128)}, bf16[128,9...) custom-call(f32[128,960]{1,0:T(8,128)} %copy-done.98, f32[128,1]{1,0:T(8,128)} %copy.194.sel_ref, ...), custom_call_target="tpu_custom_call" | custom-call | flops 4000000000 | bytes 20000000 | tf_op jit(solution)/shard_map/pallas_call | solution.py:501
  456.9 10.3 %shard_map.236 = (bf16[128,960]{1,0:T(8,128)(2,1)S(1)}, bf16[512,640]{1,0:T(8,128)(2,1)S(1)}, bf16[512,640]{1,0:T(8,128)(2,1)S(1)}, bf16[512,640]{1,0:T(8,128)(2,1)S(1)}, bf16[512,640]{1,0:T(8,128)(2,1)S(1)}) custom-call(bf16[960,128]{1,0:T(8,128)(2,1)S(1)} %copy-done.126, bf16[128,640]{1,0:T(8,128)(2,1)S(1)} %copy-done.206, ...), custom_call_target="tpu_custom_call" | custom-call | flops 20000000000 | bytes 9000000 | tf_op jit(solution)/shard_map/pallas_call | solution.py:271
  498.6 12.9 %shard_map.238 = (bf16[128,960]{1,0:T(8,128)(2,1)}, bf16[128,2560]{1,0:T(8,128)(2,1)}, bf16[128,2560]{1,0:T(8,128)(2,1)}, f32[128,960]{1,0:T(8,128)}, bf16[128,9...) custom-call(f32[128,960]{1,0:T(8,128)} %copy-done.96, f32[128,1]{1,0:T(8,128)} %copy.193.sel_ref, ...), custom_call_target="tpu_custom_call" | custom-call | flops 4000000000 | bytes 20000000 | tf_op jit(solution)/shard_map/pallas_call | solution.py:501
  532.3 10.3 %shard_map.239 = (bf16[128,960]{1,0:T(8,128)(2,1)S(1)}, bf16[512,640]{1,0:T(8,128)(2,1)S(1)}, bf16[512,640]{1,0:T(8,128)(2,1)S(1)}, bf16[512,640]{1,0:T(8,128)(2,1)S(1)}, bf16[512,640]{1,0:T(8,128)(2,1)S(1)}) custom-call(bf16[960,128]{1,0:T(8,128)(2,1)S(1)} %copy-done.120, bf16[128,640]{1,0:T(8,128)(2,1)S(1)} %copy-done.136, ...), custom_call_target="tpu_custom_call" | custom-call | flops 20000000000 | bytes 9000000 | tf_op jit(solution)/shard_map/pallas_call | solution.py:271
  544.6 11.7 %shard_map.240 = bf16[16,3,80,960]{3,2,1,0:T(8,128)(2,1)} custom-call(s32[1]{0:T(128)} %bitcast.131.which_ref, bf16[128,2560]{1,0:T(8,128)(2,1)} %get-tuple-element.412.refs_0_, bf16[128,2560]{1,0:T(8,128)(2,1)} %get-tuple-element.413.refs_1_, bf16[128,2560]{1,0:T(8,128)(2,1)} %get-tuple-element.414.refs_2_, bf16[128,960]{1,0:T(8,128)(2,1)} %get-tuple-element.415.refs_3_, ...), custom_call_target="tpu_custom_call" | custom-call | tf_op jit(solution)/shard_map/pallas_call | solution.py:699
  579.6 7.4 shard_map.241
  600.1 8.1 %shard_map.243 = bf16[4,352,960]{2,1,0:T(8,128)(2,1)} custom-call(s32[4]{0:T(128)} %pad_add_fusion.1.starts_ref, bf16[960,960]{1,0:T(8,128)(2,1)} %get-tuple-element.436.refs_0_, bf16[960,960]{1,0:T(8,128)(2,1)} %get-tuple-element.437.refs_1_, f32[16,960]{1,0:T(8,128)} %add.1250.refs_2_, bf16[128,960]{1,0:T(8,128)(2,1)} %get-tuple-element.428.refs_2_.refs_3_, ...), custom_call_target="tpu_custom_call" | custom-call | tf_op jit(solution)/shard_map/pallas_call | solution.py:768
  616.3 44.3 %collective-permute-done.293.refs_1_ = bf16[128,960]{1,0:T(8,128)(2,1)S(1)} collective-permute-done((bf16[128,960]{1,0:T(8,128)(2,1)S(1)}, bf16[128,960]{1,0:T(8,128)(2,1)S(1)}, u32[]{:S(2)}, u32[]{:S(2)}) %collective-permute-start.293) | collective-permute-done | bytes 245792 | tf_op jit(solution)/shard_map/ppermute | solution.py:49
  662.3 6.0 collective-permute-done.295.refs_3_
  674.5 9.8 %collective-permute-start.289 = (bf16[112,960]{1,0:T(8,128)(2,1)}, bf16[112,960]{1,0:T(8,128)(2,1)}, u32[]{:S(2)}, u32[]{:S(2)}) collective-permute-start(bf16[112,960]{1,0:T(8,128)(2,1)} %get-tuple-element.684), channel_id=1, source_target_pairs={{0,12},{4,0},{8,4},{12,8},{1,13},{5,1},{9,5},{13,9},{2,14},{6,2},{... | collective-permute-start | bytes 645128 | tf_op jit(solution)/shard_map/ppermute | solution.py:49
  687.8 7.1 all-to-all-start.3
  695.6 4.8 collective-permute-done.287
  703.2 8.4 %collective-permute-start.292 = (bf16[108,960]{1,0:T(8,128)(2,1)S(1)}, bf16[108,960]{1,0:T(8,128)(2,1)}, u32[]{:S(2)}, u32[]{:S(2)}) collective-permute-start(bf16[108,960]{1,0:T(8,128)(2,1)S(1)} %pad_maximum_fusion.13), channel_id=1, source_target_pairs={{0,3},{1,0},{2,1},{3,2},{4,7},{5,4},{6,5},{7,6},{8,11},{9,8},{10,9... | collective-permute-start | bytes 622088 | tf_op jit(solution)/shard_map/ppermute | solution.py:49
  715.3 5.7 collective-permute-done.292
  720.9 4.6 collective-permute-done.290
  735.1 15.4 %all_to_all.53 = f32[128,1,128]{2,1,0:T(1,128)S(1)} all-to-all(f32[128,1,128]{2,1,0:T(1,128)S(1)} %iota.151), channel_id=1, replica_groups=mesh['z'=4,'core'=2,'y'=4,'x'=4] {'z','core','y','x'}, dimensions={0} | all-to-all | bytes 131072 | tf_op jit(solution)/shard_map/all_to_all | solution.py:1210
  755.9 5.1 multiply_subtract_fusion.1
  (935 shorter events, 313.4 us)
Async XLA Ops:
  7.2 65.7 %all-gather.13.cloned.1.call-start = ((), (), s32[]{:S(2)}) async-start(), calls=%async_computation.14 | async-start | bytes 6488064 | tf_op jit(solution)/shard_map/all_gather | solution.py:878
  26.6 124.6 %all-gather.15.cloned.1.call-start = ((), (), s32[]{:S(2)}) async-start(), calls=%async_computation.15 | async-start | bytes 16220160 | tf_op jit(solution)/shard_map/all_gather | solution.py:915
  37.6 261.4 %all-gather.17.cloned.1.call-start = ((), (), s32[]{:S(2)}) async-start(), calls=%async_computation.16 | async-start | bytes 13369344 | tf_op jit(solution)/shard_map/all_gather | solution.py:921
  53.9 442.4 %reduce-scatter.15.cloned.1.call-start = ((), (), s32[]{:S(2)}) async-start(), calls=%async_computation.18 | async-start | bytes 13369344
  70.3 15.7 %collective-permute-start.153 = (bf16[128,960]{1,0:T(8,128)(2,1)S(1)}, bf16[128,960]{1,0:T(8,128)(2,1)S(1)}, u32[]{:S(2)}, u32[]{:S(2)}) collective-permute-start(bf16[128,960]{1,0:T(8,128)(2,1)S(1)} %get-tuple-element.320), channel_id=1, source_target_pairs={{0,16},{16,0},{1,17},{17,1},{2,18},{18,2},{3,19},{19,3},{4,20},{20... | collective-permute-start | bytes 737288 | tf_op jit(solution)/shard_map/ppermute | solution.py:53
  75.6 17.3 %collective-permute-start.160 = (bf16[128,960]{1,0:T(8,128)(2,1)S(1)}, bf16[128,960]{1,0:T(8,128)(2,1)S(1)}, u32[]{:S(2)}, u32[]{:S(2)}) collective-permute-start(bf16[128,960]{1,0:T(8,128)(2,1)S(1)} %add_convert_fusion.24), channel_id=1, source_target_pairs={{0,32},{32,64},{64,96},{96,0},{1,33},{33,65},{65,97},{97,1},{2,34}... | collective-permute-start | bytes 737288 | tf_op jit(solution)/shard_map/ppermute | solution.py:49
  96.1 15.1 %collective-permute-start.165 = (bf16[128,640]{1,0:T(8,128)(2,1)S(1)}, bf16[128,640]{1,0:T(8,128)(2,1)S(1)}, u32[]{:S(2)}, u32[]{:S(2)}) collective-permute-start(bf16[128,640]{1,0:T(8,128)(2,1)S(1)} %get-tuple-element.336.refs_4_), channel_id=1, source_target_pairs={{64,1},{65,2},{66,3},{67,4},{68,5},{69,6},{70,7},{71,8},{72,9},{73... | collective-permute-start | bytes 491528 | tf_op jit(solution)/shard_map/ppermute | solution.py:120
  99.7 14.9 %collective-permute-start.166 = (bf16[128,640]{1,0:T(8,128)(2,1)S(1)}, bf16[128,640]{1,0:T(8,128)(2,1)S(1)}, u32[]{:S(2)}, u32[]{:S(2)}) collective-permute-start(bf16[128,640]{1,0:T(8,128)(2,1)S(1)} %get-tuple-element.336.refs_4_), channel_id=1, source_target_pairs={{96,1},{97,2},{98,3},{99,4},{100,5},{101,6},{102,7},{103,8},{104,9... | collective-permute-start | bytes 491528 | tf_op jit(solution)/shard_map/ppermute | solution.py:120
  164.3 18.6 %collective-permute-start.178 = (bf16[128,640]{1,0:T(8,128)(2,1)}, bf16[128,640]{1,0:T(8,128)(2,1)S(1)}, u32[]{:S(2)}, u32[]{:S(2)}) collective-permute-start(bf16[128,640]{1,0:T(8,128)(2,1)} %get-tuple-element.342.refs_4_), channel_id=1, source_target_pairs={{0,1},{1,2},{2,3},{3,4},{4,5},{5,6},{6,7},{7,8},{8,9},{9,10},{10,1... | collective-permute-start | bytes 491528 | tf_op jit(solution)/shard_map/ppermute | solution.py:120
  167.6 16.7 %collective-permute-start.179 = (bf16[128,640]{1,0:T(8,128)(2,1)}, bf16[128,640]{1,0:T(8,128)(2,1)S(1)}, u32[]{:S(2)}, u32[]{:S(2)}) collective-permute-start(bf16[128,640]{1,0:T(8,128)(2,1)} %get-tuple-element.342.refs_4_), channel_id=1, source_target_pairs={{32,1},{33,2},{34,3},{35,4},{36,5},{37,6},{38,7},{39,8},{40,9},{41... | collective-permute-start | bytes 491528 | tf_op jit(solution)/shard_map/ppermute | solution.py:120
  168.2 18.6 %collective-permute-start.180 = (bf16[128,640]{1,0:T(8,128)(2,1)}, bf16[128,640]{1,0:T(8,128)(2,1)S(1)}, u32[]{:S(2)}, u32[]{:S(2)}) collective-permute-start(bf16[128,640]{1,0:T(8,128)(2,1)} %get-tuple-element.342.refs_4_), channel_id=1, source_target_pairs={{64,1},{65,2},{66,3},{67,4},{68,5},{69,6},{70,7},{71,8},{72,9},{73... | collective-permute-start | bytes 491528 | tf_op jit(solution)/shard_map/ppermute | solution.py:120
  217.5 23.7 %collective-permute-start.193 = (bf16[128,640]{1,0:T(8,128)(2,1)}, bf16[128,640]{1,0:T(8,128)(2,1)S(1)}, u32[]{:S(2)}, u32[]{:S(2)}) collective-permute-start(bf16[128,640]{1,0:T(8,128)(2,1)} %get-tuple-element.346.refs_4_), channel_id=1, source_target_pairs={{0,1},{1,2},{2,3},{3,4},{4,5},{5,6},{6,7},{7,8},{8,9},{9,10},{10,1... | collective-permute-start | bytes 491528 | tf_op jit(solution)/shard_map/ppermute | solution.py:120
  223.1 19.5 %collective-permute-start.194 = (bf16[128,640]{1,0:T(8,128)(2,1)}, bf16[128,640]{1,0:T(8,128)(2,1)S(1)}, u32[]{:S(2)}, u32[]{:S(2)}) collective-permute-start(bf16[128,640]{1,0:T(8,128)(2,1)} %get-tuple-element.346.refs_4_), channel_id=1, source_target_pairs={{32,1},{33,2},{34,3},{35,4},{36,5},{37,6},{38,7},{39,8},{40,9},{41... | collective-permute-start | bytes 491528 | tf_op jit(solution)/shard_map/ppermute | solution.py:120
  223.7 21.3 %collective-permute-start.195 = (bf16[128,640]{1,0:T(8,128)(2,1)}, bf16[128,640]{1,0:T(8,128)(2,1)S(1)}, u32[]{:S(2)}, u32[]{:S(2)}) collective-permute-start(bf16[128,640]{1,0:T(8,128)(2,1)} %get-tuple-element.346.refs_4_), channel_id=1, source_target_pairs={{64,1},{65,2},{66,3},{67,4},{68,5},{69,6},{70,7},{71,8},{72,9},{73... | collective-permute-start | bytes 491528 | tf_op jit(solution)/shard_map/ppermute | solution.py:120
  232.2 14.9 %collective-permute-start.196 = (bf16[128,640]{1,0:T(8,128)(2,1)}, bf16[128,640]{1,0:T(8,128)(2,1)S(1)}, u32[]{:S(2)}, u32[]{:S(2)}) collective-permute-start(bf16[128,640]{1,0:T(8,128)(2,1)} %get-tuple-element.346.refs_4_), channel_id=1, source_target_pairs={{96,1},{97,2},{98,3},{99,4},{100,5},{101,6},{102,7},{103,8},{104,9... | collective-permute-start | bytes 491528 | tf_op jit(solution)/shard_map/ppermute | solution.py:120
  233.5 14.8 %collective-permute-start.197 = (bf16[128,640]{1,0:T(8,128)(2,1)}, bf16[128,640]{1,0:T(8,128)(2,1)S(1)}, u32[]{:S(2)}, u32[]{:S(2)}) collective-permute-start(bf16[128,640]{1,0:T(8,128)(2,1)} %get-tuple-element.346.refs_4_), channel_id=1, source_target_pairs={{0,96},{1,97},{2,98},{3,99},{4,100},{5,101},{6,102},{7,103},{8,104... | collective-permute-start | bytes 491528 | tf_op jit(solution)/shard_map/ppermute | solution.py:113
  281.7 17.4 %collective-permute-start.211 = (bf16[128,960]{1,0:T(8,128)(2,1)S(1)}, bf16[128,960]{1,0:T(8,128)(2,1)S(1)}, u32[]{:S(2)}, u32[]{:S(2)}) collective-permute-start(bf16[128,960]{1,0:T(8,128)(2,1)S(1)} %multiply_convert_fusion.1.refs_0_), channel_id=1, source_target_pairs={{0,16},{16,0},{1,17},{17,1},{2,18},{18,2},{3,19},{19,3},{4,20},{20... | collective-permute-start | bytes 737288 | tf_op jit(solution)/shard_map/ppermute | solution.py:53
  340.5 361.4 %reduce-scatter.13.cloned.1.call-start = ((), (), s32[]{:S(2)}) async-start(), calls=%async_computation.17 | async-start | bytes 8355840 | tf_op jit(solution)/shard_map/reduce_scatter | solution.py:1101
  398.9 14.9 %collective-permute-start.233 = (bf16[128,640]{1,0:T(8,128)(2,1)S(1)}, bf16[128,640]{1,0:T(8,128)(2,1)S(1)}, u32[]{:S(2)}, u32[]{:S(2)}) collective-permute-start(bf16[128,640]{1,0:T(8,128)(2,1)S(1)} %get-tuple-element.709), channel_id=1, source_target_pairs={{1,64},{2,65},{3,66},{4,67},{5,68},{6,69},{7,70},{8,71},{9,72},{10... | collective-permute-start | bytes 491528 | tf_op jit(solution)/shard_map/ppermute | solution.py:136
  400.2 15.6 %collective-permute-start.232 = (bf16[128,640]{1,0:T(8,128)(2,1)S(1)}, bf16[128,640]{1,0:T(8,128)(2,1)S(1)}, u32[]{:S(2)}, u32[]{:S(2)}) collective-permute-start(bf16[128,640]{1,0:T(8,128)(2,1)S(1)} %get-tuple-element.710), channel_id=1, source_target_pairs={{1,32},{2,33},{3,34},{4,35},{5,36},{6,37},{7,38},{8,39},{9,40},{10... | collective-permute-start | bytes 491528 | tf_op jit(solution)/shard_map/ppermute | solution.py:136
  400.9 18.8 %collective-permute-start.231 = (bf16[128,640]{1,0:T(8,128)(2,1)S(1)}, bf16[128,640]{1,0:T(8,128)(2,1)S(1)}, u32[]{:S(2)}, u32[]{:S(2)}) collective-permute-start(bf16[128,640]{1,0:T(8,128)(2,1)S(1)} %get-tuple-element.707), channel_id=1, source_target_pairs={{1,0},{2,1},{3,2},{4,3},{5,4},{6,5},{7,6},{8,7},{9,8},{10,9},{11,1... | collective-permute-start | bytes 491528 | tf_op jit(solution)/shard_map/ppermute | solution.py:136
  402.5 17.2 %collective-permute-start.229 = (bf16[128,640]{1,0:T(8,128)(2,1)S(1)}, bf16[128,640]{1,0:T(8,128)(2,1)S(1)}, u32[]{:S(2)}, u32[]{:S(2)}) collective-permute-start(bf16[128,640]{1,0:T(8,128)(2,1)S(1)} %get-tuple-element.705), channel_id=1, source_target_pairs={{32,0},{64,32},{96,64},{33,1},{65,33},{97,65},{34,2},{66,34},{98,6... | collective-permute-start | bytes 491528 | tf_op jit(solution)/shard_map/ppermute | solution.py:130
  473.7 14.6 %collective-permute-start.240 = (bf16[128,640]{1,0:T(8,128)(2,1)S(1)}, bf16[128,640]{1,0:T(8,128)(2,1)S(1)}, u32[]{:S(2)}, u32[]{:S(2)}) collective-permute-start(bf16[128,640]{1,0:T(8,128)(2,1)S(1)} %get-tuple-element.700), channel_id=1, source_target_pairs={{1,0},{2,1},{3,2},{4,3},{5,4},{6,5},{7,6},{8,7},{9,8},{10,9},{11,1... | collective-permute-start | bytes 491528 | tf_op jit(solution)/shard_map/ppermute | solution.py:136
  483.4 28.3 %collective-permute-start.265 = (bf16[128,1280]{1,0:T(8,128)(2,1)}, bf16[128,1280]{1,0:T(8,128)(2,1)}, u32[]{:S(2)}, u32[]{:S(2)}) collective-permute-start(bf16[128,1280]{1,0:T(8,128)(2,1)} %constant_dynamic-slice_fusion.11), channel_id=1, source_target_pairs={{0,16},{16,0},{1,17},{17,1},{2,18},{18,2},{3,19},{19,3},{4,20},{20... | collective-permute-start | bytes 983048 | tf_op jit(solution)/shard_map/ppermute | solution.py:53
  488.3 23.2 %collective-permute-start.266 = (bf16[128,960]{1,0:T(8,128)(2,1)}, bf16[128,960]{1,0:T(8,128)(2,1)}, u32[]{:S(2)}, u32[]{:S(2)}) collective-permute-start(bf16[128,960]{1,0:T(8,128)(2,1)} %get-tuple-element.425.refs_23_), channel_id=1, source_target_pairs={{0,16},{16,0},{1,17},{17,1},{2,18},{18,2},{3,19},{19,3},{4,20},{20... | collective-permute-start | bytes 737288 | tf_op jit(solution)/shard_map/ppermute | solution.py:53
  489.4 22.9 %collective-permute-start.260 = (bf16[128,1280]{1,0:T(8,128)(2,1)}, bf16[128,1280]{1,0:T(8,128)(2,1)}, u32[]{:S(2)}, u32[]{:S(2)}) collective-permute-start(bf16[128,1280]{1,0:T(8,128)(2,1)} %constant_dynamic-slice_fusion.14), channel_id=1, source_target_pairs={{0,16},{16,0},{1,17},{17,1},{2,18},{18,2},{3,19},{19,3},{4,20},{20... | collective-permute-start | bytes 983048 | tf_op jit(solution)/shard_map/ppermute | solution.py:53
  489.4 22.8 %collective-permute-start.261 = (bf16[128,960]{1,0:T(8,128)(2,1)}, bf16[128,960]{1,0:T(8,128)(2,1)}, u32[]{:S(2)}, u32[]{:S(2)}) collective-permute-start(bf16[128,960]{1,0:T(8,128)(2,1)} %get-tuple-element.420.refs_13_), channel_id=1, source_target_pairs={{0,16},{16,0},{1,17},{17,1},{2,18},{18,2},{3,19},{19,3},{4,20},{20... | collective-permute-start | bytes 737288 | tf_op jit(solution)/shard_map/ppermute | solution.py:53
  492.2 20.5 %collective-permute-start.256 = (bf16[128,960]{1,0:T(8,128)(2,1)}, bf16[128,960]{1,0:T(8,128)(2,1)}, u32[]{:S(2)}, u32[]{:S(2)}) collective-permute-start(bf16[128,960]{1,0:T(8,128)(2,1)} %get-tuple-element.415.refs_3_), channel_id=1, source_target_pairs={{0,16},{16,0},{1,17},{17,1},{2,18},{18,2},{3,19},{19,3},{4,20},{20... | collective-permute-start | bytes 737288 | tf_op jit(solution)/shard_map/ppermute | solution.py:53
  514.8 27.8 %collective-permute-start.258 = (bf16[128,1280]{1,0:T(8,128)(2,1)}, bf16[128,1280]{1,0:T(8,128)(2,1)S(1)}, u32[]{:S(2)}, u32[]{:S(2)}) collective-permute-start(bf16[128,1280]{1,0:T(8,128)(2,1)} %constant_dynamic-slice_fusion.16), channel_id=1, source_target_pairs={{0,16},{16,0},{1,17},{17,1},{2,18},{18,2},{3,19},{19,3},{4,20},{20... | collective-permute-start | bytes 983048 | tf_op jit(solution)/shard_map/ppermute | solution.py:53
  515.3 27.3 %collective-permute-start.259 = (bf16[128,1280]{1,0:T(8,128)(2,1)}, bf16[128,1280]{1,0:T(8,128)(2,1)S(1)}, u32[]{:S(2)}, u32[]{:S(2)}) collective-permute-start(bf16[128,1280]{1,0:T(8,128)(2,1)} %constant_dynamic-slice_fusion.15), channel_id=1, source_target_pairs={{0,16},{16,0},{1,17},{17,1},{2,18},{18,2},{3,19},{19,3},{4,20},{20... | collective-permute-start | bytes 983048 | tf_op jit(solution)/shard_map/ppermute | solution.py:53
  515.4 27.2 %collective-permute-start.263 = (bf16[128,1280]{1,0:T(8,128)(2,1)S(1)}, bf16[128,1280]{1,0:T(8,128)(2,1)S(1)}, u32[]{:S(2)}, u32[]{:S(2)}) collective-permute-start(bf16[128,1280]{1,0:T(8,128)(2,1)S(1)} %constant_dynamic-slice_fusion.13), channel_id=1, source_target_pairs={{0,16},{16,0},{1,17},{17,1},{2,18},{18,2},{3,19},{19,3},{4,20},{20... | collective-permute-start | bytes 983048 | tf_op jit(solution)/shard_map/ppermute | solution.py:53
  515.8 26.8 %collective-permute-start.264 = (bf16[128,1280]{1,0:T(8,128)(2,1)S(1)}, bf16[128,1280]{1,0:T(8,128)(2,1)S(1)}, u32[]{:S(2)}, u32[]{:S(2)}) collective-permute-start(bf16[128,1280]{1,0:T(8,128)(2,1)S(1)} %constant_dynamic-slice_fusion.12), channel_id=1, source_target_pairs={{0,16},{16,0},{1,17},{17,1},{2,18},{18,2},{3,19},{19,3},{4,20},{20... | collective-permute-start | bytes 983048 | tf_op jit(solution)/shard_map/ppermute | solution.py:53
  515.9 26.7 %collective-permute-start.267 = (bf16[128,960]{1,0:T(8,128)(2,1)}, bf16[128,960]{1,0:T(8,128)(2,1)S(1)}, u32[]{:S(2)}, u32[]{:S(2)}) collective-permute-start(bf16[128,960]{1,0:T(8,128)(2,1)} %get-tuple-element.426.refs_24_), channel_id=1, source_target_pairs={{0,16},{16,0},{1,17},{17,1},{2,18},{18,2},{3,19},{19,3},{4,20},{20... | collective-permute-start | bytes 737288 | tf_op jit(solution)/shard_map/ppermute | solution.py:53
  568.2 18.8 %collective-permute-start.250 = (bf16[128,640]{1,0:T(8,128)(2,1)}, bf16[128,640]{1,0:T(8,128)(2,1)S(1)}, u32[]{:S(2)}, u32[]{:S(2)}) collective-permute-start(bf16[128,640]{1,0:T(8,128)(2,1)} %get-tuple-element.696), channel_id=1, source_target_pairs={{1,32},{2,33},{3,34},{4,35},{5,36},{6,37},{7,38},{8,39},{9,40},{10... | collective-permute-start | bytes 491528 | tf_op jit(solution)/shard_map/ppermute | solution.py:136
  568.9 19.8 %collective-permute-start.249 = (bf16[128,640]{1,0:T(8,128)(2,1)S(1)}, bf16[128,640]{1,0:T(8,128)(2,1)S(1)}, u32[]{:S(2)}, u32[]{:S(2)}) collective-permute-start(bf16[128,640]{1,0:T(8,128)(2,1)S(1)} %get-tuple-element.693), channel_id=1, source_target_pairs={{1,0},{2,1},{3,2},{4,3},{5,4},{6,5},{7,6},{8,7},{9,8},{10,9},{11,1... | collective-permute-start | bytes 491528 | tf_op jit(solution)/shard_map/ppermute | solution.py:136
  570.2 18.5 %collective-permute-start.247 = (bf16[128,640]{1,0:T(8,128)(2,1)S(1)}, bf16[128,640]{1,0:T(8,128)(2,1)S(1)}, u32[]{:S(2)}, u32[]{:S(2)}) collective-permute-start(bf16[128,640]{1,0:T(8,128)(2,1)S(1)} %get-tuple-element.691), channel_id=1, source_target_pairs={{32,0},{64,32},{96,64},{33,1},{65,33},{97,65},{34,2},{66,34},{98,6... | collective-permute-start | bytes 491528 | tf_op jit(solution)/shard_map/ppermute | solution.py:130
  573.9 14.8 %collective-permute-start.246 = (bf16[128,640]{1,0:T(8,128)(2,1)S(1)}, bf16[128,640]{1,0:T(8,128)(2,1)S(1)}, u32[]{:S(2)}, u32[]{:S(2)}) collective-permute-start(bf16[128,640]{1,0:T(8,128)(2,1)S(1)} %get-tuple-element.692), channel_id=1, source_target_pairs={{64,0},{96,32},{65,1},{97,33},{66,2},{98,34},{67,3},{99,35},{68,4}... | collective-permute-start | bytes 491528 | tf_op jit(solution)/shard_map/ppermute | solution.py:130
  611.1 59.5 %collective-permute-start.286 = (bf16[352,960]{1,0:T(8,128)(2,1)}, bf16[352,960]{1,0:T(8,128)(2,1)}, u32[]{:S(2)}, u32[]{:S(2)}) collective-permute-start(bf16[352,960]{1,0:T(8,128)(2,1)} %get-tuple-element.681), channel_id=1, source_target_pairs={{0,96},{32,0},{64,32},{96,64},{1,97},{33,1},{65,33},{97,65},{2,98}... | collective-permute-start | bytes 2027528 | tf_op jit(solution)/shard_map/ppermute | solution.py:49
  611.4 59.2 %collective-permute-start.285 = (bf16[352,960]{1,0:T(8,128)(2,1)}, bf16[352,960]{1,0:T(8,128)(2,1)}, u32[]{:S(2)}, u32[]{:S(2)}) collective-permute-start(bf16[352,960]{1,0:T(8,128)(2,1)} %get-tuple-element.682), channel_id=1, source_target_pairs={{0,64},{32,96},{64,0},{96,32},{1,65},{33,97},{65,1},{97,33},{2,66}... | collective-permute-start | bytes 2027528 | tf_op jit(solution)/shard_map/ppermute | solution.py:49
  611.4 59.7 %collective-permute-start.284 = (bf16[352,960]{1,0:T(8,128)(2,1)S(1)}, bf16[352,960]{1,0:T(8,128)(2,1)}, u32[]{:S(2)}, u32[]{:S(2)}) collective-permute-start(bf16[352,960]{1,0:T(8,128)(2,1)S(1)} %get-tuple-element.680), channel_id=1, source_target_pairs={{0,32},{32,64},{64,96},{96,0},{1,33},{33,65},{65,97},{97,1},{2,34}... | collective-permute-start | bytes 2027528 | tf_op jit(solution)/shard_map/ppermute | solution.py:49
  612.6 48.1 %collective-permute-start.293 = (bf16[128,960]{1,0:T(8,128)(2,1)S(1)}, bf16[128,960]{1,0:T(8,128)(2,1)S(1)}, u32[]{:S(2)}, u32[]{:S(2)}) collective-permute-start(bf16[128,960]{1,0:T(8,128)(2,1)S(1)} %convert_element_type.755.refs_0_), channel_id=1, source_target_pairs={{0,96},{32,0},{64,32},{96,64},{1,97},{33,1},{65,33},{97,65},{2,98}... | collective-permute-start | bytes 737288 | tf_op jit(solution)/shard_map/ppermute | solution.py:49
  615.1 46.5 %collective-permute-start.294 = (bf16[128,960]{1,0:T(8,128)(2,1)S(1)}, bf16[128,960]{1,0:T(8,128)(2,1)S(1)}, u32[]{:S(2)}, u32[]{:S(2)}) collective-permute-start(bf16[128,960]{1,0:T(8,128)(2,1)S(1)} %convert_element_type.755.refs_0_), channel_id=1, source_target_pairs={{0,64},{32,96},{64,0},{96,32},{1,65},{33,97},{65,1},{97,33},{2,66}... | collective-permute-start | bytes 737288 | tf_op jit(solution)/shard_map/ppermute | solution.py:49
  661.6 22.8 %collective-permute-start.296 = (bf16[128,960]{1,0:T(8,128)(2,1)S(1)}, bf16[128,960]{1,0:T(8,128)(2,1)S(1)}, u32[]{:S(2)}, u32[]{:S(2)}) collective-permute-start(bf16[128,960]{1,0:T(8,128)(2,1)S(1)} %convert_element_type.755.refs_0_), channel_id=1, source_target_pairs={{0,16},{16,0},{1,17},{17,1},{2,18},{18,2},{3,19},{19,3},{4,20},{20... | collective-permute-start | bytes 737288 | tf_op jit(solution)/shard_map/ppermute | solution.py:53
  668.3 16.0 %collective-permute-start.297 = (bf16[128,960]{1,0:T(8,128)(2,1)S(1)}, bf16[128,960]{1,0:T(8,128)(2,1)S(1)}, u32[]{:S(2)}, u32[]{:S(2)}) collective-permute-start(bf16[128,960]{1,0:T(8,128)(2,1)S(1)} %collective-permute-done.293.refs_1_), channel_id=1, source_target_pairs={{0,16},{16,0},{1,17},{17,1},{2,18},{18,2},{3,19},{19,3},{4,20},{20... | collective-permute-start | bytes 737288 | tf_op jit(solution)/shard_map/ppermute | solution.py:53
  674.5 20.3 %collective-permute-start.289 = (bf16[112,960]{1,0:T(8,128)(2,1)}, bf16[112,960]{1,0:T(8,128)(2,1)}, u32[]{:S(2)}, u32[]{:S(2)}) collective-permute-start(bf16[112,960]{1,0:T(8,128)(2,1)} %get-tuple-element.684), channel_id=1, source_target_pairs={{0,12},{4,0},{8,4},{12,8},{1,13},{5,1},{9,5},{13,9},{2,14},{6,2},{... | collective-permute-start | bytes 645128 | tf_op jit(solution)/shard_map/ppermute | solution.py:49
  684.4 16.0 %collective-permute-start.287 = (bf16[112,960]{1,0:T(8,128)(2,1)}, bf16[112,960]{1,0:T(8,128)(2,1)}, u32[]{:S(2)}, u32[]{:S(2)}) collective-permute-start(bf16[112,960]{1,0:T(8,128)(2,1)} %get-tuple-element.683), channel_id=1, source_target_pairs={{0,4},{4,8},{8,12},{12,0},{1,5},{5,9},{9,13},{13,1},{2,6},{6,10},{... | collective-permute-start | bytes 645128 | tf_op jit(solution)/shard_map/ppermute | solution.py:49
  687.8 25.0 %all-to-all-start.3 = ((bf16[16,24,960]{2,1,0:T(8,128)(2,1)}), bf16[16,24,960]{2,1,0:T(8,128)(2,1)S(1)}, u32[]{:S(2)}, u32[]{:S(2)}) async-start(bf16[16,24,960]{2,1,0:T(8,128)(2,1)} %bitcast.155), calls=%async_computation.6 | async-start | bytes 1572864 | tf_op jit(solution)/shard_map/all_to_all | solution.py:1168
  703.2 17.7 %collective-permute-start.292 = (bf16[108,960]{1,0:T(8,128)(2,1)S(1)}, bf16[108,960]{1,0:T(8,128)(2,1)}, u32[]{:S(2)}, u32[]{:S(2)}) collective-permute-start(bf16[108,960]{1,0:T(8,128)(2,1)S(1)} %pad_maximum_fusion.13), channel_id=1, source_target_pairs={{0,3},{1,0},{2,1},{3,2},{4,7},{5,4},{6,5},{7,6},{8,11},{9,8},{10,9... | collective-permute-start | bytes 622088 | tf_op jit(solution)/shard_map/ppermute | solution.py:49
  (344 other events, 2858.4 us)
Sparse Core Ops, SparseCore 0:
  17.5 55.3 all-gather.12
  76.0 75.1 all-gather.14
  153.6 108.3 all-gather.16
  340.5 101.0 reduce-scatter.14
  556.5 140.5 reduce-scatter.12

commit v6 on v5

--- a/solution.py
+++ b/solution.py
@@ -274,7 +274,7 @@
         cost_estimate=pl.CostEstimate(
             flops=20_000_000_000, bytes_accessed=9_000_000, transcendentals=4_000_000
         ),
-        compiler_params=params(24),
+        compiler_params=params(BIG),
     )(queries, *pairs, bias, log_total, attended, grads, cosine, sine)
 
 
@@ -879,7 +879,7 @@
         jnp.concatenate(pack_rows, axis=0), ("z", "core", "y"), axis=0, tiled=True
     )
     mlp_own = mlp_master.astype(BFLOAT)
-    mlp_quad = jnp.concatenate([mlp_own] + [shift(mlp_own, "x", k) for k in (1, 2, 3)], axis=1)
+    mlp_quad = jnp.concatenate([mlp_own] + [shift(mlp_own, "z", k) for k in (1, 2, 3)], axis=1)
 
     group_ids = token_ids[0]
     near_ids = reorder(group_ids.reshape(MP, TOK_DEV), near).reshape(-1)
@@ -913,7 +913,7 @@
     ).astype(BFLOAT)
     mlp_quad, owner_hot = tie(mlp_quad, owner_hot)
     mlp_weights = lax.all_gather(
-        mlp_quad.reshape(3 * 80, D), ("core", "z", "y"), axis=0, tiled=True
+        mlp_quad.reshape(3 * 80, D), ("core", "y", "x"), axis=0, tiled=True
     )
     mlp_weights = mlp_weights.reshape(32, 3, 80, D)
     asked_rows = lax.all_to_all(mm(owner_hot, own_table).astype(BFLOAT), DP_AXES, 0, 0, tiled=True)
@@ -1099,7 +1099,7 @@
         if step == 0:
             mlp_half = mlp_grads(core.astype(jnp.int32), mlp_kept, mlp_far)
             mlp_sum = lax.psum_scatter(
-                mlp_half.reshape(16 * 240, D), ("z", "y"), scatter_dimension=0, tiled=True
+                mlp_half.reshape(16 * 240, D), DP_AXES, scatter_dimension=0, tiled=True
             )
             squares = square_grads(square_kept, square_far)
             grad_own, mlp_half, *squares = tie(grad_own, mlp_half, *squares)
@@ -1112,6 +1112,11 @@
         if step == 1 and not dense:
             head_grad, grad_hidden = tie(head_grad, grad_hidden)
 
+    sent = grad_hidden.astype(BFLOAT)
+    grad_embed = [sent] + [shift(sent, "z", -k) for k in (1, 2, 3)]
+    grad_embed[1], grad_embed[3], gain_one = tie(grad_embed[1], grad_embed[3], gain_one)
+    grad_embed += [swap(part) for part in grad_embed]
+
     def aligned_row(which):
         return (pack_row(which) // 16) * 16
 
@@ -1135,23 +1140,16 @@
         return jnp.stack([value[..., i : i + 48, :] for i in (0, 16, 40, 56)])
 
     part = stage(part, "z", z).astype(BFLOAT)
-    part = stage(y_windows(part), "y", y).astype(BFLOAT)
-    part, mlp_sum = tie(x_windows(part), mlp_sum)
-    mlp_sum = mlp_sum.reshape(3, 4, UNITS, D).transpose(1, 0, 2, 3).reshape(4, 3 * UNITS, D)
-
-    def toward(k):
-        mine = lax.dynamic_index_in_dim(part, (x + k) % 4, 0, False)
-        return jnp.concatenate([mine, mlp_sum[(4 - k) % 4]], axis=0)
-
-    total = toward(0).astype(FLOAT)
+    part, mlp_sum = tie(y_windows(part), mlp_sum)
+    mlp_sum = mlp_sum.reshape(3, 4, UNITS, D).transpose(1, 0, 2, 3)
+    mlp_grad = mlp_sum[0].astype(FLOAT)
     for k in (1, 2, 3):
-        total = total + shift(toward(k), "x", k).astype(FLOAT)
-    part = total[:48].reshape(-1)
-    mlp_grad = total[48:].reshape(3, UNITS, D)
+        mlp_grad = mlp_grad + shift(mlp_sum[k], "z", -k).astype(FLOAT)
+    part = stage(part, "y", y).astype(BFLOAT)
+    part = stage(x_windows(part), "x", x).reshape(-1)
     begin = aligned_row(DP * model_index) + 80 * y + (20 * x) // 8 * 8
     pack_grad = lax.dynamic_slice(part, (PACK_DEV * device - D * begin,), (PACK_DEV,))
 
-    grad_embed = gather_group(grad_hidden.astype(BFLOAT))
     if dense:
         kept_rows = jnp.concatenate(grad_embed).astype(FLOAT) * inside.astype(FLOAT)[:, None]
         sums = jax.ops.segment_sum(

time: 780 us -> 729 us (0.935)
  local copies, waits for them, and re-layouts: 84.5 us -> 47.6 us
  waiting for transfers between devices: 153 us -> 132 us
  Pallas kernels: 210 us -> 221 us
    unnamed x475 -> x383, local copies, waits for them, and re-layouts: 55.2 us -> 22.8 us
    ppermute x30 -> x33, waiting for transfers between devices: 101 us -> 70.7 us  [shift(): return lax.ppermute(value, axis, [(i, (i + steps) % 4) for i in range(4)])]
    pallas_call x3, Pallas kernels: 31.5 us -> 41.5 us  [attend_back(): pl.pallas_call(attend_back_kernel, out_shape=(struct(BFLOAT, TOK_DEV, D),...]
    all_to_all x1, starting transfers between devices: 7.05 us -> 16.4 us  [gradients(): unique = lax.all_to_all(unique, DP_AXES, 0, 0, tiled=True)]
    ppermute x12, waiting for transfers between devices: 21.9 us -> 30.6 us  [group_scatter(): total = total + lax.ppermute(prev[k], ('z',) + DP_AXES, pairs).astype(FLOAT)]
    ppermute x30 -> x33, starting transfers between devices: 46.5 us -> 41.8 us  [shift(): return lax.ppermute(value, axis, [(i, (i + steps) % 4) for i in range(4)])]
  transfers between devices with their start and end apart: 157 -> 160, of which waited for: 53 -> 56; matrix products, arithmetic and copies ran while one was open for 8% -> 7% of each run, Pallas kernels for 22% -> 25%
where the time goes in v6:
time: 729 us; the launch traced here: 719 us
  Pallas kernels  221 us (30%)
  starting transfers between devices  215 us (29%)
  waiting for transfers between devices  132 us (18%)
  local copies, waits for them, and re-layouts  47.6 us (7%)
  other arithmetic  39.1 us (5%)
  blocking collectives  33.3 us (5%)
  between operations  23.6 us (3%)
    ppermute x33, waiting for transfers between devices, shift(): return lax.ppermute(value, axis, [(i, (i + steps) % 4) for i in range(4)])  70.7 us
    ppermute x78, starting transfers between devices, swap(): return lax.ppermute(value, 'core', [(0, 1), (1, 0)])  55.6 us
    ppermute x33, starting transfers between devices, shift(): return lax.ppermute(value, axis, [(i, (i + steps) % 4) for i in range(4)])  41.8 us
    pallas_call x3, Pallas kernels, attend_back(): pl.pallas_call(attend_back_kernel, out_shape=(struct(BFLOAT, TOK_DEV, D),...  41.5 us
    pallas_call x3, Pallas kernels, block_back(): pl.pallas_call(block_back_kernel, grid=(FF_STEPS,), in_specs=[full, whole...  39.9 us
    ppermute x12, starting transfers between devices, group_gather(): prev.append(lax.ppermute(pair, ('z',) + DP_AXES, pairs))  38.8 us
    pallas_call x3, Pallas kernels, block(): pl.pallas_call(functools.partial(block_kernel, more), grid=(FF_STEPS,), i...  38.4 us
    ppermute x12, waiting for transfers between devices, group_scatter(): total = total + lax.ppermute(prev[k], ('z',) + DP_AXES, pairs).astype(FLOAT)  30.6 us
  transfers between devices with their start and end apart: 160, of which 56 were waited for; matrix products, arithmetic and copies ran while one was open for 7% of the time, Pallas kernels for 25%

profile of v6, /device:TPU:1, one launch (start us, length us, event | category | flops | bytes accessed | tf_op | source)
XLA Modules:
  0.0 718.6 jit_solution(10334610819909613864)
XLA Ops:
  20.4 6.2 all-to-all-start.1
  26.7 3.8 collective-permute-start.155
  37.1 4.5 collective-permute-done.153
  43.9 19.4 %all_to_all.52 = bf16[16,24,960]{2,1,0:T(8,128)(2,1)S(1)} all-to-all(bf16[16,24,960]{2,1,0:T(8,128)(2,1)S(1)} %bitcast.349), channel_id=1, replica_groups=mesh['z'=4,'core'=2,'y'=4,'x'=4] {'y','x'}, dimensions={0} | all-to-all | bytes 1474560 | tf_op jit(solution)/shard_map/all_to_all | solution.py:919
  73.1 3.9 collective-permute-start.157
  86.0 4.6 shard_map.222
  90.7 4.2 collective-permute-done.163
  100.0 4.6 collective-permute-start.168
  107.4 4.4 collective-permute-start.170
  124.0 9.0 %shard_map.224 = (bf16[128,960]{1,0:T(8,128)(2,1)S(1)}, f32[8,384]{1,0:T(8,128)S(1)}) custom-call(bf16[960,128]{1,0:T(8,128)(2,1)S(1)} %get-tuple-element.341.query_ref, bf16[128,640]{1,0:T(8,128)(2,1)S(1)} %collective-permute-done.166.refs_0_, bf16[128,640]{1,0:T(8,128)(2,1)S(1)} %collective-permute-done.167.refs_1_, ...), custom_call_target="tpu_custom_call" | custom-call | flops 12000000000 | bytes 5000000 | tf_op jit(solution)/shard_map/pallas_call | solution.py:226
  141.9 13.8 %all-gather.15.cloned.1.call-done = bf16[7680,960]{1,0:T(8,128)(2,1)} async-done(((bf16[240,960]{1,0:T(8,128)(2,1)}), bf16[7680,960]{1,0:T(8,128)(2,1)}) %all-gather.15.cloned.1.call-update) | async-done | bytes 14745616 | tf_op jit(solution)/shard_map/all_gather | solution.py:915
  155.7 13.0 %shard_map.225 = (f32[128,960]{1,0:T(8,128)}, bf16[128,960]{1,0:T(8,128)(2,1)}, f32[128,2560]{1,0:T(8,128)}, f32[128,2560]{1,0:T(8,128)}, bf16[128,2560]{1,0:T(8...) custom-call(bf16[128,960]{1,0:T(8,128)(2,1)} %copy-done.34, ...), custom_call_target="tpu_custom_call" | custom-call | flops 4000000000 | bytes 20000000 | tf_op jit(solution)/shard_map/pallas_call | solution.py:402
  168.8 3.2 collective-permute-start.181
  172.7 7.7 %collective-permute-start.183 = (bf16[128,640]{1,0:T(8,128)(2,1)}, bf16[128,640]{1,0:T(8,128)(2,1)S(1)}, u32[]{:S(2)}, u32[]{:S(2)}) collective-permute-start(bf16[128,640]{1,0:T(8,128)(2,1)} %get-tuple-element.348.refs_4_), channel_id=1, source_target_pairs={{64,1},{65,2},{66,3},{67,4},{68,5},{69,6},{70,7},{71,8},{72,9},{73... | collective-permute-start | bytes 491528 | tf_op jit(solution)/shard_map/ppermute | solution.py:120
  181.8 5.7 collective-permute-start.185
  199.1 8.8 %shard_map.226 = (bf16[128,960]{1,0:T(8,128)(2,1)S(1)}, f32[8,384]{1,0:T(8,128)S(1)}) custom-call(bf16[960,128]{1,0:T(8,128)(2,1)S(1)} %copy-done.99, bf16[128,640]{1,0:T(8,128)(2,1)S(1)} %collective-permute-done.181.refs_0_, bf16[128,640]{1,0:T(8,128)(2,1)S(1)} %collective-permute-done.182.refs_1_, bf16[128,640]{1,0:T(8,128)(2,1)S(1)} %collective-permute-done.183.refs_2_, ...), custom_call_target="tpu_custom_call" | custom-call | flops 12000000000 | bytes 5000000 | tf_op jit(solution)/shard_map/pallas_call | solution.py:226
  209.3 13.4 %shard_map.227 = (f32[128,960]{1,0:T(8,128)}, bf16[128,960]{1,0:T(8,128)(2,1)}, f32[128,2560]{1,0:T(8,128)}, f32[128,2560]{1,0:T(8,128)}, bf16[128,2560]{1,0:T(8...) custom-call(bf16[128,960]{1,0:T(8,128)(2,1)} %copy-done.35, ...), custom_call_target="tpu_custom_call" | custom-call | flops 4000000000 | bytes 20000000 | tf_op jit(solution)/shard_map/pallas_call | solution.py:402
  222.7 5.5 collective-permute-start.196
  228.9 8.2 %collective-permute-start.198 = (bf16[128,640]{1,0:T(8,128)(2,1)}, bf16[128,640]{1,0:T(8,128)(2,1)S(1)}, u32[]{:S(2)}, u32[]{:S(2)}) collective-permute-start(bf16[128,640]{1,0:T(8,128)(2,1)} %get-tuple-element.352.refs_4_), channel_id=1, source_target_pairs={{64,1},{65,2},{66,3},{67,4},{68,5},{69,6},{70,7},{71,8},{72,9},{73... | collective-permute-start | bytes 491528 | tf_op jit(solution)/shard_map/ppermute | solution.py:120
  238.4 7.8 %collective-permute-start.200 = (bf16[128,640]{1,0:T(8,128)(2,1)}, bf16[128,640]{1,0:T(8,128)(2,1)S(1)}, u32[]{:S(2)}, u32[]{:S(2)}) collective-permute-start(bf16[128,640]{1,0:T(8,128)(2,1)} %get-tuple-element.352.refs_4_), channel_id=1, source_target_pairs={{0,96},{1,97},{2,98},{3,99},{4,100},{5,101},{6,102},{7,103},{8,104... | collective-permute-start | bytes 491528 | tf_op jit(solution)/shard_map/ppermute | solution.py:113
  257.8 8.8 %shard_map.228 = (bf16[128,960]{1,0:T(8,128)(2,1)S(1)}, f32[8,384]{1,0:T(8,128)S(1)}) custom-call(bf16[960,128]{1,0:T(8,128)(2,1)S(1)} %copy-done.101, bf16[128,640]{1,0:T(8,128)(2,1)S(1)} %collective-permute-done.196.refs_0_, bf16[128,640]{1,0:T(8,128)(2,1)S(1)} %collective-permute-done.197.refs_1_, bf16[128,640]{1,0:T(8,128)(2,1)S(1)} %collective-permute-done.198.refs_2_, ...), custom_call_target="tpu_custom_call" | custom-call | flops 12000000000 | bytes 5000000 | tf_op jit(solution)/shard_map/pallas_call | solution.py:226
  268.0 12.0 %shard_map.229 = (f32[128,960]{1,0:T(8,128)}, bf16[128,960]{1,0:T(8,128)(2,1)}, f32[128,2560]{1,0:T(8,128)}, f32[128,2560]{1,0:T(8,128)}, bf16[128,2560]{1,0:T(8...) custom-call(bf16[128,960]{1,0:T(8,128)(2,1)} %copy-done.38, ...), custom_call_target="tpu_custom_call" | custom-call | flops 4000000000 | bytes 20000000 | tf_op jit(solution)/shard_map/pallas_call | solution.py:402
  291.1 6.0 collective-permute-start.215
  305.2 13.4 %shard_map.230 = (f32[256,6144]{1,0:T(8,128)}, bf16[256,960]{1,0:T(8,128)(2,1)}, f32[8,256]{1,0:T(8,128)}) custom-call(s32[256,1]{1,0:T(8,128)} %copy.225.rows_ref, s32[1,1024]{1,0:T(1,128)} %bitcast.374, bf16[128,960]{1,0:T(8,128)(2,1)} %copy-done.229, bf16[128,960]{1,0:T(8,128)(2,1)} %copy-done.288, bf16[128,960]{1,0:T(8,128)(2,1)} %copy-done.289, ...), custom_call_target="tpu_custom_call" | custom-call | tf_op jit(solution)/shard_map/pallas_call | solution.py:607
  327.5 17.6 %shard_map.231 = (bf16[6144,960]{1,0:T(8,128)(2,1)}, bf16[128,960]{1,0:T(8,128)(2,1)}, bf16[128,960]{1,0:T(8,128)(2,1)}, bf16[128,960]{1,0:T(8,128)(2,1)}, bf16[...) custom-call(s32[256,1]{1,0:T(8,128)} %copy.225.rows_ref, ...), custom_call_target="tpu_custom_call" | custom-call | tf_op jit(solution)/shard_map/pallas_call | solution.py:656
  354.6 3.6 collective-permute-done.228
  360.6 6.7 collective-permute-done.224
  368.6 13.4 %shard_map.232 = (bf16[128,960]{1,0:T(8,128)(2,1)}, bf16[128,2560]{1,0:T(8,128)(2,1)}, bf16[128,2560]{1,0:T(8,128)(2,1)}, f32[128,960]{1,0:T(8,128)}, bf16[128,9...) custom-call(f32[128,960]{1,0:T(8,128)} %multiply_subtract_fusion.2.new_ref, f32[128,1]{1,0:T(8,128)} %copy.222.sel_ref, ...), custom_call_target="tpu_custom_call" | custom-call | flops 4000000000 | bytes 20000000 | tf_op jit(solution)/shard_map/pallas_call | solution.py:501
  382.1 14.1 %shard_map.233 = (bf16[128,960]{1,0:T(8,128)(2,1)}, bf16[512,640]{1,0:T(8,128)(2,1)}, bf16[512,640]{1,0:T(8,128)(2,1)}, bf16[512,640]{1,0:T(8,128)(2,1)}, bf16[512,640]{1,0:T(8,128)(2,1)}) custom-call(bf16[960,128]{1,0:T(8,128)(2,1)} %get-tuple-element.351.query_ref, bf16[128,640]{1,0:T(8,128)(2,1)} %copy-done.170, bf16[128,640]{1,0:T(8,128)(2,1)} %copy-done.172, ...), custom_call_target="tpu_custom_call" | custom-call | flops 20000000000 | bytes 9000000 | tf_op jit(solution)/shard_map/pallas_call | solution.py:271
  405.4 5.5 collective-permute-done.237
  412.2 5.1 collective-permute-done.236
  419.4 5.3 collective-permute-done.234
  430.9 13.6 %shard_map.235 = (bf16[128,960]{1,0:T(8,128)(2,1)}, bf16[128,2560]{1,0:T(8,128)(2,1)}, bf16[128,2560]{1,0:T(8,128)(2,1)}, f32[128,960]{1,0:T(8,128)}, bf16[128,9...) custom-call(f32[128,960]{1,0:T(8,128)} %copy-done.88, f32[128,1]{1,0:T(8,128)} %copy.221.sel_ref, ...), custom_call_target="tpu_custom_call" | custom-call | flops 4000000000 | bytes 20000000 | tf_op jit(solution)/shard_map/pallas_call | solution.py:501
  444.6 13.8 %shard_map.236 = (bf16[128,960]{1,0:T(8,128)(2,1)}, bf16[512,640]{1,0:T(8,128)(2,1)}, bf16[512,640]{1,0:T(8,128)(2,1)}, bf16[512,640]{1,0:T(8,128)(2,1)}, bf16[512,640]{1,0:T(8,128)(2,1)}) custom-call(bf16[960,128]{1,0:T(8,128)(2,1)} %get-tuple-element.347.query_ref, bf16[128,640]{1,0:T(8,128)(2,1)} %copy-done.139, bf16[128,640]{1,0:T(8,128)(2,1)} %copy-done.141, ...), custom_call_target="tpu_custom_call" | custom-call | flops 20000000000 | bytes 9000000 | tf_op jit(solution)/shard_map/pallas_call | solution.py:271
  489.6 12.9 %shard_map.238 = (bf16[128,960]{1,0:T(8,128)(2,1)}, bf16[128,2560]{1,0:T(8,128)(2,1)}, bf16[128,2560]{1,0:T(8,128)(2,1)}, f32[128,960]{1,0:T(8,128)}, bf16[128,9...) custom-call(f32[128,960]{1,0:T(8,128)} %copy-done.86, f32[128,1]{1,0:T(8,128)} %copy.220.sel_ref, ...), custom_call_target="tpu_custom_call" | custom-call | flops 4000000000 | bytes 20000000 | tf_op jit(solution)/shard_map/pallas_call | solution.py:501
  507.6 13.6 %shard_map.239 = (bf16[128,960]{1,0:T(8,128)(2,1)}, bf16[512,640]{1,0:T(8,128)(2,1)}, bf16[512,640]{1,0:T(8,128)(2,1)}, bf16[512,640]{1,0:T(8,128)(2,1)}, bf16[512,640]{1,0:T(8,128)(2,1)}) custom-call(bf16[960,128]{1,0:T(8,128)(2,1)} %copy-done.96, bf16[128,640]{1,0:T(8,128)(2,1)} %copy-done.104, bf16[128,640]{1,0:T(8,128)(2,1)} %copy-done.106, ...), custom_call_target="tpu_custom_call" | custom-call | flops 20000000000 | bytes 9000000 | tf_op jit(solution)/shard_map/pallas_call | solution.py:271
  522.4 11.7 %shard_map.240 = bf16[16,3,80,960]{3,2,1,0:T(8,128)(2,1)} custom-call(s32[1]{0:T(128)} %bitcast.135.which_ref, bf16[128,2560]{1,0:T(8,128)(2,1)} %get-tuple-element.418.refs_0_, bf16[128,2560]{1,0:T(8,128)(2,1)} %get-tuple-element.419.refs_1_, bf16[128,2560]{1,0:T(8,128)(2,1)} %get-tuple-element.420.refs_2_, bf16[128,960]{1,0:T(8,128)(2,1)} %get-tuple-element.421.refs_3_, ...), custom_call_target="tpu_custom_call" | custom-call | tf_op jit(solution)/shard_map/pallas_call | solution.py:699
  555.8 7.5 %shard_map.241 = (bf16[960,960]{1,0:T(8,128)(2,1)}, bf16[960,960]{1,0:T(8,128)(2,1)}) custom-call(bf16[128,960]{1,0:T(8,128)(2,1)} %copy-done.38, bf16[128,960]{1,0:T(8,128)(2,1)} %get-tuple-element.433.refs_1_, bf16[128,960]{1,0:T(8,128)(2,1)} %get-tuple-element.434.refs_2_.refs_3_, bf16[128,960]{1,0:T(8,128)(2,1)} %get-tuple-element.380.dq_ref.refs_3_, ...), custom_call_target="tpu_custom_call" | custom-call | tf_op jit(solution)/shard_map/pallas_call | solution.py:730
  566.4 5.8 collective-permute-done.252
  580.6 5.0 collective-permute-done.283.refs_1_
  590.3 8.4 %shard_map.243 = bf16[4,352,960]{2,1,0:T(8,128)(2,1)} custom-call(s32[4]{0:T(128)} %pad_add_fusion.1.starts_ref, bf16[960,960]{1,0:T(8,128)(2,1)} %get-tuple-element.442.refs_0_, bf16[960,960]{1,0:T(8,128)(2,1)} %get-tuple-element.443.refs_1_, f32[16,960]{1,0:T(8,128)} %add.1262.refs_2_, bf16[128,960]{1,0:T(8,128)(2,1)} %get-tuple-element.434.refs_2_.refs_3_, ...), custom_call_target="tpu_custom_call" | custom-call | tf_op jit(solution)/shard_map/pallas_call | solution.py:768
  611.9 16.4 %all-to-all-start.3 = ((bf16[16,24,960]{2,1,0:T(8,128)(2,1)}), bf16[16,24,960]{2,1,0:T(8,128)(2,1)S(1)}, u32[]{:S(2)}, u32[]{:S(2)}) async-start(bf16[16,24,960]{2,1,0:T(8,128)(2,1)} %bitcast.163), calls=%async_computation.6 | async-start | bytes 1572864 | tf_op jit(solution)/shard_map/all_to_all | solution.py:1166
  628.4 10.5 %collective-permute-done.289 = bf16[352,960]{1,0:T(8,128)(2,1)} collective-permute-done((bf16[352,960]{1,0:T(8,128)(2,1)S(1)}, bf16[352,960]{1,0:T(8,128)(2,1)}, u32[]{:S(2)}, u32[]{:S(2)}) %collective-permute-start.289) | collective-permute-done | bytes 675872 | tf_op jit(solution)/shard_map/ppermute | solution.py:49
  644.8 10.8 %collective-permute-start.294 = (bf16[112,960]{1,0:T(8,128)(2,1)S(1)}, bf16[112,960]{1,0:T(8,128)(2,1)S(1)}, u32[]{:S(2)}, u32[]{:S(2)}) collective-permute-start(bf16[112,960]{1,0:T(8,128)(2,1)S(1)} %get-tuple-element.693), channel_id=1, source_target_pairs={{0,12},{4,0},{8,4},{12,8},{1,13},{5,1},{9,5},{13,9},{2,14},{6,2},{... | collective-permute-start | bytes 645128 | tf_op jit(solution)/shard_map/ppermute | solution.py:49
  657.4 7.7 %collective-permute-done.294 = bf16[112,960]{1,0:T(8,128)(2,1)S(1)} collective-permute-done((bf16[112,960]{1,0:T(8,128)(2,1)S(1)}, bf16[112,960]{1,0:T(8,128)(2,1)S(1)}, u32[]{:S(2)}, u32[]{:S(2)}) %collective-permute-start.294) | collective-permute-done | bytes 215072 | tf_op jit(solution)/shard_map/ppermute | solution.py:49
  665.1 3.9 collective-permute-done.292
  686.3 13.9 %all_to_all.53 = f32[128,1,128]{2,1,0:T(1,128)S(1)} all-to-all(f32[128,1,128]{2,1,0:T(1,128)S(1)} %iota.151), channel_id=1, replica_groups=mesh['z'=4,'core'=2,'y'=4,'x'=4] {'z','core','y','x'}, dimensions={0} | all-to-all | bytes 131072 | tf_op jit(solution)/shard_map/all_to_all | solution.py:1208
  705.6 5.1 multiply_subtract_fusion.1
  (840 shorter events, 271.1 us)
Async XLA Ops:
  7.2 72.1 %all-gather.13.cloned.1.call-start = ((), (), s32[]{:S(2)}) async-start(), calls=%async_computation.14 | async-start | bytes 6488064 | tf_op jit(solution)/shard_map/all_gather | solution.py:878
  26.6 129.1 %all-gather.15.cloned.1.call-start = ((), (), s32[]{:S(2)}) async-start(), calls=%async_computation.15 | async-start | bytes 16220160 | tf_op jit(solution)/shard_map/all_gather | solution.py:915
  42.5 261.6 %all-gather.17.cloned.1.call-start = ((), (), s32[]{:S(2)}) async-start(), calls=%async_computation.16 | async-start | bytes 13369344 | tf_op jit(solution)/shard_map/all_gather | solution.py:921
  63.3 424.0 %reduce-scatter.15.cloned.1.call-start = ((), (), s32[]{:S(2)}) async-start(), calls=%async_computation.18 | async-start | bytes 13369344
  79.6 15.3 %collective-permute-start.163 = (bf16[128,960]{1,0:T(8,128)(2,1)S(1)}, bf16[128,960]{1,0:T(8,128)(2,1)}, u32[]{:S(2)}, u32[]{:S(2)}) collective-permute-start(bf16[128,960]{1,0:T(8,128)(2,1)S(1)} %add_convert_fusion.24), channel_id=1, source_target_pairs={{0,32},{32,64},{64,96},{96,0},{1,33},{33,65},{65,97},{97,1},{2,34}... | collective-permute-start | bytes 737288 | tf_op jit(solution)/shard_map/ppermute | solution.py:49
  97.1 14.7 %collective-permute-start.166 = (bf16[128,640]{1,0:T(8,128)(2,1)S(1)}, bf16[128,640]{1,0:T(8,128)(2,1)S(1)}, u32[]{:S(2)}, u32[]{:S(2)}) collective-permute-start(bf16[128,640]{1,0:T(8,128)(2,1)S(1)} %get-tuple-element.342.refs_4_), channel_id=1, source_target_pairs={{0,1},{1,2},{2,3},{3,4},{4,5},{5,6},{6,7},{7,8},{8,9},{9,10},{10,1... | collective-permute-start | bytes 491528 | tf_op jit(solution)/shard_map/ppermute | solution.py:120
  100.0 15.7 %collective-permute-start.168 = (bf16[128,640]{1,0:T(8,128)(2,1)S(1)}, bf16[128,640]{1,0:T(8,128)(2,1)S(1)}, u32[]{:S(2)}, u32[]{:S(2)}) collective-permute-start(bf16[128,640]{1,0:T(8,128)(2,1)S(1)} %get-tuple-element.342.refs_4_), channel_id=1, source_target_pairs={{64,1},{65,2},{66,3},{67,4},{68,5},{69,6},{70,7},{71,8},{72,9},{73... | collective-permute-start | bytes 491528 | tf_op jit(solution)/shard_map/ppermute | solution.py:120
  168.8 18.7 %collective-permute-start.181 = (bf16[128,640]{1,0:T(8,128)(2,1)}, bf16[128,640]{1,0:T(8,128)(2,1)S(1)}, u32[]{:S(2)}, u32[]{:S(2)}) collective-permute-start(bf16[128,640]{1,0:T(8,128)(2,1)} %get-tuple-element.348.refs_4_), channel_id=1, source_target_pairs={{0,1},{1,2},{2,3},{3,4},{4,5},{5,6},{6,7},{7,8},{8,9},{9,10},{10,1... | collective-permute-start | bytes 491528 | tf_op jit(solution)/shard_map/ppermute | solution.py:120
  172.0 16.8 %collective-permute-start.182 = (bf16[128,640]{1,0:T(8,128)(2,1)}, bf16[128,640]{1,0:T(8,128)(2,1)S(1)}, u32[]{:S(2)}, u32[]{:S(2)}) collective-permute-start(bf16[128,640]{1,0:T(8,128)(2,1)} %get-tuple-element.348.refs_4_), channel_id=1, source_target_pairs={{32,1},{33,2},{34,3},{35,4},{36,5},{37,6},{38,7},{39,8},{40,9},{41... | collective-permute-start | bytes 491528 | tf_op jit(solution)/shard_map/ppermute | solution.py:120
  172.7 18.6 %collective-permute-start.183 = (bf16[128,640]{1,0:T(8,128)(2,1)}, bf16[128,640]{1,0:T(8,128)(2,1)S(1)}, u32[]{:S(2)}, u32[]{:S(2)}) collective-permute-start(bf16[128,640]{1,0:T(8,128)(2,1)} %get-tuple-element.348.refs_4_), channel_id=1, source_target_pairs={{64,1},{65,2},{66,3},{67,4},{68,5},{69,6},{70,7},{71,8},{72,9},{73... | collective-permute-start | bytes 491528 | tf_op jit(solution)/shard_map/ppermute | solution.py:120
  222.7 23.5 %collective-permute-start.196 = (bf16[128,640]{1,0:T(8,128)(2,1)}, bf16[128,640]{1,0:T(8,128)(2,1)S(1)}, u32[]{:S(2)}, u32[]{:S(2)}) collective-permute-start(bf16[128,640]{1,0:T(8,128)(2,1)} %get-tuple-element.352.refs_4_), channel_id=1, source_target_pairs={{0,1},{1,2},{2,3},{3,4},{4,5},{5,6},{6,7},{7,8},{8,9},{9,10},{10,1... | collective-permute-start | bytes 491528 | tf_op jit(solution)/shard_map/ppermute | solution.py:120
  228.2 19.4 %collective-permute-start.197 = (bf16[128,640]{1,0:T(8,128)(2,1)}, bf16[128,640]{1,0:T(8,128)(2,1)S(1)}, u32[]{:S(2)}, u32[]{:S(2)}) collective-permute-start(bf16[128,640]{1,0:T(8,128)(2,1)} %get-tuple-element.352.refs_4_), channel_id=1, source_target_pairs={{32,1},{33,2},{34,3},{35,4},{36,5},{37,6},{38,7},{39,8},{40,9},{41... | collective-permute-start | bytes 491528 | tf_op jit(solution)/shard_map/ppermute | solution.py:120
  228.9 21.2 %collective-permute-start.198 = (bf16[128,640]{1,0:T(8,128)(2,1)}, bf16[128,640]{1,0:T(8,128)(2,1)S(1)}, u32[]{:S(2)}, u32[]{:S(2)}) collective-permute-start(bf16[128,640]{1,0:T(8,128)(2,1)} %get-tuple-element.352.refs_4_), channel_id=1, source_target_pairs={{64,1},{65,2},{66,3},{67,4},{68,5},{69,6},{70,7},{71,8},{72,9},{73... | collective-permute-start | bytes 491528 | tf_op jit(solution)/shard_map/ppermute | solution.py:120
  237.1 15.0 %collective-permute-start.199 = (bf16[128,640]{1,0:T(8,128)(2,1)}, bf16[128,640]{1,0:T(8,128)(2,1)S(1)}, u32[]{:S(2)}, u32[]{:S(2)}) collective-permute-start(bf16[128,640]{1,0:T(8,128)(2,1)} %get-tuple-element.352.refs_4_), channel_id=1, source_target_pairs={{96,1},{97,2},{98,3},{99,4},{100,5},{101,6},{102,7},{103,8},{104,9... | collective-permute-start | bytes 491528 | tf_op jit(solution)/shard_map/ppermute | solution.py:120
  238.4 14.7 %collective-permute-start.200 = (bf16[128,640]{1,0:T(8,128)(2,1)}, bf16[128,640]{1,0:T(8,128)(2,1)S(1)}, u32[]{:S(2)}, u32[]{:S(2)}) collective-permute-start(bf16[128,640]{1,0:T(8,128)(2,1)} %get-tuple-element.352.refs_4_), channel_id=1, source_target_pairs={{0,96},{1,97},{2,98},{3,99},{4,100},{5,101},{6,102},{7,103},{8,104... | collective-permute-start | bytes 491528 | tf_op jit(solution)/shard_map/ppermute | solution.py:113
  286.8 17.3 %collective-permute-start.214 = (bf16[128,960]{1,0:T(8,128)(2,1)S(1)}, bf16[128,960]{1,0:T(8,128)(2,1)S(1)}, u32[]{:S(2)}, u32[]{:S(2)}) collective-permute-start(bf16[128,960]{1,0:T(8,128)(2,1)S(1)} %multiply_convert_fusion.1.refs_0_), channel_id=1, source_target_pairs={{0,16},{16,0},{1,17},{17,1},{2,18},{18,2},{3,19},{19,3},{4,20},{20... | collective-permute-start | bytes 737288 | tf_op jit(solution)/shard_map/ppermute | solution.py:53
  345.2 299.5 %reduce-scatter.13.cloned.1.call-start = ((), (), s32[]{:S(2)}) async-start(), calls=%async_computation.17 | async-start | bytes 8355840 | tf_op jit(solution)/shard_map/reduce_scatter | solution.py:1101
  352.5 14.8 %collective-permute-start.224 = (bf16[128,960]{1,0:T(8,128)(2,1)S(1)}, bf16[128,960]{1,0:T(8,128)(2,1)S(1)}, u32[]{:S(2)}, u32[]{:S(2)}) collective-permute-start(bf16[128,960]{1,0:T(8,128)(2,1)S(1)} %add_convert_fusion.21), channel_id=1, source_target_pairs={{0,32},{32,64},{64,96},{96,0},{1,33},{33,65},{65,97},{97,1},{2,34}... | collective-permute-start | bytes 737288 | tf_op jit(solution)/shard_map/ppermute | solution.py:49
  400.3 17.0 %collective-permute-start.236 = (bf16[128,640]{1,0:T(8,128)(2,1)S(1)}, bf16[128,640]{1,0:T(8,128)(2,1)S(1)}, u32[]{:S(2)}, u32[]{:S(2)}) collective-permute-start(bf16[128,640]{1,0:T(8,128)(2,1)S(1)} %get-tuple-element.718), channel_id=1, source_target_pairs={{1,64},{2,65},{3,66},{4,67},{5,68},{6,69},{7,70},{8,71},{9,72},{10... | collective-permute-start | bytes 491528 | tf_op jit(solution)/shard_map/ppermute | solution.py:136
  401.6 17.8 %collective-permute-start.235 = (bf16[128,640]{1,0:T(8,128)(2,1)S(1)}, bf16[128,640]{1,0:T(8,128)(2,1)S(1)}, u32[]{:S(2)}, u32[]{:S(2)}) collective-permute-start(bf16[128,640]{1,0:T(8,128)(2,1)S(1)} %get-tuple-element.719), channel_id=1, source_target_pairs={{1,32},{2,33},{3,34},{4,35},{5,36},{6,37},{7,38},{8,39},{9,40},{10... | collective-permute-start | bytes 491528 | tf_op jit(solution)/shard_map/ppermute | solution.py:136
  402.3 22.5 %collective-permute-start.234 = (bf16[128,640]{1,0:T(8,128)(2,1)S(1)}, bf16[128,640]{1,0:T(8,128)(2,1)S(1)}, u32[]{:S(2)}, u32[]{:S(2)}) collective-permute-start(bf16[128,640]{1,0:T(8,128)(2,1)S(1)} %get-tuple-element.716), channel_id=1, source_target_pairs={{1,0},{2,1},{3,2},{4,3},{5,4},{6,5},{7,6},{8,7},{9,8},{10,9},{11,1... | collective-permute-start | bytes 491528 | tf_op jit(solution)/shard_map/ppermute | solution.py:136
  403.9 20.8 %collective-permute-start.232 = (bf16[128,640]{1,0:T(8,128)(2,1)S(1)}, bf16[128,640]{1,0:T(8,128)(2,1)S(1)}, u32[]{:S(2)}, u32[]{:S(2)}) collective-permute-start(bf16[128,640]{1,0:T(8,128)(2,1)S(1)} %get-tuple-element.714), channel_id=1, source_target_pairs={{32,0},{64,32},{96,64},{33,1},{65,33},{97,65},{34,2},{66,34},{98,6... | collective-permute-start | bytes 491528 | tf_op jit(solution)/shard_map/ppermute | solution.py:130
  464.8 15.0 %collective-permute-start.243 = (bf16[128,640]{1,0:T(8,128)(2,1)S(1)}, bf16[128,640]{1,0:T(8,128)(2,1)S(1)}, u32[]{:S(2)}, u32[]{:S(2)}) collective-permute-start(bf16[128,640]{1,0:T(8,128)(2,1)S(1)} %get-tuple-element.709), channel_id=1, source_target_pairs={{1,0},{2,1},{3,2},{4,3},{5,4},{6,5},{7,6},{8,7},{9,8},{10,9},{11,1... | collective-permute-start | bytes 491528 | tf_op jit(solution)/shard_map/ppermute | solution.py:136
  466.4 14.3 %collective-permute-start.241 = (bf16[128,640]{1,0:T(8,128)(2,1)S(1)}, bf16[128,640]{1,0:T(8,128)(2,1)S(1)}, u32[]{:S(2)}, u32[]{:S(2)}) collective-permute-start(bf16[128,640]{1,0:T(8,128)(2,1)S(1)} %get-tuple-element.707), channel_id=1, source_target_pairs={{32,0},{64,32},{96,64},{33,1},{65,33},{97,65},{34,2},{66,34},{98,6... | collective-permute-start | bytes 491528 | tf_op jit(solution)/shard_map/ppermute | solution.py:130
  474.9 27.8 %collective-permute-start.268 = (bf16[128,1280]{1,0:T(8,128)(2,1)}, bf16[128,1280]{1,0:T(8,128)(2,1)}, u32[]{:S(2)}, u32[]{:S(2)}) collective-permute-start(bf16[128,1280]{1,0:T(8,128)(2,1)} %constant_dynamic-slice_fusion.11), channel_id=1, source_target_pairs={{0,16},{16,0},{1,17},{17,1},{2,18},{18,2},{3,19},{19,3},{4,20},{20... | collective-permute-start | bytes 983048 | tf_op jit(solution)/shard_map/ppermute | solution.py:53
  479.8 22.8 %collective-permute-start.269 = (bf16[128,960]{1,0:T(8,128)(2,1)}, bf16[128,960]{1,0:T(8,128)(2,1)}, u32[]{:S(2)}, u32[]{:S(2)}) collective-permute-start(bf16[128,960]{1,0:T(8,128)(2,1)} %get-tuple-element.431.refs_23_), channel_id=1, source_target_pairs={{0,16},{16,0},{1,17},{17,1},{2,18},{18,2},{3,19},{19,3},{4,20},{20... | collective-permute-start | bytes 737288 | tf_op jit(solution)/shard_map/ppermute | solution.py:53
  480.7 22.6 %collective-permute-start.263 = (bf16[128,1280]{1,0:T(8,128)(2,1)}, bf16[128,1280]{1,0:T(8,128)(2,1)}, u32[]{:S(2)}, u32[]{:S(2)}) collective-permute-start(bf16[128,1280]{1,0:T(8,128)(2,1)} %constant_dynamic-slice_fusion.14), channel_id=1, source_target_pairs={{0,16},{16,0},{1,17},{17,1},{2,18},{18,2},{3,19},{19,3},{4,20},{20... | collective-permute-start | bytes 983048 | tf_op jit(solution)/shard_map/ppermute | solution.py:53
  480.7 22.4 %collective-permute-start.264 = (bf16[128,960]{1,0:T(8,128)(2,1)}, bf16[128,960]{1,0:T(8,128)(2,1)}, u32[]{:S(2)}, u32[]{:S(2)}) collective-permute-start(bf16[128,960]{1,0:T(8,128)(2,1)} %get-tuple-element.426.refs_13_), channel_id=1, source_target_pairs={{0,16},{16,0},{1,17},{17,1},{2,18},{18,2},{3,19},{19,3},{4,20},{20... | collective-permute-start | bytes 737288 | tf_op jit(solution)/shard_map/ppermute | solution.py:53
  482.8 20.8 %collective-permute-start.259 = (bf16[128,960]{1,0:T(8,128)(2,1)}, bf16[128,960]{1,0:T(8,128)(2,1)}, u32[]{:S(2)}, u32[]{:S(2)}) collective-permute-start(bf16[128,960]{1,0:T(8,128)(2,1)} %get-tuple-element.421.refs_3_), channel_id=1, source_target_pairs={{0,16},{16,0},{1,17},{17,1},{2,18},{18,2},{3,19},{19,3},{4,20},{20... | collective-permute-start | bytes 737288 | tf_op jit(solution)/shard_map/ppermute | solution.py:53
  505.8 15.4 %collective-permute-start.261 = (bf16[128,1280]{1,0:T(8,128)(2,1)S(1)}, bf16[128,1280]{1,0:T(8,128)(2,1)S(1)}, u32[]{:S(2)}, u32[]{:S(2)}) collective-permute-start(bf16[128,1280]{1,0:T(8,128)(2,1)S(1)} %copy-done.253), channel_id=1, source_target_pairs={{0,16},{16,0},{1,17},{17,1},{2,18},{18,2},{3,19},{19,3},{4,20},{20... | collective-permute-start | bytes 983048 | tf_op jit(solution)/shard_map/ppermute | solution.py:53
  506.3 14.9 %collective-permute-start.262 = (bf16[128,1280]{1,0:T(8,128)(2,1)S(1)}, bf16[128,1280]{1,0:T(8,128)(2,1)S(1)}, u32[]{:S(2)}, u32[]{:S(2)}) collective-permute-start(bf16[128,1280]{1,0:T(8,128)(2,1)S(1)} %copy-done.259), channel_id=1, source_target_pairs={{0,16},{16,0},{1,17},{17,1},{2,18},{18,2},{3,19},{19,3},{4,20},{20... | collective-permute-start | bytes 983048 | tf_op jit(solution)/shard_map/ppermute | solution.py:53
  506.5 14.8 %collective-permute-start.266 = (bf16[128,1280]{1,0:T(8,128)(2,1)S(1)}, bf16[128,1280]{1,0:T(8,128)(2,1)S(1)}, u32[]{:S(2)}, u32[]{:S(2)}) collective-permute-start(bf16[128,1280]{1,0:T(8,128)(2,1)S(1)} %constant_dynamic-slice_fusion.13), channel_id=1, source_target_pairs={{0,16},{16,0},{1,17},{17,1},{2,18},{18,2},{3,19},{19,3},{4,20},{20... | collective-permute-start | bytes 983048 | tf_op jit(solution)/shard_map/ppermute | solution.py:53
  506.9 14.4 %collective-permute-start.267 = (bf16[128,1280]{1,0:T(8,128)(2,1)S(1)}, bf16[128,1280]{1,0:T(8,128)(2,1)S(1)}, u32[]{:S(2)}, u32[]{:S(2)}) collective-permute-start(bf16[128,1280]{1,0:T(8,128)(2,1)S(1)} %constant_dynamic-slice_fusion.12), channel_id=1, source_target_pairs={{0,16},{16,0},{1,17},{17,1},{2,18},{18,2},{3,19},{19,3},{4,20},{20... | collective-permute-start | bytes 983048 | tf_op jit(solution)/shard_map/ppermute | solution.py:53
  545.4 18.0 %collective-permute-start.253 = (bf16[128,640]{1,0:T(8,128)(2,1)}, bf16[128,640]{1,0:T(8,128)(2,1)}, u32[]{:S(2)}, u32[]{:S(2)}) collective-permute-start(bf16[128,640]{1,0:T(8,128)(2,1)} %get-tuple-element.705), channel_id=1, source_target_pairs={{1,32},{2,33},{3,34},{4,35},{5,36},{6,37},{7,38},{8,39},{9,40},{10... | collective-permute-start | bytes 491528 | tf_op jit(solution)/shard_map/ppermute | solution.py:136
  546.8 25.4 %collective-permute-start.252 = (bf16[128,640]{1,0:T(8,128)(2,1)}, bf16[128,640]{1,0:T(8,128)(2,1)}, u32[]{:S(2)}, u32[]{:S(2)}) collective-permute-start(bf16[128,640]{1,0:T(8,128)(2,1)} %get-tuple-element.702), channel_id=1, source_target_pairs={{1,0},{2,1},{3,2},{4,3},{5,4},{6,5},{7,6},{8,7},{9,8},{10,9},{11,1... | collective-permute-start | bytes 491528 | tf_op jit(solution)/shard_map/ppermute | solution.py:136
  548.1 25.8 %collective-permute-start.250 = (bf16[128,640]{1,0:T(8,128)(2,1)}, bf16[128,640]{1,0:T(8,128)(2,1)}, u32[]{:S(2)}, u32[]{:S(2)}) collective-permute-start(bf16[128,640]{1,0:T(8,128)(2,1)} %get-tuple-element.700), channel_id=1, source_target_pairs={{32,0},{64,32},{96,64},{33,1},{65,33},{97,65},{34,2},{66,34},{98,6... | collective-permute-start | bytes 491528 | tf_op jit(solution)/shard_map/ppermute | solution.py:130
  550.4 23.5 %collective-permute-start.249 = (bf16[128,640]{1,0:T(8,128)(2,1)}, bf16[128,640]{1,0:T(8,128)(2,1)}, u32[]{:S(2)}, u32[]{:S(2)}) collective-permute-start(bf16[128,640]{1,0:T(8,128)(2,1)} %get-tuple-element.701), channel_id=1, source_target_pairs={{64,0},{96,32},{65,1},{97,33},{66,2},{98,34},{67,3},{99,35},{68,4}... | collective-permute-start | bytes 491528 | tf_op jit(solution)/shard_map/ppermute | solution.py:130
  554.4 19.5 %collective-permute-start.248 = (bf16[128,640]{1,0:T(8,128)(2,1)}, bf16[128,640]{1,0:T(8,128)(2,1)}, u32[]{:S(2)}, u32[]{:S(2)}) collective-permute-start(bf16[128,640]{1,0:T(8,128)(2,1)} %get-tuple-element.699), channel_id=1, source_target_pairs={{96,0},{97,1},{98,2},{99,3},{100,4},{101,5},{102,6},{103,7},{104,8... | collective-permute-start | bytes 491528 | tf_op jit(solution)/shard_map/ppermute | solution.py:130
  563.4 26.2 %collective-permute-start.286 = (bf16[128,640]{1,0:T(8,128)(2,1)}, bf16[128,640]{1,0:T(8,128)(2,1)}, u32[]{:S(2)}, u32[]{:S(2)}) collective-permute-start(bf16[128,640]{1,0:T(8,128)(2,1)} %get-tuple-element.454.refs_5_), channel_id=1, source_target_pairs={{0,16},{16,0},{1,17},{17,1},{2,18},{18,2},{3,19},{19,3},{4,20},{20... | collective-permute-start | bytes 491528 | tf_op jit(solution)/shard_map/ppermute | solution.py:53
  572.1 17.5 %collective-permute-start.287 = (bf16[128,640]{1,0:T(8,128)(2,1)}, bf16[128,640]{1,0:T(8,128)(2,1)}, u32[]{:S(2)}, u32[]{:S(2)}) collective-permute-start(bf16[128,640]{1,0:T(8,128)(2,1)} %get-tuple-element.455.refs_9_), channel_id=1, source_target_pairs={{0,16},{16,0},{1,17},{17,1},{2,18},{18,2},{3,19},{19,3},{4,20},{20... | collective-permute-start | bytes 491528 | tf_op jit(solution)/shard_map/ppermute | solution.py:53
  588.5 17.5 %collective-permute-start.301 = (bf16[128,960]{1,0:T(8,128)(2,1)S(1)}, bf16[128,960]{1,0:T(8,128)(2,1)S(1)}, u32[]{:S(2)}, u32[]{:S(2)}) collective-permute-start(bf16[128,960]{1,0:T(8,128)(2,1)S(1)} %convert_element_type.774.refs_0_), channel_id=1, source_target_pairs={{0,64},{32,96},{64,0},{96,32},{1,65},{33,97},{65,1},{97,33},{2,66}... | collective-permute-start | bytes 737288 | tf_op jit(solution)/shard_map/ppermute | solution.py:49
  601.7 26.6 %collective-permute-start.291 = (bf16[352,960]{1,0:T(8,128)(2,1)}, bf16[352,960]{1,0:T(8,128)(2,1)}, u32[]{:S(2)}, u32[]{:S(2)}) collective-permute-start(bf16[352,960]{1,0:T(8,128)(2,1)} %get-tuple-element.690), channel_id=1, source_target_pairs={{0,96},{32,0},{64,32},{96,64},{1,97},{33,1},{65,33},{97,65},{2,98}... | collective-permute-start | bytes 2027528 | tf_op jit(solution)/shard_map/ppermute | solution.py:49
  603.5 24.9 %collective-permute-start.290 = (bf16[352,960]{1,0:T(8,128)(2,1)}, bf16[352,960]{1,0:T(8,128)(2,1)}, u32[]{:S(2)}, u32[]{:S(2)}) collective-permute-start(bf16[352,960]{1,0:T(8,128)(2,1)} %get-tuple-element.691), channel_id=1, source_target_pairs={{0,64},{32,96},{64,0},{96,32},{1,65},{33,97},{65,1},{97,33},{2,66}... | collective-permute-start | bytes 2027528 | tf_op jit(solution)/shard_map/ppermute | solution.py:49
  604.3 34.6 %collective-permute-start.289 = (bf16[352,960]{1,0:T(8,128)(2,1)S(1)}, bf16[352,960]{1,0:T(8,128)(2,1)}, u32[]{:S(2)}, u32[]{:S(2)}) collective-permute-start(bf16[352,960]{1,0:T(8,128)(2,1)S(1)} %get-tuple-element.689), channel_id=1, source_target_pairs={{0,32},{32,64},{64,96},{96,0},{1,33},{33,65},{65,97},{97,1},{2,34}... | collective-permute-start | bytes 2027528 | tf_op jit(solution)/shard_map/ppermute | solution.py:49
  611.9 29.9 %all-to-all-start.3 = ((bf16[16,24,960]{2,1,0:T(8,128)(2,1)}), bf16[16,24,960]{2,1,0:T(8,128)(2,1)S(1)}, u32[]{:S(2)}, u32[]{:S(2)}) async-start(bf16[16,24,960]{2,1,0:T(8,128)(2,1)} %bitcast.163), calls=%async_computation.6 | async-start | bytes 1572864 | tf_op jit(solution)/shard_map/all_to_all | solution.py:1166
  644.8 20.2 %collective-permute-start.294 = (bf16[112,960]{1,0:T(8,128)(2,1)S(1)}, bf16[112,960]{1,0:T(8,128)(2,1)S(1)}, u32[]{:S(2)}, u32[]{:S(2)}) collective-permute-start(bf16[112,960]{1,0:T(8,128)(2,1)S(1)} %get-tuple-element.693), channel_id=1, source_target_pairs={{0,12},{4,0},{8,4},{12,8},{1,13},{5,1},{9,5},{13,9},{2,14},{6,2},{... | collective-permute-start | bytes 645128 | tf_op jit(solution)/shard_map/ppermute | solution.py:49
  656.5 15.5 %collective-permute-start.300 = (bf16[3,20,960]{2,1,0:T(8,128)(2,1)S(1)}, bf16[3,20,960]{2,1,0:T(8,128)(2,1)S(1)}, u32[]{:S(2)}, u32[]{:S(2)}) collective-permute-start(bf16[3,20,960]{2,1,0:T(8,128)(2,1)S(1)} %get-tuple-element.721), channel_id=1, source_target_pairs={{0,32},{32,64},{64,96},{96,0},{1,33},{33,65},{65,97},{97,1},{2,34}... | collective-permute-start | bytes 345608 | tf_op jit(solution)/shard_map/ppermute | solution.py:49
  656.6 16.1 %collective-permute-start.299 = (bf16[3,20,960]{2,1,0:T(8,128)(2,1)S(1)}, bf16[3,20,960]{2,1,0:T(8,128)(2,1)S(1)}, u32[]{:S(2)}, u32[]{:S(2)}) collective-permute-start(bf16[3,20,960]{2,1,0:T(8,128)(2,1)S(1)} %get-tuple-element.722), channel_id=1, source_target_pairs={{0,64},{32,96},{64,0},{96,32},{1,65},{33,97},{65,1},{97,33},{2,66}... | collective-permute-start | bytes 345608 | tf_op jit(solution)/shard_map/ppermute | solution.py:49
  (301 other events, 2627.7 us)
Sparse Core Ops, SparseCore 0:
  17.5 61.5 all-gather.12
  82.3 73.4 all-gather.14
  158.1 108.4 all-gather.16
  345.3 105.0 reduce-scatter.14
  534.3 93.1 reduce-scatter.12

commit v7 on v6

--- a/solution.py
+++ b/solution.py
@@ -626,7 +626,7 @@
 
 
 def head_back_kernel(
-    rows_ref, near_ref, target_ref, stat_ref, logit_ref, pick_ref, table_ref, grad_ref, *refs
+    rows_ref, near_ref, target_ref, stat_ref, logit_ref, table_ref, grad_ref, *refs
 ):
     block_refs, (sum_ref, norm_ref) = refs[:8], refs[8:]
     step = pl.program_id(0)
@@ -641,7 +641,7 @@
     probs = jnp.exp(logit_ref[...] - norm_ref[:, 0:1])
     hit = jnp.where(place == target_ref[...], 1.0, 0.0)
     grads = ((probs - hit) * (1.0 / TOK_DEV)).astype(BFLOAT)
-    grad_ref[...] = contract_rows(grads, pick_ref[...]).astype(BFLOAT)
+    grad_ref[...] = grads
     sum_ref[...] += nn(grads, table_ref[...])
 
     @pl.when(step == pl.num_programs(0) - 1)
@@ -652,7 +652,8 @@
             ref[...] = contract_rows(hot.astype(FLOAT).astype(BFLOAT), total).astype(BFLOAT)
 
 
-def head_back(loss_rows, near_rows, local_targets, stats, logits, picked, table):
+def head_back(loss_rows, near_rows, local_targets, stats, logits, table):
+    cols = pl.BlockSpec((256, HEAD_BLOCK), lambda i: (0, i))
     return pl.pallas_call(
         head_back_kernel,
         grid=(VOCAB_MP // HEAD_BLOCK,),
@@ -661,15 +662,29 @@
             whole(1, ROWS),
             whole(256, 1),
             whole(8, 256),
-            pl.BlockSpec((256, HEAD_BLOCK), lambda i: (0, i)),
-            whole(256, D),
+            cols,
             pl.BlockSpec((HEAD_BLOCK, D), lambda i: (i, 0)),
         ],
-        out_specs=[pl.BlockSpec((HEAD_BLOCK, D), lambda i: (i, 0))] + [whole(TOK_DEV, D)] * MP,
-        out_shape=[struct(BFLOAT, VOCAB_MP, D)] + [struct(BFLOAT, TOK_DEV, D)] * MP,
+        out_specs=[cols] + [whole(TOK_DEV, D)] * MP,
+        out_shape=[struct(BFLOAT, 256, VOCAB_MP)] + [struct(BFLOAT, TOK_DEV, D)] * MP,
         scratch_shapes=[pltpu.VMEM((256, D), FLOAT), pltpu.VMEM((256, 128), FLOAT)],
         compiler_params=params(BIG),
-    )(loss_rows, near_rows, local_targets, stats, logits, picked, table)
+    )(loss_rows, near_rows, local_targets, stats, logits, table)
+
+
+def head_table_kernel(grad_ref, pick_ref, out_ref):
+    out_ref[...] = contract_rows(grad_ref[...], pick_ref[...]).astype(BFLOAT)
+
+
+def head_table(grads, picked):
+    return pl.pallas_call(
+        head_table_kernel,
+        grid=(VOCAB_MP // HEAD_BLOCK,),
+        in_specs=[pl.BlockSpec((256, HEAD_BLOCK), lambda i: (0, i)), whole(256, D)],
+        out_specs=pl.BlockSpec((HEAD_BLOCK, D), lambda i: (i, 0)),
+        out_shape=struct(BFLOAT, VOCAB_MP, D),
+        compiler_params=params(BIG),
+    )(grads, picked)
 
 
 def mlp_grad_kernel(which_ref, *refs):
@@ -1034,8 +1049,9 @@
         jnp.sum(lax.dynamic_slice_in_dim(cross, model_index * per_device, per_device))
         + ROUTER_LOSS * penalty_total
     )
-    head_grad, *scattered = head_back(*head_args, local_targets, stats, logits, picked, table)
-    grad_final = scatter_group(scattered)
+    grad_logits, *scattered = head_back(*head_args, local_targets, stats, logits, table)
+    grad_final, grad_logits = scatter_group(scattered, grad_logits)
+    head_grad = head_table(grad_logits, picked)
     grad_hidden, grad_gain_final = rms_back(hidden, gains[2], grad_final)
     if not dense:
         head_grad = lax.psum_scatter(head_grad, DP_AXES, scatter_dimension=0, tiled=True)
@@ -1089,9 +1105,9 @@
         grad_query, *grad_sides = attend_back(
             queries, pairs, biases[step], log_total, attended, grad_attended, *turns
         )
-        far_normed = swap(normed)
+        far_normed, far_attended = early if step == 0 else (swap(normed), swap(attended))
         square_kept.append((attended, grad_attn, normed, grad_query))
-        square_far.append((swap(attended), swap(grad_attn), far_normed, swap(grad_query)))
+        square_far.append((far_attended, swap(grad_attn), far_normed, swap(grad_query)))
         if step == 0:
             tied = tie(*grad_sides, *mlp_kept[-1])
             grad_sides, mlp_kept[-1] = tied[:4], tied[4:]
@@ -1109,8 +1125,18 @@
         gain_one = gain_one + small[0:1]
         pack_kept.append((normed, grad_pair))
         pack_far.append((far_normed, swap(grad_pair)))
-        if step == 1 and not dense:
-            head_grad, grad_hidden = tie(head_grad, grad_hidden)
+        if step > 0:
+            count = len(mlp_far[-1])
+            tied = tie(grad_hidden, *mlp_far[-1], *square_far[-1])
+            grad_hidden, mlp_far[-1] = tied[0], tied[1 : 1 + count]
+            square_far[-1] = tied[1 + count :]
+            pack_far[-1] = (square_far[-1][2], pack_far[-1][1])
+        if step == 1:
+            early = swap(saves[0][1]), swap(saves[0][4])
+            if dense:
+                *early, grad_hidden = tie(*early, grad_hidden)
+            else:
+                *early, head_grad, grad_hidden = tie(*early, head_grad, grad_hidden)
 
     sent = grad_hidden.astype(BFLOAT)
     grad_embed = [sent] + [shift(sent, "z", -k) for k in (1, 2, 3)]
@@ -1140,13 +1166,13 @@
         return jnp.stack([value[..., i : i + 48, :] for i in (0, 16, 40, 56)])
 
     part = stage(part, "z", z).astype(BFLOAT)
-    part, mlp_sum = tie(y_windows(part), mlp_sum)
+    part = stage(y_windows(part), "y", y).astype(BFLOAT)
+    part, mlp_sum = tie(x_windows(part), mlp_sum)
     mlp_sum = mlp_sum.reshape(3, 4, UNITS, D).transpose(1, 0, 2, 3)
     mlp_grad = mlp_sum[0].astype(FLOAT)
     for k in (1, 2, 3):
         mlp_grad = mlp_grad + shift(mlp_sum[k], "z", -k).astype(FLOAT)
-    part = stage(part, "y", y).astype(BFLOAT)
-    part = stage(x_windows(part), "x", x).reshape(-1)
+    part = stage(part, "x", x).reshape(-1)
     begin = aligned_row(DP * model_index) + 80 * y + (20 * x) // 8 * 8
     pack_grad = lax.dynamic_slice(part, (PACK_DEV * device - D * begin,), (PACK_DEV,))
 

time: 729 us -> 750 us (1.029)
  starting transfers between devices: 215 us -> 231 us
    ppermute x33, waiting for transfers between devices: 70.7 us -> 51.7 us  [shift(): return lax.ppermute(value, axis, [(i, (i + steps) % 4) for i in range(4)])]
    ppermute x33, starting transfers between devices: 41.8 us -> 55.6 us  [shift(): return lax.ppermute(value, axis, [(i, (i + steps) % 4) for i in range(4)])]
    ppermute x9, waiting for transfers between devices: 4.72 us -> 17.1 us  [group_scatter(): total = total + lax.ppermute(own[k], 'z', pairs).astype(FLOAT)]
    pallas_call x0 -> x1, Pallas kernels: none -> 8.94 us  [head_table(): pl.pallas_call(head_table_kernel, grid=(VOCAB_MP // HEAD_BLOCK,), in_spec...]
    unnamed x383 -> x357, local copies, waits for them, and re-layouts: 22.8 us -> 23.3 us
  transfers between devices with their start and end apart: 160 -> 160, of which waited for: 56 -> 52; matrix products, arithmetic and copies ran while one was open for 7% -> 7% of each run, Pallas kernels for 25% -> 24%
where the time goes in v7:
time: 750 us; the launch traced here: 740 us
  starting transfers between devices  231 us (31%)
  Pallas kernels  226 us (30%)
  waiting for transfers between devices  128 us (17%)
  local copies, waits for them, and re-layouts  46.7 us (6%)
  other arithmetic  41.6 us (6%)
  blocking collectives  35.4 us (5%)
  between operations  23.4 us (3%)
    ppermute x78, starting transfers between devices, swap(): return lax.ppermute(value, 'core', [(0, 1), (1, 0)])  58 us
    ppermute x33, starting transfers between devices, shift(): return lax.ppermute(value, axis, [(i, (i + steps) % 4) for i in range(4)])  55.6 us
    ppermute x33, waiting for transfers between devices, shift(): return lax.ppermute(value, axis, [(i, (i + steps) % 4) for i in range(4)])  51.7 us
    ppermute x12, starting transfers between devices, group_gather(): prev.append(lax.ppermute(pair, ('z',) + DP_AXES, pairs))  41.6 us
    pallas_call x3, Pallas kernels, attend_back(): pl.pallas_call(attend_back_kernel, out_shape=(struct(BFLOAT, TOK_DEV, D),...  41.3 us
    pallas_call x3, Pallas kernels, block_back(): pl.pallas_call(block_back_kernel, grid=(FF_STEPS,), in_specs=[full, whole...  39.8 us
    pallas_call x3, Pallas kernels, block(): pl.pallas_call(functools.partial(block_kernel, more), grid=(FF_STEPS,), i...  38.4 us
    ppermute x12, waiting for transfers between devices, group_scatter(): total = total + lax.ppermute(prev[k], ('z',) + DP_AXES, pairs).astype(FLOAT)  32.2 us
  transfers between devices with their start and end apart: 160, of which 52 were waited for; matrix products, arithmetic and copies ran while one was open for 7% of the time, Pallas kernels for 24%

profile of v7, /device:TPU:1, one launch (start us, length us, event | category | flops | bytes accessed | tf_op | source)
XLA Modules:
  0.0 739.7 jit_solution(3085014002721109358)
XLA Ops:
  20.4 6.2 all-to-all-start.1
  33.2 4.2 collective-permute-done.154
  40.3 16.7 %all_to_all.52 = bf16[16,24,960]{2,1,0:T(8,128)(2,1)S(1)} all-to-all(bf16[16,24,960]{2,1,0:T(8,128)(2,1)S(1)} %bitcast.349), channel_id=1, replica_groups=mesh['z'=4,'core'=2,'y'=4,'x'=4] {'y','x'}, dimensions={0} | all-to-all | bytes 1474560 | tf_op jit(solution)/shard_map/all_to_all | solution.py:934
  67.4 5.6 collective-permute-start.159
  86.2 4.6 shard_map.222
  96.5 8.7 %collective-permute-start.168 = (bf16[128,640]{1,0:T(8,128)(2,1)S(1)}, bf16[128,640]{1,0:T(8,128)(2,1)S(1)}, u32[]{:S(2)}, u32[]{:S(2)}) collective-permute-start(bf16[128,640]{1,0:T(8,128)(2,1)S(1)} %get-tuple-element.395.refs_4_), channel_id=1, source_target_pairs={{64,1},{65,2},{66,3},{67,4},{68,5},{69,6},{70,7},{71,8},{72,9},{73... | collective-permute-start | bytes 491528 | tf_op jit(solution)/shard_map/ppermute | solution.py:120
  106.5 6.5 collective-permute-start.170
  125.3 9.5 %shard_map.224 = (bf16[128,960]{1,0:T(8,128)(2,1)}, f32[8,384]{1,0:T(8,128)S(1)}) custom-call(bf16[960,128]{1,0:T(8,128)(2,1)S(1)} %get-tuple-element.394.query_ref, bf16[128,640]{1,0:T(8,128)(2,1)S(1)} %collective-permute-done.166.refs_0_, bf16[128,640]{1,0:T(8,128)(2,1)S(1)} %collective-permute-done.167.refs_1_, ...), custom_call_target="tpu_custom_call" | custom-call | flops 12000000000 | bytes 5000000 | tf_op jit(solution)/shard_map/pallas_call | solution.py:226
  143.0 11.4 %all-gather.15.cloned.1.call-done = bf16[7680,960]{1,0:T(8,128)(2,1)} async-done(((bf16[240,960]{1,0:T(8,128)(2,1)}), bf16[7680,960]{1,0:T(8,128)(2,1)}) %all-gather.15.cloned.1.call-update) | async-done | bytes 14745616 | tf_op jit(solution)/shard_map/all_gather | solution.py:930
  154.4 13.1 %shard_map.225 = (f32[128,960]{1,0:T(8,128)}, bf16[128,960]{1,0:T(8,128)(2,1)}, f32[128,2560]{1,0:T(8,128)}, f32[128,2560]{1,0:T(8,128)}, bf16[128,2560]{1,0:T(8...) custom-call(bf16[128,960]{1,0:T(8,128)(2,1)} %get-tuple-element.397., ...), custom_call_target="tpu_custom_call" | custom-call | flops 4000000000 | bytes 20000000 | tf_op jit(solution)/shard_map/pallas_call | solution.py:402
  171.4 7.7 %collective-permute-start.185 = (bf16[128,640]{1,0:T(8,128)(2,1)}, bf16[128,640]{1,0:T(8,128)(2,1)S(1)}, u32[]{:S(2)}, u32[]{:S(2)}) collective-permute-start(bf16[128,640]{1,0:T(8,128)(2,1)} %get-tuple-element.402.refs_4_), channel_id=1, source_target_pairs={{64,1},{65,2},{66,3},{67,4},{68,5},{69,6},{70,7},{71,8},{72,9},{73... | collective-permute-start | bytes 491528 | tf_op jit(solution)/shard_map/ppermute | solution.py:120
  180.4 5.7 collective-permute-start.187
  197.7 8.8 %shard_map.226 = (bf16[128,960]{1,0:T(8,128)(2,1)S(1)}, f32[8,384]{1,0:T(8,128)S(1)}) custom-call(bf16[960,128]{1,0:T(8,128)(2,1)S(1)} %copy-done.89, bf16[128,640]{1,0:T(8,128)(2,1)S(1)} %collective-permute-done.183.refs_0_, bf16[128,640]{1,0:T(8,128)(2,1)S(1)} %collective-permute-done.184.refs_1_, bf16[128,640]{1,0:T(8,128)(2,1)S(1)} %collective-permute-done.185.refs_2_, ...), custom_call_target="tpu_custom_call" | custom-call | flops 12000000000 | bytes 5000000 | tf_op jit(solution)/shard_map/pallas_call | solution.py:226
  208.0 13.4 %shard_map.227 = (f32[128,960]{1,0:T(8,128)}, bf16[128,960]{1,0:T(8,128)(2,1)}, f32[128,2560]{1,0:T(8,128)}, f32[128,2560]{1,0:T(8,128)}, bf16[128,2560]{1,0:T(8...) custom-call(bf16[128,960]{1,0:T(8,128)(2,1)} %copy-done.34, ...), custom_call_target="tpu_custom_call" | custom-call | flops 4000000000 | bytes 20000000 | tf_op jit(solution)/shard_map/pallas_call | solution.py:402
  221.4 5.2 collective-permute-start.198
  227.3 8.8 %collective-permute-start.200 = (bf16[128,640]{1,0:T(8,128)(2,1)}, bf16[128,640]{1,0:T(8,128)(2,1)S(1)}, u32[]{:S(2)}, u32[]{:S(2)}) collective-permute-start(bf16[128,640]{1,0:T(8,128)(2,1)} %get-tuple-element.406.refs_4_), channel_id=1, source_target_pairs={{64,1},{65,2},{66,3},{67,4},{68,5},{69,6},{70,7},{71,8},{72,9},{73... | collective-permute-start | bytes 491528 | tf_op jit(solution)/shard_map/ppermute | solution.py:120
  237.4 7.7 %collective-permute-start.202 = (bf16[128,640]{1,0:T(8,128)(2,1)}, bf16[128,640]{1,0:T(8,128)(2,1)S(1)}, u32[]{:S(2)}, u32[]{:S(2)}) collective-permute-start(bf16[128,640]{1,0:T(8,128)(2,1)} %get-tuple-element.406.refs_4_), channel_id=1, source_target_pairs={{0,96},{1,97},{2,98},{3,99},{4,100},{5,101},{6,102},{7,103},{8,104... | collective-permute-start | bytes 491528 | tf_op jit(solution)/shard_map/ppermute | solution.py:113
  256.7 9.5 %shard_map.228 = (bf16[128,960]{1,0:T(8,128)(2,1)}, f32[8,384]{1,0:T(8,128)S(1)}) custom-call(bf16[960,128]{1,0:T(8,128)(2,1)S(1)} %copy-done.91, bf16[128,640]{1,0:T(8,128)(2,1)S(1)} %collective-permute-done.198.refs_0_, bf16[128,640]{1,0:T(8,128)(2,1)S(1)} %collective-permute-done.199.refs_1_, bf16[128,640]{1,0:T(8,128)(2,1)S(1)} %collective-permute-done.200.refs_2_, ...), custom_call_target="tpu_custom_call" | custom-call | flops 12000000000 | bytes 5000000 | tf_op jit(solution)/shard_map/pallas_call | solution.py:226
  266.9 12.0 %shard_map.229 = (f32[128,960]{1,0:T(8,128)}, bf16[128,960]{1,0:T(8,128)(2,1)}, f32[128,2560]{1,0:T(8,128)}, f32[128,2560]{1,0:T(8,128)}, bf16[128,2560]{1,0:T(8...) custom-call(bf16[128,960]{1,0:T(8,128)(2,1)} %get-tuple-element.407.att_ref.refs_18_.refs_0_, ...), custom_call_target="tpu_custom_call" | custom-call | flops 4000000000 | bytes 20000000 | tf_op jit(solution)/shard_map/pallas_call | solution.py:402
  290.0 6.0 collective-permute-start.217
  303.8 13.4 %shard_map.230 = (f32[256,6144]{1,0:T(8,128)}, bf16[256,960]{1,0:T(8,128)(2,1)}, f32[8,256]{1,0:T(8,128)}) custom-call(s32[256,1]{1,0:T(8,128)} %copy.225.rows_ref, s32[1,1024]{1,0:T(1,128)} %bitcast.374, bf16[128,960]{1,0:T(8,128)(2,1)} %copy-done.220, bf16[128,960]{1,0:T(8,128)(2,1)} %copy-done.285, bf16[128,960]{1,0:T(8,128)(2,1)} %copy-done.286, ...), custom_call_target="tpu_custom_call" | custom-call | tf_op jit(solution)/shard_map/pallas_call | solution.py:607
  325.2 13.1 %shard_map.231 = (bf16[256,6144]{1,0:T(8,128)(2,1)}, bf16[128,960]{1,0:T(8,128)(2,1)}, bf16[128,960]{1,0:T(8,128)(2,1)}, bf16[128,960]{1,0:T(8,128)(2,1)}, bf16[...) custom-call(s32[256,1]{1,0:T(8,128)} %copy.225.rows_ref, ...), custom_call_target="tpu_custom_call" | custom-call | tf_op jit(solution)/shard_map/pallas_call | solution.py:657
  343.3 8.9 %shard_map.232 = bf16[6144,960]{1,0:T(8,128)(2,1)} custom-call(bf16[256,6144]{1,0:T(8,128)(2,1)} %get-tuple-element.420.grad_ref, bf16[256,960]{1,0:T(8,128)(2,1)} %get-tuple-element.421.pick_ref), custom_call_target="tpu_custom_call" | custom-call | tf_op jit(solution)/shard_map/pallas_call | solution.py:680
  364.8 6.5 collective-permute-done.229
  372.6 13.8 %shard_map.233 = (bf16[128,960]{1,0:T(8,128)(2,1)}, bf16[128,2560]{1,0:T(8,128)(2,1)}, bf16[128,2560]{1,0:T(8,128)(2,1)}, f32[128,960]{1,0:T(8,128)}, bf16[128,9...) custom-call(f32[128,960]{1,0:T(8,128)} %multiply_subtract_fusion.2.new_ref, f32[128,1]{1,0:T(8,128)} %copy.222.sel_ref, ...), custom_call_target="tpu_custom_call" | custom-call | flops 4000000000 | bytes 20000000 | tf_op jit(solution)/shard_map/pallas_call | solution.py:501
  386.5 13.9 %shard_map.234 = (bf16[128,960]{1,0:T(8,128)(2,1)}, bf16[512,640]{1,0:T(8,128)(2,1)}, bf16[512,640]{1,0:T(8,128)(2,1)}, bf16[512,640]{1,0:T(8,128)(2,1)}, bf16[512,640]{1,0:T(8,128)(2,1)}) custom-call(bf16[960,128]{1,0:T(8,128)(2,1)} %get-tuple-element.405.query_ref, bf16[128,640]{1,0:T(8,128)(2,1)} %copy-done.159, bf16[128,640]{1,0:T(8,128)(2,1)} %copy-done.161, ...), custom_call_target="tpu_custom_call" | custom-call | flops 20000000000 | bytes 9000000 | tf_op jit(solution)/shard_map/pallas_call | solution.py:271
  412.2 5.3 collective-permute-done.232
  422.0 9.3 %collective-permute-done.238 = bf16[128,640]{1,0:T(8,128)(2,1)S(1)} collective-permute-done((bf16[128,640]{1,0:T(8,128)(2,1)S(1)}, bf16[128,640]{1,0:T(8,128)(2,1)S(1)}, u32[]{:S(2)}, u32[]{:S(2)}) %collective-permute-start.238) | collective-permute-done | bytes 163872 | tf_op jit(solution)/shard_map/ppermute | solution.py:136
  438.5 13.2 %shard_map.236 = (bf16[128,960]{1,0:T(8,128)(2,1)}, bf16[128,2560]{1,0:T(8,128)(2,1)}, bf16[128,2560]{1,0:T(8,128)(2,1)}, f32[128,960]{1,0:T(8,128)}, bf16[128,9...) custom-call(f32[128,960]{1,0:T(8,128)} %copy-done.78, f32[128,1]{1,0:T(8,128)} %copy.221.sel_ref, ...), custom_call_target="tpu_custom_call" | custom-call | flops 4000000000 | bytes 20000000 | tf_op jit(solution)/shard_map/pallas_call | solution.py:501
  451.7 13.8 %shard_map.237 = (bf16[128,960]{1,0:T(8,128)(2,1)}, bf16[512,640]{1,0:T(8,128)(2,1)}, bf16[512,640]{1,0:T(8,128)(2,1)}, bf16[512,640]{1,0:T(8,128)(2,1)}, bf16[512,640]{1,0:T(8,128)(2,1)}) custom-call(bf16[960,128]{1,0:T(8,128)(2,1)} %get-tuple-element.401.query_ref, bf16[128,640]{1,0:T(8,128)(2,1)} %copy-done.128, bf16[128,640]{1,0:T(8,128)(2,1)} %copy-done.130, ...), custom_call_target="tpu_custom_call" | custom-call | flops 20000000000 | bytes 9000000 | tf_op jit(solution)/shard_map/pallas_call | solution.py:271
  477.0 6.3 collective-permute-done.250
  488.6 7.2 collective-permute-done.256
  504.8 12.8 %shard_map.239 = (bf16[128,960]{1,0:T(8,128)(2,1)}, bf16[128,2560]{1,0:T(8,128)(2,1)}, bf16[128,2560]{1,0:T(8,128)(2,1)}, f32[128,960]{1,0:T(8,128)}, bf16[128,9...) custom-call(f32[128,960]{1,0:T(8,128)} %copy-done.76, f32[128,1]{1,0:T(8,128)} %copy.220.sel_ref, ...), custom_call_target="tpu_custom_call" | custom-call | flops 4000000000 | bytes 20000000 | tf_op jit(solution)/shard_map/pallas_call | solution.py:501
  521.1 13.6 %shard_map.240 = (bf16[128,960]{1,0:T(8,128)(2,1)}, bf16[512,640]{1,0:T(8,128)(2,1)}, bf16[512,640]{1,0:T(8,128)(2,1)}, bf16[512,640]{1,0:T(8,128)(2,1)}, bf16[512,640]{1,0:T(8,128)(2,1)}) custom-call(bf16[960,128]{1,0:T(8,128)(2,1)} %copy-done.86, bf16[128,640]{1,0:T(8,128)(2,1)} %copy-done.94, bf16[128,640]{1,0:T(8,128)(2,1)} %copy-done.95, ...), custom_call_target="tpu_custom_call" | custom-call | flops 20000000000 | bytes 9000000 | tf_op jit(solution)/shard_map/pallas_call | solution.py:271
  535.6 11.7 %shard_map.241 = bf16[16,3,80,960]{3,2,1,0:T(8,128)(2,1)} custom-call(s32[1]{0:T(128)} %bitcast.135.which_ref, bf16[128,2560]{1,0:T(8,128)(2,1)} %get-tuple-element.444.refs_0_, bf16[128,2560]{1,0:T(8,128)(2,1)} %get-tuple-element.445.refs_1_, bf16[128,2560]{1,0:T(8,128)(2,1)} %get-tuple-element.446.refs_2_, bf16[128,960]{1,0:T(8,128)(2,1)} %get-tuple-element.447.refs_3_, ...), custom_call_target="tpu_custom_call" | custom-call | tf_op jit(solution)/shard_map/pallas_call | solution.py:714
  559.4 5.4 collective-permute-done.268
  567.5 7.5 %shard_map.242 = (bf16[960,960]{1,0:T(8,128)(2,1)}, bf16[960,960]{1,0:T(8,128)(2,1)}) custom-call(bf16[128,960]{1,0:T(8,128)(2,1)} %get-tuple-element.407.att_ref.refs_18_.refs_0_, bf16[128,960]{1,0:T(8,128)(2,1)} %get-tuple-element.449.refs_1_, bf16[128,960]{1,0:T(8,128)(2,1)} %get-tuple-element.450.refs_2_.refs_3_, ...), custom_call_target="tpu_custom_call" | custom-call | tf_op jit(solution)/shard_map/pallas_call | solution.py:745
  575.9 10.2 %collective-permute-done.274 = bf16[128,640]{1,0:T(8,128)(2,1)} collective-permute-done((bf16[128,640]{1,0:T(8,128)(2,1)}, bf16[128,640]{1,0:T(8,128)(2,1)}, u32[]{:S(2)}, u32[]{:S(2)}) %collective-permute-start.274) | collective-permute-done | bytes 163872 | tf_op jit(solution)/shard_map/ppermute | solution.py:136
  586.1 5.3 collective-permute-done.275
  609.6 8.2 %shard_map.244 = bf16[4,352,960]{2,1,0:T(8,128)(2,1)} custom-call(s32[4]{0:T(128)} %pad_add_fusion.1.starts_ref, bf16[960,960]{1,0:T(8,128)(2,1)} %get-tuple-element.521.refs_0_, bf16[960,960]{1,0:T(8,128)(2,1)} %get-tuple-element.522.refs_1_, f32[16,960]{1,0:T(8,128)} %add.1262.refs_2_, bf16[128,960]{1,0:T(8,128)(2,1)} %get-tuple-element.450.refs_2_.refs_3_, ...), custom_call_target="tpu_custom_call" | custom-call | tf_op jit(solution)/shard_map/pallas_call | solution.py:783
  631.0 11.9 %all-to-all-start.3 = ((bf16[16,24,960]{2,1,0:T(8,128)(2,1)}), bf16[16,24,960]{2,1,0:T(8,128)(2,1)S(1)}, u32[]{:S(2)}, u32[]{:S(2)}) async-start(bf16[16,24,960]{2,1,0:T(8,128)(2,1)} %bitcast.163), calls=%async_computation.6 | async-start | bytes 1572864 | tf_op jit(solution)/shard_map/all_to_all | solution.py:1192
  643.0 12.2 %collective-permute-done.289 = bf16[352,960]{1,0:T(8,128)(2,1)} collective-permute-done((bf16[352,960]{1,0:T(8,128)(2,1)}, bf16[352,960]{1,0:T(8,128)(2,1)}, u32[]{:S(2)}, u32[]{:S(2)}) %collective-permute-start.289) | collective-permute-done | bytes 675872 | tf_op jit(solution)/shard_map/ppermute | solution.py:49
  658.9 5.8 collective-permute-start.292
  670.7 5.4 collective-permute-done.293
  679.1 4.6 collective-permute-start.296
  684.3 4.1 collective-permute-start.298
  704.2 18.7 %all_to_all.53 = f32[128,1,128]{2,1,0:T(1,128)S(1)} all-to-all(f32[128,1,128]{2,1,0:T(1,128)S(1)} %iota.151), channel_id=1, replica_groups=mesh['z'=4,'core'=2,'y'=4,'x'=4] {'z','core','y','x'}, dimensions={0} | all-to-all | bytes 131072 | tf_op jit(solution)/shard_map/all_to_all | solution.py:1234
  724.3 5.6 multiply_subtract_fusion.1
  (815 shorter events, 277.3 us)
Async XLA Ops:
  7.2 68.3 %all-gather.13.cloned.1.call-start = ((), (), s32[]{:S(2)}) async-start(), calls=%async_computation.14 | async-start | bytes 6488064 | tf_op jit(solution)/shard_map/all_gather | solution.py:893
  26.6 127.8 %all-gather.15.cloned.1.call-start = ((), (), s32[]{:S(2)}) async-start(), calls=%async_computation.15 | async-start | bytes 16220160 | tf_op jit(solution)/shard_map/all_gather | solution.py:930
  38.9 263.9 %all-gather.17.cloned.1.call-start = ((), (), s32[]{:S(2)}) async-start(), calls=%async_computation.16 | async-start | bytes 13369344 | tf_op jit(solution)/shard_map/all_gather | solution.py:936
  57.0 445.5 %reduce-scatter.15.cloned.1.call-start = ((), (), s32[]{:S(2)}) async-start(), calls=%async_computation.18 | async-start | bytes 13369344
  73.8 17.0 %collective-permute-start.156 = (bf16[128,960]{1,0:T(8,128)(2,1)S(1)}, bf16[128,960]{1,0:T(8,128)(2,1)S(1)}, u32[]{:S(2)}, u32[]{:S(2)}) collective-permute-start(bf16[128,960]{1,0:T(8,128)(2,1)S(1)} %get-tuple-element.379), channel_id=1, source_target_pairs={{0,16},{16,0},{1,17},{17,1},{2,18},{18,2},{3,19},{19,3},{4,20},{20... | collective-permute-start | bytes 737288 | tf_op jit(solution)/shard_map/ppermute | solution.py:53
  75.5 15.4 %collective-permute-start.163 = (bf16[128,960]{1,0:T(8,128)(2,1)S(1)}, bf16[128,960]{1,0:T(8,128)(2,1)S(1)}, u32[]{:S(2)}, u32[]{:S(2)}) collective-permute-start(bf16[128,960]{1,0:T(8,128)(2,1)S(1)} %add_convert_fusion.24), channel_id=1, source_target_pairs={{0,32},{32,64},{64,96},{96,0},{1,33},{33,65},{65,97},{97,1},{2,34}... | collective-permute-start | bytes 737288 | tf_op jit(solution)/shard_map/ppermute | solution.py:49
  93.7 19.2 %collective-permute-start.166 = (bf16[128,640]{1,0:T(8,128)(2,1)S(1)}, bf16[128,640]{1,0:T(8,128)(2,1)S(1)}, u32[]{:S(2)}, u32[]{:S(2)}) collective-permute-start(bf16[128,640]{1,0:T(8,128)(2,1)S(1)} %get-tuple-element.395.refs_4_), channel_id=1, source_target_pairs={{0,1},{1,2},{2,3},{3,4},{4,5},{5,6},{6,7},{7,8},{8,9},{9,10},{10,1... | collective-permute-start | bytes 491528 | tf_op jit(solution)/shard_map/ppermute | solution.py:120
  95.8 18.5 %collective-permute-start.167 = (bf16[128,640]{1,0:T(8,128)(2,1)S(1)}, bf16[128,640]{1,0:T(8,128)(2,1)S(1)}, u32[]{:S(2)}, u32[]{:S(2)}) collective-permute-start(bf16[128,640]{1,0:T(8,128)(2,1)S(1)} %get-tuple-element.395.refs_4_), channel_id=1, source_target_pairs={{32,1},{33,2},{34,3},{35,4},{36,5},{37,6},{38,7},{39,8},{40,9},{41... | collective-permute-start | bytes 491528 | tf_op jit(solution)/shard_map/ppermute | solution.py:120
  96.5 20.3 %collective-permute-start.168 = (bf16[128,640]{1,0:T(8,128)(2,1)S(1)}, bf16[128,640]{1,0:T(8,128)(2,1)S(1)}, u32[]{:S(2)}, u32[]{:S(2)}) collective-permute-start(bf16[128,640]{1,0:T(8,128)(2,1)S(1)} %get-tuple-element.395.refs_4_), channel_id=1, source_target_pairs={{64,1},{65,2},{66,3},{67,4},{68,5},{69,6},{70,7},{71,8},{72,9},{73... | collective-permute-start | bytes 491528 | tf_op jit(solution)/shard_map/ppermute | solution.py:120
  105.2 14.1 %collective-permute-start.169 = (bf16[128,640]{1,0:T(8,128)(2,1)S(1)}, bf16[128,640]{1,0:T(8,128)(2,1)S(1)}, u32[]{:S(2)}, u32[]{:S(2)}) collective-permute-start(bf16[128,640]{1,0:T(8,128)(2,1)S(1)} %get-tuple-element.395.refs_4_), channel_id=1, source_target_pairs={{96,1},{97,2},{98,3},{99,4},{100,5},{101,6},{102,7},{103,8},{104,9... | collective-permute-start | bytes 491528 | tf_op jit(solution)/shard_map/ppermute | solution.py:120
  167.5 18.7 %collective-permute-start.183 = (bf16[128,640]{1,0:T(8,128)(2,1)}, bf16[128,640]{1,0:T(8,128)(2,1)S(1)}, u32[]{:S(2)}, u32[]{:S(2)}) collective-permute-start(bf16[128,640]{1,0:T(8,128)(2,1)} %get-tuple-element.402.refs_4_), channel_id=1, source_target_pairs={{0,1},{1,2},{2,3},{3,4},{4,5},{5,6},{6,7},{7,8},{8,9},{9,10},{10,1... | collective-permute-start | bytes 491528 | tf_op jit(solution)/shard_map/ppermute | solution.py:120
  170.7 16.8 %collective-permute-start.184 = (bf16[128,640]{1,0:T(8,128)(2,1)}, bf16[128,640]{1,0:T(8,128)(2,1)S(1)}, u32[]{:S(2)}, u32[]{:S(2)}) collective-permute-start(bf16[128,640]{1,0:T(8,128)(2,1)} %get-tuple-element.402.refs_4_), channel_id=1, source_target_pairs={{32,1},{33,2},{34,3},{35,4},{36,5},{37,6},{38,7},{39,8},{40,9},{41... | collective-permute-start | bytes 491528 | tf_op jit(solution)/shard_map/ppermute | solution.py:120
  171.4 18.6 %collective-permute-start.185 = (bf16[128,640]{1,0:T(8,128)(2,1)}, bf16[128,640]{1,0:T(8,128)(2,1)S(1)}, u32[]{:S(2)}, u32[]{:S(2)}) collective-permute-start(bf16[128,640]{1,0:T(8,128)(2,1)} %get-tuple-element.402.refs_4_), channel_id=1, source_target_pairs={{64,1},{65,2},{66,3},{67,4},{68,5},{69,6},{70,7},{71,8},{72,9},{73... | collective-permute-start | bytes 491528 | tf_op jit(solution)/shard_map/ppermute | solution.py:120
  221.4 23.8 %collective-permute-start.198 = (bf16[128,640]{1,0:T(8,128)(2,1)}, bf16[128,640]{1,0:T(8,128)(2,1)S(1)}, u32[]{:S(2)}, u32[]{:S(2)}) collective-permute-start(bf16[128,640]{1,0:T(8,128)(2,1)} %get-tuple-element.406.refs_4_), channel_id=1, source_target_pairs={{0,1},{1,2},{2,3},{3,4},{4,5},{5,6},{6,7},{7,8},{8,9},{9,10},{10,1... | collective-permute-start | bytes 491528 | tf_op jit(solution)/shard_map/ppermute | solution.py:120
  226.6 19.8 %collective-permute-start.199 = (bf16[128,640]{1,0:T(8,128)(2,1)}, bf16[128,640]{1,0:T(8,128)(2,1)S(1)}, u32[]{:S(2)}, u32[]{:S(2)}) collective-permute-start(bf16[128,640]{1,0:T(8,128)(2,1)} %get-tuple-element.406.refs_4_), channel_id=1, source_target_pairs={{32,1},{33,2},{34,3},{35,4},{36,5},{37,6},{38,7},{39,8},{40,9},{41... | collective-permute-start | bytes 491528 | tf_op jit(solution)/shard_map/ppermute | solution.py:120
  227.3 21.7 %collective-permute-start.200 = (bf16[128,640]{1,0:T(8,128)(2,1)}, bf16[128,640]{1,0:T(8,128)(2,1)S(1)}, u32[]{:S(2)}, u32[]{:S(2)}) collective-permute-start(bf16[128,640]{1,0:T(8,128)(2,1)} %get-tuple-element.406.refs_4_), channel_id=1, source_target_pairs={{64,1},{65,2},{66,3},{67,4},{68,5},{69,6},{70,7},{71,8},{72,9},{73... | collective-permute-start | bytes 491528 | tf_op jit(solution)/shard_map/ppermute | solution.py:120
  236.1 14.9 %collective-permute-start.201 = (bf16[128,640]{1,0:T(8,128)(2,1)}, bf16[128,640]{1,0:T(8,128)(2,1)S(1)}, u32[]{:S(2)}, u32[]{:S(2)}) collective-permute-start(bf16[128,640]{1,0:T(8,128)(2,1)} %get-tuple-element.406.refs_4_), channel_id=1, source_target_pairs={{96,1},{97,2},{98,3},{99,4},{100,5},{101,6},{102,7},{103,8},{104,9... | collective-permute-start | bytes 491528 | tf_op jit(solution)/shard_map/ppermute | solution.py:120
  237.4 14.7 %collective-permute-start.202 = (bf16[128,640]{1,0:T(8,128)(2,1)}, bf16[128,640]{1,0:T(8,128)(2,1)S(1)}, u32[]{:S(2)}, u32[]{:S(2)}) collective-permute-start(bf16[128,640]{1,0:T(8,128)(2,1)} %get-tuple-element.406.refs_4_), channel_id=1, source_target_pairs={{0,96},{1,97},{2,98},{3,99},{4,100},{5,101},{6,102},{7,103},{8,104... | collective-permute-start | bytes 491528 | tf_op jit(solution)/shard_map/ppermute | solution.py:113
  285.2 14.0 %collective-permute-start.215 = (bf16[128,960]{1,0:T(8,128)(2,1)S(1)}, bf16[128,960]{1,0:T(8,128)(2,1)S(1)}, u32[]{:S(2)}, u32[]{:S(2)}) collective-permute-start(bf16[128,960]{1,0:T(8,128)(2,1)S(1)} %multiply_convert_fusion.1.refs_0_), channel_id=1, source_target_pairs={{0,32},{32,64},{64,96},{96,0},{1,33},{33,65},{65,97},{97,1},{2,34}... | collective-permute-start | bytes 737288 | tf_op jit(solution)/shard_map/ppermute | solution.py:49
  285.7 17.1 %collective-permute-start.216 = (bf16[128,960]{1,0:T(8,128)(2,1)S(1)}, bf16[128,960]{1,0:T(8,128)(2,1)S(1)}, u32[]{:S(2)}, u32[]{:S(2)}) collective-permute-start(bf16[128,960]{1,0:T(8,128)(2,1)S(1)} %multiply_convert_fusion.1.refs_0_), channel_id=1, source_target_pairs={{0,16},{16,0},{1,17},{17,1},{2,18},{18,2},{3,19},{19,3},{4,20},{20... | collective-permute-start | bytes 737288 | tf_op jit(solution)/shard_map/ppermute | solution.py:53
  352.3 325.1 %reduce-scatter.13.cloned.1.call-start = ((), (), s32[]{:S(2)}) async-start(), calls=%async_computation.17 | async-start | bytes 8355840 | tf_op jit(solution)/shard_map/reduce_scatter | solution.py:1117
  356.8 14.5 %collective-permute-start.229 = (bf16[128,960]{1,0:T(8,128)(2,1)S(1)}, bf16[128,960]{1,0:T(8,128)(2,1)S(1)}, u32[]{:S(2)}, u32[]{:S(2)}) collective-permute-start(bf16[128,960]{1,0:T(8,128)(2,1)S(1)} %add_convert_fusion.20), channel_id=1, source_target_pairs={{0,64},{32,96},{64,0},{96,32},{1,65},{33,97},{65,1},{97,33},{2,66}... | collective-permute-start | bytes 737288 | tf_op jit(solution)/shard_map/ppermute | solution.py:49
  417.6 13.8 %collective-permute-start.238 = (bf16[128,640]{1,0:T(8,128)(2,1)S(1)}, bf16[128,640]{1,0:T(8,128)(2,1)S(1)}, u32[]{:S(2)}, u32[]{:S(2)}) collective-permute-start(bf16[128,640]{1,0:T(8,128)(2,1)S(1)} %get-tuple-element.797), channel_id=1, source_target_pairs={{1,64},{2,65},{3,66},{4,67},{5,68},{6,69},{7,70},{8,71},{9,72},{10... | collective-permute-start | bytes 491528 | tf_op jit(solution)/shard_map/ppermute | solution.py:136
  418.9 14.2 %collective-permute-start.239 = (bf16[128,640]{1,0:T(8,128)(2,1)S(1)}, bf16[128,640]{1,0:T(8,128)(2,1)S(1)}, u32[]{:S(2)}, u32[]{:S(2)}) collective-permute-start(bf16[128,640]{1,0:T(8,128)(2,1)S(1)} %get-tuple-element.796), channel_id=1, source_target_pairs={{1,96},{2,97},{3,98},{4,99},{5,100},{6,101},{7,102},{8,103},{9,104... | collective-permute-start | bytes 491528 | tf_op jit(solution)/shard_map/ppermute | solution.py:136
  420.2 16.7 %collective-permute-start.240 = (bf16[128,1280]{1,0:T(8,128)(2,1)S(1)}, bf16[128,1280]{1,0:T(8,128)(2,1)S(1)}, u32[]{:S(2)}, u32[]{:S(2)}) collective-permute-start(bf16[128,1280]{1,0:T(8,128)(2,1)S(1)} %constant_dynamic-slice_fusion.19), channel_id=1, source_target_pairs={{0,16},{16,0},{1,17},{17,1},{2,18},{18,2},{3,19},{19,3},{4,20},{20... | collective-permute-start | bytes 983048 | tf_op jit(solution)/shard_map/ppermute | solution.py:53
  421.5 15.4 %collective-permute-start.241 = (bf16[128,1280]{1,0:T(8,128)(2,1)S(1)}, bf16[128,1280]{1,0:T(8,128)(2,1)S(1)}, u32[]{:S(2)}, u32[]{:S(2)}) collective-permute-start(bf16[128,1280]{1,0:T(8,128)(2,1)S(1)} %constant_dynamic-slice_fusion.18), channel_id=1, source_target_pairs={{0,16},{16,0},{1,17},{17,1},{2,18},{18,2},{3,19},{19,3},{4,20},{20... | collective-permute-start | bytes 983048 | tf_op jit(solution)/shard_map/ppermute | solution.py:53
  421.6 15.3 %collective-permute-start.248 = (bf16[128,960]{1,0:T(8,128)(2,1)S(1)}, bf16[128,960]{1,0:T(8,128)(2,1)S(1)}, u32[]{:S(2)}, u32[]{:S(2)}) collective-permute-start(bf16[128,960]{1,0:T(8,128)(2,1)S(1)} %copy-done.42), channel_id=1, source_target_pairs={{0,16},{16,0},{1,17},{17,1},{2,18},{18,2},{3,19},{19,3},{4,20},{20... | collective-permute-start | bytes 737288 | tf_op jit(solution)/shard_map/ppermute | solution.py:53
  476.7 24.3 %collective-permute-start.258 = (bf16[128,1280]{1,0:T(8,128)(2,1)S(1)}, bf16[128,1280]{1,0:T(8,128)(2,1)S(1)}, u32[]{:S(2)}, u32[]{:S(2)}) collective-permute-start(bf16[128,1280]{1,0:T(8,128)(2,1)S(1)} %constant_dynamic-slice_fusion.16), channel_id=1, source_target_pairs={{0,16},{16,0},{1,17},{17,1},{2,18},{18,2},{3,19},{19,3},{4,20},{20... | collective-permute-start | bytes 983048 | tf_op jit(solution)/shard_map/ppermute | solution.py:53
  483.4 18.1 %collective-permute-start.259 = (bf16[128,1280]{1,0:T(8,128)(2,1)S(1)}, bf16[128,1280]{1,0:T(8,128)(2,1)S(1)}, u32[]{:S(2)}, u32[]{:S(2)}) collective-permute-start(bf16[128,1280]{1,0:T(8,128)(2,1)S(1)} %constant_dynamic-slice_fusion.15), channel_id=1, source_target_pairs={{0,16},{16,0},{1,17},{17,1},{2,18},{18,2},{3,19},{19,3},{4,20},{20... | collective-permute-start | bytes 983048 | tf_op jit(solution)/shard_map/ppermute | solution.py:53
  488.5 16.2 %collective-permute-start.181 = (bf16[128,960]{1,0:T(8,128)(2,1)}, bf16[128,960]{1,0:T(8,128)(2,1)}, u32[]{:S(2)}, u32[]{:S(2)}) collective-permute-start(bf16[128,960]{1,0:T(8,128)(2,1)} %get-tuple-element.398.refs_18_.refs_11_), channel_id=1, source_target_pairs={{0,16},{16,0},{1,17},{17,1},{2,18},{18,2},{3,19},{19,3},{4,20},{20... | collective-permute-start | bytes 737288 | tf_op jit(solution)/shard_map/ppermute | solution.py:53
  500.9 33.8 %collective-permute-start.278 = (bf16[128,1280]{1,0:T(8,128)(2,1)}, bf16[128,1280]{1,0:T(8,128)(2,1)}, u32[]{:S(2)}, u32[]{:S(2)}) collective-permute-start(bf16[128,1280]{1,0:T(8,128)(2,1)} %constant_dynamic-slice_fusion.11), channel_id=1, source_target_pairs={{0,16},{16,0},{1,17},{17,1},{2,18},{18,2},{3,19},{19,3},{4,20},{20... | collective-permute-start | bytes 983048 | tf_op jit(solution)/shard_map/ppermute | solution.py:53
  501.0 33.7 %collective-permute-start.279 = (bf16[128,960]{1,0:T(8,128)(2,1)}, bf16[128,960]{1,0:T(8,128)(2,1)}, u32[]{:S(2)}, u32[]{:S(2)}) collective-permute-start(bf16[128,960]{1,0:T(8,128)(2,1)} %get-tuple-element.505.refs_23_), channel_id=1, source_target_pairs={{0,16},{16,0},{1,17},{17,1},{2,18},{18,2},{3,19},{19,3},{4,20},{20... | collective-permute-start | bytes 737288 | tf_op jit(solution)/shard_map/ppermute | solution.py:53
  518.6 16.1 %collective-permute-start.276 = (bf16[128,1280]{1,0:T(8,128)(2,1)S(1)}, bf16[128,1280]{1,0:T(8,128)(2,1)S(1)}, u32[]{:S(2)}, u32[]{:S(2)}) collective-permute-start(bf16[128,1280]{1,0:T(8,128)(2,1)S(1)} %constant_dynamic-slice_fusion.13), channel_id=1, source_target_pairs={{0,16},{16,0},{1,17},{17,1},{2,18},{18,2},{3,19},{19,3},{4,20},{20... | collective-permute-start | bytes 983048 | tf_op jit(solution)/shard_map/ppermute | solution.py:53
  520.1 14.6 %collective-permute-start.277 = (bf16[128,1280]{1,0:T(8,128)(2,1)S(1)}, bf16[128,1280]{1,0:T(8,128)(2,1)S(1)}, u32[]{:S(2)}, u32[]{:S(2)}) collective-permute-start(bf16[128,1280]{1,0:T(8,128)(2,1)S(1)} %constant_dynamic-slice_fusion.12), channel_id=1, source_target_pairs={{0,16},{16,0},{1,17},{17,1},{2,18},{18,2},{3,19},{19,3},{4,20},{20... | collective-permute-start | bytes 983048 | tf_op jit(solution)/shard_map/ppermute | solution.py:53
  520.3 14.4 %collective-permute-start.280 = (bf16[128,960]{1,0:T(8,128)(2,1)}, bf16[128,960]{1,0:T(8,128)(2,1)S(1)}, u32[]{:S(2)}, u32[]{:S(2)}) collective-permute-start(bf16[128,960]{1,0:T(8,128)(2,1)} %get-tuple-element.506.refs_24_), channel_id=1, source_target_pairs={{0,16},{16,0},{1,17},{17,1},{2,18},{18,2},{3,19},{19,3},{4,20},{20... | collective-permute-start | bytes 737288 | tf_op jit(solution)/shard_map/ppermute | solution.py:53
  553.1 13.0 %collective-permute-start.269 = (bf16[128,640]{1,0:T(8,128)(2,1)S(1)}, bf16[128,640]{1,0:T(8,128)(2,1)}, u32[]{:S(2)}, u32[]{:S(2)}) collective-permute-start(bf16[128,640]{1,0:T(8,128)(2,1)S(1)} %get-tuple-element.780), channel_id=1, source_target_pairs={{64,0},{96,32},{65,1},{97,33},{66,2},{98,34},{67,3},{99,35},{68,4}... | collective-permute-start | bytes 491528 | tf_op jit(solution)/shard_map/ppermute | solution.py:130
  554.4 20.6 %collective-permute-start.270 = (bf16[128,640]{1,0:T(8,128)(2,1)}, bf16[128,640]{1,0:T(8,128)(2,1)}, u32[]{:S(2)}, u32[]{:S(2)}) collective-permute-start(bf16[128,640]{1,0:T(8,128)(2,1)} %get-tuple-element.779), channel_id=1, source_target_pairs={{32,0},{64,32},{96,64},{33,1},{65,33},{97,65},{34,2},{66,34},{98,6... | collective-permute-start | bytes 491528 | tf_op jit(solution)/shard_map/ppermute | solution.py:130
  556.7 19.1 %collective-permute-start.272 = (bf16[128,640]{1,0:T(8,128)(2,1)}, bf16[128,640]{1,0:T(8,128)(2,1)}, u32[]{:S(2)}, u32[]{:S(2)}) collective-permute-start(bf16[128,640]{1,0:T(8,128)(2,1)} %get-tuple-element.781), channel_id=1, source_target_pairs={{1,0},{2,1},{3,2},{4,3},{5,4},{6,5},{7,6},{8,7},{9,8},{10,9},{11,1... | collective-permute-start | bytes 491528 | tf_op jit(solution)/shard_map/ppermute | solution.py:136
  558.0 17.9 %collective-permute-start.273 = (bf16[128,640]{1,0:T(8,128)(2,1)}, bf16[128,640]{1,0:T(8,128)(2,1)}, u32[]{:S(2)}, u32[]{:S(2)}) collective-permute-start(bf16[128,640]{1,0:T(8,128)(2,1)} %get-tuple-element.784), channel_id=1, source_target_pairs={{1,32},{2,33},{3,34},{4,35},{5,36},{6,37},{7,38},{8,39},{9,40},{10... | collective-permute-start | bytes 491528 | tf_op jit(solution)/shard_map/ppermute | solution.py:136
  564.8 21.3 %collective-permute-start.274 = (bf16[128,640]{1,0:T(8,128)(2,1)}, bf16[128,640]{1,0:T(8,128)(2,1)}, u32[]{:S(2)}, u32[]{:S(2)}) collective-permute-start(bf16[128,640]{1,0:T(8,128)(2,1)} %get-tuple-element.783), channel_id=1, source_target_pairs={{1,64},{2,65},{3,66},{4,67},{5,68},{6,69},{7,70},{8,71},{9,72},{10... | collective-permute-start | bytes 491528 | tf_op jit(solution)/shard_map/ppermute | solution.py:136
  566.1 25.3 %collective-permute-start.275 = (bf16[128,640]{1,0:T(8,128)(2,1)}, bf16[128,640]{1,0:T(8,128)(2,1)}, u32[]{:S(2)}, u32[]{:S(2)}) collective-permute-start(bf16[128,640]{1,0:T(8,128)(2,1)} %get-tuple-element.782), channel_id=1, source_target_pairs={{1,96},{2,97},{3,98},{4,99},{5,100},{6,101},{7,102},{8,103},{9,104... | collective-permute-start | bytes 491528 | tf_op jit(solution)/shard_map/ppermute | solution.py:136
  575.1 33.9 %collective-permute-start.286 = (bf16[128,640]{1,0:T(8,128)(2,1)}, bf16[128,640]{1,0:T(8,128)(2,1)}, u32[]{:S(2)}, u32[]{:S(2)}) collective-permute-start(bf16[128,640]{1,0:T(8,128)(2,1)} %get-tuple-element.533.refs_5_), channel_id=1, source_target_pairs={{0,16},{16,0},{1,17},{17,1},{2,18},{18,2},{3,19},{19,3},{4,20},{20... | collective-permute-start | bytes 491528 | tf_op jit(solution)/shard_map/ppermute | solution.py:53
  575.8 33.1 %collective-permute-start.287 = (bf16[128,640]{1,0:T(8,128)(2,1)}, bf16[128,640]{1,0:T(8,128)(2,1)}, u32[]{:S(2)}, u32[]{:S(2)}) collective-permute-start(bf16[128,640]{1,0:T(8,128)(2,1)} %get-tuple-element.534.refs_9_), channel_id=1, source_target_pairs={{0,16},{16,0},{1,17},{17,1},{2,18},{18,2},{3,19},{19,3},{4,20},{20... | collective-permute-start | bytes 491528 | tf_op jit(solution)/shard_map/ppermute | solution.py:53
  606.1 19.1 %collective-permute-start.301 = (bf16[128,960]{1,0:T(8,128)(2,1)S(1)}, bf16[128,960]{1,0:T(8,128)(2,1)S(1)}, u32[]{:S(2)}, u32[]{:S(2)}) collective-permute-start(bf16[128,960]{1,0:T(8,128)(2,1)S(1)} %convert_element_type.774.refs_0_), channel_id=1, source_target_pairs={{0,64},{32,96},{64,0},{96,32},{1,65},{33,97},{65,1},{97,33},{2,66}... | collective-permute-start | bytes 737288 | tf_op jit(solution)/shard_map/ppermute | solution.py:49
  620.8 34.4 %collective-permute-start.289 = (bf16[352,960]{1,0:T(8,128)(2,1)}, bf16[352,960]{1,0:T(8,128)(2,1)}, u32[]{:S(2)}, u32[]{:S(2)}) collective-permute-start(bf16[352,960]{1,0:T(8,128)(2,1)} %get-tuple-element.768), channel_id=1, source_target_pairs={{0,32},{32,64},{64,96},{96,0},{1,33},{33,65},{65,97},{97,1},{2,34}... | collective-permute-start | bytes 2027528 | tf_op jit(solution)/shard_map/ppermute | solution.py:49
  620.8 34.4 %collective-permute-start.290 = (bf16[352,960]{1,0:T(8,128)(2,1)}, bf16[352,960]{1,0:T(8,128)(2,1)}, u32[]{:S(2)}, u32[]{:S(2)}) collective-permute-start(bf16[352,960]{1,0:T(8,128)(2,1)} %get-tuple-element.770), channel_id=1, source_target_pairs={{0,64},{32,96},{64,0},{96,32},{1,65},{33,97},{65,1},{97,33},{2,66}... | collective-permute-start | bytes 2027528 | tf_op jit(solution)/shard_map/ppermute | solution.py:49
  622.6 33.0 %collective-permute-start.291 = (bf16[352,960]{1,0:T(8,128)(2,1)S(1)}, bf16[352,960]{1,0:T(8,128)(2,1)}, u32[]{:S(2)}, u32[]{:S(2)}) collective-permute-start(bf16[352,960]{1,0:T(8,128)(2,1)S(1)} %get-tuple-element.769), channel_id=1, source_target_pairs={{0,96},{32,0},{64,32},{96,64},{1,97},{33,1},{65,33},{97,65},{2,98}... | collective-permute-start | bytes 2027528 | tf_op jit(solution)/shard_map/ppermute | solution.py:49
  631.0 37.2 %all-to-all-start.3 = ((bf16[16,24,960]{2,1,0:T(8,128)(2,1)}), bf16[16,24,960]{2,1,0:T(8,128)(2,1)S(1)}, u32[]{:S(2)}, u32[]{:S(2)}) async-start(bf16[16,24,960]{2,1,0:T(8,128)(2,1)} %bitcast.163), calls=%async_computation.6 | async-start | bytes 1572864 | tf_op jit(solution)/shard_map/all_to_all | solution.py:1192
  (288 other events, 2791.4 us)
Sparse Core Ops, SparseCore 0:
  17.5 57.8 all-gather.12
  78.5 75.8 all-gather.14
  156.8 108.4 all-gather.16
  352.4 98.8 reduce-scatter.14
  547.5 92.3 reduce-scatter.12

commit v8 on v6

--- a/solution.py
+++ b/solution.py
@@ -266,7 +266,7 @@
             dq_ref[:, place : place + 64] = back[128 * i : 128 * i + 128]
 
 
-def attend_back(queries, pairs, bias, log_total, attended, grads, cosine, sine):
+def attend_back(mib, queries, pairs, bias, log_total, attended, grads, cosine, sine):
     side = struct(BFLOAT, 4 * TOK_DEV, 640)
     return pl.pallas_call(
         attend_back_kernel,
@@ -274,7 +274,7 @@
         cost_estimate=pl.CostEstimate(
             flops=20_000_000_000, bytes_accessed=9_000_000, transcendentals=4_000_000
         ),
-        compiler_params=params(BIG),
+        compiler_params=params(mib),
     )(queries, *pairs, bias, log_total, attended, grads, cosine, sine)
 
 
@@ -1087,26 +1087,24 @@
             + [swap(mlp_input), swap(grad_rows)]
         )
         grad_query, *grad_sides = attend_back(
+            24 if step == RECUR - 1 else BIG,
             queries, pairs, biases[step], log_total, attended, grad_attended, *turns
         )
         far_normed = swap(normed)
         square_kept.append((attended, grad_attn, normed, grad_query))
         square_far.append((swap(attended), swap(grad_attn), far_normed, swap(grad_query)))
+        grad_own = group_scatter(*grad_sides)
+        grad_pair, grad_hidden, small = enter_back(
+            grad_in, grad_query, grad_own, hidden_in, gains, *projections
+        )
+        gain_one = gain_one + small[0:1]
         if step == 0:
-            tied = tie(*grad_sides, *mlp_kept[-1])
-            grad_sides, mlp_kept[-1] = tied[:4], tied[4:]
-        grad_own = group_scatter(*grad_sides)
-        if step == 0:
+            _, *mlp_kept[-1] = tie(grad_hidden, *mlp_kept[-1])
             mlp_half = mlp_grads(core.astype(jnp.int32), mlp_kept, mlp_far)
             mlp_sum = lax.psum_scatter(
                 mlp_half.reshape(16 * 240, D), DP_AXES, scatter_dimension=0, tiled=True
             )
             squares = square_grads(square_kept, square_far)
-            grad_own, mlp_half, *squares = tie(grad_own, mlp_half, *squares)
-        grad_pair, grad_hidden, small = enter_back(
-            grad_in, grad_query, grad_own, hidden_in, gains, *projections
-        )
-        gain_one = gain_one + small[0:1]
         pack_kept.append((normed, grad_pair))
         pack_far.append((far_normed, swap(grad_pair)))
         if step == 1 and not dense:
@@ -1140,13 +1138,13 @@
         return jnp.stack([value[..., i : i + 48, :] for i in (0, 16, 40, 56)])
 
     part = stage(part, "z", z).astype(BFLOAT)
-    part, mlp_sum = tie(y_windows(part), mlp_sum)
+    part = stage(y_windows(part), "y", y).astype(BFLOAT)
+    part, mlp_sum = tie(x_windows(part), mlp_sum)
     mlp_sum = mlp_sum.reshape(3, 4, UNITS, D).transpose(1, 0, 2, 3)
     mlp_grad = mlp_sum[0].astype(FLOAT)
     for k in (1, 2, 3):
         mlp_grad = mlp_grad + shift(mlp_sum[k], "z", -k).astype(FLOAT)
-    part = stage(part, "y", y).astype(BFLOAT)
-    part = stage(x_windows(part), "x", x).reshape(-1)
+    part = stage(part, "x", x).reshape(-1)
     begin = aligned_row(DP * model_index) + 80 * y + (20 * x) // 8 * 8
     pack_grad = lax.dynamic_slice(part, (PACK_DEV * device - D * begin,), (PACK_DEV,))
 

time: 729 us -> 736 us (level)
  waiting for transfers between devices: 132 us -> 119 us
  other arithmetic: 39.1 us -> 49 us
    ppermute x33, waiting for transfers between devices: 70.7 us -> 62.3 us  [shift(): return lax.ppermute(value, axis, [(i, (i + steps) % 4) for i in range(4)])]
    all_gather x1, waiting for transfers between devices: 13.8 us -> 5.68 us  [gradients(): lax.all_gather(mlp_quad.reshape(3 * 80, D), ('core', 'y', 'x'), axis=0, t...]
    unnamed x383 -> x443, local copies, waits for them, and re-layouts: 22.8 us -> 30.3 us
  transfers between devices with their start and end apart: 160 -> 160, of which waited for: 56 -> 61; matrix products, arithmetic and copies ran while one was open for 7% -> 8% of each run, Pallas kernels for 25% -> 24%
where the time goes in v8:
time: 736 us; the launch traced here: 724 us
  starting transfers between devices  218 us (30%)
  Pallas kernels  216 us (29%)
  waiting for transfers between devices  119 us (16%)
  local copies, waits for them, and re-layouts  53.9 us (7%)
  other arithmetic  49 us (7%)
  blocking collectives  37.6 us (5%)
  between operations  23.5 us (3%)
    ppermute x33, waiting for transfers between devices, shift(): return lax.ppermute(value, axis, [(i, (i + steps) % 4) for i in range(4)])  62.3 us
    ppermute x78, starting transfers between devices, swap(): return lax.ppermute(value, 'core', [(0, 1), (1, 0)])  54.9 us
    ppermute x33, starting transfers between devices, shift(): return lax.ppermute(value, axis, [(i, (i + steps) % 4) for i in range(4)])  46 us
    pallas_call x3, Pallas kernels, block_back(): pl.pallas_call(block_back_kernel, grid=(FF_STEPS,), in_specs=[full, whole...  40.4 us
    pallas_call x3, Pallas kernels, attend_back(): pl.pallas_call(attend_back_kernel, out_shape=(struct(BFLOAT, TOK_DEV, D),...  38.4 us
    pallas_call x3, Pallas kernels, block(): pl.pallas_call(functools.partial(block_kernel, more), grid=(FF_STEPS,), i...  38.3 us
    ppermute x12, starting transfers between devices, group_gather(): prev.append(lax.ppermute(pair, ('z',) + DP_AXES, pairs))  35.3 us
    ppermute x9, starting transfers between devices, group_gather(): lax.ppermute(pair, 'z', [((i + k) % 4, i) for i in range(4) if (i + k) %...  32.5 us
  transfers between devices with their start and end apart: 160, of which 61 were waited for; matrix products, arithmetic and copies ran while one was open for 8% of the time, Pallas kernels for 24%

profile of v8, /device:TPU:1, one launch (start us, length us, event | category | flops | bytes accessed | tf_op | source)
XLA Modules:
  0.0 724.2 jit_solution(2010732582194393032)
XLA Ops:
  20.4 6.2 all-to-all-start.1
  26.7 3.8 collective-permute-start.155
  37.1 4.5 collective-permute-done.153
  43.9 19.4 %all_to_all.52 = bf16[16,24,960]{2,1,0:T(8,128)(2,1)S(1)} all-to-all(bf16[16,24,960]{2,1,0:T(8,128)(2,1)S(1)} %bitcast.349), channel_id=1, replica_groups=mesh['z'=4,'core'=2,'y'=4,'x'=4] {'y','x'}, dimensions={0} | all-to-all | bytes 1474560 | tf_op jit(solution)/shard_map/all_to_all | solution.py:919
  76.7 3.9 collective-permute-start.157
  87.9 3.1 copy-done.18
  90.9 4.6 shard_map.222
  95.7 4.0 collective-permute-done.163
  105.0 5.4 collective-permute-start.168
  112.4 5.2 collective-permute-start.170
  130.1 8.8 %shard_map.224 = (bf16[128,960]{1,0:T(8,128)(2,1)S(1)}, f32[8,384]{1,0:T(8,128)S(1)}) custom-call(bf16[960,128]{1,0:T(8,128)(2,1)S(1)} %get-tuple-element.327.query_ref, bf16[128,640]{1,0:T(8,128)(2,1)S(1)} %collective-permute-done.166.refs_0_, bf16[128,640]{1,0:T(8,128)(2,1)S(1)} %collective-permute-done.167.refs_1_, ...), custom_call_target="tpu_custom_call" | custom-call | flops 12000000000 | bytes 5000000 | tf_op jit(solution)/shard_map/pallas_call | solution.py:226
  147.8 5.7 all-gather.15.cloned.1.call-done
  153.5 13.1 %shard_map.225 = (f32[128,960]{1,0:T(8,128)}, bf16[128,960]{1,0:T(8,128)(2,1)}, f32[128,2560]{1,0:T(8,128)}, f32[128,2560]{1,0:T(8,128)}, bf16[128,2560]{1,0:T(8...) custom-call(bf16[128,960]{1,0:T(8,128)(2,1)} %copy-done.36, ...), custom_call_target="tpu_custom_call" | custom-call | flops 4000000000 | bytes 20000000 | tf_op jit(solution)/shard_map/pallas_call | solution.py:402
  169.5 5.2 collective-permute-start.183
  176.2 7.4 %collective-permute-start.185 = (bf16[128,640]{1,0:T(8,128)(2,1)}, bf16[128,640]{1,0:T(8,128)(2,1)S(1)}, u32[]{:S(2)}, u32[]{:S(2)}) collective-permute-start(bf16[128,640]{1,0:T(8,128)(2,1)} %get-tuple-element.333.refs_4_), channel_id=1, source_target_pairs={{0,96},{1,97},{2,98},{3,99},{4,100},{5,101},{6,102},{7,103},{8,104... | collective-permute-start | bytes 491528 | tf_op jit(solution)/shard_map/ppermute | solution.py:113
  195.3 8.8 %shard_map.226 = (bf16[128,960]{1,0:T(8,128)(2,1)S(1)}, f32[8,384]{1,0:T(8,128)S(1)}) custom-call(bf16[960,128]{1,0:T(8,128)(2,1)S(1)} %copy-done.111, bf16[128,640]{1,0:T(8,128)(2,1)S(1)} %collective-permute-done.181.refs_0_, bf16[128,640]{1,0:T(8,128)(2,1)S(1)} %collective-permute-done.182.refs_1_, bf16[128,640]{1,0:T(8,128)(2,1)S(1)} %collective-permute-done.183.refs_2_, ...), custom_call_target="tpu_custom_call" | custom-call | flops 12000000000 | bytes 5000000 | tf_op jit(solution)/shard_map/pallas_call | solution.py:226
  205.5 13.3 %shard_map.227 = (f32[128,960]{1,0:T(8,128)}, bf16[128,960]{1,0:T(8,128)(2,1)}, f32[128,2560]{1,0:T(8,128)}, f32[128,2560]{1,0:T(8,128)}, bf16[128,2560]{1,0:T(8...) custom-call(bf16[128,960]{1,0:T(8,128)(2,1)} %copy-done.40, ...), custom_call_target="tpu_custom_call" | custom-call | flops 4000000000 | bytes 20000000 | tf_op jit(solution)/shard_map/pallas_call | solution.py:402
  218.8 4.9 collective-permute-start.196
  224.4 8.6 %collective-permute-start.198 = (bf16[128,640]{1,0:T(8,128)(2,1)}, bf16[128,640]{1,0:T(8,128)(2,1)S(1)}, u32[]{:S(2)}, u32[]{:S(2)}) collective-permute-start(bf16[128,640]{1,0:T(8,128)(2,1)} %get-tuple-element.337.refs_4_), channel_id=1, source_target_pairs={{64,1},{65,2},{66,3},{67,4},{68,5},{69,6},{70,7},{71,8},{72,9},{73... | collective-permute-start | bytes 491528 | tf_op jit(solution)/shard_map/ppermute | solution.py:120
  234.4 8.5 %collective-permute-start.200 = (bf16[128,640]{1,0:T(8,128)(2,1)}, bf16[128,640]{1,0:T(8,128)(2,1)S(1)}, u32[]{:S(2)}, u32[]{:S(2)}) collective-permute-start(bf16[128,640]{1,0:T(8,128)(2,1)} %get-tuple-element.337.refs_4_), channel_id=1, source_target_pairs={{0,96},{1,97},{2,98},{3,99},{4,100},{5,101},{6,102},{7,103},{8,104... | collective-permute-start | bytes 491528 | tf_op jit(solution)/shard_map/ppermute | solution.py:113
  254.4 8.8 %shard_map.228 = (bf16[128,960]{1,0:T(8,128)(2,1)S(1)}, f32[8,384]{1,0:T(8,128)S(1)}) custom-call(bf16[960,128]{1,0:T(8,128)(2,1)S(1)} %copy-done.113, bf16[128,640]{1,0:T(8,128)(2,1)S(1)} %collective-permute-done.196.refs_0_, bf16[128,640]{1,0:T(8,128)(2,1)S(1)} %collective-permute-done.197.refs_1_, bf16[128,640]{1,0:T(8,128)(2,1)S(1)} %collective-permute-done.198.refs_2_, ...), custom_call_target="tpu_custom_call" | custom-call | flops 12000000000 | bytes 5000000 | tf_op jit(solution)/shard_map/pallas_call | solution.py:226
  264.0 11.9 %shard_map.229 = (f32[128,960]{1,0:T(8,128)}, bf16[128,960]{1,0:T(8,128)(2,1)}, f32[128,2560]{1,0:T(8,128)}, f32[128,2560]{1,0:T(8,128)}, bf16[128,2560]{1,0:T(8...) custom-call(bf16[128,960]{1,0:T(8,128)(2,1)} %copy-done.44, ...), custom_call_target="tpu_custom_call" | custom-call | flops 4000000000 | bytes 20000000 | tf_op jit(solution)/shard_map/pallas_call | solution.py:402
  283.9 3.1 collective-permute-done.211.refs_1_
  287.0 6.1 collective-permute-start.215
  293.2 3.1 collective-permute-done.213.refs_3_
  300.9 13.4 %shard_map.230 = (f32[256,6144]{1,0:T(8,128)}, bf16[256,960]{1,0:T(8,128)(2,1)}, f32[8,256]{1,0:T(8,128)}) custom-call(s32[256,1]{1,0:T(8,128)} %copy.223.rows_ref, s32[1,1024]{1,0:T(1,128)} %bitcast.374, bf16[128,960]{1,0:T(8,128)(2,1)} %copy-done.262, bf16[128,960]{1,0:T(8,128)(2,1)} %copy-done.336, bf16[128,960]{1,0:T(8,128)(2,1)} %copy-done.337, ...), custom_call_target="tpu_custom_call" | custom-call | tf_op jit(solution)/shard_map/pallas_call | solution.py:607
  323.2 17.6 %shard_map.231 = (bf16[6144,960]{1,0:T(8,128)(2,1)}, bf16[128,960]{1,0:T(8,128)(2,1)}, bf16[128,960]{1,0:T(8,128)(2,1)}, bf16[128,960]{1,0:T(8,128)(2,1)}, bf16[...) custom-call(s32[256,1]{1,0:T(8,128)} %copy.223.rows_ref, ...), custom_call_target="tpu_custom_call" | custom-call | tf_op jit(solution)/shard_map/pallas_call | solution.py:656
  358.0 6.7 collective-permute-done.224
  367.9 13.9 %shard_map.232 = (bf16[128,960]{1,0:T(8,128)(2,1)}, bf16[128,2560]{1,0:T(8,128)(2,1)}, bf16[128,2560]{1,0:T(8,128)(2,1)}, f32[128,960]{1,0:T(8,128)}, bf16[128,9...) custom-call(f32[128,960]{1,0:T(8,128)} %multiply_subtract_fusion.2.new_ref, f32[128,1]{1,0:T(8,128)} %copy.222.sel_ref, ...), custom_call_target="tpu_custom_call" | custom-call | flops 4000000000 | bytes 20000000 | tf_op jit(solution)/shard_map/pallas_call | solution.py:501
  382.9 10.9 %shard_map.233 = (bf16[128,960]{1,0:T(8,128)(2,1)S(1)}, bf16[512,640]{1,0:T(8,128)(2,1)S(1)}, bf16[512,640]{1,0:T(8,128)(2,1)S(1)}, bf16[512,640]{1,0:T(8,128)(2,1)}, bf16[512,640]{1,0:T(8,128)(2,1)S(1)}) custom-call(bf16[960,128]{1,0:T(8,128)(2,1)S(1)} %copy-done.114, bf16[128,640]{1,0:T(8,128)(2,1)S(1)} %copy-done.182, bf16[128,640]{1,0:T(8,128)(2,1)S(1)} %copy-done.184, ...), custom_call_target="tpu_custom_call" | custom-call | flops 20000000000 | bytes 9000000 | tf_op jit(solution)/shard_map/pallas_call | solution.py:271
  405.9 3.8 collective-permute-done.241
  411.0 4.0 collective-permute-done.240
  422.3 3.5 collective-permute-done.234
  429.0 13.6 %shard_map.235 = (bf16[128,960]{1,0:T(8,128)(2,1)}, bf16[128,2560]{1,0:T(8,128)(2,1)}, bf16[128,2560]{1,0:T(8,128)(2,1)}, f32[128,960]{1,0:T(8,128)}, bf16[128,9...) custom-call(f32[128,960]{1,0:T(8,128)} %copy-done.90, f32[128,1]{1,0:T(8,128)} %copy.221.sel_ref, ...), custom_call_target="tpu_custom_call" | custom-call | flops 4000000000 | bytes 20000000 | tf_op jit(solution)/shard_map/pallas_call | solution.py:501
  442.6 13.8 %shard_map.236 = (bf16[128,960]{1,0:T(8,128)(2,1)}, bf16[512,640]{1,0:T(8,128)(2,1)}, bf16[512,640]{1,0:T(8,128)(2,1)}, bf16[512,640]{1,0:T(8,128)(2,1)}, bf16[512,640]{1,0:T(8,128)(2,1)}) custom-call(bf16[960,128]{1,0:T(8,128)(2,1)} %get-tuple-element.332.query_ref, bf16[128,640]{1,0:T(8,128)(2,1)} %copy-done.152, bf16[128,640]{1,0:T(8,128)(2,1)} %copy-done.154, ...), custom_call_target="tpu_custom_call" | custom-call | flops 20000000000 | bytes 9000000 | tf_op jit(solution)/shard_map/pallas_call | solution.py:271
  487.0 12.9 %shard_map.238 = (bf16[128,960]{1,0:T(8,128)(2,1)}, bf16[128,2560]{1,0:T(8,128)(2,1)}, bf16[128,2560]{1,0:T(8,128)(2,1)}, f32[128,960]{1,0:T(8,128)}, bf16[128,9...) custom-call(f32[128,960]{1,0:T(8,128)} %copy-done.88, f32[128,1]{1,0:T(8,128)} %copy.220.sel_ref, ...), custom_call_target="tpu_custom_call" | custom-call | flops 4000000000 | bytes 20000000 | tf_op jit(solution)/shard_map/pallas_call | solution.py:501
  499.9 13.7 %shard_map.239 = (bf16[128,960]{1,0:T(8,128)(2,1)}, bf16[512,640]{1,0:T(8,128)(2,1)}, bf16[512,640]{1,0:T(8,128)(2,1)}, bf16[512,640]{1,0:T(8,128)(2,1)}, bf16[512,640]{1,0:T(8,128)(2,1)}) custom-call(bf16[960,128]{1,0:T(8,128)(2,1)} %copy-done.108, bf16[128,640]{1,0:T(8,128)(2,1)} %copy-done.117, bf16[128,640]{1,0:T(8,128)(2,1)} %copy-done.119, ...), custom_call_target="tpu_custom_call" | custom-call | flops 20000000000 | bytes 9000000 | tf_op jit(solution)/shard_map/pallas_call | solution.py:271
  534.6 3.9 collective-permute-done.264
  547.4 11.5 %shard_map.243 = bf16[16,3,80,960]{3,2,1,0:T(8,128)(2,1)} custom-call(s32[1]{0:T(128)} %bitcast.152.which_ref, bf16[128,2560]{1,0:T(8,128)(2,1)} %get-tuple-element.416.refs_0_, bf16[128,2560]{1,0:T(8,128)(2,1)} %get-tuple-element.417.refs_1_, bf16[128,2560]{1,0:T(8,128)(2,1)} %get-tuple-element.418.refs_2_, bf16[128,960]{1,0:T(8,128)(2,1)} %get-tuple-element.419.refs_3_, ...), custom_call_target="tpu_custom_call" | custom-call | tf_op jit(solution)/shard_map/pallas_call | solution.py:699
  568.5 3.3 collective-permute-done.268.refs_1_
  577.2 7.4 %shard_map.240 = (bf16[960,960]{1,0:T(8,128)(2,1)}, bf16[960,960]{1,0:T(8,128)(2,1)}) custom-call(bf16[128,960]{1,0:T(8,128)(2,1)} %copy-done.44, bf16[128,960]{1,0:T(8,128)(2,1)} %get-tuple-element.361.refs_1_, bf16[128,960]{1,0:T(8,128)(2,1)} %get-tuple-element.362.refs_2_.refs_3_, bf16[128,960]{1,0:T(8,128)(2,1)} %copy-done.52, ...), custom_call_target="tpu_custom_call" | custom-call | tf_op jit(solution)/shard_map/pallas_call | solution.py:730
  585.4 8.2 %shard_map.242 = bf16[4,352,960]{2,1,0:T(8,128)(2,1)} custom-call(s32[4]{0:T(128)} %pad_add_fusion.1.starts_ref, bf16[960,960]{1,0:T(8,128)(2,1)} %get-tuple-element.398.refs_0_, bf16[960,960]{1,0:T(8,128)(2,1)} %get-tuple-element.399.refs_1_, f32[16,960]{1,0:T(8,128)} %add.1261.refs_2_, bf16[128,960]{1,0:T(8,128)(2,1)} %get-tuple-element.362.refs_2_.refs_3_, ...), custom_call_target="tpu_custom_call" | custom-call | tf_op jit(solution)/shard_map/pallas_call | solution.py:768
  607.7 17.2 %all-to-all-start.3 = ((bf16[16,24,960]{2,1,0:T(8,128)(2,1)}), bf16[16,24,960]{2,1,0:T(8,128)(2,1)S(1)}, u32[]{:S(2)}, u32[]{:S(2)}) async-start(bf16[16,24,960]{2,1,0:T(8,128)(2,1)} %bitcast.163), calls=%async_computation.6 | async-start | bytes 1572864 | tf_op jit(solution)/shard_map/all_to_all | solution.py:1164
  624.9 9.3 %collective-permute-done.274 = bf16[352,960]{1,0:T(8,128)(2,1)} collective-permute-done((bf16[352,960]{1,0:T(8,128)(2,1)S(1)}, bf16[352,960]{1,0:T(8,128)(2,1)}, u32[]{:S(2)}, u32[]{:S(2)}) %collective-permute-start.274) | collective-permute-done | bytes 675872 | tf_op jit(solution)/shard_map/ppermute | solution.py:49
  637.5 12.5 %collective-permute-start.279 = (bf16[112,960]{1,0:T(8,128)(2,1)}, bf16[112,960]{1,0:T(8,128)(2,1)S(1)}, u32[]{:S(2)}, u32[]{:S(2)}) collective-permute-start(bf16[112,960]{1,0:T(8,128)(2,1)} %get-tuple-element.672), channel_id=1, source_target_pairs={{0,12},{4,0},{8,4},{12,8},{1,13},{5,1},{9,5},{13,9},{2,14},{6,2},{... | collective-permute-start | bytes 645128 | tf_op jit(solution)/shard_map/ppermute | solution.py:49
  653.0 8.4 %collective-permute-done.279 = bf16[112,960]{1,0:T(8,128)(2,1)S(1)} collective-permute-done((bf16[112,960]{1,0:T(8,128)(2,1)}, bf16[112,960]{1,0:T(8,128)(2,1)S(1)}, u32[]{:S(2)}, u32[]{:S(2)}) %collective-permute-start.279) | collective-permute-done | bytes 215072 | tf_op jit(solution)/shard_map/ppermute | solution.py:49
  687.7 18.2 %all_to_all.53 = f32[128,1,128]{2,1,0:T(1,128)S(1)} all-to-all(f32[128,1,128]{2,1,0:T(1,128)S(1)} %iota.151), channel_id=1, replica_groups=mesh['z'=4,'core'=2,'y'=4,'x'=4] {'z','core','y','x'}, dimensions={0} | all-to-all | bytes 131072 | tf_op jit(solution)/shard_map/all_to_all | solution.py:1206
  711.2 5.1 multiply_subtract_fusion.1
  (900 shorter events, 290.5 us)
Async XLA Ops:
  7.2 76.8 %all-gather.13.cloned.1.call-start = ((), (), s32[]{:S(2)}) async-start(), calls=%async_computation.14 | async-start | bytes 6488064 | tf_op jit(solution)/shard_map/all_gather | solution.py:878
  26.6 126.9 %all-gather.15.cloned.1.call-start = ((), (), s32[]{:S(2)}) async-start(), calls=%async_computation.15 | async-start | bytes 16220160 | tf_op jit(solution)/shard_map/all_gather | solution.py:915
  42.5 257.4 %all-gather.17.cloned.1.call-start = ((), (), s32[]{:S(2)}) async-start(), calls=%async_computation.16 | async-start | bytes 13369344 | tf_op jit(solution)/shard_map/all_gather | solution.py:921
  63.3 421.4 %reduce-scatter.15.cloned.1.call-start = ((), (), s32[]{:S(2)}) async-start(), calls=%async_computation.18 | async-start | bytes 13369344
  81.4 14.3 %collective-permute-start.156 = (bf16[128,960]{1,0:T(8,128)(2,1)}, bf16[128,960]{1,0:T(8,128)(2,1)}, u32[]{:S(2)}, u32[]{:S(2)}) collective-permute-start(bf16[128,960]{1,0:T(8,128)(2,1)} %get-tuple-element.312), channel_id=1, source_target_pairs={{0,16},{16,0},{1,17},{17,1},{2,18},{18,2},{3,19},{19,3},{4,20},{20... | collective-permute-start | bytes 737288 | tf_op jit(solution)/shard_map/ppermute | solution.py:53
  84.0 15.7 %collective-permute-start.163 = (bf16[128,960]{1,0:T(8,128)(2,1)}, bf16[128,960]{1,0:T(8,128)(2,1)}, u32[]{:S(2)}, u32[]{:S(2)}) collective-permute-start(bf16[128,960]{1,0:T(8,128)(2,1)} %add_convert_fusion.24), channel_id=1, source_target_pairs={{0,32},{32,64},{64,96},{96,0},{1,33},{33,65},{65,97},{97,1},{2,34}... | collective-permute-start | bytes 737288 | tf_op jit(solution)/shard_map/ppermute | solution.py:49
  102.2 15.5 %collective-permute-start.166 = (bf16[128,640]{1,0:T(8,128)(2,1)S(1)}, bf16[128,640]{1,0:T(8,128)(2,1)S(1)}, u32[]{:S(2)}, u32[]{:S(2)}) collective-permute-start(bf16[128,640]{1,0:T(8,128)(2,1)S(1)} %get-tuple-element.328.refs_4_), channel_id=1, source_target_pairs={{0,1},{1,2},{2,3},{3,4},{4,5},{5,6},{6,7},{7,8},{8,9},{9,10},{10,1... | collective-permute-start | bytes 491528 | tf_op jit(solution)/shard_map/ppermute | solution.py:120
  104.3 14.6 %collective-permute-start.167 = (bf16[128,640]{1,0:T(8,128)(2,1)S(1)}, bf16[128,640]{1,0:T(8,128)(2,1)S(1)}, u32[]{:S(2)}, u32[]{:S(2)}) collective-permute-start(bf16[128,640]{1,0:T(8,128)(2,1)S(1)} %get-tuple-element.328.refs_4_), channel_id=1, source_target_pairs={{32,1},{33,2},{34,3},{35,4},{36,5},{37,6},{38,7},{39,8},{40,9},{41... | collective-permute-start | bytes 491528 | tf_op jit(solution)/shard_map/ppermute | solution.py:120
  105.0 16.5 %collective-permute-start.168 = (bf16[128,640]{1,0:T(8,128)(2,1)S(1)}, bf16[128,640]{1,0:T(8,128)(2,1)S(1)}, u32[]{:S(2)}, u32[]{:S(2)}) collective-permute-start(bf16[128,640]{1,0:T(8,128)(2,1)S(1)} %get-tuple-element.328.refs_4_), channel_id=1, source_target_pairs={{64,1},{65,2},{66,3},{67,4},{68,5},{69,6},{70,7},{71,8},{72,9},{73... | collective-permute-start | bytes 491528 | tf_op jit(solution)/shard_map/ppermute | solution.py:120
  110.4 13.7 %collective-permute-start.169 = (bf16[128,640]{1,0:T(8,128)(2,1)S(1)}, bf16[128,640]{1,0:T(8,128)(2,1)S(1)}, u32[]{:S(2)}, u32[]{:S(2)}) collective-permute-start(bf16[128,640]{1,0:T(8,128)(2,1)S(1)} %get-tuple-element.328.refs_4_), channel_id=1, source_target_pairs={{96,1},{97,2},{98,3},{99,4},{100,5},{101,6},{102,7},{103,8},{104,9... | collective-permute-start | bytes 491528 | tf_op jit(solution)/shard_map/ppermute | solution.py:120
  112.4 13.6 %collective-permute-start.170 = (bf16[128,640]{1,0:T(8,128)(2,1)S(1)}, bf16[128,640]{1,0:T(8,128)(2,1)S(1)}, u32[]{:S(2)}, u32[]{:S(2)}) collective-permute-start(bf16[128,640]{1,0:T(8,128)(2,1)S(1)} %get-tuple-element.328.refs_4_), channel_id=1, source_target_pairs={{0,96},{1,97},{2,98},{3,99},{4,100},{5,101},{6,102},{7,103},{8,104... | collective-permute-start | bytes 491528 | tf_op jit(solution)/shard_map/ppermute | solution.py:113
  166.7 17.0 %collective-permute-start.181 = (bf16[128,640]{1,0:T(8,128)(2,1)}, bf16[128,640]{1,0:T(8,128)(2,1)S(1)}, u32[]{:S(2)}, u32[]{:S(2)}) collective-permute-start(bf16[128,640]{1,0:T(8,128)(2,1)} %get-tuple-element.333.refs_4_), channel_id=1, source_target_pairs={{0,1},{1,2},{2,3},{3,4},{4,5},{5,6},{6,7},{7,8},{8,9},{9,10},{10,1... | collective-permute-start | bytes 491528 | tf_op jit(solution)/shard_map/ppermute | solution.py:120
  168.9 16.2 %collective-permute-start.182 = (bf16[128,640]{1,0:T(8,128)(2,1)}, bf16[128,640]{1,0:T(8,128)(2,1)S(1)}, u32[]{:S(2)}, u32[]{:S(2)}) collective-permute-start(bf16[128,640]{1,0:T(8,128)(2,1)} %get-tuple-element.333.refs_4_), channel_id=1, source_target_pairs={{32,1},{33,2},{34,3},{35,4},{36,5},{37,6},{38,7},{39,8},{40,9},{41... | collective-permute-start | bytes 491528 | tf_op jit(solution)/shard_map/ppermute | solution.py:120
  169.5 18.0 %collective-permute-start.183 = (bf16[128,640]{1,0:T(8,128)(2,1)}, bf16[128,640]{1,0:T(8,128)(2,1)S(1)}, u32[]{:S(2)}, u32[]{:S(2)}) collective-permute-start(bf16[128,640]{1,0:T(8,128)(2,1)} %get-tuple-element.333.refs_4_), channel_id=1, source_target_pairs={{64,1},{65,2},{66,3},{67,4},{68,5},{69,6},{70,7},{71,8},{72,9},{73... | collective-permute-start | bytes 491528 | tf_op jit(solution)/shard_map/ppermute | solution.py:120
  174.7 14.9 %collective-permute-start.184 = (bf16[128,640]{1,0:T(8,128)(2,1)}, bf16[128,640]{1,0:T(8,128)(2,1)S(1)}, u32[]{:S(2)}, u32[]{:S(2)}) collective-permute-start(bf16[128,640]{1,0:T(8,128)(2,1)} %get-tuple-element.333.refs_4_), channel_id=1, source_target_pairs={{96,1},{97,2},{98,3},{99,4},{100,5},{101,6},{102,7},{103,8},{104,9... | collective-permute-start | bytes 491528 | tf_op jit(solution)/shard_map/ppermute | solution.py:120
  176.2 13.5 %collective-permute-start.185 = (bf16[128,640]{1,0:T(8,128)(2,1)}, bf16[128,640]{1,0:T(8,128)(2,1)S(1)}, u32[]{:S(2)}, u32[]{:S(2)}) collective-permute-start(bf16[128,640]{1,0:T(8,128)(2,1)} %get-tuple-element.333.refs_4_), channel_id=1, source_target_pairs={{0,96},{1,97},{2,98},{3,99},{4,100},{5,101},{6,102},{7,103},{8,104... | collective-permute-start | bytes 491528 | tf_op jit(solution)/shard_map/ppermute | solution.py:113
  218.8 24.1 %collective-permute-start.196 = (bf16[128,640]{1,0:T(8,128)(2,1)}, bf16[128,640]{1,0:T(8,128)(2,1)S(1)}, u32[]{:S(2)}, u32[]{:S(2)}) collective-permute-start(bf16[128,640]{1,0:T(8,128)(2,1)} %get-tuple-element.337.refs_4_), channel_id=1, source_target_pairs={{0,1},{1,2},{2,3},{3,4},{4,5},{5,6},{6,7},{7,8},{8,9},{9,10},{10,1... | collective-permute-start | bytes 491528 | tf_op jit(solution)/shard_map/ppermute | solution.py:120
  223.8 20.5 %collective-permute-start.197 = (bf16[128,640]{1,0:T(8,128)(2,1)}, bf16[128,640]{1,0:T(8,128)(2,1)S(1)}, u32[]{:S(2)}, u32[]{:S(2)}) collective-permute-start(bf16[128,640]{1,0:T(8,128)(2,1)} %get-tuple-element.337.refs_4_), channel_id=1, source_target_pairs={{32,1},{33,2},{34,3},{35,4},{36,5},{37,6},{38,7},{39,8},{40,9},{41... | collective-permute-start | bytes 491528 | tf_op jit(solution)/shard_map/ppermute | solution.py:120
  224.4 22.3 %collective-permute-start.198 = (bf16[128,640]{1,0:T(8,128)(2,1)}, bf16[128,640]{1,0:T(8,128)(2,1)S(1)}, u32[]{:S(2)}, u32[]{:S(2)}) collective-permute-start(bf16[128,640]{1,0:T(8,128)(2,1)} %get-tuple-element.337.refs_4_), channel_id=1, source_target_pairs={{64,1},{65,2},{66,3},{67,4},{68,5},{69,6},{70,7},{71,8},{72,9},{73... | collective-permute-start | bytes 491528 | tf_op jit(solution)/shard_map/ppermute | solution.py:120
  233.1 15.6 %collective-permute-start.199 = (bf16[128,640]{1,0:T(8,128)(2,1)}, bf16[128,640]{1,0:T(8,128)(2,1)S(1)}, u32[]{:S(2)}, u32[]{:S(2)}) collective-permute-start(bf16[128,640]{1,0:T(8,128)(2,1)} %get-tuple-element.337.refs_4_), channel_id=1, source_target_pairs={{96,1},{97,2},{98,3},{99,4},{100,5},{101,6},{102,7},{103,8},{104,9... | collective-permute-start | bytes 491528 | tf_op jit(solution)/shard_map/ppermute | solution.py:120
  234.4 14.8 %collective-permute-start.200 = (bf16[128,640]{1,0:T(8,128)(2,1)}, bf16[128,640]{1,0:T(8,128)(2,1)S(1)}, u32[]{:S(2)}, u32[]{:S(2)}) collective-permute-start(bf16[128,640]{1,0:T(8,128)(2,1)} %get-tuple-element.337.refs_4_), channel_id=1, source_target_pairs={{0,96},{1,97},{2,98},{3,99},{4,100},{5,101},{6,102},{7,103},{8,104... | collective-permute-start | bytes 491528 | tf_op jit(solution)/shard_map/ppermute | solution.py:113
  282.3 14.0 %collective-permute-start.213 = (bf16[128,960]{1,0:T(8,128)(2,1)S(1)}, bf16[128,960]{1,0:T(8,128)(2,1)S(1)}, u32[]{:S(2)}, u32[]{:S(2)}) collective-permute-start(bf16[128,960]{1,0:T(8,128)(2,1)S(1)} %multiply_convert_fusion.1.refs_0_), channel_id=1, source_target_pairs={{0,32},{32,64},{64,96},{96,0},{1,33},{33,65},{65,97},{97,1},{2,34}... | collective-permute-start | bytes 737288 | tf_op jit(solution)/shard_map/ppermute | solution.py:49
  282.8 17.1 %collective-permute-start.214 = (bf16[128,960]{1,0:T(8,128)(2,1)S(1)}, bf16[128,960]{1,0:T(8,128)(2,1)S(1)}, u32[]{:S(2)}, u32[]{:S(2)}) collective-permute-start(bf16[128,960]{1,0:T(8,128)(2,1)S(1)} %multiply_convert_fusion.1.refs_0_), channel_id=1, source_target_pairs={{0,16},{16,0},{1,17},{17,1},{2,18},{18,2},{3,19},{19,3},{4,20},{20... | collective-permute-start | bytes 737288 | tf_op jit(solution)/shard_map/ppermute | solution.py:53
  287.0 12.9 %collective-permute-start.215 = (bf16[128,960]{1,0:T(8,128)(2,1)S(1)}, bf16[128,960]{1,0:T(8,128)(2,1)S(1)}, u32[]{:S(2)}, u32[]{:S(2)}) collective-permute-start(bf16[128,960]{1,0:T(8,128)(2,1)S(1)} %collective-permute-done.211.refs_1_), channel_id=1, source_target_pairs={{0,16},{16,0},{1,17},{17,1},{2,18},{18,2},{3,19},{19,3},{4,20},{20... | collective-permute-start | bytes 737288 | tf_op jit(solution)/shard_map/ppermute | solution.py:53
  341.0 323.5 %reduce-scatter.13.cloned.1.call-start = ((), (), s32[]{:S(2)}) async-start(), calls=%async_computation.17 | async-start | bytes 8355840 | tf_op jit(solution)/shard_map/reduce_scatter | solution.py:1104
  350.5 14.3 %collective-permute-start.224 = (bf16[128,960]{1,0:T(8,128)(2,1)}, bf16[128,960]{1,0:T(8,128)(2,1)S(1)}, u32[]{:S(2)}, u32[]{:S(2)}) collective-permute-start(bf16[128,960]{1,0:T(8,128)(2,1)} %add_convert_fusion.21), channel_id=1, source_target_pairs={{0,32},{32,64},{64,96},{96,0},{1,33},{33,65},{65,97},{97,1},{2,34}... | collective-permute-start | bytes 737288 | tf_op jit(solution)/shard_map/ppermute | solution.py:49
  400.7 14.3 %collective-permute-start.240 = (bf16[128,640]{1,0:T(8,128)(2,1)S(1)}, bf16[128,640]{1,0:T(8,128)(2,1)S(1)}, u32[]{:S(2)}, u32[]{:S(2)}) collective-permute-start(bf16[128,640]{1,0:T(8,128)(2,1)S(1)} %get-tuple-element.697), channel_id=1, source_target_pairs={{1,64},{2,65},{3,66},{4,67},{5,68},{6,69},{7,70},{8,71},{9,72},{10... | collective-permute-start | bytes 491528 | tf_op jit(solution)/shard_map/ppermute | solution.py:136
  402.0 15.1 %collective-permute-start.239 = (bf16[128,640]{1,0:T(8,128)(2,1)S(1)}, bf16[128,640]{1,0:T(8,128)(2,1)S(1)}, u32[]{:S(2)}, u32[]{:S(2)}) collective-permute-start(bf16[128,640]{1,0:T(8,128)(2,1)S(1)} %get-tuple-element.698), channel_id=1, source_target_pairs={{1,32},{2,33},{3,34},{4,35},{5,36},{6,37},{7,38},{8,39},{9,40},{10... | collective-permute-start | bytes 491528 | tf_op jit(solution)/shard_map/ppermute | solution.py:136
  402.7 17.3 %collective-permute-start.238 = (bf16[128,640]{1,0:T(8,128)(2,1)S(1)}, bf16[128,640]{1,0:T(8,128)(2,1)S(1)}, u32[]{:S(2)}, u32[]{:S(2)}) collective-permute-start(bf16[128,640]{1,0:T(8,128)(2,1)S(1)} %get-tuple-element.695), channel_id=1, source_target_pairs={{1,0},{2,1},{3,2},{4,3},{5,4},{6,5},{7,6},{8,7},{9,8},{10,9},{11,1... | collective-permute-start | bytes 491528 | tf_op jit(solution)/shard_map/ppermute | solution.py:136
  404.3 15.7 %collective-permute-start.236 = (bf16[128,640]{1,0:T(8,128)(2,1)S(1)}, bf16[128,640]{1,0:T(8,128)(2,1)S(1)}, u32[]{:S(2)}, u32[]{:S(2)}) collective-permute-start(bf16[128,640]{1,0:T(8,128)(2,1)S(1)} %get-tuple-element.693), channel_id=1, source_target_pairs={{32,0},{64,32},{96,64},{33,1},{65,33},{97,65},{34,2},{66,34},{98,6... | collective-permute-start | bytes 491528 | tf_op jit(solution)/shard_map/ppermute | solution.py:130
  409.7 12.6 %collective-permute-start.235 = (bf16[128,640]{1,0:T(8,128)(2,1)S(1)}, bf16[128,640]{1,0:T(8,128)(2,1)S(1)}, u32[]{:S(2)}, u32[]{:S(2)}) collective-permute-start(bf16[128,640]{1,0:T(8,128)(2,1)S(1)} %get-tuple-element.694), channel_id=1, source_target_pairs={{64,0},{96,32},{65,1},{97,33},{66,2},{98,34},{67,3},{99,35},{68,4}... | collective-permute-start | bytes 491528 | tf_op jit(solution)/shard_map/ppermute | solution.py:130
  462.9 14.0 %collective-permute-start.251 = (bf16[128,640]{1,0:T(8,128)(2,1)S(1)}, bf16[128,640]{1,0:T(8,128)(2,1)S(1)}, u32[]{:S(2)}, u32[]{:S(2)}) collective-permute-start(bf16[128,640]{1,0:T(8,128)(2,1)S(1)} %get-tuple-element.688), channel_id=1, source_target_pairs={{1,0},{2,1},{3,2},{4,3},{5,4},{6,5},{7,6},{8,7},{9,8},{10,9},{11,1... | collective-permute-start | bytes 491528 | tf_op jit(solution)/shard_map/ppermute | solution.py:136
  464.5 13.4 %collective-permute-start.249 = (bf16[128,640]{1,0:T(8,128)(2,1)S(1)}, bf16[128,640]{1,0:T(8,128)(2,1)S(1)}, u32[]{:S(2)}, u32[]{:S(2)}) collective-permute-start(bf16[128,640]{1,0:T(8,128)(2,1)S(1)} %get-tuple-element.686), channel_id=1, source_target_pairs={{32,0},{64,32},{96,64},{33,1},{65,33},{97,65},{34,2},{66,34},{98,6... | collective-permute-start | bytes 491528 | tf_op jit(solution)/shard_map/ppermute | solution.py:130
  473.0 44.9 %collective-permute-start.292 = (bf16[128,1280]{1,0:T(8,128)(2,1)}, bf16[128,1280]{1,0:T(8,128)(2,1)}, u32[]{:S(2)}, u32[]{:S(2)}) collective-permute-start(bf16[128,1280]{1,0:T(8,128)(2,1)} %constant_dynamic-slice_fusion.11), channel_id=1, source_target_pairs={{0,16},{16,0},{1,17},{17,1},{2,18},{18,2},{3,19},{19,3},{4,20},{20... | collective-permute-start | bytes 983048 | tf_op jit(solution)/shard_map/ppermute | solution.py:53
  476.9 40.7 %collective-permute-start.293 = (bf16[128,960]{1,0:T(8,128)(2,1)}, bf16[128,960]{1,0:T(8,128)(2,1)}, u32[]{:S(2)}, u32[]{:S(2)}) collective-permute-start(bf16[128,960]{1,0:T(8,128)(2,1)} %get-tuple-element.434.refs_23_), channel_id=1, source_target_pairs={{0,16},{16,0},{1,17},{17,1},{2,18},{18,2},{3,19},{19,3},{4,20},{20... | collective-permute-start | bytes 737288 | tf_op jit(solution)/shard_map/ppermute | solution.py:53
  477.9 41.3 %collective-permute-start.287 = (bf16[128,1280]{1,0:T(8,128)(2,1)}, bf16[128,1280]{1,0:T(8,128)(2,1)}, u32[]{:S(2)}, u32[]{:S(2)}) collective-permute-start(bf16[128,1280]{1,0:T(8,128)(2,1)} %constant_dynamic-slice_fusion.14), channel_id=1, source_target_pairs={{0,16},{16,0},{1,17},{17,1},{2,18},{18,2},{3,19},{19,3},{4,20},{20... | collective-permute-start | bytes 983048 | tf_op jit(solution)/shard_map/ppermute | solution.py:53
  523.6 14.9 %collective-permute-start.264 = (bf16[128,640]{1,0:T(8,128)(2,1)S(1)}, bf16[128,640]{1,0:T(8,128)(2,1)S(1)}, u32[]{:S(2)}, u32[]{:S(2)}) collective-permute-start(bf16[128,640]{1,0:T(8,128)(2,1)S(1)} %get-tuple-element.681), channel_id=1, source_target_pairs={{1,0},{2,1},{3,2},{4,3},{5,4},{6,5},{7,6},{8,7},{9,8},{10,9},{11,1... | collective-permute-start | bytes 491528 | tf_op jit(solution)/shard_map/ppermute | solution.py:136
  525.0 14.4 %collective-permute-start.262 = (bf16[128,640]{1,0:T(8,128)(2,1)S(1)}, bf16[128,640]{1,0:T(8,128)(2,1)S(1)}, u32[]{:S(2)}, u32[]{:S(2)}) collective-permute-start(bf16[128,640]{1,0:T(8,128)(2,1)S(1)} %get-tuple-element.679), channel_id=1, source_target_pairs={{32,0},{64,32},{96,64},{33,1},{65,33},{97,65},{34,2},{66,34},{98,6... | collective-permute-start | bytes 491528 | tf_op jit(solution)/shard_map/ppermute | solution.py:130
  532.7 13.5 %collective-permute-start.285 = (bf16[128,1280]{1,0:T(8,128)(2,1)S(1)}, bf16[128,1280]{1,0:T(8,128)(2,1)S(1)}, u32[]{:S(2)}, u32[]{:S(2)}) collective-permute-start(bf16[128,1280]{1,0:T(8,128)(2,1)S(1)} %constant_dynamic-slice_fusion.16), channel_id=1, source_target_pairs={{0,16},{16,0},{1,17},{17,1},{2,18},{18,2},{3,19},{19,3},{4,20},{20... | collective-permute-start | bytes 983048 | tf_op jit(solution)/shard_map/ppermute | solution.py:53
  567.6 17.8 %collective-permute-start.271 = (bf16[128,640]{1,0:T(8,128)(2,1)S(1)}, bf16[128,640]{1,0:T(8,128)(2,1)}, u32[]{:S(2)}, u32[]{:S(2)}) collective-permute-start(bf16[128,640]{1,0:T(8,128)(2,1)S(1)} %copy-done.98), channel_id=1, source_target_pairs={{0,16},{16,0},{1,17},{17,1},{2,18},{18,2},{3,19},{19,3},{4,20},{20... | collective-permute-start | bytes 491528 | tf_op jit(solution)/shard_map/ppermute | solution.py:53
  567.7 17.6 %collective-permute-start.272 = (bf16[128,640]{1,0:T(8,128)(2,1)S(1)}, bf16[128,640]{1,0:T(8,128)(2,1)}, u32[]{:S(2)}, u32[]{:S(2)}) collective-permute-start(bf16[128,640]{1,0:T(8,128)(2,1)S(1)} %copy-done.101), channel_id=1, source_target_pairs={{0,16},{16,0},{1,17},{17,1},{2,18},{18,2},{3,19},{19,3},{4,20},{20... | collective-permute-start | bytes 491528 | tf_op jit(solution)/shard_map/ppermute | solution.py:53
  584.6 17.2 %collective-permute-start.301 = (bf16[128,960]{1,0:T(8,128)(2,1)S(1)}, bf16[128,960]{1,0:T(8,128)(2,1)S(1)}, u32[]{:S(2)}, u32[]{:S(2)}) collective-permute-start(bf16[128,960]{1,0:T(8,128)(2,1)S(1)} %convert_element_type.774.refs_0_), channel_id=1, source_target_pairs={{0,64},{32,96},{64,0},{96,32},{1,65},{33,97},{65,1},{97,33},{2,66}... | collective-permute-start | bytes 737288 | tf_op jit(solution)/shard_map/ppermute | solution.py:49
  596.5 28.4 %collective-permute-start.276 = (bf16[352,960]{1,0:T(8,128)(2,1)}, bf16[352,960]{1,0:T(8,128)(2,1)}, u32[]{:S(2)}, u32[]{:S(2)}) collective-permute-start(bf16[352,960]{1,0:T(8,128)(2,1)} %get-tuple-element.669), channel_id=1, source_target_pairs={{0,96},{32,0},{64,32},{96,64},{1,97},{33,1},{65,33},{97,65},{2,98}... | collective-permute-start | bytes 2027528 | tf_op jit(solution)/shard_map/ppermute | solution.py:49
  598.9 26.0 %collective-permute-start.275 = (bf16[352,960]{1,0:T(8,128)(2,1)}, bf16[352,960]{1,0:T(8,128)(2,1)}, u32[]{:S(2)}, u32[]{:S(2)}) collective-permute-start(bf16[352,960]{1,0:T(8,128)(2,1)} %get-tuple-element.670), channel_id=1, source_target_pairs={{0,64},{32,96},{64,0},{96,32},{1,65},{33,97},{65,1},{97,33},{2,66}... | collective-permute-start | bytes 2027528 | tf_op jit(solution)/shard_map/ppermute | solution.py:49
  599.3 34.8 %collective-permute-start.274 = (bf16[352,960]{1,0:T(8,128)(2,1)S(1)}, bf16[352,960]{1,0:T(8,128)(2,1)}, u32[]{:S(2)}, u32[]{:S(2)}) collective-permute-start(bf16[352,960]{1,0:T(8,128)(2,1)S(1)} %get-tuple-element.668), channel_id=1, source_target_pairs={{0,32},{32,64},{64,96},{96,0},{1,33},{33,65},{65,97},{97,1},{2,34}... | collective-permute-start | bytes 2027528 | tf_op jit(solution)/shard_map/ppermute | solution.py:49
  607.7 42.9 %all-to-all-start.3 = ((bf16[16,24,960]{2,1,0:T(8,128)(2,1)}), bf16[16,24,960]{2,1,0:T(8,128)(2,1)S(1)}, u32[]{:S(2)}, u32[]{:S(2)}) async-start(bf16[16,24,960]{2,1,0:T(8,128)(2,1)} %bitcast.163), calls=%async_computation.6 | async-start | bytes 1572864 | tf_op jit(solution)/shard_map/all_to_all | solution.py:1164
  637.5 23.9 %collective-permute-start.279 = (bf16[112,960]{1,0:T(8,128)(2,1)}, bf16[112,960]{1,0:T(8,128)(2,1)S(1)}, u32[]{:S(2)}, u32[]{:S(2)}) collective-permute-start(bf16[112,960]{1,0:T(8,128)(2,1)} %get-tuple-element.672), channel_id=1, source_target_pairs={{0,12},{4,0},{8,4},{12,8},{1,13},{5,1},{9,5},{13,9},{2,14},{6,2},{... | collective-permute-start | bytes 645128 | tf_op jit(solution)/shard_map/ppermute | solution.py:49
  650.0 13.2 %collective-permute-start.277 = (bf16[112,960]{1,0:T(8,128)(2,1)S(1)}, bf16[112,960]{1,0:T(8,128)(2,1)}, u32[]{:S(2)}, u32[]{:S(2)}) collective-permute-start(bf16[112,960]{1,0:T(8,128)(2,1)S(1)} %get-tuple-element.671), channel_id=1, source_target_pairs={{0,4},{4,8},{8,12},{12,0},{1,5},{5,9},{9,13},{13,1},{2,6},{6,10},{... | collective-permute-start | bytes 645128 | tf_op jit(solution)/shard_map/ppermute | solution.py:49
  (331 other events, 3015.1 us)
Sparse Core Ops, SparseCore 0:
  17.5 61.1 all-gather.12
  81.8 71.6 all-gather.14
  155.9 108.0 all-gather.16
  341.1 107.4 reduce-scatter.14
  559.2 97.4 reduce-scatter.12
